TPU v7x, 512 devices: a whole 4x8x8 slice. The times are simulated.
512 devices in a mesh: pool: 2 (over core), grp: 32 (over x, z), tp: 8 (over y).
Axes of the slice: x: 4, y: 8, z: 8, core: 2. Of those that a mesh axis runs over, the one named last changes fastest.
Arguments:
- queries: bfloat16 [1024, 8192], P('grp', ('pool', 'tp')), may hold values from -6 to 6
- keys: bfloat16 [1024, 32, 256], P('grp'), may hold values from -6 to 6
- values: bfloat16 [1024, 32, 256], P('grp'), may hold values from -6 to 6
- lengths: int32 [1024], P('grp'), may hold values from 2 to 32
- out_weight: bfloat16 [8192, 7168], P(('pool', 'tp'), 'grp'), may hold values from -0.0625 to 0.0625
- residual: bfloat16 [1024, 7168], P(('pool', 'tp'), 'grp'), may hold values from -6 to 6
- norm_gain: float32 [7168], replicated, may hold values from 0.25 to 1.75
- routes: int32 [1024, 3], replicated, may hold values from 0 to 15, all different within a row; in each aligned block of 64 rows (0 to 63, 64 to 127, ...) at most 24 rows name the same one
- route_weight: float32 [1024, 3], replicated, may hold values from 0.2 to 1
- up_weight: bfloat16 [16, 7168, 4096], P(('pool', 'tp'), None, 'grp'), may hold values from -0.0625 to 0.0625
- down_weight: bfloat16 [16, 7168, 4096], P(('pool', 'tp'), 'grp'), may hold values from -0.09375 to 0.09375
Outputs:
- expert_sum: bfloat16 [1024, 7168], P(('pool', 'tp'), 'grp')
Inputs may be any that keep to these rules, and one draw needn't show every extreme that they name: `routes`: in the rows of one block, no expert is named more than 24 times, a bound that some block reaches.
All inputs are finite; a program needn't handle non-finite values.
Results may differ from a plain program's by a relative error of at most 0.029.
Values may be sent and summed in bfloat16 or wider, within the bound.
No kernel may reach another device: no remote copies, remote signals or barrier semaphores. Data moves between devices by JAX's collectives and lax.ppermute only.
A program may use at most 64 MiB of HBM per device.

v0:
```python
import jax
import jax.numpy as jnp
from jax import lax
from jax.sharding import PartitionSpec as P


def shards(
    queries,
    keys,
    values,
    lengths,
    out_weight,
    residual,
    norm_gain,
    routes,
    route_weight,
    up_weight,
    down_weight,
):
    experts = lax.axis_size(("pool", "tp"))
    block_index = lax.axis_index(("pool", "tp"))
    block_rows = residual.shape[0]
    top_count = routes.shape[1]
    slot_cap = min(block_rows, block_rows * top_count * 2 // experts)
    head_size = keys.shape[2]
    group_rows = queries.shape[0]
    head_count = queries.shape[1] // head_size
    ctx_len = keys.shape[1]
    width = norm_gain.shape[0]
    query_heads = queries.reshape(group_rows, head_count, head_size)
    scores = jnp.einsum(
        "rhd,rjd->rhj", query_heads, keys, preferred_element_type=jnp.float32
    ) * head_size ** (-0.5)
    valid = jnp.arange(ctx_len, dtype=jnp.int32)[None, None, :] < lengths[:, None, None]
    scores = jnp.where(valid, scores, -1e30)
    highest = jnp.max(scores, axis=-1, keepdims=True)
    weights = jnp.exp(scores - highest)
    probs = (weights / jnp.sum(weights, axis=-1, keepdims=True)).astype(jnp.bfloat16)
    attn = jnp.einsum("rhj,rjd->rhd", probs, values, preferred_element_type=jnp.float32)
    attn = attn.astype(jnp.bfloat16).reshape(group_rows, head_count * head_size)
    projected = jnp.dot(
        lax.all_gather(attn, "grp", axis=0, tiled=True),
        out_weight,
        preferred_element_type=jnp.float32,
    )
    own_block = lax.dynamic_slice_in_dim(
        projected, block_index * block_rows, block_rows, 0
    ) + residual.astype(jnp.float32)
    partial_value = lax.dynamic_update_slice_in_dim(
        projected, own_block, block_index * block_rows, 0
    )
    flat = routes.reshape(-1)
    pair_count = flat.shape[0]
    onehot = (flat[:, None] == jnp.arange(experts, dtype=jnp.int32)[None, :]).astype(jnp.int32)
    onehot = onehot.reshape(experts, block_rows * top_count, experts)
    earlier = jnp.cumsum(onehot, axis=1) - onehot
    position = jnp.sum(earlier * onehot, axis=2).reshape(-1)
    pair_block = jnp.arange(pair_count, dtype=jnp.int32) // (block_rows * top_count)
    slot_index = flat * (experts * slot_cap) + pair_block * slot_cap + position
    slot_pair = (
        jnp.full((experts * experts * slot_cap,), -1, jnp.int32)
        .at[slot_index]
        .set(jnp.arange(pair_count, dtype=jnp.int32))
    )
    chosen = jnp.maximum(slot_pair, 0) // top_count
    slot_input = lax.psum_scatter(
        jnp.where(slot_pair[:, None] >= 0, partial_value[chosen], 0.0).astype(jnp.bfloat16),
        ("pool", "tp"),
        scatter_dimension=0,
        tiled=True,
    )
    up_local = up_weight[0]
    down_local = down_weight[0]
    piece_f = lax.all_gather(slot_input, "grp", axis=1, tiled=True).astype(jnp.float32)
    normed = (piece_f * norm_gain[None, :]).astype(jnp.bfloat16)
    accum = jnp.dot(normed, up_local, preferred_element_type=jnp.float32)
    squares = jnp.sum(piece_f * piece_f, axis=1)
    scale = lax.rsqrt(squares / width + 1e-06)
    act = jax.nn.silu(accum * scale[:, None]).astype(jnp.bfloat16)
    expert_out = lax.dot_general(
        lax.all_gather(act, "grp", axis=1, tiled=True),
        down_local,
        (((1,), (1,)), ((), ())),
        preferred_element_type=jnp.float32,
    )
    expert_out = expert_out.astype(jnp.bfloat16).reshape(experts, slot_cap, down_local.shape[0])
    returned = lax.all_to_all(expert_out, ("pool", "tp"), split_axis=0, concat_axis=0, tiled=True)
    returned = returned.reshape(experts * slot_cap, returned.shape[2])
    own_experts = lax.dynamic_slice_in_dim(
        flat, block_index * block_rows * top_count, block_rows * top_count, 0
    )
    own_position = lax.dynamic_slice_in_dim(
        position, block_index * block_rows * top_count, block_rows * top_count, 0
    )
    gathered = returned[own_experts * slot_cap + own_position].astype(jnp.float32)
    gathered = gathered.reshape(block_rows, top_count, gathered.shape[1])
    own_weight = lax.dynamic_slice_in_dim(route_weight, block_index * block_rows, block_rows, 0)
    return jnp.sum(own_weight[:, :, None] * gathered, axis=1).astype(jnp.bfloat16)


def solution(mesh):
    placed = (
        P("grp", ("pool", "tp")),
        P("grp", None, None),
        P("grp", None, None),
        P("grp"),
        P(("pool", "tp"), "grp"),
        P(("pool", "tp"), "grp"),
        P(),
        P(),
        P(),
        P(("pool", "tp"), None, "grp"),
        P(("pool", "tp"), "grp", None),
    )
    return jax.shard_map(
        shards, mesh=mesh, in_specs=placed, out_specs=P(("pool", "tp"), "grp"), check_vma=False
    )
```

profile of v0, /device:TPU:12, one launch (start us, length us, event | category | flops | bytes accessed | tf_op | source)
XLA Modules:
  0.0 421.1 jit_solution(13781770960448313379)
XLA Ops:
  6.5 0.0 copy-start
  6.5 0.0 all-gather.4.cloned.1.call-start
  6.5 0.9 iota_compare_fusion.2
  7.4 0.8 reshape.151
  8.2 1.3 fusion.19
  9.5 0.0 copy-start.2
  9.5 0.2 fusion.36
  9.7 1.6 convolution_convert_fusion
  11.3 0.6 copy.41
  11.9 0.0 all-gather.4.cloned.1.call-update
  11.9 0.0 reduce-scatter.2.cloned.1.call-start
  12.0 0.7 broadcast_multiply_fusion
  12.7 0.9 copy.29
  13.7 0.9 copy.34
  14.5 0.2 copy.28
  14.8 0.4 mul.94
  15.1 0.3 eq.23
  15.5 9.1 %reduce-window.6 = s32[16,16,2,128]{3,1,2,0:T(8,128)S(1)} reduce-window(s32[16,16,2,128]{3,1,2,0:T(8,128)S(1)} %copy_bitcast_fusion, s32[]{:T(128)} %constant.28.clone.1), window={size=1x1x1x128 pad=0_0x0_0x0_0x127_0}, to_apply=%region_0.1 | reduce-window | flops 8323072 | bytes 524292 | tf_op jit(solution)/shard_map/reduce-window
  24.5 0.1 slice.16
  24.7 0.3 copy.31
  24.9 0.1 fusion.28
  25.0 0.1 bitcast_bitcast_fusion
  25.2 0.1 fusion.21
  25.3 0.1 reshape.150
  25.4 11.8 %scatter_custom_fusion = s32[6144]{0:T(1024)S(1)} fusion(s32[3072]{0:T(1024)S(1)} %bitcast.44, s32[3072]{0:T(1024)S(1)} %iota.24, s32[]{:T(128)} %constant.30.clone.1), kind=kCustom, calls=%fused_computation.53 | custom fusion | bytes 24580 | tf_op jit(solution)/shard_map/scatter | solution.py:63
  37.3 60.7 %all-gather.4.cloned.1.call-done = bf16[1024,512]{1,0:T(8,128)(2,1)} async-done(((bf16[32,512]{1,0:T(8,128)(2,1)}), bf16[1024,512]{1,0:T(8,128)(2,1)}) %all-gather.4.cloned.1.call-update) | async-done | bytes 1048592 | tf_op jit(solution)/shard_map/all_gather | solution.py:42
  98.0 0.0 copy-done.2
  98.0 2.7 fusion.37
  100.7 1.0 convert_add_fusion
  101.7 1.9 dynamic_update_slice.3
  103.6 1.4 copy.35
  104.9 24.9 %gather_fusion = bf16[6144,224]{1,0:T(8,128)(2,1)} fusion(bf16[1024,224]{1,0:T(8,128)(2,1)S(1)} %copy.35, s32[6144]{0:T(1024)S(1)} %fusion.26), kind=kCustom, calls=%fused_computation | custom fusion | bytes 5529600 | tf_op jit(solution)/shard_map/gather | solution.py:67
  129.9 4.9 %select_convert_fusion = bf16[6144,224]{1,0:T(8,128)(2,1)} fusion(bf16[6144,224]{1,0:T(8,128)(2,1)} %gather_fusion, pred[6144]{0:T(1024)(128)(4,1)S(1)} %broadcast_compare_fusion), kind=kLoop, calls=%fused_computation.8 | loop fusion | flops 1376256 | bytes 5511168 | tf_op jit(solution)/shard_map/convert_element_type | solution.py:67
  134.7 0.0 reduce-scatter.2.cloned.1.call-update
  134.8 0.0 copy-start.3
  134.8 0.0 all-gather.6.cloned.1.call-start
  134.8 70.3 %reduce-scatter.2.cloned.1.call-done = bf16[384,224]{1,0:T(8,128)(2,1)} async-done(((bf16[6144,224]{1,0:T(8,128)(2,1)}), bf16[384,224]{1,0:T(8,128)(2,1)}) %reduce-scatter.2.cloned.1.call-update) | async-done | bytes 172048 | tf_op jit(solution)/shard_map/reduce_scatter | solution.py:66
  205.1 1.7 copy.36
  206.9 0.0 all-gather.6.cloned.1.call-update
  206.9 0.0 all-gather.8.cloned.1.call-start
  206.9 91.2 %all-gather.6.cloned.1.call-done = bf16[384,7168]{0,1:T(8,128)(2,1)} async-done(((bf16[384,224]{0,1:T(8,128)(2,1)}), bf16[384,7168]{0,1:T(8,128)(2,1)}) %all-gather.6.cloned.1.call-update) | async-done | bytes 5505040 | tf_op jit(solution)/shard_map/all_gather | solution.py:74
  298.2 0.0 copy-start.1
  298.2 4.0 fusion.2
  302.1 0.0 copy-done.3
  302.1 0.2 copy-done.1
  302.4 4.9 %multiply_convert_fusion = bf16[384,128]{1,0:T(8,128)(2,1)} fusion(bf16[1,7168,128]{2,1,0:T(8,128)(2,1)} %param.20, bf16[384,7168]{0,1:T(8,128)(2,1)S(1)} %copy-done.1, f32[7168]{0:T(1024)S(1)} %copy-done.3, f32[384]{0:T(512)S(1)} %add_rsqrt_fusion), kind=kOutput, calls=%fused_computation.31 | convolution fusion | flops 713195520 | bytes 7468544 | tf_op jit(solution)/shard_map/dot_general | solution.py:76
  307.3 0.0 all-gather.8.cloned.1.call-update
  307.3 0.3 reshape.155
  307.6 0.1 reshape.156
  307.7 84.1 %all-gather.8.cloned.1.call-done = bf16[384,4096]{1,0:T(8,128)(2,1)} async-done(((bf16[384,128]{1,0:T(8,128)(2,1)}), bf16[384,4096]{1,0:T(8,128)(2,1)}) %all-gather.8.cloned.1.call-update) | async-done | bytes 3145744 | tf_op jit(solution)/shard_map/all_gather | solution.py:81
  391.8 0.0 copy-done
  391.8 3.1 fusion.9
  394.9 0.8 copy.37
  395.7 7.3 %all-to-all-start = ((bf16[16,24,224]{2,1,0:T(8,128)(2,1)}), bf16[16,24,224]{2,1,0:T(8,128)(2,1)S(1)}, u32[]{:S(2)}, u32[]{:S(2)}) async-start(bf16[16,24,224]{2,1,0:T(8,128)(2,1)} %bitcast.5), calls=%async_computation.1 | async-start | bytes 393216 | tf_op jit(solution)/shard_map/all_to_all | solution.py:87
  403.0 0.8 constant_dynamic-slice_fusion
  403.8 0.1 copy.27
  403.9 0.1 compare_select_fusion.2
  403.9 8.7 %all-to-all-done = bf16[16,24,224]{2,1,0:T(8,128)(2,1)S(1)} async-done(((bf16[16,24,224]{2,1,0:T(8,128)(2,1)}), bf16[16,24,224]{2,1,0:T(8,128)(2,1)S(1)}, u32[]{:S(2)}, u32[]{:S(2)}) %all-to-all-start) | async-done | bytes 172064 | tf_op jit(solution)/shard_map/all_to_all | solution.py:87
  412.6 1.0 gather_fusion.1
  413.6 0.1 reshape.158
  413.7 0.9 multiply_reduce_fusion
  (10 shorter events, 0.2 us)
Async XLA Ops:
  6.5 385.3 %copy-start = (bf16[1,224,4096]{2,1,0:T(8,128)(2,1)S(1)}, bf16[1,224,4096]{2,1,0:T(8,128)(2,1)}, u32[]{:S(2)}) copy-start(bf16[1,224,4096]{2,1,0:T(8,128)(2,1)} %param.21) | copy-start | bytes 5505028
  6.5 91.5 %all-gather.4.cloned.1.call-start = ((), (), s32[]{:S(2)}) async-start(), calls=%async_computation.2 | async-start | bytes 1081344 | tf_op jit(solution)/shard_map/all_gather | solution.py:42
  9.5 88.5 %copy-start.2 = (bf16[512,224]{0,1:T(8,128)(2,1)S(1)}, bf16[512,224]{0,1:T(8,128)(2,1)}, u32[]{:S(2)}) copy-start(bf16[512,224]{0,1:T(8,128)(2,1)} %param.15) | copy-start | bytes 688132
  11.9 193.2 %reduce-scatter.2.cloned.1.call-start = ((), (), s32[]{:S(2)}) async-start(), calls=%async_computation.3 | async-start | bytes 3342336 | tf_op jit(solution)/shard_map/reduce_scatter | solution.py:66
  134.8 167.4 %copy-start.3 = (f32[7168]{0:T(1024)S(1)}, f32[7168]{0:T(1024)}, u32[]{:S(2)}) copy-start(f32[7168]{0:T(1024)} %param.17) | copy-start | bytes 86020
  134.8 163.4 %all-gather.6.cloned.1.call-start = ((), (), s32[]{:S(2)}) async-start(), calls=%async_computation.4 | async-start | bytes 5677056 | tf_op jit(solution)/shard_map/all_gather | solution.py:74
  206.9 184.9 %all-gather.8.cloned.1.call-start = ((), (), s32[]{:S(2)}) async-start(), calls=%async_computation.5 | async-start | bytes 3244032 | tf_op jit(solution)/shard_map/all_gather | solution.py:81
  298.2 4.2 copy-start.1
  395.7 16.9 %all-to-all-start = ((bf16[16,24,224]{2,1,0:T(8,128)(2,1)}), bf16[16,24,224]{2,1,0:T(8,128)(2,1)S(1)}, u32[]{:S(2)}, u32[]{:S(2)}) async-start(bf16[16,24,224]{2,1,0:T(8,128)(2,1)} %bitcast.5), calls=%async_computation.1 | async-start | bytes 393216 | tf_op jit(solution)/shard_map/all_to_all | solution.py:87
Sparse Core Ops, SparseCore 0:
  12.0 85.9 all-gather.3
  134.9 70.1 reduce-scatter.1
  208.3 89.8 all-gather.5
  307.4 84.3 all-gather.7
where the time goes:
time: 422 us; the launch traced here: 421 us
  waiting for transfers between devices  315 us (75%)
  local copies, waits for them, and re-layouts  49.6 us (12%)
  other arithmetic  22.1 us (5%)
  matrix products  13.6 us (3%)
  between operations  13.3 us (3%)
  starting transfers between devices  7.43 us (2%)
    all_gather x1, waiting for transfers between devices, shards(): lax.all_gather(slot_input, 'grp', axis=1, tiled=True).astype(jnp.float32)  91.2 us
    all_gather x1, waiting for transfers between devices, shards(): lax.all_gather(act, 'grp', axis=1, tiled=True)  84.1 us
    reduce_scatter x1, waiting for transfers between devices, shards(): lax.psum_scatter(jnp.where(slot_pair[:, None] >= 0, partial_value[chosen]...  70.3 us
    all_gather x1, waiting for transfers between devices, shards(): lax.all_gather(attn, 'grp', axis=0, tiled=True)  60.7 us
    gather x1, local copies, waits for them, and re-layouts, shards(): partial_value[chosen]  24.9 us
    scatter x1, local copies, waits for them, and re-layouts, shards(): slot_pair = jnp.full((experts * experts * slot_cap,), -1, jnp.int32).at[s...  11.8 us
    another operation x4, other arithmetic  9.3 us
    all_to_all x1, waiting for transfers between devices, shards(): lax.all_to_all(expert_out, ('pool', 'tp'), split_axis=0, concat_axis=0, t...  8.67 us
  transfers between devices with their start and end apart: 5, of which 5 were waited for; matrix products, arithmetic and copies ran while one was open for 6% of the time, Pallas kernels for 0%

commit v1 on v0

v1 whole, which is shorter than its diff:
```python
import jax
import jax.numpy as jnp
from jax import lax
from jax.sharding import PartitionSpec as P

BF16 = jnp.bfloat16
F32 = jnp.float32
NX, NZ, PAIR = 4, 4, 2
GATHER = [[x * 8 + z * 2 + m for z in range(NZ)] for x in range(NX) for m in range(PAIR)]
REDUCE = [[x * 8 + z * 2 + m for x in range(NX) for m in range(PAIR)] for z in range(NZ)]


def spread(value, count, axis, groups=None):
    sent = jnp.broadcast_to(value[None], (count,) + value.shape)
    return lax.all_to_all(sent, axis, 0, 0, tiled=True, axis_index_groups=groups)


def exchange(value, axis, groups=None):
    return lax.all_to_all(value, axis, 0, 0, tiled=True, axis_index_groups=groups)


def attend(queries, keys, values, lengths):
    group_rows, ctx_len, head_size = keys.shape
    query_heads = queries.reshape(group_rows, -1, head_size)
    scores = jnp.einsum("rhd,rjd->rhj", query_heads, keys, preferred_element_type=F32)
    scores = scores * head_size ** (-0.5)
    valid = jnp.arange(ctx_len, dtype=jnp.int32)[None, None, :] < lengths[:, None, None]
    scores = jnp.where(valid, scores, -1e30)
    highest = jnp.max(scores, axis=-1, keepdims=True)
    weights = jnp.exp(scores - highest)
    probs = (weights / jnp.sum(weights, axis=-1, keepdims=True)).astype(BF16)
    attn = jnp.einsum("rhj,rjd->rhd", probs, values, preferred_element_type=F32)
    return attn.astype(BF16).reshape(queries.shape)


def shards(
    queries,
    keys,
    values,
    lengths,
    out_weight,
    residual,
    norm_gain,
    routes,
    route_weight,
    up_weight,
    down_weight,
):
    experts = lax.axis_size(("pool", "tp"))
    groups = lax.axis_size("grp")
    block_index = lax.axis_index(("pool", "tp"))
    pool_index = lax.axis_index("pool")
    group_index = lax.axis_index("grp")
    x_index, member = group_index // (NZ * PAIR), group_index % PAIR
    rows, columns = residual.shape
    top_count = routes.shape[1]
    slot_cap = min(rows, rows * top_count * 2 // experts)
    slots = experts * slot_cap
    width = norm_gain.shape[0]
    units = up_weight.shape[2]
    parts = NX * PAIR

    own_routes = lax.dynamic_slice_in_dim(routes, block_index * rows, rows, 0)
    own_weight = lax.dynamic_slice_in_dim(route_weight, block_index * rows, rows, 0)
    named = own_routes.T[:, None, :] == jnp.arange(experts, dtype=jnp.int32)[None, :, None]
    weight_of = jnp.sum(jnp.where(named, own_weight.T[:, None, :], 0.0), axis=0)
    named = jnp.any(named, axis=0)
    earlier = jnp.arange(rows)[:, None] < jnp.arange(rows)[None, :]
    place = jnp.dot(named.astype(BF16), earlier.astype(BF16), preferred_element_type=F32)
    here = place.astype(jnp.int32)[:, None, :] == jnp.arange(slot_cap, dtype=jnp.int32)[None, :, None]
    here = jnp.logical_and(here, named[:, None, :])
    select = here.astype(BF16).reshape(slots, rows)
    combine = jnp.where(here, weight_of[:, None, :], 0.0).reshape(slots, rows)

    attn = attend(queries, keys, values, lengths)
    attn = spread(attn, groups, "grp").reshape(groups * attn.shape[0], attn.shape[1])

    up_parts = up_weight[0].reshape(NX, NZ, PAIR, columns, units).transpose(0, 2, 1, 3, 4)
    down_parts = down_weight[0].reshape(columns, NX, NZ, PAIR, units).transpose(1, 3, 2, 0, 4)
    both = jnp.concatenate(
        [up_parts.reshape(parts, NZ * columns, units), down_parts.reshape(parts, NZ * columns, units)],
        axis=1,
    )
    attn, both = lax.optimization_barrier((attn, both))
    both = exchange(both, "grp", REDUCE)
    up_own = both[:, : NZ * columns].transpose(1, 0, 2).reshape(NZ * columns, parts * units)
    down_own = both[:, NZ * columns :].reshape(parts, NZ, columns, units).transpose(0, 2, 1, 3)
    down_own = down_own.reshape(parts * columns, NZ * units)

    projected = jnp.dot(attn, out_weight, preferred_element_type=F32).astype(BF16)
    projected = projected.reshape(2, experts // 2 * rows, columns)
    kept = lax.dynamic_index_in_dim(projected, pool_index, 0, keepdims=False)
    sent = lax.dynamic_index_in_dim(projected, 1 - pool_index, 0, keepdims=False)
    got = lax.ppermute(sent, "pool", [(0, 1), (1, 0)])
    pair_sum = (kept.astype(F32) + got.astype(F32)).astype(BF16).reshape(experts // 2, rows, columns)
    hidden = jnp.sum(exchange(pair_sum, "tp").astype(F32), axis=0) + residual.astype(F32)
    hidden = hidden.astype(BF16)

    slot_rows = jnp.dot(select, hidden, preferred_element_type=F32).astype(BF16)
    slot_rows = exchange(slot_rows.reshape(experts, slot_cap, columns), ("pool", "tp"))
    slot_rows = spread(slot_rows.reshape(slots, columns), NZ, "grp", GATHER).astype(F32)
    gain = norm_gain.reshape(NX, NZ, PAIR, columns)
    gain = lax.dynamic_index_in_dim(gain, x_index, 0, keepdims=False)
    gain = lax.dynamic_index_in_dim(gain, member, 1, keepdims=False)
    normed = (slot_rows * gain[:, None, :]).astype(BF16)
    normed = normed.transpose(1, 0, 2).reshape(slots, NZ * columns)
    squares = jnp.sum(slot_rows * slot_rows, axis=(0, 2)).reshape(slots // units, units)
    high = lax.reduce_precision(squares, 8, 7)
    low = squares - high
    pad = jnp.zeros((16 - 2 * (slots // units), units), F32)
    tail = jnp.concatenate([high, low, pad], axis=0).astype(BF16)
    partial_up = jnp.dot(normed, up_own, preferred_element_type=F32).astype(BF16)
    partial_up = partial_up.reshape(slots, parts, units).transpose(1, 0, 2)
    partial_up = jnp.concatenate(
        [partial_up, jnp.broadcast_to(tail[None], (parts,) + tail.shape)], axis=1
    )
    total_up = jnp.sum(exchange(partial_up, "grp", REDUCE).astype(F32), axis=0)
    count = slots // units
    squares = (total_up[slots : slots + count] + total_up[slots + count : slots + 2 * count]).reshape(slots, 1)
    scale = lax.rsqrt(squares / width + 1e-06)
    act = jax.nn.silu(total_up[:slots] * scale).astype(BF16)

    act = spread(act, NZ, "grp", GATHER).transpose(1, 0, 2).reshape(slots, NZ * units)
    partial_out = lax.dot_general(
        down_own, act, (((1,), (1,)), ((), ())), preferred_element_type=F32
    ).astype(BF16)
    partial_out = exchange(partial_out.reshape(parts, columns, slots), "grp", REDUCE)
    expert_out = jnp.sum(partial_out.astype(F32), axis=0).astype(BF16).T
    returned = exchange(expert_out.reshape(experts, slot_cap, columns), ("pool", "tp"))
    returned = returned.reshape(slots, columns)
    high = lax.reduce_precision(combine, 8, 7)
    dims = (((0,), (0,)), ((), ()))
    result = lax.dot_general(high.astype(BF16), returned, dims, preferred_element_type=F32)
    result += lax.dot_general((combine - high).astype(BF16), returned, dims, preferred_element_type=F32)
    return result.astype(BF16)


def solution(mesh):
    placed = (
        P("grp", ("pool", "tp")),
        P("grp", None, None),
        P("grp", None, None),
        P("grp"),
        P(("pool", "tp"), "grp"),
        P(("pool", "tp"), "grp"),
        P(),
        P(),
        P(),
        P(("pool", "tp"), None, "grp"),
        P(("pool", "tp"), "grp", None),
    )
    return jax.shard_map(
        shards, mesh=mesh, in_specs=placed, out_specs=P(("pool", "tp"), "grp"), check_vma=False
    )
```

time: 422 us -> 239 us (0.57)
  the two profiles are of different devices: /device:TPU:12 before, /device:TPU:8 now
where the time goes in v1:
time: 239 us; the launch traced here: 238 us
  waiting for transfers between devices  88.9 us (37%)
  blocking collectives  74.5 us (31%)
  starting transfers between devices  35.2 us (15%)
  local copies, waits for them, and re-layouts  23.8 us (10%)
  matrix products  9.82 us (4%)
  other arithmetic  5.58 us (2%)
    all_to_all x3, waiting for transfers between devices, exchange(): lax.all_to_all(value, axis, 0, 0, tiled=True, axis_index_groups=groups)  59.3 us
    all_to_all x3, blocking collectives, exchange(): lax.all_to_all(value, axis, 0, 0, tiled=True, axis_index_groups=groups)  51.4 us
    all_to_all x2, waiting for transfers between devices, spread(): lax.all_to_all(sent, axis, 0, 0, tiled=True, axis_index_groups=groups)  28.3 us
    all_to_all x1, blocking collectives, spread(): lax.all_to_all(sent, axis, 0, 0, tiled=True, axis_index_groups=groups)  23 us
    all_to_all x2, starting transfers between devices, spread(): lax.all_to_all(sent, axis, 0, 0, tiled=True, axis_index_groups=groups)  16.7 us
    all_to_all x3, starting transfers between devices, exchange(): lax.all_to_all(value, axis, 0, 0, tiled=True, axis_index_groups=groups)  16.6 us
  transfers between devices with their start and end apart: 6, of which 6 were waited for; matrix products, arithmetic and copies ran while one was open for 6% of the time, Pallas kernels for 0%

profile of v1, /device:TPU:8, one launch (start us, length us, event | category | flops | bytes accessed | tf_op | source)
XLA Modules:
  0.0 238.1 jit_solution(17591610480484466152)
XLA Ops:
  0.0 0.0 copy-start
  0.0 0.8 reshape.144
  0.8 0.7 iota_compare_fusion.4
  1.6 1.3 fusion.10
  2.9 0.2 fusion.34
  3.1 0.0 copy-done
  3.1 0.6 convolution_convert_fusion.4
  3.6 0.0 copy-start.1
  3.7 1.1 broadcast_in_dim.86
  4.8 13.2 %all-to-all-start = ((bf16[32,32,512]{2,1,0:T(8,128)(2,1)}), bf16[32,32,512]{2,1,0:T(8,128)(2,1)S(1)}, u32[]{:S(2)}, u32[]{:S(2)}) async-start(bf16[32,32,512]{2,1,0:T(8,128)(2,1)} %broadcast_in_dim.86), calls=%async_computation | async-start | bytes 2097152 | tf_op jit(solution)/shard_map/all_to_all | solution.py:15
  18.0 0.0 copy-done.1
  18.0 2.3 reshape_squeeze.7
  20.3 2.3 copy.43
  22.6 1.4 copy.42
  24.0 3.6 %pad_maximum_fusion = bf16[8,1792,128]{2,1,0:T(8,128)(2,1)} fusion(bf16[8,896,128]{2,1,0:T(8,128)(2,1)S(1)} %bitcast.90, bf16[8,896,128]{2,1,0:T(8,128)(2,1)} %bitcast.91), kind=kLoop, calls=%fused_computation.1 | loop fusion | flops 7340032 | bytes 7340032 | tf_op jit(solution)/shard_map/concatenate | solution.py:80
  27.6 19.0 %all-to-all-done = bf16[32,32,512]{2,1,0:T(8,128)(2,1)S(1)} async-done(((bf16[32,32,512]{2,1,0:T(8,128)(2,1)}), bf16[32,32,512]{2,1,0:T(8,128)(2,1)S(1)}, u32[]{:S(2)}, u32[]{:S(2)}) %all-to-all-start) | async-done | bytes 1048608 | tf_op jit(solution)/shard_map/all_to_all | solution.py:15
  46.6 1.4 convolution_convert_fusion.2
  48.0 0.3 reshape.150
  48.3 1.0 constant_dynamic-slice_fusion.2
  49.3 0.0 copy-start.3
  49.4 1.9 collective-permute-start
  51.3 0.1 eq.50
  51.4 1.3 collective-permute-done
  52.7 0.1 fusion.11
  52.8 0.8 copy.47
  53.6 7.5 %all-to-all-start.2 = ((bf16[8,64,224]{2,1,0:T(8,128)(2,1)}), bf16[8,64,224]{2,1,0:T(8,128)(2,1)S(1)}, u32[]{:S(2)}, u32[]{:S(2)}) async-start(bf16[8,64,224]{2,1,0:T(8,128)(2,1)} %bitcast.14), calls=%async_computation.2 | async-start | bytes 524288 | tf_op jit(solution)/shard_map/all_to_all | solution.py:19
  61.2 0.8 dynamic-slice_bitcast_fusion.1
  62.0 0.1 convolution_convert_fusion.5
  62.1 0.1 fusion.14
  62.2 9.7 %all-to-all-done.2 = bf16[8,64,224]{2,1,0:T(8,128)(2,1)S(1)} async-done(((bf16[8,64,224]{2,1,0:T(8,128)(2,1)}), bf16[8,64,224]{2,1,0:T(8,128)(2,1)S(1)}, u32[]{:S(2)}, u32[]{:S(2)}) %all-to-all-start.2) | async-done | bytes 229408 | tf_op jit(solution)/shard_map/all_to_all | solution.py:19
  72.0 0.2 convolution_convert_fusion.3
  72.2 0.1 copy.48
  72.4 13.5 %all_to_all.45 = bf16[16,24,224]{2,1,0:T(8,128)(2,1)S(1)} all-to-all(bf16[16,24,224]{2,1,0:T(8,128)(2,1)S(1)} %bitcast.99), channel_id=1, replica_groups=mesh['pool'=2,'grp'=32,'tp'=8] {'pool','tp'}, dimensions={0} | all-to-all | bytes 344064 | tf_op jit(solution)/shard_map/all_to_all | solution.py:19
  85.9 0.1 copy.49
  86.0 0.1 broadcast_in_dim.88
  86.1 23.0 %all_to_all.46 = bf16[4,384,224]{1,2,0:T(8,128)(2,1)S(1)} all-to-all(bf16[4,384,224]{1,2,0:T(8,128)(2,1)S(1)} %broadcast_in_dim.88), channel_id=1, replica_groups={{0,16,32,48},{8,24,40,56},{64,80,96,112},{72,88,104,120},{128,144,160,1..., dimensions={0} | all-to-all | bytes 1376256 | tf_op jit(solution)/shard_map/all_to_all | solution.py:15
  109.1 4.6 %all-to-all-start.1 = ((bf16[8,1792,128]{2,1,0:T(8,128)(2,1)}), bf16[8,1792,128]{2,1,0:T(8,128)(2,1)}, u32[]{:S(2)}, u32[]{:S(2)}) async-start(bf16[8,1792,128]{2,1,0:T(8,128)(2,1)} %pad_maximum_fusion), calls=%async_computation.1 | async-start | bytes 7340032 | tf_op jit(solution)/shard_map/all_to_all | solution.py:19
  113.8 0.1 reshape.153
  114.0 0.1 pad.4.clone
  114.0 0.2 fusion.3
  114.3 0.1 maximum_maximum_fusion
  114.4 40.8 %all-to-all-done.1 = bf16[8,1792,128]{2,1,0:T(8,128)(2,1)} async-done(((bf16[8,1792,128]{2,1,0:T(8,128)(2,1)}), bf16[8,1792,128]{2,1,0:T(8,128)(2,1)}, u32[]{:S(2)}, u32[]{:S(2)}) %all-to-all-start.1) | async-done | bytes 3670048 | tf_op jit(solution)/shard_map/all_to_all | solution.py:19
  155.1 3.6 %fusion.33 = (bf16[8,896,128]{2,1,0:T(8,128)(2,1)S(1)}, bf16[896,8,128]{2,0,1:T(8,128)(2,1)}) fusion(bf16[8,1792,128]{2,1,0:T(8,128)(2,1)} %all-to-all-done.1), kind=kLoop, calls=%fused_computation.74 | loop fusion | bytes 7340032 | tf_op jit(solution)/shard_map/slice | solution.py:87
  158.8 3.8 %copy.50 = bf16[896,8,128]{0,2,1:T(8,128)(2,1)} copy(bf16[896,8,128]{2,0,1:T(8,128)(2,1)} %get-tuple-element.10) | data formatting | bytes 3670016 | tf_op jit(solution)/shard_map/transpose | solution.py:86
  162.5 2.5 %fusion.5 = bf16[48,8,8,128]{3,2,1,0:T(8,128)(2,1)S(1)} fusion(bf16[384,896]{0,1:T(8,128)(2,1)S(1)} %bitcast.101, bf16[896,1024]{0,1:T(8,128)(2,1)} %bitcast.97), kind=kOutput, calls=%fused_computation.12 | convolution fusion | flops 705036288 | bytes 3309568 | tf_op jit(solution)/shard_map/dot_general | solution.py:112
  165.1 0.1 copy.70
  165.2 0.1 pad_maximum_fusion.1
  165.3 16.1 %all_to_all.47 = bf16[8,400,128]{2,1,0:T(8,128)(2,1)S(1)} all-to-all(bf16[8,400,128]{2,1,0:T(8,128)(2,1)S(1)} %pad_maximum_fusion.1), channel_id=1, replica_groups={{0,8,64,72,128,136,192,200},{16,24,80,88,144,152,208,216},{32,40,96,104..., dimensions={0} | all-to-all | bytes 1638400 | tf_op jit(solution)/shard_map/all_to_all | solution.py:19
  181.4 0.1 convert_reduce_fusion
  181.5 0.1 multiply_convert_fusion
  181.7 0.1 copy.52
  181.8 0.8 broadcast_in_dim.91
  182.6 3.5 %all-to-all-start.6 = ((bf16[4,384,128]{1,2,0:T(8,128)(2,1)}), bf16[4,384,128]{1,2,0:T(8,128)(2,1)S(1)}, u32[]{:S(2)}, u32[]{:S(2)}) async-start(bf16[4,384,128]{1,2,0:T(8,128)(2,1)} %broadcast_in_dim.91), calls=%async_computation.6 | async-start | bytes 786432 | tf_op jit(solution)/shard_map/all_to_all | solution.py:15
  186.1 2.2 copy.44
  188.3 9.3 %all-to-all-done.6 = bf16[4,384,128]{1,2,0:T(8,128)(2,1)S(1)} async-done(((bf16[4,384,128]{1,2,0:T(8,128)(2,1)}), bf16[4,384,128]{1,2,0:T(8,128)(2,1)S(1)}, u32[]{:S(2)}, u32[]{:S(2)}) %all-to-all-start.6) | async-done | bytes 393248 | tf_op jit(solution)/shard_map/all_to_all | solution.py:15
  197.6 2.6 %convolution_convert_fusion = bf16[1792,384]{1,0:T(8,128)(2,1)S(1)} fusion(bf16[384,512]{0,1:T(8,128)(2,1)S(1)} %bitcast.103, bf16[224,8,4,128]{3,2,1,0:T(4,128)(2,1)} %bitcast.96), kind=kOutput, calls=%fused_computation.2 | convolution fusion | flops 705331200 | bytes 3604480 | tf_op jit(solution)/shard_map/dot_general | solution.py:124
  200.2 21.8 %all_to_all.48 = bf16[8,224,384]{2,1,0:T(8,128)(2,1)S(1)} all-to-all(bf16[8,224,384]{2,1,0:T(8,128)(2,1)S(1)} %bitcast.98), channel_id=1, replica_groups={{0,8,64,72,128,136,192,200},{16,24,80,88,144,152,208,216},{32,40,96,104..., dimensions={0} | all-to-all | bytes 2752512 | tf_op jit(solution)/shard_map/all_to_all | solution.py:19
  222.0 0.2 reduce_sum.62
  222.2 0.8 copy.53
  223.1 4.4 %all-to-all-start.8 = ((bf16[16,24,224]{2,1,0:T(8,128)(2,1)}), bf16[16,24,224]{2,1,0:T(8,128)(2,1)S(1)}, u32[]{:S(2)}, u32[]{:S(2)}) async-start(bf16[16,24,224]{2,1,0:T(8,128)(2,1)} %bitcast.28), calls=%async_computation.8 | async-start | bytes 393216 | tf_op jit(solution)/shard_map/all_to_all | solution.py:19
  227.5 0.8 dynamic-slice_bitcast_fusion
  228.2 8.8 %all-to-all-done.8 = bf16[16,24,224]{2,1,0:T(8,128)(2,1)S(1)} async-done(((bf16[16,24,224]{2,1,0:T(8,128)(2,1)}), bf16[16,24,224]{2,1,0:T(8,128)(2,1)S(1)}, u32[]{:S(2)}, u32[]{:S(2)}) %all-to-all-start.8) | async-done | bytes 172064 | tf_op jit(solution)/shard_map/all_to_all | solution.py:19
  237.1 0.2 convolution_bitcast_fusion.1
  237.3 0.8 fusion.7
  (17 shorter events, 0.2 us)
Async XLA Ops:
  0.0 3.1 %copy-start = (bf16[32,32,256]{2,1,0:T(8,128)(2,1)S(1)}, bf16[32,32,256]{2,1,0:T(8,128)(2,1)}, u32[]{:S(2)}) copy-start(bf16[32,32,256]{2,1,0:T(8,128)(2,1)} %param.13) | copy-start | bytes 1572868
  3.6 14.3 %copy-start.1 = (bf16[1,224,4096]{2,1,0:T(8,128)(2,1)S(1)}, bf16[1,224,4096]{2,1,0:T(8,128)(2,1)}, u32[]{:S(2)}) copy-start(bf16[1,224,4096]{2,1,0:T(8,128)(2,1)} %param.21) | copy-start | bytes 5505028
  4.8 41.8 %all-to-all-start = ((bf16[32,32,512]{2,1,0:T(8,128)(2,1)}), bf16[32,32,512]{2,1,0:T(8,128)(2,1)S(1)}, u32[]{:S(2)}, u32[]{:S(2)}) async-start(bf16[32,32,512]{2,1,0:T(8,128)(2,1)} %broadcast_in_dim.86), calls=%async_computation | async-start | bytes 2097152 | tf_op jit(solution)/shard_map/all_to_all | solution.py:15
  20.3 2.3 copy-start.2
  49.3 22.7 %copy-start.3 = (bf16[64,224]{1,0:T(8,128)(2,1)S(1)}, bf16[64,224]{1,0:T(8,128)(2,1)}, u32[]{:S(2)}) copy-start(bf16[64,224]{1,0:T(8,128)(2,1)} %param.16) | copy-start | bytes 86020
  49.4 3.4 %collective-permute-start = (bf16[512,224]{0,1:T(8,128)(2,1)S(1)}, bf16[512,224]{0,1:T(8,128)(2,1)S(1)}, u32[]{:S(2)}, u32[]{:S(2)}) collective-permute-start(bf16[512,224]{0,1:T(8,128)(2,1)S(1)} %bitcast.104), channel_id=1, source_target_pairs={{0,256},{256,0},{1,257},{257,1},{2,258},{258,2},{3,259},{259,3},{4... | collective-permute-start | bytes 688136 | tf_op jit(solution)/shard_map/ppermute | solution.py:94
  53.6 18.3 %all-to-all-start.2 = ((bf16[8,64,224]{2,1,0:T(8,128)(2,1)}), bf16[8,64,224]{2,1,0:T(8,128)(2,1)S(1)}, u32[]{:S(2)}, u32[]{:S(2)}) async-start(bf16[8,64,224]{2,1,0:T(8,128)(2,1)} %bitcast.14), calls=%async_computation.2 | async-start | bytes 524288 | tf_op jit(solution)/shard_map/all_to_all | solution.py:19
  109.1 4.7 %copy-start.4 = (f32[7168]{0:T(1024)S(1)}, f32[7168]{0:T(1024)}, u32[]{:S(2)}) copy-start(f32[7168]{0:T(1024)} %param.17) | copy-start | bytes 86020
  109.1 46.0 %all-to-all-start.1 = ((bf16[8,1792,128]{2,1,0:T(8,128)(2,1)}), bf16[8,1792,128]{2,1,0:T(8,128)(2,1)}, u32[]{:S(2)}, u32[]{:S(2)}) async-start(bf16[8,1792,128]{2,1,0:T(8,128)(2,1)} %pad_maximum_fusion), calls=%async_computation.1 | async-start | bytes 7340032 | tf_op jit(solution)/shard_map/all_to_all | solution.py:19
  182.6 15.0 %all-to-all-start.6 = ((bf16[4,384,128]{1,2,0:T(8,128)(2,1)}), bf16[4,384,128]{1,2,0:T(8,128)(2,1)S(1)}, u32[]{:S(2)}, u32[]{:S(2)}) async-start(bf16[4,384,128]{1,2,0:T(8,128)(2,1)} %broadcast_in_dim.91), calls=%async_computation.6 | async-start | bytes 786432 | tf_op jit(solution)/shard_map/all_to_all | solution.py:15
  223.1 14.0 %all-to-all-start.8 = ((bf16[16,24,224]{2,1,0:T(8,128)(2,1)}), bf16[16,24,224]{2,1,0:T(8,128)(2,1)S(1)}, u32[]{:S(2)}, u32[]{:S(2)}) async-start(bf16[16,24,224]{2,1,0:T(8,128)(2,1)} %bitcast.28), calls=%async_computation.8 | async-start | bytes 393216 | tf_op jit(solution)/shard_map/all_to_all | solution.py:19

commit v2 on v1

--- a/solution.py
+++ b/solution.py
@@ -8,6 +8,15 @@
 NX, NZ, PAIR = 4, 4, 2
 GATHER = [[x * 8 + z * 2 + m for z in range(NZ)] for x in range(NX) for m in range(PAIR)]
 REDUCE = [[x * 8 + z * 2 + m for x in range(NX) for m in range(PAIR)] for z in range(NZ)]
+
+
+def moves(by_x, by_member):
+    return [
+        (x * 8 + z * 2 + m, (x + by_x) % NX * 8 + z * 2 + (m + by_member) % PAIR)
+        for x in range(NX)
+        for z in range(NZ)
+        for m in range(PAIR)
+    ]
 
 
 def spread(value, count, axis, groups=None):
@@ -47,7 +56,6 @@
     down_weight,
 ):
     experts = lax.axis_size(("pool", "tp"))
-    groups = lax.axis_size("grp")
     block_index = lax.axis_index(("pool", "tp"))
     pool_index = lax.axis_index("pool")
     group_index = lax.axis_index("grp")
@@ -73,18 +81,29 @@
     combine = jnp.where(here, weight_of[:, None, :], 0.0).reshape(slots, rows)
 
     attn = attend(queries, keys, values, lengths)
-    attn = spread(attn, groups, "grp").reshape(groups * attn.shape[0], attn.shape[1])
+    attn = spread(attn, NZ, "grp", GATHER)
+    attn = spread(attn.reshape(-1, attn.shape[2]), parts, "grp", REDUCE)
+    attn = attn.reshape(NX, PAIR, NZ, -1, attn.shape[2]).transpose(0, 2, 1, 3, 4)
+    attn = attn.reshape(experts * rows, attn.shape[4])
 
-    up_parts = up_weight[0].reshape(NX, NZ, PAIR, columns, units).transpose(0, 2, 1, 3, 4)
-    down_parts = down_weight[0].reshape(columns, NX, NZ, PAIR, units).transpose(1, 3, 2, 0, 4)
-    both = jnp.concatenate(
-        [up_parts.reshape(parts, NZ * columns, units), down_parts.reshape(parts, NZ * columns, units)],
-        axis=1,
-    )
-    attn, both = lax.optimization_barrier((attn, both))
-    both = exchange(both, "grp", REDUCE)
-    up_own = both[:, : NZ * columns].transpose(1, 0, 2).reshape(NZ * columns, parts * units)
-    down_own = both[:, NZ * columns :].reshape(parts, NZ, columns, units).transpose(0, 2, 1, 3)
+    up_parts = up_weight[0].reshape(NX, NZ, PAIR, columns, units)
+    down_parts = down_weight[0].reshape(columns, NX, NZ, PAIR, units).transpose(1, 2, 3, 0, 4)
+    held = []
+    for step in range(NX):
+        wanted = (x_index + step) % NX
+        block = jnp.stack(
+            [lax.dynamic_index_in_dim(w, wanted, 0, keepdims=False) for w in (up_parts, down_parts)]
+        )
+        held.append(lax.ppermute(block, "grp", moves(step, 0)) if step else block)
+    held = jnp.stack([lax.dynamic_index_in_dim(jnp.stack(held), (x_index - x) % NX, 0, False) for x in range(NX)])
+    kept = lax.dynamic_index_in_dim(held, member, 3, keepdims=False)
+    sent = lax.dynamic_index_in_dim(held, 1 - member, 3, keepdims=False)
+    got = lax.ppermute(sent, "grp", moves(0, 1))
+    first, second = jnp.where(member == 0, kept, got), jnp.where(member == 0, got, kept)
+    both = jnp.stack([first, second], axis=1)
+    up_own = both[:, :, 0].reshape(parts, NZ * columns, units).transpose(1, 0, 2)
+    up_own = up_own.reshape(NZ * columns, parts * units)
+    down_own = both[:, :, 1].reshape(parts, NZ, columns, units).transpose(0, 2, 1, 3)
     down_own = down_own.reshape(parts * columns, NZ * units)
 
     projected = jnp.dot(attn, out_weight, preferred_element_type=F32).astype(BF16)

time: 239 us -> 236 us (0.987)
  blocking collectives: 74.5 us -> 51.9 us
  starting transfers between devices: 35.2 us -> 57.2 us
  waiting for transfers between devices: 88.9 us -> 77.1 us
  other arithmetic: 5.58 us -> 11.6 us
  local copies, waits for them, and re-layouts: 23.8 us -> 29.5 us
  matrix products: 9.82 us -> 7.42 us
    all_to_all x3 -> x2, waiting for transfers between devices: 59.3 us -> 18.6 us  [exchange(): lax.all_to_all(value, axis, 0, 0, tiled=True, axis_index_groups=groups)]
    ppermute x0 -> x4, waiting for transfers between devices: none -> 37.5 us  [the longest x3 37.5 us: shards(): held.append(lax.ppermute(block, 'grp', moves(step, 0)) if step else block)]
    all_to_all x1 -> x0, blocking collectives: 23 us -> none  [spread(): lax.all_to_all(sent, axis, 0, 0, tiled=True, axis_index_groups=groups)]
    ppermute x0 -> x4, starting transfers between devices: none -> 15.3 us  [the longest x3 11.8 us: shards(): held.append(lax.ppermute(block, 'grp', moves(step, 0)) if step else block)]
    all_to_all x2 -> x4, starting transfers between devices: 16.7 us -> 26.4 us  [spread(): lax.all_to_all(sent, axis, 0, 0, tiled=True, axis_index_groups=groups)]
    another operation x1 -> x9, other arithmetic: 0.01 us -> 9.56 us  [the longest x3 4.39 us: shards(): jnp.stack([lax.dynamic_index_in_dim(w, wanted, 0, keepdims=False) for w i...]
    all_to_all x2 -> x4, waiting for transfers between devices: 28.3 us -> 20.9 us  [spread(): lax.all_to_all(sent, axis, 0, 0, tiled=True, axis_index_groups=groups)]
    concatenate x1 -> x0, other arithmetic: 3.56 us -> none  [shards(): jnp.concatenate([up_parts.reshape(parts, NZ * columns, units), down_parts...]
  transfers between devices with their start and end apart: 6 -> 11, of which waited for: 6 -> 7; matrix products, arithmetic and copies ran while one was open for 6% -> 14% of each run, Pallas kernels for 0% -> 0%
where the time goes in v2:
time: 236 us; the launch traced here: 235 us
  waiting for transfers between devices  77.1 us (33%)
  starting transfers between devices  57.2 us (24%)
  blocking collectives  51.9 us (22%)
  local copies, waits for them, and re-layouts  29.5 us (12%)
  other arithmetic  11.6 us (5%)
  matrix products  7.42 us (3%)
    all_to_all x3, blocking collectives, exchange(): lax.all_to_all(value, axis, 0, 0, tiled=True, axis_index_groups=groups)  51.9 us
    ppermute x3, waiting for transfers between devices, shards(): held.append(lax.ppermute(block, 'grp', moves(step, 0)) if step else block)  37.5 us
    all_to_all x4, starting transfers between devices, spread(): lax.all_to_all(sent, axis, 0, 0, tiled=True, axis_index_groups=groups)  26.4 us
    all_to_all x4, waiting for transfers between devices, spread(): lax.all_to_all(sent, axis, 0, 0, tiled=True, axis_index_groups=groups)  20.9 us
    all_to_all x2, waiting for transfers between devices, exchange(): lax.all_to_all(value, axis, 0, 0, tiled=True, axis_index_groups=groups)  18.6 us
    all_to_all x2, starting transfers between devices, exchange(): lax.all_to_all(value, axis, 0, 0, tiled=True, axis_index_groups=groups)  13.6 us
    ppermute x3, starting transfers between devices, shards(): held.append(lax.ppermute(block, 'grp', moves(step, 0)) if step else block)  11.8 us
  transfers between devices with their start and end apart: 11, of which 7 were waited for; matrix products, arithmetic and copies ran while one was open for 14% of the time, Pallas kernels for 0%

profile of v2, /device:TPU:8, one launch (start us, length us, event | category | flops | bytes accessed | tf_op | source)
XLA Modules:
  0.0 235.2 jit_solution(1473137193249874505)
XLA Ops:
  0.0 0.8 reshape.140
  0.8 0.7 iota_compare_fusion.4
  1.6 1.3 fusion.13
  2.9 0.2 fusion.38
  3.1 0.6 convolution_convert_fusion.4
  3.6 0.7 broadcast_in_dim.93
  4.3 10.3 %all-to-all-start = ((bf16[4,32,512]{2,1,0:T(8,128)(2,1)}), bf16[4,32,512]{2,1,0:T(8,128)(2,1)S(1)}, u32[]{:S(2)}, u32[]{:S(2)}) async-start(bf16[4,32,512]{2,1,0:T(8,128)(2,1)} %broadcast_in_dim.93), calls=%async_computation | async-start | bytes 262144 | tf_op jit(solution)/shard_map/all_to_all | solution.py:24
  14.6 4.6 %reshape_squeeze.13 = bf16[224,4,4,2,128]{4,3,2,1,0:T(2,128)(2,1)S(1)} reshape(bf16[1,224,4096]{2,1,0:T(8,128)(2,1)} %param.21) | data formatting | bytes 3670016 | tf_op jit(solution)/shard_map/reshape;squeeze | solution.py:90
  19.2 2.0 constant_dynamic-slice_fusion.13
  21.3 0.8 copy.105
  22.1 1.1 constant_dynamic-slice_fusion.14
  23.2 0.6 all-to-all-done
  23.9 1.1 broadcast_in_dim.95
  24.9 4.6 %all-to-all-start.1 = ((bf16[8,128,512]{2,1,0:T(8,128)(2,1)}), bf16[8,128,512]{2,1,0:T(8,128)(2,1)S(1)}, u32[]{:S(2)}, u32[]{:S(2)}) async-start(bf16[8,128,512]{2,1,0:T(8,128)(2,1)} %broadcast_in_dim.95), calls=%async_computation.1 | async-start | bytes 2097152 | tf_op jit(solution)/shard_map/all_to_all | solution.py:24
  29.5 2.3 pad_maximum_fusion.3
  31.8 3.9 %collective-permute-start = (bf16[2,4,2,224,128]{4,3,2,1,0:T(8,128)(2,1)}, bf16[2,4,2,224,128]{4,3,2,1,0:T(8,128)(2,1)}, u32[]{:S(2)}, u32[]{:S(2)}) collective-permute-start(bf16[2,4,2,224,128]{4,3,2,1,0:T(8,128)(2,1)} %pad_maximum_fusion.3), channel_id=1, source_target_pairs={{0,64},{8,72},{16,80},{24,88},{32,96},{40,104},{48,112},{56,120},{... | collective-permute-start | bytes 2752520 | tf_op jit(solution)/shard_map/ppermute | solution.py:97
  35.8 1.1 pad_maximum_fusion.4
  36.9 4.6 %collective-permute-start.1 = (bf16[2,4,2,224,128]{4,3,2,1,0:T(8,128)(2,1)}, bf16[2,4,2,224,128]{4,3,2,1,0:T(8,128)(2,1)}, u32[]{:S(2)}, u32[]{:S(2)}) collective-permute-start(bf16[2,4,2,224,128]{4,3,2,1,0:T(8,128)(2,1)} %pad_maximum_fusion.4), channel_id=1, source_target_pairs={{0,128},{8,136},{16,144},{24,152},{32,160},{40,168},{48,176},{56,1... | collective-permute-start | bytes 2752520 | tf_op jit(solution)/shard_map/ppermute | solution.py:97
  41.6 1.0 pad_maximum_fusion.5
  42.6 3.4 %collective-permute-start.2 = (bf16[2,4,2,224,128]{4,3,2,1,0:T(8,128)(2,1)}, bf16[2,4,2,224,128]{4,3,2,1,0:T(8,128)(2,1)}, u32[]{:S(2)}, u32[]{:S(2)}) collective-permute-start(bf16[2,4,2,224,128]{4,3,2,1,0:T(8,128)(2,1)} %pad_maximum_fusion.5), channel_id=1, source_target_pairs={{0,192},{8,200},{16,208},{24,216},{32,224},{40,232},{48,240},{56,2... | collective-permute-start | bytes 2752520 | tf_op jit(solution)/shard_map/ppermute | solution.py:97
  46.2 19.6 %collective-permute-done = bf16[2,4,2,224,128]{4,3,2,1,0:T(8,128)(2,1)} collective-permute-done((bf16[2,4,2,224,128]{4,3,2,1,0:T(8,128)(2,1)}, bf16[2,4,2,224,128]{4,3,2,1,0:T(8,128)(2,1)}, u32[]{:S(2)}, u32[]{:S(2)}) %collective-permute-start) | collective-permute-done | bytes 917536 | tf_op jit(solution)/shard_map/ppermute | solution.py:97
  65.8 17.9 %collective-permute-done.1 = bf16[2,4,2,224,128]{4,3,2,1,0:T(8,128)(2,1)} collective-permute-done((bf16[2,4,2,224,128]{4,3,2,1,0:T(8,128)(2,1)}, bf16[2,4,2,224,128]{4,3,2,1,0:T(8,128)(2,1)}, u32[]{:S(2)}, u32[]{:S(2)}) %collective-permute-start.1) | collective-permute-done | bytes 917536 | tf_op jit(solution)/shard_map/ppermute | solution.py:97
  83.8 2.0 pad_maximum_fusion
  85.7 1.6 constant_dynamic-slice_fusion.6
  87.4 0.8 copy-done.8
  88.3 0.5 convolution_convert_fusion.2
  88.8 0.3 reshape.143
  89.1 1.0 constant_dynamic-slice_fusion.2
  90.1 1.9 collective-permute-start.4
  92.1 0.5 pad_maximum_fusion.1
  92.6 1.5 dynamic-slice_bitcast_fusion
  94.1 0.8 copy-done.1
  94.9 3.5 %collective-permute-start.3 = (bf16[4,2,4,224,128]{4,3,2,1,0:T(8,128)(2,1)}, bf16[4,2,4,224,128]{4,3,2,1,0:T(8,128)(2,1)}, u32[]{:S(2)}, u32[]{:S(2)}) collective-permute-start(bf16[4,2,4,224,128]{4,3,2,1,0:T(8,128)(2,1)} %dynamic-slice_bitcast_fusion), channel_id=1, source_target_pairs={{0,8},{8,0},{16,24},{24,16},{32,40},{40,32},{48,56},{56,48},{64,72... | collective-permute-start | bytes 5505032 | tf_op jit(solution)/shard_map/ppermute | solution.py:101
  98.6 0.8 copy.70
  99.4 7.5 %all-to-all-start.2 = ((bf16[8,64,224]{2,1,0:T(8,128)(2,1)}), bf16[8,64,224]{2,1,0:T(8,128)(2,1)S(1)}, u32[]{:S(2)}, u32[]{:S(2)}) async-start(bf16[8,64,224]{2,1,0:T(8,128)(2,1)} %bitcast.25), calls=%async_computation.2 | async-start | bytes 524288 | tf_op jit(solution)/shard_map/all_to_all | solution.py:28
  107.0 0.8 fusion.30
  108.0 9.8 %all-to-all-done.2 = bf16[8,64,224]{2,1,0:T(8,128)(2,1)S(1)} async-done(((bf16[8,64,224]{2,1,0:T(8,128)(2,1)}), bf16[8,64,224]{2,1,0:T(8,128)(2,1)S(1)}, u32[]{:S(2)}, u32[]{:S(2)}) %all-to-all-start.2) | async-done | bytes 229408 | tf_op jit(solution)/shard_map/all_to_all | solution.py:28
  117.9 0.2 convolution_convert_fusion.3
  118.1 0.1 copy.71
  118.3 13.5 %all_to_all.45 = bf16[16,24,224]{2,1,0:T(8,128)(2,1)S(1)} all-to-all(bf16[16,24,224]{2,1,0:T(8,128)(2,1)S(1)} %bitcast.133), channel_id=1, replica_groups=mesh['pool'=2,'grp'=32,'tp'=8] {'pool','tp'}, dimensions={0} | all-to-all | bytes 344064 | tf_op jit(solution)/shard_map/all_to_all | solution.py:28
  131.8 0.1 copy.72
  131.9 0.9 broadcast_in_dim.97
  132.8 6.9 %all-to-all-start.4 = ((bf16[4,384,224]{1,2,0:T(8,128)(2,1)}), bf16[4,384,224]{1,2,0:T(8,128)(2,1)S(1)}, u32[]{:S(2)}, u32[]{:S(2)}) async-start(bf16[4,384,224]{1,2,0:T(8,128)(2,1)} %broadcast_in_dim.97), calls=%async_computation.4 | async-start | bytes 1376256 | tf_op jit(solution)/shard_map/all_to_all | solution.py:24
  140.0 2.3 fusion.4
  142.3 0.3 fusion.1
  142.6 1.4 copy.73
  144.0 3.8 %copy.74 = bf16[896,8,128]{0,2,1:T(8,128)(2,1)} copy(bf16[896,8,128]{2,0,1:T(8,128)(2,1)} %bitcast.120) | data formatting | bytes 3670016 | tf_op jit(solution)/shard_map/transpose | solution.py:104
  147.8 9.5 %all-to-all-done.4 = bf16[4,384,224]{1,2,0:T(8,128)(2,1)S(1)} async-done(((bf16[4,384,224]{1,2,0:T(8,128)(2,1)}), bf16[4,384,224]{1,2,0:T(8,128)(2,1)S(1)}, u32[]{:S(2)}, u32[]{:S(2)}) %all-to-all-start.4) | async-done | bytes 688160 | tf_op jit(solution)/shard_map/all_to_all | solution.py:24
  157.3 0.2 fusion.6
  157.5 2.5 %fusion.8 = bf16[48,8,8,128]{3,2,1,0:T(8,128)(2,1)S(1)} fusion(bf16[384,896]{0,1:T(8,128)(2,1)S(1)} %bitcast.135, bf16[896,1024]{0,1:T(8,128)(2,1)} %bitcast.130), kind=kOutput, calls=%fused_computation.21 | convolution fusion | flops 705036288 | bytes 3309568 | tf_op jit(solution)/shard_map/dot_general | solution.py:131
  160.4 16.0 %all_to_all.46 = bf16[8,400,128]{2,1,0:T(8,128)(2,1)S(1)} all-to-all(bf16[8,400,128]{2,1,0:T(8,128)(2,1)S(1)} %pad_maximum_fusion.6), channel_id=1, replica_groups={{0,8,64,72,128,136,192,200},{16,24,80,88,144,152,208,216},{32,40,96,104..., dimensions={0} | all-to-all | bytes 1638400 | tf_op jit(solution)/shard_map/all_to_all | solution.py:28
  176.8 0.8 broadcast_in_dim.100
  177.5 4.6 %all-to-all-start.6 = ((bf16[4,384,128]{1,2,0:T(8,128)(2,1)}), bf16[4,384,128]{1,2,0:T(8,128)(2,1)S(1)}, u32[]{:S(2)}, u32[]{:S(2)}) async-start(bf16[4,384,128]{1,2,0:T(8,128)(2,1)} %broadcast_in_dim.100), calls=%async_computation.6 | async-start | bytes 786432 | tf_op jit(solution)/shard_map/all_to_all | solution.py:24
  182.3 0.9 copy.66
  183.2 10.8 %all-to-all-done.6 = bf16[4,384,128]{1,2,0:T(8,128)(2,1)S(1)} async-done(((bf16[4,384,128]{1,2,0:T(8,128)(2,1)}), bf16[4,384,128]{1,2,0:T(8,128)(2,1)S(1)}, u32[]{:S(2)}, u32[]{:S(2)}) %all-to-all-start.6) | async-done | bytes 393248 | tf_op jit(solution)/shard_map/all_to_all | solution.py:24
  194.0 1.1 convolution_convert_fusion
  195.1 22.4 %all_to_all.47 = bf16[8,224,384]{2,1,0:T(8,128)(2,1)S(1)} all-to-all(bf16[8,224,384]{2,1,0:T(8,128)(2,1)S(1)} %bitcast.132), channel_id=1, replica_groups={{0,8,64,72,128,136,192,200},{16,24,80,88,144,152,208,216},{32,40,96,104..., dimensions={0} | all-to-all | bytes 2752512 | tf_op jit(solution)/shard_map/all_to_all | solution.py:28
  217.5 0.2 reduce_sum.62
  217.7 0.8 copy.77
  218.5 6.0 %all-to-all-start.8 = ((bf16[16,24,224]{2,1,0:T(8,128)(2,1)}), bf16[16,24,224]{2,1,0:T(8,128)(2,1)S(1)}, u32[]{:S(2)}, u32[]{:S(2)}) async-start(bf16[16,24,224]{2,1,0:T(8,128)(2,1)} %bitcast.40), calls=%async_computation.8 | async-start | bytes 393216 | tf_op jit(solution)/shard_map/all_to_all | solution.py:28
  224.6 0.8 fusion.31
  225.3 8.8 %all-to-all-done.8 = bf16[16,24,224]{2,1,0:T(8,128)(2,1)S(1)} async-done(((bf16[16,24,224]{2,1,0:T(8,128)(2,1)}), bf16[16,24,224]{2,1,0:T(8,128)(2,1)S(1)}, u32[]{:S(2)}, u32[]{:S(2)}) %all-to-all-start.8) | async-done | bytes 172064 | tf_op jit(solution)/shard_map/all_to_all | solution.py:28
  234.2 0.2 convolution_bitcast_fusion.1
  234.4 0.8 fusion.10
  (54 shorter events, 1.9 us)
Async XLA Ops:
  0.0 3.1 %copy-start = (bf16[32,32,256]{2,1,0:T(8,128)(2,1)S(1)}, bf16[32,32,256]{2,1,0:T(8,128)(2,1)}, u32[]{:S(2)}) copy-start(bf16[32,32,256]{2,1,0:T(8,128)(2,1)} %param.13) | copy-start | bytes 1572868
  4.3 19.6 %all-to-all-start = ((bf16[4,32,512]{2,1,0:T(8,128)(2,1)}), bf16[4,32,512]{2,1,0:T(8,128)(2,1)S(1)}, u32[]{:S(2)}, u32[]{:S(2)}) async-start(bf16[4,32,512]{2,1,0:T(8,128)(2,1)} %broadcast_in_dim.93), calls=%async_computation | async-start | bytes 262144 | tf_op jit(solution)/shard_map/all_to_all | solution.py:24
  19.2 2.9 %copy-start.7 = (bf16[1,7168,128]{2,1,0:T(8,128)(2,1)S(1)}, bf16[1,7168,128]{2,1,0:T(8,128)(2,1)}, u32[]{:S(2)}) copy-start(bf16[1,7168,128]{2,1,0:T(8,128)(2,1)} %param.20) | copy-start | bytes 5505028
  24.9 62.4 %all-to-all-start.1 = ((bf16[8,128,512]{2,1,0:T(8,128)(2,1)}), bf16[8,128,512]{2,1,0:T(8,128)(2,1)S(1)}, u32[]{:S(2)}, u32[]{:S(2)}) async-start(bf16[8,128,512]{2,1,0:T(8,128)(2,1)} %broadcast_in_dim.95), calls=%async_computation.1 | async-start | bytes 2097152 | tf_op jit(solution)/shard_map/all_to_all | solution.py:24
  29.5 6.2 %copy-start.5 = (bf16[224,1,4,2,128]{4,3,2,1,0:T(2,128)(2,1)S(1)}, bf16[224,1,4,2,128]{4,3,2,1,0:T(2,128)(2,1)}, u32[]{:S(2)}) copy-start(bf16[224,1,4,2,128]{4,3,2,1,0:T(2,128)(2,1)} %get-tuple-element.18) | copy-start | bytes 1376260
  29.5 6.3 %copy-start.6 = (bf16[1,4,2,224,128]{4,3,2,1,0:T(8,128)(2,1)S(1)}, bf16[1,4,2,224,128]{4,3,2,1,0:T(8,128)(2,1)}, u32[]{:S(2)}) copy-start(bf16[1,4,2,224,128]{4,3,2,1,0:T(8,128)(2,1)} %get-tuple-element.15) | copy-start | bytes 1376260
  31.8 34.0 %collective-permute-start = (bf16[2,4,2,224,128]{4,3,2,1,0:T(8,128)(2,1)}, bf16[2,4,2,224,128]{4,3,2,1,0:T(8,128)(2,1)}, u32[]{:S(2)}, u32[]{:S(2)}) collective-permute-start(bf16[2,4,2,224,128]{4,3,2,1,0:T(8,128)(2,1)} %pad_maximum_fusion.3), channel_id=1, source_target_pairs={{0,64},{8,72},{16,80},{24,88},{32,96},{40,104},{48,112},{56,120},{... | collective-permute-start | bytes 2752520 | tf_op jit(solution)/shard_map/ppermute | solution.py:97
  35.8 5.8 %copy-start.4 = (bf16[1,4,2,224,128]{4,3,2,1,0:T(8,128)(2,1)S(1)}, bf16[1,4,2,224,128]{4,3,2,1,0:T(8,128)(2,1)}, u32[]{:S(2)}) copy-start(bf16[1,4,2,224,128]{4,3,2,1,0:T(8,128)(2,1)} %get-tuple-element.14) | copy-start | bytes 1376260
  36.9 46.8 %collective-permute-start.1 = (bf16[2,4,2,224,128]{4,3,2,1,0:T(8,128)(2,1)}, bf16[2,4,2,224,128]{4,3,2,1,0:T(8,128)(2,1)}, u32[]{:S(2)}, u32[]{:S(2)}) collective-permute-start(bf16[2,4,2,224,128]{4,3,2,1,0:T(8,128)(2,1)} %pad_maximum_fusion.4), channel_id=1, source_target_pairs={{0,128},{8,136},{16,144},{24,152},{32,160},{40,168},{48,176},{56,1... | collective-permute-start | bytes 2752520 | tf_op jit(solution)/shard_map/ppermute | solution.py:97
  42.6 41.2 %collective-permute-start.2 = (bf16[2,4,2,224,128]{4,3,2,1,0:T(8,128)(2,1)}, bf16[2,4,2,224,128]{4,3,2,1,0:T(8,128)(2,1)}, u32[]{:S(2)}, u32[]{:S(2)}) collective-permute-start(bf16[2,4,2,224,128]{4,3,2,1,0:T(8,128)(2,1)} %pad_maximum_fusion.5), channel_id=1, source_target_pairs={{0,192},{8,200},{16,208},{24,216},{32,224},{40,232},{48,240},{56,2... | collective-permute-start | bytes 2752520 | tf_op jit(solution)/shard_map/ppermute | solution.py:97
  87.3 0.9 copy-start.8
  89.1 3.0 %copy-start.2 = (bf16[1,2,4,2,224,128]{5,4,3,2,1,0:T(8,128)(2,1)S(1)}, bf16[1,2,4,2,224,128]{5,4,3,2,1,0:T(8,128)(2,1)}, u32[]{:S(2)}) copy-start(bf16[1,2,4,2,224,128]{5,4,3,2,1,0:T(8,128)(2,1)} %get-tuple-element.11) | copy-start | bytes 2752516
  89.1 3.0 %copy-start.3 = (bf16[1,2,4,2,224,128]{5,4,3,2,1,0:T(8,128)(2,1)S(1)}, bf16[1,2,4,2,224,128]{5,4,3,2,1,0:T(8,128)(2,1)}, u32[]{:S(2)}) copy-start(bf16[1,2,4,2,224,128]{5,4,3,2,1,0:T(8,128)(2,1)} %get-tuple-element.12) | copy-start | bytes 2752516
  90.1 8.4 %collective-permute-start.4 = (bf16[512,224]{0,1:T(8,128)(2,1)S(1)}, bf16[512,224]{0,1:T(8,128)(2,1)S(1)}, u32[]{:S(2)}, u32[]{:S(2)}) collective-permute-start(bf16[512,224]{0,1:T(8,128)(2,1)S(1)} %bitcast.139), channel_id=1, source_target_pairs={{0,256},{256,0},{1,257},{257,1},{2,258},{258,2},{3,259},{259,3},{4... | collective-permute-start | bytes 688136 | tf_op jit(solution)/shard_map/ppermute | solution.py:113
  92.6 2.3 copy-start.1
  94.9 22.9 %copy-start.9 = (bf16[64,224]{1,0:T(8,128)(2,1)S(1)}, bf16[64,224]{1,0:T(8,128)(2,1)}, u32[]{:S(2)}) copy-start(bf16[64,224]{1,0:T(8,128)(2,1)} %param.16) | copy-start | bytes 86020
  94.9 45.1 %collective-permute-start.3 = (bf16[4,2,4,224,128]{4,3,2,1,0:T(8,128)(2,1)}, bf16[4,2,4,224,128]{4,3,2,1,0:T(8,128)(2,1)}, u32[]{:S(2)}, u32[]{:S(2)}) collective-permute-start(bf16[4,2,4,224,128]{4,3,2,1,0:T(8,128)(2,1)} %dynamic-slice_bitcast_fusion), channel_id=1, source_target_pairs={{0,8},{8,0},{16,24},{24,16},{32,40},{40,32},{48,56},{56,48},{64,72... | collective-permute-start | bytes 5505032 | tf_op jit(solution)/shard_map/ppermute | solution.py:101
  99.4 18.4 %all-to-all-start.2 = ((bf16[8,64,224]{2,1,0:T(8,128)(2,1)}), bf16[8,64,224]{2,1,0:T(8,128)(2,1)S(1)}, u32[]{:S(2)}, u32[]{:S(2)}) async-start(bf16[8,64,224]{2,1,0:T(8,128)(2,1)} %bitcast.25), calls=%async_computation.2 | async-start | bytes 524288 | tf_op jit(solution)/shard_map/all_to_all | solution.py:28
  117.8 21.9 %copy-start.10 = (f32[7168]{0:T(1024)S(1)}, f32[7168]{0:T(1024)}, u32[]{:S(2)}) copy-start(f32[7168]{0:T(1024)} %param.17) | copy-start | bytes 86020
  132.8 24.4 %all-to-all-start.4 = ((bf16[4,384,224]{1,2,0:T(8,128)(2,1)}), bf16[4,384,224]{1,2,0:T(8,128)(2,1)S(1)}, u32[]{:S(2)}, u32[]{:S(2)}) async-start(bf16[4,384,224]{1,2,0:T(8,128)(2,1)} %broadcast_in_dim.97), calls=%async_computation.4 | async-start | bytes 1376256 | tf_op jit(solution)/shard_map/all_to_all | solution.py:24
  177.5 16.5 %all-to-all-start.6 = ((bf16[4,384,128]{1,2,0:T(8,128)(2,1)}), bf16[4,384,128]{1,2,0:T(8,128)(2,1)S(1)}, u32[]{:S(2)}, u32[]{:S(2)}) async-start(bf16[4,384,128]{1,2,0:T(8,128)(2,1)} %broadcast_in_dim.100), calls=%async_computation.6 | async-start | bytes 786432 | tf_op jit(solution)/shard_map/all_to_all | solution.py:24
  218.5 15.6 %all-to-all-start.8 = ((bf16[16,24,224]{2,1,0:T(8,128)(2,1)}), bf16[16,24,224]{2,1,0:T(8,128)(2,1)S(1)}, u32[]{:S(2)}, u32[]{:S(2)}) async-start(bf16[16,24,224]{2,1,0:T(8,128)(2,1)} %bitcast.40), calls=%async_computation.8 | async-start | bytes 393216 | tf_op jit(solution)/shard_map/all_to_all | solution.py:28

commit v3 on v2

--- a/solution.py
+++ b/solution.py
@@ -1,12 +1,16 @@
 import jax
 import jax.numpy as jnp
 from jax import lax
+from jax.experimental import pallas as pl
+from jax.experimental.pallas import tpu as pltpu
 from jax.sharding import PartitionSpec as P
 
 BF16 = jnp.bfloat16
 F32 = jnp.float32
 NX, NZ, PAIR = 4, 4, 2
 GATHER = [[x * 8 + z * 2 + m for z in range(NZ)] for x in range(NX) for m in range(PAIR)]
+LINE = [[x * 8 + z for z in range(8)] for x in range(NX)]
+CROSS = [[x * 8 + z for x in range(NX)] for z in range(8)]
 REDUCE = [[x * 8 + z * 2 + m for x in range(NX) for m in range(PAIR)] for z in range(NZ)]
 
 
@@ -26,6 +30,87 @@
 
 def exchange(value, axis, groups=None):
     return lax.all_to_all(value, axis, 0, 0, tiled=True, axis_index_groups=groups)
+
+
+def up_kernel(place, rows, gain, block0, block1, block2, block3, got, out):
+    x_index, member = place[0], place[1]
+    slots, units = rows.shape[1], out.shape[2]
+    normed, squares = [], 0.0
+    ones = jnp.ones((16, rows.shape[2]), BF16)
+    dims = (((1,), (1,)), ((), ()))
+    for z in range(NZ):
+        value = rows[z].astype(F32)
+        normed.append((value * gain[z][None, :]).astype(BF16))
+        square = value * value
+        high = square.astype(BF16)
+        low = (square - high.astype(F32)).astype(BF16)
+        squares += lax.dot_general(ones, high, dims, preferred_element_type=F32)
+        squares += lax.dot_general(ones, low, dims, preferred_element_type=F32)
+    row = lax.broadcasted_iota(jnp.int32, (16, units), 0)
+    count = slots // units
+    tail = jnp.zeros((16, units), F32)
+    for i in range(count):
+        part = squares[:, i * units : (i + 1) * units]
+        high = part.astype(BF16).astype(F32)
+        tail = jnp.where(row == i, high, tail)
+        tail = jnp.where(row == count + i, part - high, tail)
+    tail = tail.astype(BF16)
+    for step, block in enumerate((block0, block1, block2, block3)):
+        total = 0.0
+        for z in range(NZ):
+            both = jnp.concatenate([block[z, member], got[step, z]], axis=1)
+            total += jnp.dot(normed[z], both, preferred_element_type=F32)
+        total = total.astype(BF16)
+        first = lax.rem(x_index + NX - step, NX) * PAIR
+        for target, part in ((first + member, total[:, :units]), (first + 1 - member, total[:, units:])):
+            out[target, :slots] = part
+            out[target, slots:] = tail
+
+
+def up_product(place, rows, gain, blocks, got):
+    slots, columns = rows.shape[1:]
+    units = got.shape[3]
+    vmem = pl.BlockSpec(memory_space=pltpu.VMEM)
+    return pl.pallas_call(
+        up_kernel,
+        out_shape=jax.ShapeDtypeStruct((NX * PAIR, slots + 16, units), BF16),
+        in_specs=[pl.BlockSpec(memory_space=pltpu.SMEM)] + [vmem] * 7,
+        out_specs=vmem,
+        compiler_params=pltpu.CompilerParams(vmem_limit_bytes=40 * 2**20),
+        cost_estimate=pl.CostEstimate(
+            flops=2 * slots * columns * NZ * NX * PAIR * units, bytes_accessed=6 * 2**20, transcendentals=0
+        ),
+    )(place, rows, gain, *blocks, got)
+
+
+def down_kernel(place, act, block0, block1, block2, block3, out):
+    x_index = place[0]
+    count = act.shape[0]
+    dims = (((1,), (1,)), ((), ()))
+    units = act.shape[2]
+    joined = [jnp.concatenate([act[z], act[z + 1]], axis=1) for z in range(0, count, 2)]
+    for step, block in enumerate((block0, block1, block2, block3)):
+        total = 0.0
+        for z in range(count // 2):
+            weight = block[:, 2 * z * units : 2 * (z + 1) * units]
+            total += lax.dot_general(weight, joined[z], dims, preferred_element_type=F32)
+        out[lax.rem(x_index + NX - step, NX)] = total.astype(BF16)
+
+
+def down_product(place, act, blocks):
+    count, slots, units = act.shape
+    columns = blocks[0].shape[0]
+    vmem = pl.BlockSpec(memory_space=pltpu.VMEM)
+    return pl.pallas_call(
+        down_kernel,
+        out_shape=jax.ShapeDtypeStruct((NX, columns, slots), BF16),
+        in_specs=[pl.BlockSpec(memory_space=pltpu.SMEM)] + [vmem] * 5,
+        out_specs=vmem,
+        compiler_params=pltpu.CompilerParams(vmem_limit_bytes=40 * 2**20),
+        cost_estimate=pl.CostEstimate(
+            flops=2 * slots * columns * NX * count * units, bytes_accessed=5 * 2**20, transcendentals=0
+        ),
+    )(place, act, *blocks)
 
 
 def attend(queries, keys, values, lengths):
@@ -57,7 +142,6 @@
 ):
     experts = lax.axis_size(("pool", "tp"))
     block_index = lax.axis_index(("pool", "tp"))
-    pool_index = lax.axis_index("pool")
     group_index = lax.axis_index("grp")
     x_index, member = group_index // (NZ * PAIR), group_index % PAIR
     rows, columns = residual.shape
@@ -86,64 +170,41 @@
     attn = attn.reshape(NX, PAIR, NZ, -1, attn.shape[2]).transpose(0, 2, 1, 3, 4)
     attn = attn.reshape(experts * rows, attn.shape[4])
 
-    up_parts = up_weight[0].reshape(NX, NZ, PAIR, columns, units)
-    down_parts = down_weight[0].reshape(columns, NX, NZ, PAIR, units).transpose(1, 2, 3, 0, 4)
-    held = []
+    up_blocks, down_blocks = [], []
     for step in range(NX):
         wanted = (x_index + step) % NX
-        block = jnp.stack(
-            [lax.dynamic_index_in_dim(w, wanted, 0, keepdims=False) for w in (up_parts, down_parts)]
-        )
-        held.append(lax.ppermute(block, "grp", moves(step, 0)) if step else block)
-    held = jnp.stack([lax.dynamic_index_in_dim(jnp.stack(held), (x_index - x) % NX, 0, False) for x in range(NX)])
-    kept = lax.dynamic_index_in_dim(held, member, 3, keepdims=False)
-    sent = lax.dynamic_index_in_dim(held, 1 - member, 3, keepdims=False)
+        block = lax.dynamic_slice_in_dim(up_weight[0], wanted * (width // NX), width // NX, 0)
+        block = lax.ppermute(block, "grp", moves(step, 0)) if step else block
+        up_blocks.append(block.reshape(NZ, PAIR, columns, units))
+    sent = jnp.stack([lax.dynamic_index_in_dim(w, 1 - member, 1, keepdims=False) for w in up_blocks])
+    projected = jnp.dot(attn, out_weight, preferred_element_type=F32).astype(BF16)
+    projected, sent = lax.optimization_barrier((projected, sent))
     got = lax.ppermute(sent, "grp", moves(0, 1))
-    first, second = jnp.where(member == 0, kept, got), jnp.where(member == 0, got, kept)
-    both = jnp.stack([first, second], axis=1)
-    up_own = both[:, :, 0].reshape(parts, NZ * columns, units).transpose(1, 0, 2)
-    up_own = up_own.reshape(NZ * columns, parts * units)
-    down_own = both[:, :, 1].reshape(parts, NZ, columns, units).transpose(0, 2, 1, 3)
-    down_own = down_own.reshape(parts * columns, NZ * units)
-
-    projected = jnp.dot(attn, out_weight, preferred_element_type=F32).astype(BF16)
-    projected = projected.reshape(2, experts // 2 * rows, columns)
-    kept = lax.dynamic_index_in_dim(projected, pool_index, 0, keepdims=False)
-    sent = lax.dynamic_index_in_dim(projected, 1 - pool_index, 0, keepdims=False)
-    got = lax.ppermute(sent, "pool", [(0, 1), (1, 0)])
-    pair_sum = (kept.astype(F32) + got.astype(F32)).astype(BF16).reshape(experts // 2, rows, columns)
-    hidden = jnp.sum(exchange(pair_sum, "tp").astype(F32), axis=0) + residual.astype(F32)
+    projected = exchange(projected.reshape(experts, rows, columns), ("pool", "tp"))
+    hidden = jnp.sum(projected.astype(F32), axis=0) + residual.astype(F32)
     hidden = hidden.astype(BF16)
+    hidden, down_weight = lax.optimization_barrier((hidden, down_weight))
+    for step in range(NX):
+        wanted = (x_index + step) % NX
+        block = lax.dynamic_slice_in_dim(down_weight[0], wanted * (8 * units), 8 * units, 1)
+        down_blocks.append(lax.ppermute(block, "grp", moves(step, 0)) if step else block)
 
     slot_rows = jnp.dot(select, hidden, preferred_element_type=F32).astype(BF16)
     slot_rows = exchange(slot_rows.reshape(experts, slot_cap, columns), ("pool", "tp"))
-    slot_rows = spread(slot_rows.reshape(slots, columns), NZ, "grp", GATHER).astype(F32)
+    slot_rows = spread(slot_rows.reshape(slots, columns), NZ, "grp", GATHER)
     gain = norm_gain.reshape(NX, NZ, PAIR, columns)
     gain = lax.dynamic_index_in_dim(gain, x_index, 0, keepdims=False)
     gain = lax.dynamic_index_in_dim(gain, member, 1, keepdims=False)
-    normed = (slot_rows * gain[:, None, :]).astype(BF16)
-    normed = normed.transpose(1, 0, 2).reshape(slots, NZ * columns)
-    squares = jnp.sum(slot_rows * slot_rows, axis=(0, 2)).reshape(slots // units, units)
-    high = lax.reduce_precision(squares, 8, 7)
-    low = squares - high
-    pad = jnp.zeros((16 - 2 * (slots // units), units), F32)
-    tail = jnp.concatenate([high, low, pad], axis=0).astype(BF16)
-    partial_up = jnp.dot(normed, up_own, preferred_element_type=F32).astype(BF16)
-    partial_up = partial_up.reshape(slots, parts, units).transpose(1, 0, 2)
-    partial_up = jnp.concatenate(
-        [partial_up, jnp.broadcast_to(tail[None], (parts,) + tail.shape)], axis=1
-    )
+    place = jnp.stack([x_index, member]).astype(jnp.int32)
+    partial_up = up_product(place, slot_rows, gain, up_blocks, got)
     total_up = jnp.sum(exchange(partial_up, "grp", REDUCE).astype(F32), axis=0)
     count = slots // units
     squares = (total_up[slots : slots + count] + total_up[slots + count : slots + 2 * count]).reshape(slots, 1)
     scale = lax.rsqrt(squares / width + 1e-06)
     act = jax.nn.silu(total_up[:slots] * scale).astype(BF16)
 
-    act = spread(act, NZ, "grp", GATHER).transpose(1, 0, 2).reshape(slots, NZ * units)
-    partial_out = lax.dot_general(
-        down_own, act, (((1,), (1,)), ((), ())), preferred_element_type=F32
-    ).astype(BF16)
-    partial_out = exchange(partial_out.reshape(parts, columns, slots), "grp", REDUCE)
+    act = spread(act, 8, "grp", LINE)
+    partial_out = exchange(down_product(place, act, down_blocks), "grp", CROSS)
     expert_out = jnp.sum(partial_out.astype(F32), axis=0).astype(BF16).T
     returned = exchange(expert_out.reshape(experts, slot_cap, columns), ("pool", "tp"))
     returned = returned.reshape(slots, columns)

time: 236 us -> 233 us (0.987)
  local copies, waits for them, and re-layouts: 29.5 us -> 13.1 us
  waiting for transfers between devices: 77.1 us -> 91.9 us
  blocking collectives: 51.9 us -> 62.1 us
  other arithmetic: 11.6 us -> 2.67 us
  Pallas kernels: 0 us -> 4.33 us
  matrix products: 7.42 us -> 3.76 us
  starting transfers between devices: 57.2 us -> 54.2 us
    all_to_all x0 -> x1, blocking collectives: none -> 19.5 us  [spread(): lax.all_to_all(sent, axis, 0, 0, tiled=True, axis_index_groups=groups)]
    ppermute x1, waiting for transfers between devices: 0.01 us -> 12.3 us  [shards(): got = lax.ppermute(sent, 'grp', moves(0, 1))]
    all_to_all x4 -> x3, starting transfers between devices: 26.4 us -> 14.5 us  [spread(): lax.all_to_all(sent, axis, 0, 0, tiled=True, axis_index_groups=groups)]
    all_to_all x3, blocking collectives: 51.9 us -> 42.6 us  [exchange(): lax.all_to_all(value, axis, 0, 0, tiled=True, axis_index_groups=groups)]
    another operation x9 -> x2, other arithmetic: 9.56 us -> 1.12 us  [the longest x1 1.04 us: shards(): jnp.stack([lax.dynamic_index_in_dim(w, 1 - member, 1, keepdims=False) for...]
    another operation x2 -> x4, local copies, waits for them, and re-layouts: 6.63 us -> 0.08 us  [shards(): jnp.stack([lax.dynamic_index_in_dim(w, 1 - member, 1, keepdims=False) for...]
    ppermute x4 -> x6, starting transfers between devices: 13.8 us -> 20.2 us  [the longest x3 10.6 us: shards(): block = lax.ppermute(block, 'grp', moves(step, 0)) if step else block]
    all_to_all x2, waiting for transfers between devices: 18.6 us -> 24.1 us  [exchange(): lax.all_to_all(value, axis, 0, 0, tiled=True, axis_index_groups=groups)]
  transfers between devices with their start and end apart: 11 -> 12, of which waited for: 7 -> 8; matrix products, arithmetic and copies ran while one was open for 14% -> 3% of each run, Pallas kernels for 0% -> 0%
where the time goes in v3:
time: 233 us; the launch traced here: 232 us
  waiting for transfers between devices  91.9 us (39%)
  blocking collectives  62.1 us (27%)
  starting transfers between devices  54.2 us (23%)
  local copies, waits for them, and re-layouts  13.1 us (6%)
  Pallas kernels  4.33 us (2%)
  matrix products  3.76 us (2%)
  other arithmetic  2.67 us (1%)
    all_to_all x3, blocking collectives, exchange(): lax.all_to_all(value, axis, 0, 0, tiled=True, axis_index_groups=groups)  42.6 us
    all_to_all x2, waiting for transfers between devices, exchange(): lax.all_to_all(value, axis, 0, 0, tiled=True, axis_index_groups=groups)  24.1 us
    ppermute x3, waiting for transfers between devices, shards(): block = lax.ppermute(block, 'grp', moves(step, 0)) if step else block  21.8 us
    all_to_all x1, blocking collectives, spread(): lax.all_to_all(sent, axis, 0, 0, tiled=True, axis_index_groups=groups)  19.5 us
    all_to_all x3, waiting for transfers between devices, spread(): lax.all_to_all(sent, axis, 0, 0, tiled=True, axis_index_groups=groups)  18.8 us
    all_to_all x2, starting transfers between devices, exchange(): lax.all_to_all(value, axis, 0, 0, tiled=True, axis_index_groups=groups)  16.2 us
    ppermute x3, waiting for transfers between devices, shards(): lax.ppermute(block, 'grp', moves(step, 0))  14.9 us
    all_to_all x3, starting transfers between devices, spread(): lax.all_to_all(sent, axis, 0, 0, tiled=True, axis_index_groups=groups)  14.5 us
  transfers between devices with their start and end apart: 12, of which 8 were waited for; matrix products, arithmetic and copies ran while one was open for 3% of the time, Pallas kernels for 0%

profile of v3, /device:TPU:8, one launch (start us, length us, event | category | flops | bytes accessed | tf_op | source)
XLA Modules:
  0.0 232.4 jit_solution(10252855763890028174)
XLA Ops:
  0.0 0.8 reshape.119
  0.8 0.7 iota_compare_fusion.4
  1.6 1.3 fusion.5
  2.9 0.2 fusion.28
  3.1 0.6 convolution_convert_fusion.2
  3.7 0.0 copy-start.1
  3.7 19.5 %all_to_all.45 = bf16[4,32,512]{2,1,0:T(8,128)(2,1)S(1)} all-to-all(bf16[4,32,512]{2,1,0:T(8,128)(2,1)S(1)} %broadcast_in_dim.83), channel_id=1, replica_groups={{0,16,32,48},{8,24,40,56},{64,80,96,112},{72,88,104,120},{128,144,160,1..., dimensions={0} | all-to-all | bytes 262144 | tf_op jit(solution)/shard_map/all_to_all | solution.py:28
  23.2 1.1 broadcast_in_dim.85
  24.2 4.3 %all-to-all-start.1 = ((bf16[8,128,512]{2,1,0:T(8,128)(2,1)}), bf16[8,128,512]{2,1,0:T(8,128)(2,1)}, u32[]{:S(2)}, u32[]{:S(2)}) async-start(bf16[8,128,512]{2,1,0:T(8,128)(2,1)} %broadcast_in_dim.85), calls=%async_computation.1 | async-start | bytes 2097152 | tf_op jit(solution)/shard_map/all_to_all | solution.py:28
  28.6 1.1 constant_dynamic-slice_fusion.1
  29.7 5.1 %collective-permute-start.2 = (bf16[1792,128]{1,0:T(8,128)(2,1)}, bf16[1792,128]{1,0:T(8,128)(2,1)S(1)}, u32[]{:S(2)}, u32[]{:S(2)}) collective-permute-start(bf16[1792,128]{1,0:T(8,128)(2,1)} %get-tuple-element.19), channel_id=1, source_target_pairs={{0,192},{8,200},{16,208},{24,216},{32,224},{40,232},{48,240},{56,2... | collective-permute-start | bytes 1376264 | tf_op jit(solution)/shard_map/ppermute | solution.py:177
  34.7 2.8 %collective-permute-start.1 = (bf16[1792,128]{1,0:T(8,128)(2,1)}, bf16[1792,128]{1,0:T(8,128)(2,1)S(1)}, u32[]{:S(2)}, u32[]{:S(2)}) collective-permute-start(bf16[1792,128]{1,0:T(8,128)(2,1)} %get-tuple-element.20), channel_id=1, source_target_pairs={{0,128},{8,136},{16,144},{24,152},{32,160},{40,168},{48,176},{56,1... | collective-permute-start | bytes 1376264 | tf_op jit(solution)/shard_map/ppermute | solution.py:177
  37.5 2.8 %collective-permute-start = (bf16[1792,128]{1,0:T(8,128)(2,1)S(1)}, bf16[1792,128]{1,0:T(8,128)(2,1)S(1)}, u32[]{:S(2)}, u32[]{:S(2)}) collective-permute-start(bf16[1792,128]{1,0:T(8,128)(2,1)S(1)} %get-tuple-element.18), channel_id=1, source_target_pairs={{0,64},{8,72},{16,80},{24,88},{32,96},{40,104},{48,112},{56,120},{... | collective-permute-start | bytes 1376264 | tf_op jit(solution)/shard_map/ppermute | solution.py:177
  40.3 13.0 %collective-permute-done.2 = bf16[1792,128]{1,0:T(8,128)(2,1)S(1)} collective-permute-done((bf16[1792,128]{1,0:T(8,128)(2,1)}, bf16[1792,128]{1,0:T(8,128)(2,1)S(1)}, u32[]{:S(2)}, u32[]{:S(2)}) %collective-permute-start.2) | collective-permute-done | bytes 458784 | tf_op jit(solution)/shard_map/ppermute | solution.py:177
  53.4 8.8 %collective-permute-done = bf16[1792,128]{1,0:T(8,128)(2,1)S(1)} collective-permute-done((bf16[1792,128]{1,0:T(8,128)(2,1)S(1)}, bf16[1792,128]{1,0:T(8,128)(2,1)S(1)}, u32[]{:S(2)}, u32[]{:S(2)}) %collective-permute-start) | collective-permute-done | bytes 458784 | tf_op jit(solution)/shard_map/ppermute | solution.py:177
  62.2 0.0 copy-start.2
  62.2 1.0 pad_maximum_fusion
  63.3 0.0 all-to-all-done.1
  63.3 1.3 copy.24
  64.6 0.0 copy-start.3
  64.6 0.5 convolution_convert_fusion
  65.1 1.0 copy.25
  66.1 7.6 %all-to-all-start.2 = ((bf16[16,64,224]{2,1,0:T(8,128)(2,1)}), bf16[16,64,224]{2,1,0:T(8,128)(2,1)S(1)}, u32[]{:S(2)}, u32[]{:S(2)}) async-start(bf16[16,64,224]{2,1,0:T(8,128)(2,1)} %bitcast.21), calls=%async_computation.2 | async-start | bytes 1048576 | tf_op jit(solution)/shard_map/all_to_all | solution.py:32
  73.7 0.1 eq.58
  73.8 0.8 fusion.20
  74.5 0.1 convolution_convert_fusion.3
  74.7 0.1 fusion.8
  74.8 15.3 %all-to-all-done.2 = bf16[16,64,224]{2,1,0:T(8,128)(2,1)S(1)} async-done(((bf16[16,64,224]{2,1,0:T(8,128)(2,1)}), bf16[16,64,224]{2,1,0:T(8,128)(2,1)S(1)}, u32[]{:S(2)}, u32[]{:S(2)}) %all-to-all-start.2) | async-done | bytes 458784 | tf_op jit(solution)/shard_map/all_to_all | solution.py:32
  90.0 0.1 convert_reduce_fusion.1
  90.2 0.0 copy-start.4
  90.2 0.3 convolution_convert_fusion.1
  90.4 0.1 copy.26
  90.6 13.2 %all_to_all.46 = bf16[16,24,224]{2,1,0:T(8,128)(2,1)S(1)} all-to-all(bf16[16,24,224]{2,1,0:T(8,128)(2,1)S(1)} %bitcast.85), channel_id=1, replica_groups=mesh['pool'=2,'grp'=32,'tp'=8] {'pool','tp'}, dimensions={0} | all-to-all | bytes 344064 | tf_op jit(solution)/shard_map/all_to_all | solution.py:32
  103.8 0.1 copy.27
  104.0 0.9 broadcast_in_dim.87
  104.9 4.2 %all-to-all-start.4 = ((bf16[4,384,224]{1,2,0:T(8,128)(2,1)}), bf16[4,384,224]{1,2,0:T(8,128)(2,1)}, u32[]{:S(2)}, u32[]{:S(2)}) async-start(bf16[4,384,224]{1,2,0:T(8,128)(2,1)} %broadcast_in_dim.87), calls=%async_computation.4 | async-start | bytes 1376256 | tf_op jit(solution)/shard_map/all_to_all | solution.py:28
  109.1 3.3 %collective-permute-start.3 = (bf16[4,4,224,128]{3,2,1,0:T(8,128)(2,1)}, bf16[4,4,224,128]{3,2,1,0:T(8,128)(2,1)}, u32[]{:S(2)}, u32[]{:S(2)}) collective-permute-start(bf16[4,4,224,128]{3,2,1,0:T(8,128)(2,1)} %pad_maximum_fusion), channel_id=1, source_target_pairs={{0,8},{8,0},{16,24},{24,16},{32,40},{40,32},{48,56},{56,48},{64,72... | collective-permute-start | bytes 2752520 | tf_op jit(solution)/shard_map/ppermute | solution.py:182
  112.4 0.1 reshape.128
  112.6 0.1 pad_add_fusion.place
  112.7 18.8 %all-to-all-done.4 = bf16[4,384,224]{1,2,0:T(8,128)(2,1)} async-done(((bf16[4,384,224]{1,2,0:T(8,128)(2,1)}), bf16[4,384,224]{1,2,0:T(8,128)(2,1)}, u32[]{:S(2)}, u32[]{:S(2)}) %all-to-all-start.4) | async-done | bytes 688160 | tf_op jit(solution)/shard_map/all_to_all | solution.py:28
  131.5 1.4 copy.28.rows
  132.8 12.3 %collective-permute-done.3.got = bf16[4,4,224,128]{3,2,1,0:T(8,128)(2,1)} collective-permute-done((bf16[4,4,224,128]{3,2,1,0:T(8,128)(2,1)}, bf16[4,4,224,128]{3,2,1,0:T(8,128)(2,1)}, u32[]{:S(2)}, u32[]{:S(2)}) %collective-permute-start.3) | collective-permute-done | bytes 917536 | tf_op jit(solution)/shard_map/ppermute | solution.py:182
  145.2 2.6 %shard_map.109 = bf16[8,400,128]{2,1,0:T(8,128)(2,1)S(1)} custom-call(s32[2]{0:T(128)S(1)} %pad_add_fusion.place, bf16[4,384,224]{2,1,0:T(8,128)(2,1)S(1)} %copy.28.rows, f32[4,224]{1,0:T(4,128)S(1)} %bitcast.83, bf16[4,2,224,128]{3,2,1,0:T(8,128)(2,1)S(1)} %bitcast.76, bf16[4,2,224,128]{3,2,1,0:T(8,128)(2,1)S(1)} %bitcast.82, ...), custom_call_target="tpu_custom_call" | custom-call | flops 704643072 | bytes 6291456 | tf_op jit(solution)/shard_map/pallas_call | solution.py:74
  147.8 15.1 %all_to_all.47 = bf16[8,400,128]{2,1,0:T(8,128)(2,1)S(1)} all-to-all(bf16[8,400,128]{2,1,0:T(8,128)(2,1)S(1)} %shard_map.109), channel_id=1, replica_groups={{0,8,64,72,128,136,192,200},{16,24,80,88,144,152,208,216},{32,40,96,104..., dimensions={0} | all-to-all | bytes 1638400 | tf_op jit(solution)/shard_map/all_to_all | solution.py:32
  162.8 0.1 convert_reduce_fusion
  162.9 0.1 multiply_convert_fusion
  163.1 1.0 broadcast_in_dim.88
  164.1 6.0 %all-to-all-start.6 = ((bf16[8,384,128]{2,1,0:T(8,128)(2,1)}), bf16[8,384,128]{2,1,0:T(8,128)(2,1)S(1)}, u32[]{:S(2)}, u32[]{:S(2)}) async-start(bf16[8,384,128]{2,1,0:T(8,128)(2,1)} %broadcast_in_dim.88), calls=%async_computation.6 | async-start | bytes 1572864 | tf_op jit(solution)/shard_map/all_to_all | solution.py:28
  170.1 1.6 dynamic-slice_bitcast_fusion
  171.7 2.5 %collective-permute-start.4 = (bf16[224,1024]{1,0:T(8,128)(2,1)S(1)}, bf16[224,1024]{1,0:T(8,128)(2,1)S(1)}, u32[]{:S(2)}, u32[]{:S(2)}) collective-permute-start(bf16[224,1024]{1,0:T(8,128)(2,1)S(1)} %get-tuple-element.15), channel_id=1, source_target_pairs={{0,64},{8,72},{16,80},{24,88},{32,96},{40,104},{48,112},{56,120},{... | collective-permute-start | bytes 1376264 | tf_op jit(solution)/shard_map/ppermute | solution.py:190
  174.2 4.0 %collective-permute-start.5 = (bf16[224,1024]{1,0:T(8,128)(2,1)S(1)}, bf16[224,1024]{1,0:T(8,128)(2,1)S(1)}, u32[]{:S(2)}, u32[]{:S(2)}) collective-permute-start(bf16[224,1024]{1,0:T(8,128)(2,1)S(1)} %get-tuple-element.14), channel_id=1, source_target_pairs={{0,128},{8,136},{16,144},{24,152},{32,160},{40,168},{48,176},{56,1... | collective-permute-start | bytes 1376264 | tf_op jit(solution)/shard_map/ppermute | solution.py:190
  178.2 3.1 %collective-permute-start.6 = (bf16[224,1024]{1,0:T(8,128)(2,1)S(1)}, bf16[224,1024]{1,0:T(8,128)(2,1)S(1)}, u32[]{:S(2)}, u32[]{:S(2)}) collective-permute-start(bf16[224,1024]{1,0:T(8,128)(2,1)S(1)} %get-tuple-element.13), channel_id=1, source_target_pairs={{0,192},{8,200},{16,208},{24,216},{32,224},{40,232},{48,240},{56,2... | collective-permute-start | bytes 1376264 | tf_op jit(solution)/shard_map/ppermute | solution.py:190
  181.3 12.3 %collective-permute-done.4.block1 = bf16[224,1024]{1,0:T(8,128)(2,1)S(1)} collective-permute-done((bf16[224,1024]{1,0:T(8,128)(2,1)S(1)}, bf16[224,1024]{1,0:T(8,128)(2,1)S(1)}, u32[]{:S(2)}, u32[]{:S(2)}) %collective-permute-start.4) | collective-permute-done | bytes 458784 | tf_op jit(solution)/shard_map/ppermute | solution.py:190
  193.6 0.0 collective-permute-done.5.block2
  193.7 2.5 %collective-permute-done.6.block3 = bf16[224,1024]{1,0:T(8,128)(2,1)S(1)} collective-permute-done((bf16[224,1024]{1,0:T(8,128)(2,1)S(1)}, bf16[224,1024]{1,0:T(8,128)(2,1)S(1)}, u32[]{:S(2)}, u32[]{:S(2)}) %collective-permute-start.6) | collective-permute-done | bytes 458784 | tf_op jit(solution)/shard_map/ppermute | solution.py:190
  196.2 1.7 shard_map.110
  197.9 14.3 %all_to_all.48 = bf16[4,224,384]{2,1,0:T(8,128)(2,1)S(1)} all-to-all(bf16[4,224,384]{2,1,0:T(8,128)(2,1)S(1)} %shard_map.110), channel_id=1, replica_groups={{0,64,128,192},{8,72,136,200},{16,80,144,208},{24,88,152,216},{32,96,16..., dimensions={0} | all-to-all | bytes 1376256 | tf_op jit(solution)/shard_map/all_to_all | solution.py:32
  212.2 0.1 reduce_sum.52
  212.3 0.8 copy.29
  213.1 8.6 %all-to-all-start.8 = ((bf16[16,24,224]{2,1,0:T(8,128)(2,1)}), bf16[16,24,224]{2,1,0:T(8,128)(2,1)S(1)}, u32[]{:S(2)}, u32[]{:S(2)}) async-start(bf16[16,24,224]{2,1,0:T(8,128)(2,1)} %bitcast.30), calls=%async_computation.8 | async-start | bytes 393216 | tf_op jit(solution)/shard_map/all_to_all | solution.py:32
  221.7 0.8 fusion.21
  222.5 8.8 %all-to-all-done.8 = bf16[16,24,224]{2,1,0:T(8,128)(2,1)S(1)} async-done(((bf16[16,24,224]{2,1,0:T(8,128)(2,1)}), bf16[16,24,224]{2,1,0:T(8,128)(2,1)S(1)}, u32[]{:S(2)}, u32[]{:S(2)}) %all-to-all-start.8) | async-done | bytes 172064 | tf_op jit(solution)/shard_map/all_to_all | solution.py:32
  231.3 0.2 convolution_bitcast_fusion.1
  231.5 0.8 fusion.2
  (21 shorter events, 0.2 us)
Async XLA Ops:
  0.0 3.1 %copy-start = (bf16[32,32,256]{2,1,0:T(8,128)(2,1)S(1)}, bf16[32,32,256]{2,1,0:T(8,128)(2,1)}, u32[]{:S(2)}) copy-start(bf16[32,32,256]{2,1,0:T(8,128)(2,1)} %param.13) | copy-start | bytes 1572868
  3.7 25.0 %copy-start.1 = (bf16[1,7168,128]{2,1,0:T(8,128)(2,1)S(1)}, bf16[1,7168,128]{2,1,0:T(8,128)(2,1)}, u32[]{:S(2)}) copy-start(bf16[1,7168,128]{2,1,0:T(8,128)(2,1)} %param.20) | copy-start | bytes 5505028
  24.2 39.0 %all-to-all-start.1 = ((bf16[8,128,512]{2,1,0:T(8,128)(2,1)}), bf16[8,128,512]{2,1,0:T(8,128)(2,1)}, u32[]{:S(2)}, u32[]{:S(2)}) async-start(bf16[8,128,512]{2,1,0:T(8,128)(2,1)} %broadcast_in_dim.85), calls=%async_computation.1 | async-start | bytes 2097152 | tf_op jit(solution)/shard_map/all_to_all | solution.py:28
  29.7 23.7 %collective-permute-start.2 = (bf16[1792,128]{1,0:T(8,128)(2,1)}, bf16[1792,128]{1,0:T(8,128)(2,1)S(1)}, u32[]{:S(2)}, u32[]{:S(2)}) collective-permute-start(bf16[1792,128]{1,0:T(8,128)(2,1)} %get-tuple-element.19), channel_id=1, source_target_pairs={{0,192},{8,200},{16,208},{24,216},{32,224},{40,232},{48,240},{56,2... | collective-permute-start | bytes 1376264 | tf_op jit(solution)/shard_map/ppermute | solution.py:177
  34.7 18.6 %collective-permute-start.1 = (bf16[1792,128]{1,0:T(8,128)(2,1)}, bf16[1792,128]{1,0:T(8,128)(2,1)S(1)}, u32[]{:S(2)}, u32[]{:S(2)}) collective-permute-start(bf16[1792,128]{1,0:T(8,128)(2,1)} %get-tuple-element.20), channel_id=1, source_target_pairs={{0,128},{8,136},{16,144},{24,152},{32,160},{40,168},{48,176},{56,1... | collective-permute-start | bytes 1376264 | tf_op jit(solution)/shard_map/ppermute | solution.py:177
  37.5 24.7 %collective-permute-start = (bf16[1792,128]{1,0:T(8,128)(2,1)S(1)}, bf16[1792,128]{1,0:T(8,128)(2,1)S(1)}, u32[]{:S(2)}, u32[]{:S(2)}) collective-permute-start(bf16[1792,128]{1,0:T(8,128)(2,1)S(1)} %get-tuple-element.18), channel_id=1, source_target_pairs={{0,64},{8,72},{16,80},{24,88},{32,96},{40,104},{48,112},{56,120},{... | collective-permute-start | bytes 1376264 | tf_op jit(solution)/shard_map/ppermute | solution.py:177
  62.2 2.4 %copy-start.2 = (bf16[512,224]{0,1:T(8,128)(2,1)S(1)}, bf16[512,224]{0,1:T(8,128)(2,1)}, u32[]{:S(2)}) copy-start(bf16[512,224]{0,1:T(8,128)(2,1)} %param.15) | copy-start | bytes 688132
  64.6 25.6 %copy-start.3 = (bf16[64,224]{1,0:T(8,128)(2,1)S(1)}, bf16[64,224]{1,0:T(8,128)(2,1)}, u32[]{:S(2)}) copy-start(bf16[64,224]{1,0:T(8,128)(2,1)} %param.16) | copy-start | bytes 86020
  66.1 23.9 %all-to-all-start.2 = ((bf16[16,64,224]{2,1,0:T(8,128)(2,1)}), bf16[16,64,224]{2,1,0:T(8,128)(2,1)S(1)}, u32[]{:S(2)}, u32[]{:S(2)}) async-start(bf16[16,64,224]{2,1,0:T(8,128)(2,1)} %bitcast.21), calls=%async_computation.2 | async-start | bytes 1048576 | tf_op jit(solution)/shard_map/all_to_all | solution.py:32
  90.2 22.3 %copy-start.4 = (f32[7168]{0:T(1024)S(1)}, f32[7168]{0:T(1024)}, u32[]{:S(2)}) copy-start(f32[7168]{0:T(1024)} %param.17) | copy-start | bytes 86020
  104.9 26.6 %all-to-all-start.4 = ((bf16[4,384,224]{1,2,0:T(8,128)(2,1)}), bf16[4,384,224]{1,2,0:T(8,128)(2,1)}, u32[]{:S(2)}, u32[]{:S(2)}) async-start(bf16[4,384,224]{1,2,0:T(8,128)(2,1)} %broadcast_in_dim.87), calls=%async_computation.4 | async-start | bytes 1376256 | tf_op jit(solution)/shard_map/all_to_all | solution.py:28
  109.1 36.1 %collective-permute-start.3 = (bf16[4,4,224,128]{3,2,1,0:T(8,128)(2,1)}, bf16[4,4,224,128]{3,2,1,0:T(8,128)(2,1)}, u32[]{:S(2)}, u32[]{:S(2)}) collective-permute-start(bf16[4,4,224,128]{3,2,1,0:T(8,128)(2,1)} %pad_maximum_fusion), channel_id=1, source_target_pairs={{0,8},{8,0},{16,24},{24,16},{32,40},{40,32},{48,56},{56,48},{64,72... | collective-permute-start | bytes 2752520 | tf_op jit(solution)/shard_map/ppermute | solution.py:182
  164.1 32.1 %all-to-all-start.6 = ((bf16[8,384,128]{2,1,0:T(8,128)(2,1)}), bf16[8,384,128]{2,1,0:T(8,128)(2,1)S(1)}, u32[]{:S(2)}, u32[]{:S(2)}) async-start(bf16[8,384,128]{2,1,0:T(8,128)(2,1)} %broadcast_in_dim.88), calls=%async_computation.6 | async-start | bytes 1572864 | tf_op jit(solution)/shard_map/all_to_all | solution.py:28
  171.7 22.0 %collective-permute-start.4 = (bf16[224,1024]{1,0:T(8,128)(2,1)S(1)}, bf16[224,1024]{1,0:T(8,128)(2,1)S(1)}, u32[]{:S(2)}, u32[]{:S(2)}) collective-permute-start(bf16[224,1024]{1,0:T(8,128)(2,1)S(1)} %get-tuple-element.15), channel_id=1, source_target_pairs={{0,64},{8,72},{16,80},{24,88},{32,96},{40,104},{48,112},{56,120},{... | collective-permute-start | bytes 1376264 | tf_op jit(solution)/shard_map/ppermute | solution.py:190
  174.2 19.5 %collective-permute-start.5 = (bf16[224,1024]{1,0:T(8,128)(2,1)S(1)}, bf16[224,1024]{1,0:T(8,128)(2,1)S(1)}, u32[]{:S(2)}, u32[]{:S(2)}) collective-permute-start(bf16[224,1024]{1,0:T(8,128)(2,1)S(1)} %get-tuple-element.14), channel_id=1, source_target_pairs={{0,128},{8,136},{16,144},{24,152},{32,160},{40,168},{48,176},{56,1... | collective-permute-start | bytes 1376264 | tf_op jit(solution)/shard_map/ppermute | solution.py:190
  178.2 18.0 %collective-permute-start.6 = (bf16[224,1024]{1,0:T(8,128)(2,1)S(1)}, bf16[224,1024]{1,0:T(8,128)(2,1)S(1)}, u32[]{:S(2)}, u32[]{:S(2)}) collective-permute-start(bf16[224,1024]{1,0:T(8,128)(2,1)S(1)} %get-tuple-element.13), channel_id=1, source_target_pairs={{0,192},{8,200},{16,208},{24,216},{32,224},{40,232},{48,240},{56,2... | collective-permute-start | bytes 1376264 | tf_op jit(solution)/shard_map/ppermute | solution.py:190
  213.1 18.2 %all-to-all-start.8 = ((bf16[16,24,224]{2,1,0:T(8,128)(2,1)}), bf16[16,24,224]{2,1,0:T(8,128)(2,1)S(1)}, u32[]{:S(2)}, u32[]{:S(2)}) async-start(bf16[16,24,224]{2,1,0:T(8,128)(2,1)} %bitcast.30), calls=%async_computation.8 | async-start | bytes 393216 | tf_op jit(solution)/shard_map/all_to_all | solution.py:32

commit v4 on v3

--- a/solution.py
+++ b/solution.py
@@ -32,7 +32,7 @@
     return lax.all_to_all(value, axis, 0, 0, tiled=True, axis_index_groups=groups)
 
 
-def up_kernel(place, rows, gain, block0, block1, block2, block3, got, out):
+def up_kernel(place, rows, gain, block0, block1, block2, block3, got, got2, out):
     x_index, member = place[0], place[1]
     slots, units = rows.shape[1], out.shape[2]
     normed, squares = [], 0.0
@@ -58,7 +58,8 @@
     for step, block in enumerate((block0, block1, block2, block3)):
         total = 0.0
         for z in range(NZ):
-            both = jnp.concatenate([block[z, member], got[step, z]], axis=1)
+            other = got2[z] if step == 2 else got[min(step, 2), z]
+            both = jnp.concatenate([block[z, member], other], axis=1)
             total += jnp.dot(normed[z], both, preferred_element_type=F32)
         total = total.astype(BF16)
         first = lax.rem(x_index + NX - step, NX) * PAIR
@@ -67,20 +68,20 @@
             out[target, slots:] = tail
 
 
-def up_product(place, rows, gain, blocks, got):
+def up_product(place, rows, gain, blocks, got, got2):
     slots, columns = rows.shape[1:]
     units = got.shape[3]
     vmem = pl.BlockSpec(memory_space=pltpu.VMEM)
     return pl.pallas_call(
         up_kernel,
         out_shape=jax.ShapeDtypeStruct((NX * PAIR, slots + 16, units), BF16),
-        in_specs=[pl.BlockSpec(memory_space=pltpu.SMEM)] + [vmem] * 7,
+        in_specs=[pl.BlockSpec(memory_space=pltpu.SMEM)] + [vmem] * 8,
         out_specs=vmem,
         compiler_params=pltpu.CompilerParams(vmem_limit_bytes=40 * 2**20),
         cost_estimate=pl.CostEstimate(
             flops=2 * slots * columns * NZ * NX * PAIR * units, bytes_accessed=6 * 2**20, transcendentals=0
         ),
-    )(place, rows, gain, *blocks, got)
+    )(place, rows, gain, *blocks, got, got2)
 
 
 def down_kernel(place, act, block0, block1, block2, block3, out):
@@ -165,38 +166,45 @@
     combine = jnp.where(here, weight_of[:, None, :], 0.0).reshape(slots, rows)
 
     attn = attend(queries, keys, values, lengths)
+    def up_block(step):
+        wanted = (x_index + step) % NX
+        block = lax.dynamic_slice_in_dim(up_weight[0], wanted * (width // NX), width // NX, 0)
+        block = lax.ppermute(block, "grp", moves(step, 0)) if step else block
+        return block.reshape(NZ, PAIR, columns, units)
+
+    def down_block(step):
+        wanted = (x_index + step) % NX
+        block = lax.dynamic_slice_in_dim(down_weight[0], wanted * (8 * units), 8 * units, 1)
+        return lax.ppermute(block, "grp", moves(step, 0)) if step else block
+
+    def other_half(block):
+        return lax.dynamic_index_in_dim(block, 1 - member, 1, keepdims=False)
+
     attn = spread(attn, NZ, "grp", GATHER)
+    attn, up1, up3 = lax.optimization_barrier((attn, up_block(1), up_block(3)))
     attn = spread(attn.reshape(-1, attn.shape[2]), parts, "grp", REDUCE)
     attn = attn.reshape(NX, PAIR, NZ, -1, attn.shape[2]).transpose(0, 2, 1, 3, 4)
     attn = attn.reshape(experts * rows, attn.shape[4])
-
-    up_blocks, down_blocks = [], []
-    for step in range(NX):
-        wanted = (x_index + step) % NX
-        block = lax.dynamic_slice_in_dim(up_weight[0], wanted * (width // NX), width // NX, 0)
-        block = lax.ppermute(block, "grp", moves(step, 0)) if step else block
-        up_blocks.append(block.reshape(NZ, PAIR, columns, units))
-    sent = jnp.stack([lax.dynamic_index_in_dim(w, 1 - member, 1, keepdims=False) for w in up_blocks])
     projected = jnp.dot(attn, out_weight, preferred_element_type=F32).astype(BF16)
-    projected, sent = lax.optimization_barrier((projected, sent))
-    got = lax.ppermute(sent, "grp", moves(0, 1))
+
+    up0 = up_block(0)
+    got = lax.ppermute(jnp.stack([other_half(w) for w in (up0, up1, up3)]), "grp", moves(0, 1))
     projected = exchange(projected.reshape(experts, rows, columns), ("pool", "tp"))
+    projected, up2, got = lax.optimization_barrier((projected, up_block(2), got))
     hidden = jnp.sum(projected.astype(F32), axis=0) + residual.astype(F32)
     hidden = hidden.astype(BF16)
-    hidden, down_weight = lax.optimization_barrier((hidden, down_weight))
-    for step in range(NX):
-        wanted = (x_index + step) % NX
-        block = lax.dynamic_slice_in_dim(down_weight[0], wanted * (8 * units), 8 * units, 1)
-        down_blocks.append(lax.ppermute(block, "grp", moves(step, 0)) if step else block)
 
     slot_rows = jnp.dot(select, hidden, preferred_element_type=F32).astype(BF16)
     slot_rows = exchange(slot_rows.reshape(experts, slot_cap, columns), ("pool", "tp"))
+    got2 = lax.ppermute(other_half(up2), "grp", moves(0, 1))
+    slot_rows, got2 = lax.optimization_barrier((slot_rows, got2))
     slot_rows = spread(slot_rows.reshape(slots, columns), NZ, "grp", GATHER)
+    slot_rows, down1, down3 = lax.optimization_barrier((slot_rows, down_block(1), down_block(3)))
     gain = norm_gain.reshape(NX, NZ, PAIR, columns)
     gain = lax.dynamic_index_in_dim(gain, x_index, 0, keepdims=False)
     gain = lax.dynamic_index_in_dim(gain, member, 1, keepdims=False)
     place = jnp.stack([x_index, member]).astype(jnp.int32)
-    partial_up = up_product(place, slot_rows, gain, up_blocks, got)
+    partial_up = up_product(place, slot_rows, gain, (up0, up1, up2, up3), got, got2)
     total_up = jnp.sum(exchange(partial_up, "grp", REDUCE).astype(F32), axis=0)
     count = slots // units
     squares = (total_up[slots : slots + count] + total_up[slots + count : slots + 2 * count]).reshape(slots, 1)
@@ -204,7 +212,7 @@
     act = jax.nn.silu(total_up[:slots] * scale).astype(BF16)
 
     act = spread(act, 8, "grp", LINE)
-    partial_out = exchange(down_product(place, act, down_blocks), "grp", CROSS)
+    partial_out = exchange(down_product(place, act, (down_block(0), down1, down_block(2), down3)), "grp", CROSS)
     expert_out = jnp.sum(partial_out.astype(F32), axis=0).astype(BF16).T
     returned = exchange(expert_out.reshape(experts, slot_cap, columns), ("pool", "tp"))
     returned = returned.reshape(slots, columns)

time: 233 us -> 209 us (0.90)
  waiting for transfers between devices: 91.9 us -> 67.7 us
  blocking collectives: 62.1 us -> 47.2 us
  starting transfers between devices: 54.2 us -> 62.3 us
  local copies, waits for them, and re-layouts: 13.1 us -> 19.3 us
    all_to_all x2 -> x3, waiting for transfers between devices: 24.1 us -> 8.98 us  [exchange(): lax.all_to_all(value, axis, 0, 0, tiled=True, axis_index_groups=groups)]
    all_to_all x3 -> x2, blocking collectives: 42.6 us -> 28.1 us  [exchange(): lax.all_to_all(value, axis, 0, 0, tiled=True, axis_index_groups=groups)]
    ppermute x7 -> x8, waiting for transfers between devices: 49 us -> 37.3 us  [the longest x3 17.2 us: down_block(): return lax.ppermute(block, 'grp', moves(step, 0)) if step else block]
    all_to_all x2 -> x3, starting transfers between devices: 16.2 us -> 22.1 us  [exchange(): lax.all_to_all(value, axis, 0, 0, tiled=True, axis_index_groups=groups)]
    unnamed x12 -> x30, local copies, waits for them, and re-layouts: 0.04 us -> 2.94 us
    all_to_all x3, waiting for transfers between devices: 18.8 us -> 21.4 us  [spread(): lax.all_to_all(sent, axis, 0, 0, tiled=True, axis_index_groups=groups)]
    dynamic_slice x2, local copies, waits for them, and re-layouts: 2.65 us -> 5.13 us  [the longest x1 2.58 us: up_block(): lax.dynamic_slice_in_dim(up_weight[0], wanted * (width // NX), width // N...]
    ppermute x7 -> x8, starting transfers between devices: 23.5 us -> 25.1 us  [the longest x3 10.2 us: down_block(): return lax.ppermute(block, 'grp', moves(step, 0)) if step else block]
  transfers between devices with their start and end apart: 12 -> 14, of which waited for: 8 -> 10; matrix products, arithmetic and copies ran while one was open for 3% -> 4% of each run, Pallas kernels for 0% -> 0%
where the time goes in v4:
time: 209 us; the launch traced here: 208 us
  waiting for transfers between devices  67.7 us (32%)
  starting transfers between devices  62.3 us (30%)
  blocking collectives  47.2 us (23%)
  local copies, waits for them, and re-layouts  19.3 us (9%)
  Pallas kernels  4.18 us (2%)
  matrix products  3.76 us (2%)
  other arithmetic  3.19 us (2%)
    all_to_all x2, blocking collectives, exchange(): lax.all_to_all(value, axis, 0, 0, tiled=True, axis_index_groups=groups)  28.1 us
    all_to_all x3, starting transfers between devices, exchange(): lax.all_to_all(value, axis, 0, 0, tiled=True, axis_index_groups=groups)  22.1 us
    all_to_all x3, waiting for transfers between devices, spread(): lax.all_to_all(sent, axis, 0, 0, tiled=True, axis_index_groups=groups)  21.4 us
    all_to_all x1, blocking collectives, spread(): lax.all_to_all(sent, axis, 0, 0, tiled=True, axis_index_groups=groups)  19.2 us
    ppermute x3, waiting for transfers between devices, down_block(): return lax.ppermute(block, 'grp', moves(step, 0)) if step else block  17.2 us
    all_to_all x3, starting transfers between devices, spread(): lax.all_to_all(sent, axis, 0, 0, tiled=True, axis_index_groups=groups)  15.1 us
    ppermute x3, waiting for transfers between devices, up_block(): block = lax.ppermute(block, 'grp', moves(step, 0)) if step else block  12.2 us
    ppermute x3, starting transfers between devices, down_block(): return lax.ppermute(block, 'grp', moves(step, 0)) if step else block  10.2 us
  transfers between devices with their start and end apart: 14, of which 10 were waited for; matrix products, arithmetic and copies ran while one was open for 4% of the time, Pallas kernels for 0%

profile of v4, /device:TPU:8, one launch (start us, length us, event | category | flops | bytes accessed | tf_op | source)
XLA Modules:
  0.0 208.0 jit_solution(12929282958543320616)
XLA Ops:
  0.0 2.6 %constant_dynamic-slice_fusion.1 = (bf16[1,1792,128]{2,1,0:T(8,128)(2,1)S(1)}, bf16[1792,128]{1,0:T(8,128)(2,1)S(1)}, bf16[1792,128]{1,0:T(8,128)(2,1)}, bf16[1792,128]{1,0:T(8,128)(2,1)}) fusion(bf16[1,7168,128]{2,1,0:T(8,128)(2,1)} %param.20, s32[]{:T(128)S(6)} %select_n.110, s32[]{:T(128)S(6)} %select_n.106, s32[]{:T(128)S(6)} %select_n.104, s32[]{:T(128)S(6)} %select_n.108), kind=kLoop, calls=%fused_computation.54 | loop fusion | bytes 3670032 | tf_op jit(solution)/shard_map/dynamic_slice | solution.py:171
  2.6 3.4 %collective-permute-start = (bf16[1792,128]{1,0:T(8,128)(2,1)}, bf16[1792,128]{1,0:T(8,128)(2,1)S(1)}, u32[]{:S(2)}, u32[]{:S(2)}) collective-permute-start(bf16[1792,128]{1,0:T(8,128)(2,1)} %get-tuple-element.33), channel_id=1, source_target_pairs={{0,64},{8,72},{16,80},{24,88},{32,96},{40,104},{48,112},{56,120},{... | collective-permute-start | bytes 1376264 | tf_op jit(solution)/shard_map/ppermute | solution.py:172
  6.0 3.7 %collective-permute-start.1 = (bf16[1792,128]{1,0:T(8,128)(2,1)S(1)}, bf16[1792,128]{1,0:T(8,128)(2,1)S(1)}, u32[]{:S(2)}, u32[]{:S(2)}) collective-permute-start(bf16[1792,128]{1,0:T(8,128)(2,1)S(1)} %get-tuple-element.32), channel_id=1, source_target_pairs={{0,192},{8,200},{16,208},{24,216},{32,224},{40,232},{48,240},{56,2... | collective-permute-start | bytes 1376264 | tf_op jit(solution)/shard_map/ppermute | solution.py:172
  9.7 0.1 iota_compare_fusion.4
  9.8 1.3 fusion.5
  11.0 0.2 fusion.28
  11.3 0.6 convolution_convert_fusion.2
  11.9 19.2 %all_to_all.45 = bf16[4,32,512]{2,1,0:T(8,128)(2,1)S(1)} all-to-all(bf16[4,32,512]{2,1,0:T(8,128)(2,1)S(1)} %broadcast_in_dim.83), channel_id=1, replica_groups={{0,16,32,48},{8,24,40,56},{64,80,96,112},{72,88,104,120},{128,144,160,1..., dimensions={0} | all-to-all | bytes 262144 | tf_op jit(solution)/shard_map/all_to_all | solution.py:28
  31.0 1.1 broadcast_in_dim.85
  32.1 4.4 %all-to-all-start.1 = ((bf16[8,128,512]{2,1,0:T(8,128)(2,1)}), bf16[8,128,512]{2,1,0:T(8,128)(2,1)}, u32[]{:S(2)}, u32[]{:S(2)}) async-start(bf16[8,128,512]{2,1,0:T(8,128)(2,1)} %broadcast_in_dim.85), calls=%async_computation.1 | async-start | bytes 2097152 | tf_op jit(solution)/shard_map/all_to_all | solution.py:28
  36.6 13.8 %all-to-all-done.1 = bf16[8,128,512]{2,1,0:T(8,128)(2,1)} async-done(((bf16[8,128,512]{2,1,0:T(8,128)(2,1)}), bf16[8,128,512]{2,1,0:T(8,128)(2,1)}, u32[]{:S(2)}, u32[]{:S(2)}) %all-to-all-start.1) | async-done | bytes 1048608 | tf_op jit(solution)/shard_map/all_to_all | solution.py:28
  50.3 1.3 copy.24
  51.7 0.5 convolution_convert_fusion
  52.1 1.0 copy.25
  53.2 7.7 %all-to-all-start.2 = ((bf16[16,64,224]{2,1,0:T(8,128)(2,1)}), bf16[16,64,224]{2,1,0:T(8,128)(2,1)}, u32[]{:S(2)}, u32[]{:S(2)}) async-start(bf16[16,64,224]{2,1,0:T(8,128)(2,1)} %bitcast.14), calls=%async_computation.2 | async-start | bytes 1048576 | tf_op jit(solution)/shard_map/all_to_all | solution.py:32
  60.9 0.9 pad_maximum_fusion
  61.8 2.7 %collective-permute-start.3 = (bf16[3,4,224,128]{3,2,1,0:T(8,128)(2,1)}, bf16[3,4,224,128]{3,2,1,0:T(8,128)(2,1)S(1)}, u32[]{:S(2)}, u32[]{:S(2)}) collective-permute-start(bf16[3,4,224,128]{3,2,1,0:T(8,128)(2,1)} %pad_maximum_fusion), channel_id=1, source_target_pairs={{0,8},{8,0},{16,24},{24,16},{32,40},{40,32},{48,56},{56,48},{64,72... | collective-permute-start | bytes 2064392 | tf_op jit(solution)/shard_map/ppermute | solution.py:191
  64.5 2.6 %collective-permute-start.2 = (bf16[1792,128]{1,0:T(8,128)(2,1)}, bf16[1792,128]{1,0:T(8,128)(2,1)S(1)}, u32[]{:S(2)}, u32[]{:S(2)}) collective-permute-start(bf16[1792,128]{1,0:T(8,128)(2,1)} %get-tuple-element.34), channel_id=1, source_target_pairs={{0,128},{8,136},{16,144},{24,152},{32,160},{40,168},{48,176},{56,1... | collective-permute-start | bytes 1376264 | tf_op jit(solution)/shard_map/ppermute | solution.py:172
  67.1 0.1 eq.58
  67.1 0.8 fusion.20
  67.9 0.1 convolution_convert_fusion.3
  68.1 0.1 fusion.8
  68.2 12.2 %collective-permute-done.2 = bf16[1792,128]{1,0:T(8,128)(2,1)S(1)} collective-permute-done((bf16[1792,128]{1,0:T(8,128)(2,1)}, bf16[1792,128]{1,0:T(8,128)(2,1)S(1)}, u32[]{:S(2)}, u32[]{:S(2)}) %collective-permute-start.2) | collective-permute-done | bytes 458784 | tf_op jit(solution)/shard_map/ppermute | solution.py:172
  80.4 1.0 collective-permute-done.3.got
  81.4 1.4 convert_reduce_fusion.1
  82.8 0.3 convolution_convert_fusion.1
  83.1 0.8 copy.26
  83.9 7.2 %all-to-all-start.3 = ((bf16[16,24,224]{2,1,0:T(8,128)(2,1)}), bf16[16,24,224]{2,1,0:T(8,128)(2,1)}, u32[]{:S(2)}, u32[]{:S(2)}) async-start(bf16[16,24,224]{2,1,0:T(8,128)(2,1)} %bitcast.21), calls=%async_computation.3 | async-start | bytes 393216 | tf_op jit(solution)/shard_map/all_to_all | solution.py:32
  91.1 2.7 %collective-permute-start.4 = (bf16[4,224,128]{2,1,0:T(8,128)(2,1)S(1)}, bf16[4,224,128]{2,1,0:T(8,128)(2,1)S(1)}, u32[]{:S(2)}, u32[]{:S(2)}) collective-permute-start(bf16[4,224,128]{2,1,0:T(8,128)(2,1)S(1)} %dynamic-slice_bitcast_fusion.7), channel_id=1, source_target_pairs={{0,8},{8,0},{16,24},{24,16},{32,40},{40,32},{48,56},{56,48},{64,72... | collective-permute-start | bytes 688136 | tf_op jit(solution)/shard_map/ppermute | solution.py:199
  93.8 6.9 %collective-permute-done.4.got2 = bf16[4,224,128]{2,1,0:T(8,128)(2,1)S(1)} collective-permute-done((bf16[4,224,128]{2,1,0:T(8,128)(2,1)S(1)}, bf16[4,224,128]{2,1,0:T(8,128)(2,1)S(1)}, u32[]{:S(2)}, u32[]{:S(2)}) %collective-permute-start.4) | collective-permute-done | bytes 229408 | tf_op jit(solution)/shard_map/ppermute | solution.py:199
  100.7 0.1 all-to-all-done.3
  100.8 1.1 copy.27
  101.9 0.9 broadcast_in_dim.87
  102.8 4.2 %all-to-all-start.4 = ((bf16[4,384,224]{1,2,0:T(8,128)(2,1)}), bf16[4,384,224]{1,2,0:T(8,128)(2,1)}, u32[]{:S(2)}, u32[]{:S(2)}) async-start(bf16[4,384,224]{1,2,0:T(8,128)(2,1)} %broadcast_in_dim.87), calls=%async_computation.4 | async-start | bytes 1376256 | tf_op jit(solution)/shard_map/all_to_all | solution.py:28
  107.0 0.0 copy-start.10
  107.0 2.6 %dynamic-slice_bitcast_fusion = (bf16[224,1024]{1,0:T(8,128)(2,1)}, bf16[224,1024]{1,0:T(8,128)(2,1)}, bf16[224,1024]{1,0:T(8,128)(2,1)}, bf16[224,1024]{1,0:T(8,128)(2,1)S(1)}) fusion(bf16[1,224,4096]{2,1,0:T(8,128)(2,1)} %param.21, s32[]{:T(128)S(6)} %select_n.119, s32[]{:T(128)S(6)} %select_n.113, s32[]{:T(128)S(6)} %select_n.112, s32[]{:T(128)S(6)} %select_n.118), kind=kLoop, calls=%fused_computation.16 | loop fusion | bytes 3670032 | tf_op jit(solution)/shard_map/dynamic_slice | solution.py:177
  109.6 1.9 collective-permute-start.5
  111.5 5.1 %collective-permute-start.6 = (bf16[224,1024]{1,0:T(8,128)(2,1)}, bf16[224,1024]{1,0:T(8,128)(2,1)}, u32[]{:S(2)}, u32[]{:S(2)}) collective-permute-start(bf16[224,1024]{1,0:T(8,128)(2,1)} %get-tuple-element.28), channel_id=1, source_target_pairs={{0,192},{8,200},{16,208},{24,216},{32,224},{40,232},{48,240},{56,2... | collective-permute-start | bytes 1376264 | tf_op jit(solution)/shard_map/ppermute | solution.py:178
  116.7 0.1 reshape.127
  116.8 0.1 pad_add_fusion.place
  116.9 7.7 %collective-permute-done.5.block1 = bf16[224,1024]{1,0:T(8,128)(2,1)S(1)} collective-permute-done((bf16[224,1024]{1,0:T(8,128)(2,1)}, bf16[224,1024]{1,0:T(8,128)(2,1)S(1)}, u32[]{:S(2)}, u32[]{:S(2)}) %collective-permute-start.5) | collective-permute-done | bytes 458784 | tf_op jit(solution)/shard_map/ppermute | solution.py:178
  124.6 0.8 copy-done.5
  125.4 0.5 collective-permute-done.6.block3
  125.9 1.4 copy.28.rows
  127.3 1.0 copy-done.2
  128.3 1.1 copy-done.4
  129.4 2.0 shard_map.109
  131.4 16.7 %all_to_all.46 = bf16[8,400,128]{2,1,0:T(8,128)(2,1)S(1)} all-to-all(bf16[8,400,128]{2,1,0:T(8,128)(2,1)S(1)} %shard_map.109), channel_id=1, replica_groups={{0,8,64,72,128,136,192,200},{16,24,80,88,144,152,208,216},{32,40,96,104..., dimensions={0} | all-to-all | bytes 1638400 | tf_op jit(solution)/shard_map/all_to_all | solution.py:32
  148.0 0.1 convert_reduce_fusion
  148.1 0.1 multiply_convert_fusion
  148.3 1.0 broadcast_in_dim.88
  149.3 6.6 %all-to-all-start.6 = ((bf16[8,384,128]{2,1,0:T(8,128)(2,1)}), bf16[8,384,128]{2,1,0:T(8,128)(2,1)S(1)}, u32[]{:S(2)}, u32[]{:S(2)}) async-start(bf16[8,384,128]{2,1,0:T(8,128)(2,1)} %broadcast_in_dim.88), calls=%async_computation.6 | async-start | bytes 1572864 | tf_op jit(solution)/shard_map/all_to_all | solution.py:28
  155.9 3.1 %collective-permute-start.7 = (bf16[224,1024]{1,0:T(8,128)(2,1)}, bf16[224,1024]{1,0:T(8,128)(2,1)S(1)}, u32[]{:S(2)}, u32[]{:S(2)}) collective-permute-start(bf16[224,1024]{1,0:T(8,128)(2,1)} %get-tuple-element.27), channel_id=1, source_target_pairs={{0,128},{8,136},{16,144},{24,152},{32,160},{40,168},{48,176},{56,1... | collective-permute-start | bytes 1376264 | tf_op jit(solution)/shard_map/ppermute | solution.py:178
  159.0 9.0 %collective-permute-done.7.block2 = bf16[224,1024]{1,0:T(8,128)(2,1)S(1)} collective-permute-done((bf16[224,1024]{1,0:T(8,128)(2,1)}, bf16[224,1024]{1,0:T(8,128)(2,1)S(1)}, u32[]{:S(2)}, u32[]{:S(2)}) %collective-permute-start.7) | collective-permute-done | bytes 458784 | tf_op jit(solution)/shard_map/ppermute | solution.py:178
  168.0 7.6 %all-to-all-done.6.act = bf16[8,384,128]{2,1,0:T(8,128)(2,1)S(1)} async-done(((bf16[8,384,128]{2,1,0:T(8,128)(2,1)}), bf16[8,384,128]{2,1,0:T(8,128)(2,1)S(1)}, u32[]{:S(2)}, u32[]{:S(2)}) %all-to-all-start.6) | async-done | bytes 786464 | tf_op jit(solution)/shard_map/all_to_all | solution.py:28
  175.6 2.2 %shard_map.110 = bf16[4,224,384]{2,1,0:T(8,128)(2,1)S(1)} custom-call(s32[2]{0:T(128)S(1)} %pad_add_fusion.place, bf16[8,384,128]{2,1,0:T(8,128)(2,1)S(1)} %all-to-all-done.6.act, bf16[224,1024]{1,0:T(8,128)(2,1)S(1)} %get-tuple-element.30.block0, bf16[224,1024]{1,0:T(8,128)(2,1)S(1)} %copy-done.6, bf16[224,1024]{1,0:T(8,128)(2,1)S(1)} %collective-permute-done.7.block2, ...), custom_call_target="tpu_custom_call" | custom-call | flops 704643072 | bytes 5242880 | tf_op jit(solution)/shard_map/pallas_call | solution.py:105
  177.8 11.4 %all_to_all.47 = bf16[4,224,384]{2,1,0:T(8,128)(2,1)S(1)} all-to-all(bf16[4,224,384]{2,1,0:T(8,128)(2,1)S(1)} %shard_map.110), channel_id=1, replica_groups={{0,64,128,192},{8,72,136,200},{16,80,144,208},{24,88,152,216},{32,96,16..., dimensions={0} | all-to-all | bytes 1376256 | tf_op jit(solution)/shard_map/all_to_all | solution.py:32
  189.2 0.1 reduce_sum.52
  189.3 0.8 copy.29
  190.2 7.2 %all-to-all-start.8 = ((bf16[16,24,224]{2,1,0:T(8,128)(2,1)}), bf16[16,24,224]{2,1,0:T(8,128)(2,1)S(1)}, u32[]{:S(2)}, u32[]{:S(2)}) async-start(bf16[16,24,224]{2,1,0:T(8,128)(2,1)} %bitcast.30), calls=%async_computation.8 | async-start | bytes 393216 | tf_op jit(solution)/shard_map/all_to_all | solution.py:32
  197.3 0.8 fusion.21
  198.1 8.8 %all-to-all-done.8 = bf16[16,24,224]{2,1,0:T(8,128)(2,1)S(1)} async-done(((bf16[16,24,224]{2,1,0:T(8,128)(2,1)}), bf16[16,24,224]{2,1,0:T(8,128)(2,1)S(1)}, u32[]{:S(2)}, u32[]{:S(2)}) %all-to-all-start.8) | async-done | bytes 172064 | tf_op jit(solution)/shard_map/all_to_all | solution.py:32
  207.0 0.2 convolution_bitcast_fusion.1
  207.2 0.8 fusion.2
  (40 shorter events, 0.2 us)
Async XLA Ops:
  0.0 11.3 %copy-start = (bf16[32,32,256]{2,1,0:T(8,128)(2,1)S(1)}, bf16[32,32,256]{2,1,0:T(8,128)(2,1)}, u32[]{:S(2)}) copy-start(bf16[32,32,256]{2,1,0:T(8,128)(2,1)} %param.13) | copy-start | bytes 1572868
  0.0 9.6 %copy-start.9 = (bf16[32,512]{1,0:T(8,128)(2,1)S(1)}, bf16[32,512]{1,0:T(8,128)(2,1)}, u32[]{:S(2)}) copy-start(bf16[32,512]{1,0:T(8,128)(2,1)} %param.11) | copy-start | bytes 98308
  0.0 9.7 %copy-start.13 = (s32[32]{0:T(128)S(1)}, s32[32]{0:T(128)}, u32[]{:S(2)}) copy-start(s32[32]{0:T(128)} %param.14) | copy-start | bytes 388
  2.6 28.5 %collective-permute-start = (bf16[1792,128]{1,0:T(8,128)(2,1)}, bf16[1792,128]{1,0:T(8,128)(2,1)S(1)}, u32[]{:S(2)}, u32[]{:S(2)}) collective-permute-start(bf16[1792,128]{1,0:T(8,128)(2,1)} %get-tuple-element.33), channel_id=1, source_target_pairs={{0,64},{8,72},{16,80},{24,88},{32,96},{40,104},{48,112},{56,120},{... | collective-permute-start | bytes 1376264 | tf_op jit(solution)/shard_map/ppermute | solution.py:172
  6.0 25.1 %collective-permute-start.1 = (bf16[1792,128]{1,0:T(8,128)(2,1)S(1)}, bf16[1792,128]{1,0:T(8,128)(2,1)S(1)}, u32[]{:S(2)}, u32[]{:S(2)}) collective-permute-start(bf16[1792,128]{1,0:T(8,128)(2,1)S(1)} %get-tuple-element.32), channel_id=1, source_target_pairs={{0,192},{8,200},{16,208},{24,216},{32,224},{40,232},{48,240},{56,2... | collective-permute-start | bytes 1376264 | tf_op jit(solution)/shard_map/ppermute | solution.py:172
  32.1 19.5 %copy-start.7 = (bf16[512,224]{0,1:T(8,128)(2,1)S(1)}, bf16[512,224]{0,1:T(8,128)(2,1)}, u32[]{:S(2)}) copy-start(bf16[512,224]{0,1:T(8,128)(2,1)} %param.15) | copy-start | bytes 688132
  32.1 18.2 %all-to-all-start.1 = ((bf16[8,128,512]{2,1,0:T(8,128)(2,1)}), bf16[8,128,512]{2,1,0:T(8,128)(2,1)}, u32[]{:S(2)}, u32[]{:S(2)}) async-start(bf16[8,128,512]{2,1,0:T(8,128)(2,1)} %broadcast_in_dim.85), calls=%async_computation.1 | async-start | bytes 2097152 | tf_op jit(solution)/shard_map/all_to_all | solution.py:28
  53.2 29.6 %copy-start.8 = (bf16[64,224]{1,0:T(8,128)(2,1)S(1)}, bf16[64,224]{1,0:T(8,128)(2,1)}, u32[]{:S(2)}) copy-start(bf16[64,224]{1,0:T(8,128)(2,1)} %param.16) | copy-start | bytes 86020
  53.2 28.2 %all-to-all-start.2 = ((bf16[16,64,224]{2,1,0:T(8,128)(2,1)}), bf16[16,64,224]{2,1,0:T(8,128)(2,1)}, u32[]{:S(2)}, u32[]{:S(2)}) async-start(bf16[16,64,224]{2,1,0:T(8,128)(2,1)} %bitcast.14), calls=%async_computation.2 | async-start | bytes 1048576 | tf_op jit(solution)/shard_map/all_to_all | solution.py:32
  61.8 19.6 %collective-permute-start.3 = (bf16[3,4,224,128]{3,2,1,0:T(8,128)(2,1)}, bf16[3,4,224,128]{3,2,1,0:T(8,128)(2,1)S(1)}, u32[]{:S(2)}, u32[]{:S(2)}) collective-permute-start(bf16[3,4,224,128]{3,2,1,0:T(8,128)(2,1)} %pad_maximum_fusion), channel_id=1, source_target_pairs={{0,8},{8,0},{16,24},{24,16},{32,40},{40,32},{48,56},{56,48},{64,72... | collective-permute-start | bytes 2064392 | tf_op jit(solution)/shard_map/ppermute | solution.py:191
  64.5 15.9 %collective-permute-start.2 = (bf16[1792,128]{1,0:T(8,128)(2,1)}, bf16[1792,128]{1,0:T(8,128)(2,1)S(1)}, u32[]{:S(2)}, u32[]{:S(2)}) collective-permute-start(bf16[1792,128]{1,0:T(8,128)(2,1)} %get-tuple-element.34), channel_id=1, source_target_pairs={{0,128},{8,136},{16,144},{24,152},{32,160},{40,168},{48,176},{56,1... | collective-permute-start | bytes 1376264 | tf_op jit(solution)/shard_map/ppermute | solution.py:172
  68.0 13.4 %copy-start.11 = (s32[16,64]{1,0:T(8,128)}, s32[16,64]{1,0:T(8,128)S(1)}, u32[]{:S(2)}) copy-start(s32[16,64]{1,0:T(8,128)S(1)} %convolution_convert_fusion.3) | copy-start | bytes 12292
  80.4 22.4 %copy-start.1 = (bf16[1792,128]{1,0:T(8,128)(2,1)}, bf16[1792,128]{1,0:T(8,128)(2,1)S(1)}, u32[]{:S(2)}) copy-start(bf16[1792,128]{1,0:T(8,128)(2,1)S(1)} %collective-permute-done.2) | copy-start | bytes 1376260
  81.4 21.4 %copy-start.3 = (bf16[3,4,224,128]{3,2,1,0:T(8,128)(2,1)}, bf16[3,4,224,128]{3,2,1,0:T(8,128)(2,1)S(1)}, u32[]{:S(2)}) copy-start(bf16[3,4,224,128]{3,2,1,0:T(8,128)(2,1)S(1)} %collective-permute-done.3.got) | copy-start | bytes 2064388
  83.9 16.9 %all-to-all-start.3 = ((bf16[16,24,224]{2,1,0:T(8,128)(2,1)}), bf16[16,24,224]{2,1,0:T(8,128)(2,1)}, u32[]{:S(2)}, u32[]{:S(2)}) async-start(bf16[16,24,224]{2,1,0:T(8,128)(2,1)} %bitcast.21), calls=%async_computation.3 | async-start | bytes 393216 | tf_op jit(solution)/shard_map/all_to_all | solution.py:32
  91.1 9.6 %collective-permute-start.4 = (bf16[4,224,128]{2,1,0:T(8,128)(2,1)S(1)}, bf16[4,224,128]{2,1,0:T(8,128)(2,1)S(1)}, u32[]{:S(2)}, u32[]{:S(2)}) collective-permute-start(bf16[4,224,128]{2,1,0:T(8,128)(2,1)S(1)} %dynamic-slice_bitcast_fusion.7), channel_id=1, source_target_pairs={{0,8},{8,0},{16,24},{24,16},{32,40},{40,32},{48,56},{56,48},{64,72... | collective-permute-start | bytes 688136 | tf_op jit(solution)/shard_map/ppermute | solution.py:199
  102.8 23.1 %all-to-all-start.4 = ((bf16[4,384,224]{1,2,0:T(8,128)(2,1)}), bf16[4,384,224]{1,2,0:T(8,128)(2,1)}, u32[]{:S(2)}, u32[]{:S(2)}) async-start(bf16[4,384,224]{1,2,0:T(8,128)(2,1)} %broadcast_in_dim.87), calls=%async_computation.4 | async-start | bytes 1376256 | tf_op jit(solution)/shard_map/all_to_all | solution.py:28
  107.0 9.6 %copy-start.10 = (f32[7168]{0:T(1024)S(1)}, f32[7168]{0:T(1024)}, u32[]{:S(2)}) copy-start(f32[7168]{0:T(1024)} %param.17) | copy-start | bytes 86020
  109.6 15.0 %collective-permute-start.5 = (bf16[224,1024]{1,0:T(8,128)(2,1)}, bf16[224,1024]{1,0:T(8,128)(2,1)S(1)}, u32[]{:S(2)}, u32[]{:S(2)}) collective-permute-start(bf16[224,1024]{1,0:T(8,128)(2,1)} %get-tuple-element.29), channel_id=1, source_target_pairs={{0,64},{8,72},{16,80},{24,88},{32,96},{40,104},{48,112},{56,120},{... | collective-permute-start | bytes 1376264 | tf_op jit(solution)/shard_map/ppermute | solution.py:178
  111.5 14.4 %collective-permute-start.6 = (bf16[224,1024]{1,0:T(8,128)(2,1)}, bf16[224,1024]{1,0:T(8,128)(2,1)}, u32[]{:S(2)}, u32[]{:S(2)}) collective-permute-start(bf16[224,1024]{1,0:T(8,128)(2,1)} %get-tuple-element.28), channel_id=1, source_target_pairs={{0,192},{8,200},{16,208},{24,216},{32,224},{40,232},{48,240},{56,2... | collective-permute-start | bytes 1376264 | tf_op jit(solution)/shard_map/ppermute | solution.py:178
  124.6 0.8 copy-start.5
  127.3 1.0 copy-start.2
  128.3 1.1 copy-start.4
  148.0 27.6 %copy-start.6 = (bf16[224,1024]{1,0:T(8,128)(2,1)S(1)}, bf16[224,1024]{1,0:T(8,128)(2,1)}, u32[]{:S(2)}) copy-start(bf16[224,1024]{1,0:T(8,128)(2,1)} %copy-done.5) | copy-start | bytes 1376260
  149.3 26.3 %all-to-all-start.6 = ((bf16[8,384,128]{2,1,0:T(8,128)(2,1)}), bf16[8,384,128]{2,1,0:T(8,128)(2,1)S(1)}, u32[]{:S(2)}, u32[]{:S(2)}) async-start(bf16[8,384,128]{2,1,0:T(8,128)(2,1)} %broadcast_in_dim.88), calls=%async_computation.6 | async-start | bytes 1572864 | tf_op jit(solution)/shard_map/all_to_all | solution.py:28
  155.9 12.1 %collective-permute-start.7 = (bf16[224,1024]{1,0:T(8,128)(2,1)}, bf16[224,1024]{1,0:T(8,128)(2,1)S(1)}, u32[]{:S(2)}, u32[]{:S(2)}) collective-permute-start(bf16[224,1024]{1,0:T(8,128)(2,1)} %get-tuple-element.27), channel_id=1, source_target_pairs={{0,128},{8,136},{16,144},{24,152},{32,160},{40,168},{48,176},{56,1... | collective-permute-start | bytes 1376264 | tf_op jit(solution)/shard_map/ppermute | solution.py:178
  177.8 29.2 %copy-start.12 = (s32[16,64]{1,0:T(8,128)S(1)}, s32[16,64]{1,0:T(8,128)}, u32[]{:S(2)}) copy-start(s32[16,64]{1,0:T(8,128)} %copy-done.11) | copy-start | bytes 12292
  190.2 16.8 %all-to-all-start.8 = ((bf16[16,24,224]{2,1,0:T(8,128)(2,1)}), bf16[16,24,224]{2,1,0:T(8,128)(2,1)S(1)}, u32[]{:S(2)}, u32[]{:S(2)}) async-start(bf16[16,24,224]{2,1,0:T(8,128)(2,1)} %bitcast.30), calls=%async_computation.8 | async-start | bytes 393216 | tf_op jit(solution)/shard_map/all_to_all | solution.py:32

commit v5 on v4

--- a/solution.py
+++ b/solution.py
@@ -32,63 +32,105 @@
     return lax.all_to_all(value, axis, 0, 0, tiled=True, axis_index_groups=groups)
 
 
-def up_kernel(place, rows, gain, block0, block1, block2, block3, got, got2, out):
+def whole(count):
+    return [pl.BlockSpec(memory_space=pltpu.VMEM)] * count
+
+
+PARAMS = pltpu.CompilerParams(vmem_limit_bytes=40 * 2**20)
+
+
+def project_kernel(attn, weight, out):
+    run = attn.shape[2]
+    for x in range(NX):
+        value = jnp.concatenate(
+            [attn[x * PAIR + m].reshape(NZ * run, attn.shape[3]) for m in range(PAIR)], axis=0
+        )
+        value = jnp.dot(value, weight[...], preferred_element_type=F32).astype(BF16)
+        for m in range(PAIR):
+            for z in range(NZ):
+                first = (m * NZ + z) * run
+                out[x * NZ + z, m * run : (m + 1) * run] = value[first : first + run]
+
+
+def project(attn, weight):
+    rows, columns = PAIR * attn.shape[2], weight.shape[1]
+    return pl.pallas_call(
+        project_kernel,
+        out_shape=jax.ShapeDtypeStruct((NX * NZ, rows, columns), BF16),
+        in_specs=whole(2),
+        out_specs=whole(1)[0],
+        compiler_params=PARAMS,
+        cost_estimate=pl.CostEstimate(
+            flops=2 * NX * NZ * rows * columns * weight.shape[0], bytes_accessed=2 * 2**20, transcendentals=0
+        ),
+    )(attn, weight)
+
+
+def head_sum_kernel(parts, residual, select, out):
+    total = residual[...].astype(F32)
+    for i in range(parts.shape[0]):
+        total += parts[i].astype(F32)
+    out[...] = jnp.dot(select[...], total.astype(BF16), preferred_element_type=F32).astype(BF16)
+
+
+def head_sum(parts, residual, select):
+    slots, columns = select.shape[0], residual.shape[1]
+    return pl.pallas_call(
+        head_sum_kernel,
+        out_shape=jax.ShapeDtypeStruct((slots, columns), BF16),
+        in_specs=whole(3),
+        out_specs=whole(1)[0],
+        compiler_params=PARAMS,
+        cost_estimate=pl.CostEstimate(
+            flops=2 * slots * columns * residual.shape[0], bytes_accessed=2**20, transcendentals=0
+        ),
+    )(parts, residual, select)
+
+
+def up_kernel(place, rows, gain, own, got, left, far, right, out):
     x_index, member = place[0], place[1]
-    slots, units = rows.shape[1], out.shape[2]
-    normed, squares = [], 0.0
-    ones = jnp.ones((16, rows.shape[2]), BF16)
-    dims = (((1,), (1,)), ((), ()))
-    for z in range(NZ):
-        value = rows[z].astype(F32)
-        normed.append((value * gain[z][None, :]).astype(BF16))
-        square = value * value
-        high = square.astype(BF16)
-        low = (square - high.astype(F32)).astype(BF16)
-        squares += lax.dot_general(ones, high, dims, preferred_element_type=F32)
-        squares += lax.dot_general(ones, low, dims, preferred_element_type=F32)
+    slots, units = rows.shape[2], out.shape[2]
+    depth = NZ * rows.shape[1]
+    value = rows[...].astype(F32).reshape(depth, slots)
+    squares = jnp.sum(value * value, axis=0, keepdims=True)
+    normed = (value * gain[...]).astype(BF16).T
     row = lax.broadcasted_iota(jnp.int32, (16, units), 0)
     count = slots // units
     tail = jnp.zeros((16, units), F32)
     for i in range(count):
-        part = squares[:, i * units : (i + 1) * units]
+        part = jnp.broadcast_to(squares[:, i * units : (i + 1) * units], (16, units))
         high = part.astype(BF16).astype(F32)
         tail = jnp.where(row == i, high, tail)
         tail = jnp.where(row == count + i, part - high, tail)
     tail = tail.astype(BF16)
-    for step, block in enumerate((block0, block1, block2, block3)):
-        total = 0.0
-        for z in range(NZ):
-            other = got2[z] if step == 2 else got[min(step, 2), z]
-            both = jnp.concatenate([block[z, member], other], axis=1)
-            total += jnp.dot(normed[z], both, preferred_element_type=F32)
-        total = total.astype(BF16)
+    blocks = [(own[x_index], got[x_index])] + [(b[0], b[1]) for b in (left, far, right)]
+    for step, block in enumerate(blocks):
+        total = jnp.dot(normed, jnp.concatenate(block, axis=1), preferred_element_type=F32).astype(BF16)
         first = lax.rem(x_index + NX - step, NX) * PAIR
         for target, part in ((first + member, total[:, :units]), (first + 1 - member, total[:, units:])):
             out[target, :slots] = part
             out[target, slots:] = tail
 
 
-def up_product(place, rows, gain, blocks, got, got2):
-    slots, columns = rows.shape[1:]
-    units = got.shape[3]
-    vmem = pl.BlockSpec(memory_space=pltpu.VMEM)
+def up_product(place, rows, gain, blocks):
+    columns, slots = rows.shape[1:]
+    units = blocks[0].shape[2]
     return pl.pallas_call(
         up_kernel,
         out_shape=jax.ShapeDtypeStruct((NX * PAIR, slots + 16, units), BF16),
-        in_specs=[pl.BlockSpec(memory_space=pltpu.SMEM)] + [vmem] * 8,
-        out_specs=vmem,
-        compiler_params=pltpu.CompilerParams(vmem_limit_bytes=40 * 2**20),
+        in_specs=[pl.BlockSpec(memory_space=pltpu.SMEM)] + whole(7),
+        out_specs=whole(1)[0],
+        compiler_params=PARAMS,
         cost_estimate=pl.CostEstimate(
             flops=2 * slots * columns * NZ * NX * PAIR * units, bytes_accessed=6 * 2**20, transcendentals=0
         ),
-    )(place, rows, gain, *blocks, got, got2)
+    )(place, rows, gain, *blocks)
 
 
 def down_kernel(place, act, block0, block1, block2, block3, out):
     x_index = place[0]
-    count = act.shape[0]
+    count, units = act.shape[0], act.shape[2]
     dims = (((1,), (1,)), ((), ()))
-    units = act.shape[2]
     joined = [jnp.concatenate([act[z], act[z + 1]], axis=1) for z in range(0, count, 2)]
     for step, block in enumerate((block0, block1, block2, block3)):
         total = 0.0
@@ -101,13 +143,12 @@
 def down_product(place, act, blocks):
     count, slots, units = act.shape
     columns = blocks[0].shape[0]
-    vmem = pl.BlockSpec(memory_space=pltpu.VMEM)
     return pl.pallas_call(
         down_kernel,
         out_shape=jax.ShapeDtypeStruct((NX, columns, slots), BF16),
-        in_specs=[pl.BlockSpec(memory_space=pltpu.SMEM)] + [vmem] * 5,
-        out_specs=vmem,
-        compiler_params=pltpu.CompilerParams(vmem_limit_bytes=40 * 2**20),
+        in_specs=[pl.BlockSpec(memory_space=pltpu.SMEM)] + whole(5),
+        out_specs=whole(1)[0],
+        compiler_params=PARAMS,
         cost_estimate=pl.CostEstimate(
             flops=2 * slots * columns * NX * count * units, bytes_accessed=5 * 2**20, transcendentals=0
         ),
@@ -166,53 +207,47 @@
     combine = jnp.where(here, weight_of[:, None, :], 0.0).reshape(slots, rows)
 
     attn = attend(queries, keys, values, lengths)
+
+    def up_half(which):
+        up_parts = up_weight[0].reshape(NX, NZ, PAIR, columns, units)
+        half = lax.dynamic_index_in_dim(up_parts, which, 2, keepdims=False)
+        return half.reshape(NX, NZ * columns, units)
+
     def up_block(step):
         wanted = (x_index + step) % NX
-        block = lax.dynamic_slice_in_dim(up_weight[0], wanted * (width // NX), width // NX, 0)
-        block = lax.ppermute(block, "grp", moves(step, 0)) if step else block
-        return block.reshape(NZ, PAIR, columns, units)
+        block = [lax.dynamic_index_in_dim(w, wanted, 0, keepdims=False) for w in (own, got)]
+        return lax.ppermute(jnp.stack(block), "grp", moves(step, 0))
 
     def down_block(step):
         wanted = (x_index + step) % NX
         block = lax.dynamic_slice_in_dim(down_weight[0], wanted * (8 * units), 8 * units, 1)
         return lax.ppermute(block, "grp", moves(step, 0)) if step else block
 
-    def other_half(block):
-        return lax.dynamic_index_in_dim(block, 1 - member, 1, keepdims=False)
-
     attn = spread(attn, NZ, "grp", GATHER)
-    attn, up1, up3 = lax.optimization_barrier((attn, up_block(1), up_block(3)))
     attn = spread(attn.reshape(-1, attn.shape[2]), parts, "grp", REDUCE)
-    attn = attn.reshape(NX, PAIR, NZ, -1, attn.shape[2]).transpose(0, 2, 1, 3, 4)
-    attn = attn.reshape(experts * rows, attn.shape[4])
-    projected = jnp.dot(attn, out_weight, preferred_element_type=F32).astype(BF16)
-
-    up0 = up_block(0)
-    got = lax.ppermute(jnp.stack([other_half(w) for w in (up0, up1, up3)]), "grp", moves(0, 1))
-    projected = exchange(projected.reshape(experts, rows, columns), ("pool", "tp"))
-    projected, up2, got = lax.optimization_barrier((projected, up_block(2), got))
-    hidden = jnp.sum(projected.astype(F32), axis=0) + residual.astype(F32)
-    hidden = hidden.astype(BF16)
-
-    slot_rows = jnp.dot(select, hidden, preferred_element_type=F32).astype(BF16)
+    attn, up_weight = lax.optimization_barrier((attn, up_weight))
+    projected = project(attn.reshape(parts, NZ, -1, attn.shape[2]), out_weight)
+    projected = exchange(projected, ("pool", "tp"))
+    own, got = up_half(member), lax.ppermute(up_half(1 - member), "grp", moves(0, 1))
+    projected, got = lax.optimization_barrier((projected, got))
+    slot_rows = head_sum(projected, residual, select)
     slot_rows = exchange(slot_rows.reshape(experts, slot_cap, columns), ("pool", "tp"))
-    got2 = lax.ppermute(other_half(up2), "grp", moves(0, 1))
-    slot_rows, got2 = lax.optimization_barrier((slot_rows, got2))
-    slot_rows = spread(slot_rows.reshape(slots, columns), NZ, "grp", GATHER)
-    slot_rows, down1, down3 = lax.optimization_barrier((slot_rows, down_block(1), down_block(3)))
+    slot_rows, own, got = lax.optimization_barrier((slot_rows, own, got))
+    slot_rows = spread(slot_rows.reshape(slots, columns).T, NZ, "grp", GATHER)
     gain = norm_gain.reshape(NX, NZ, PAIR, columns)
     gain = lax.dynamic_index_in_dim(gain, x_index, 0, keepdims=False)
-    gain = lax.dynamic_index_in_dim(gain, member, 1, keepdims=False)
+    gain = lax.dynamic_index_in_dim(gain, member, 1, keepdims=False).reshape(NZ * columns, 1)
     place = jnp.stack([x_index, member]).astype(jnp.int32)
-    partial_up = up_product(place, slot_rows, gain, (up0, up1, up2, up3), got, got2)
+    partial_up = up_product(place, slot_rows, gain, (own, got, up_block(1), up_block(2), up_block(3)))
     total_up = jnp.sum(exchange(partial_up, "grp", REDUCE).astype(F32), axis=0)
     count = slots // units
     squares = (total_up[slots : slots + count] + total_up[slots + count : slots + 2 * count]).reshape(slots, 1)
     scale = lax.rsqrt(squares / width + 1e-06)
     act = jax.nn.silu(total_up[:slots] * scale).astype(BF16)
 
+    act, down_weight = lax.optimization_barrier((act, down_weight))
     act = spread(act, 8, "grp", LINE)
-    partial_out = exchange(down_product(place, act, (down_block(0), down1, down_block(2), down3)), "grp", CROSS)
+    partial_out = exchange(down_product(place, act, [down_block(step) for step in range(NX)]), "grp", CROSS)
     expert_out = jnp.sum(partial_out.astype(F32), axis=0).astype(BF16).T
     returned = exchange(expert_out.reshape(experts, slot_cap, columns), ("pool", "tp"))
     returned = returned.reshape(slots, columns)

time: 209 us -> 213 us (1.019)
  blocking collectives: 47.2 us -> 64 us
  starting transfers between devices: 62.3 us -> 47.3 us
  waiting for transfers between devices: 67.7 us -> 73.4 us
  local copies, waits for them, and re-layouts: 19.3 us -> 14.6 us
    all_to_all x2 -> x3, blocking collectives: 28.1 us -> 44.6 us  [exchange(): lax.all_to_all(value, axis, 0, 0, tiled=True, axis_index_groups=groups)]
    all_to_all x3 -> x2, waiting for transfers between devices: 8.98 us -> 24.1 us  [exchange(): lax.all_to_all(value, axis, 0, 0, tiled=True, axis_index_groups=groups)]
    all_to_all x3 -> x2, starting transfers between devices: 22.1 us -> 11.9 us  [exchange(): lax.all_to_all(value, axis, 0, 0, tiled=True, axis_index_groups=groups)]
    all_to_all x3, waiting for transfers between devices: 21.4 us -> 14.6 us  [spread(): lax.all_to_all(sent, axis, 0, 0, tiled=True, axis_index_groups=groups)]
    ppermute x5 -> x4, starting transfers between devices: 14.9 us -> 11.2 us  [the longest x3 8.33 us: up_block(): return lax.ppermute(jnp.stack(block), 'grp', moves(step, 0))]
    ppermute x5 -> x4, waiting for transfers between devices: 20.1 us -> 18.1 us  [the longest x3 18.1 us: up_block(): return lax.ppermute(jnp.stack(block), 'grp', moves(step, 0))]
  transfers between devices with their start and end apart: 14 -> 12, of which waited for: 10 -> 8; matrix products, arithmetic and copies ran while one was open for 4% -> 4% of each run, Pallas kernels for 0% -> 0%
where the time goes in v5:
time: 213 us; the launch traced here: 212 us
  waiting for transfers between devices  73.4 us (34%)
  blocking collectives  64 us (30%)
  starting transfers between devices  47.3 us (22%)
  local copies, waits for them, and re-layouts  14.6 us (7%)
  Pallas kernels  4.99 us (2%)
  other arithmetic  3.96 us (2%)
  matrix products  3.03 us (1%)
    all_to_all x3, blocking collectives, exchange(): lax.all_to_all(value, axis, 0, 0, tiled=True, axis_index_groups=groups)  44.6 us
    all_to_all x2, waiting for transfers between devices, exchange(): lax.all_to_all(value, axis, 0, 0, tiled=True, axis_index_groups=groups)  24.1 us
    all_to_all x1, blocking collectives, spread(): lax.all_to_all(sent, axis, 0, 0, tiled=True, axis_index_groups=groups)  19.4 us
    ppermute x3, waiting for transfers between devices, up_block(): return lax.ppermute(jnp.stack(block), 'grp', moves(step, 0))  18.1 us
    ppermute x3, waiting for transfers between devices, down_block(): return lax.ppermute(block, 'grp', moves(step, 0)) if step else block  16.6 us
    all_to_all x3, waiting for transfers between devices, spread(): lax.all_to_all(sent, axis, 0, 0, tiled=True, axis_index_groups=groups)  14.6 us
    all_to_all x3, starting transfers between devices, spread(): lax.all_to_all(sent, axis, 0, 0, tiled=True, axis_index_groups=groups)  14.6 us
    all_to_all x2, starting transfers between devices, exchange(): lax.all_to_all(value, axis, 0, 0, tiled=True, axis_index_groups=groups)  11.9 us
  transfers between devices with their start and end apart: 12, of which 8 were waited for; matrix products, arithmetic and copies ran while one was open for 4% of the time, Pallas kernels for 0%

profile of v5, /device:TPU:8, one launch (start us, length us, event | category | flops | bytes accessed | tf_op | source)
XLA Modules:
  0.0 211.5 jit_solution(9780585289090350320)
XLA Ops:
  0.0 0.8 reshape.107
  0.8 0.7 iota_compare_fusion.4
  1.6 1.3 fusion.5
  2.9 0.2 fusion.29
  3.1 0.6 convolution_convert_fusion
  3.7 19.4 %all_to_all.45 = bf16[4,32,512]{2,1,0:T(8,128)(2,1)S(1)} all-to-all(bf16[4,32,512]{2,1,0:T(8,128)(2,1)S(1)} %broadcast_in_dim.82), channel_id=1, replica_groups={{0,16,32,48},{8,24,40,56},{64,80,96,112},{72,88,104,120},{128,144,160,1..., dimensions={0} | all-to-all | bytes 262144 | tf_op jit(solution)/shard_map/all_to_all | solution.py:28
  23.0 1.1 broadcast_in_dim.84
  24.1 4.3 %all-to-all-start.1 = ((bf16[8,128,512]{2,1,0:T(8,128)(2,1)}), bf16[8,128,512]{2,1,0:T(8,128)(2,1)S(1)}, u32[]{:S(2)}, u32[]{:S(2)}) async-start(bf16[8,128,512]{2,1,0:T(8,128)(2,1)} %broadcast_in_dim.84), calls=%async_computation.1 | async-start | bytes 2097152 | tf_op jit(solution)/shard_map/all_to_all | solution.py:28
  28.4 14.6 %all-to-all-done.1 = bf16[8,128,512]{2,1,0:T(8,128)(2,1)S(1)} async-done(((bf16[8,128,512]{2,1,0:T(8,128)(2,1)}), bf16[8,128,512]{2,1,0:T(8,128)(2,1)S(1)}, u32[]{:S(2)}, u32[]{:S(2)}) %all-to-all-start.1) | async-done | bytes 1048608 | tf_op jit(solution)/shard_map/all_to_all | solution.py:28
  43.0 2.5 %constant_dynamic-slice_fusion.6 = (bf16[4,4,1,224,128]{4,3,2,1,0:T(8,128)(2,1)S(1)}, bf16[4,4,1,224,128]{4,3,2,1,0:T(8,128)(2,1)}) fusion(bf16[4,4,2,224,128]{4,3,2,1,0:T(8,128)(2,1)} %bitcast.61, s32[]{:T(128)S(6)} %select_n.101, s32[]{:T(128)S(6)} %select_n.100), kind=kLoop, calls=%fused_computation.51 | loop fusion | bytes 3670024 | tf_op jit(solution)/shard_map/jit(dynamic_index_in_dim)/dynamic_slice | solution.py:213
  45.6 2.8 %collective-permute-start = (bf16[4,896,128]{2,1,0:T(8,128)(2,1)}, bf16[4,896,128]{2,1,0:T(8,128)(2,1)S(1)}, u32[]{:S(2)}, u32[]{:S(2)}) collective-permute-start(bf16[4,896,128]{2,1,0:T(8,128)(2,1)} %bitcast.7), channel_id=1, source_target_pairs={{0,8},{8,0},{16,24},{24,16},{32,40},{40,32},{48,56},{56,48},{64,72... | collective-permute-start | bytes 2752520 | tf_op jit(solution)/shard_map/ppermute | solution.py:231
  48.4 1.8 copy.27.weight
  50.2 0.9 copy-done.2
  51.1 0.4 shard_map.109
  51.6 0.8 copy-done.1
  52.4 7.6 %all-to-all-start.2 = ((bf16[16,64,224]{2,1,0:T(8,128)(2,1)}), bf16[16,64,224]{2,1,0:T(8,128)(2,1)S(1)}, u32[]{:S(2)}, u32[]{:S(2)}) async-start(bf16[16,64,224]{2,1,0:T(8,128)(2,1)} %copy-done.1), calls=%async_computation.2 | async-start | bytes 1048576 | tf_op jit(solution)/shard_map/all_to_all | solution.py:32
  60.0 0.1 eq.57
  60.0 0.8 fusion.21
  60.8 0.1 convolution_convert_fusion.1
  60.9 0.1 fusion.9.select
  61.1 15.3 %all-to-all-done.2.parts = bf16[16,64,224]{2,1,0:T(8,128)(2,1)S(1)} async-done(((bf16[16,64,224]{2,1,0:T(8,128)(2,1)}), bf16[16,64,224]{2,1,0:T(8,128)(2,1)S(1)}, u32[]{:S(2)}, u32[]{:S(2)}) %all-to-all-start.2) | async-done | bytes 458784 | tf_op jit(solution)/shard_map/all_to_all | solution.py:32
  76.3 0.3 shard_map.110
  76.6 13.2 %all_to_all.46 = bf16[16,24,224]{2,1,0:T(8,128)(2,1)S(1)} all-to-all(bf16[16,24,224]{2,1,0:T(8,128)(2,1)S(1)} %bitcast.60), channel_id=1, replica_groups=mesh['pool'=2,'grp'=32,'tp'=8] {'pool','tp'}, dimensions={0} | all-to-all | bytes 344064 | tf_op jit(solution)/shard_map/all_to_all | solution.py:32
  89.8 0.1 copy.30
  90.0 0.9 broadcast_in_dim.85
  90.9 3.5 %all-to-all-start.4 = ((bf16[4,224,384]{2,1,0:T(8,128)(2,1)}), bf16[4,224,384]{2,1,0:T(8,128)(2,1)S(1)}, u32[]{:S(2)}, u32[]{:S(2)}) async-start(bf16[4,224,384]{2,1,0:T(8,128)(2,1)} %broadcast_in_dim.85), calls=%async_computation.4 | async-start | bytes 1376256 | tf_op jit(solution)/shard_map/all_to_all | solution.py:28
  94.5 0.1 constant_dynamic-slice_fusion
  94.6 0.0 copy-start.4
  94.6 0.8 pad_maximum_fusion.2
  95.4 3.1 %collective-permute-start.3 = (bf16[2,896,128]{2,1,0:T(8,128)(2,1)}, bf16[2,896,128]{2,1,0:T(8,128)(2,1)}, u32[]{:S(2)}, u32[]{:S(2)}) collective-permute-start(bf16[2,896,128]{2,1,0:T(8,128)(2,1)} %pad_maximum_fusion.2), channel_id=1, source_target_pairs={{0,192},{8,200},{16,208},{24,216},{32,224},{40,232},{48,240},{56,2... | collective-permute-start | bytes 1376264 | tf_op jit(solution)/shard_map/ppermute | solution.py:219
  98.5 0.8 pad_maximum_fusion.1
  99.3 3.4 %collective-permute-start.2 = (bf16[2,896,128]{2,1,0:T(8,128)(2,1)}, bf16[2,896,128]{2,1,0:T(8,128)(2,1)}, u32[]{:S(2)}, u32[]{:S(2)}) collective-permute-start(bf16[2,896,128]{2,1,0:T(8,128)(2,1)} %pad_maximum_fusion.1), channel_id=1, source_target_pairs={{0,128},{8,136},{16,144},{24,152},{32,160},{40,168},{48,176},{56,1... | collective-permute-start | bytes 1376264 | tf_op jit(solution)/shard_map/ppermute | solution.py:219
  102.6 0.8 pad_maximum_fusion
  103.5 1.9 collective-permute-start.1
  105.4 0.1 reshape.113
  105.5 0.3 reshape.118.gain
  105.9 0.1 pad_add_fusion.place
  105.9 5.1 %collective-permute-done.3.right = bf16[2,896,128]{2,1,0:T(8,128)(2,1)} collective-permute-done((bf16[2,896,128]{2,1,0:T(8,128)(2,1)}, bf16[2,896,128]{2,1,0:T(8,128)(2,1)}, u32[]{:S(2)}, u32[]{:S(2)}) %collective-permute-start.3) | collective-permute-done | bytes 458784 | tf_op jit(solution)/shard_map/ppermute | solution.py:219
  111.1 5.4 %collective-permute-done.2.far = bf16[2,896,128]{2,1,0:T(8,128)(2,1)} collective-permute-done((bf16[2,896,128]{2,1,0:T(8,128)(2,1)}, bf16[2,896,128]{2,1,0:T(8,128)(2,1)}, u32[]{:S(2)}, u32[]{:S(2)}) %collective-permute-start.2) | collective-permute-done | bytes 458784 | tf_op jit(solution)/shard_map/ppermute | solution.py:219
  116.5 7.5 %collective-permute-done.1.left = bf16[2,896,128]{2,1,0:T(8,128)(2,1)} collective-permute-done((bf16[2,896,128]{2,1,0:T(8,128)(2,1)}, bf16[2,896,128]{2,1,0:T(8,128)(2,1)}, u32[]{:S(2)}, u32[]{:S(2)}) %collective-permute-start.1) | collective-permute-done | bytes 458784 | tf_op jit(solution)/shard_map/ppermute | solution.py:219
  124.0 0.0 all-to-all-done.4.rows
  124.0 2.6 %shard_map.111 = bf16[8,400,128]{2,1,0:T(8,128)(2,1)S(1)} custom-call(s32[2]{0:T(128)S(1)} %pad_add_fusion.place, bf16[4,224,384]{2,1,0:T(8,128)(2,1)S(1)} %all-to-all-done.4.rows, f32[896,1]{1,0:T(8,128)S(1)} %reshape.118.gain, bf16[4,896,128]{2,1,0:T(8,128)(2,1)S(1)} %bitcast.58, bf16[4,896,128]{2,1,0:T(8,128)(2,1)S(1)} %collective-permute-done.got, ...), custom_call_target="tpu_custom_call" | custom-call | flops 704643072 | bytes 6291456 | tf_op jit(solution)/shard_map/pallas_call | solution.py:118
  126.6 16.3 %all_to_all.47 = bf16[8,400,128]{2,1,0:T(8,128)(2,1)S(1)} all-to-all(bf16[8,400,128]{2,1,0:T(8,128)(2,1)S(1)} %shard_map.111), channel_id=1, replica_groups={{0,8,64,72,128,136,192,200},{16,24,80,88,144,152,208,216},{32,40,96,104..., dimensions={0} | all-to-all | bytes 1638400 | tf_op jit(solution)/shard_map/all_to_all | solution.py:32
  142.9 0.1 convert_reduce_fusion
  143.0 0.1 multiply_convert_fusion
  143.1 1.0 broadcast_in_dim.86
  144.1 6.8 %all-to-all-start.6 = ((bf16[8,384,128]{2,1,0:T(8,128)(2,1)}), bf16[8,384,128]{2,1,0:T(8,128)(2,1)S(1)}, u32[]{:S(2)}, u32[]{:S(2)}) async-start(bf16[8,384,128]{2,1,0:T(8,128)(2,1)} %broadcast_in_dim.86), calls=%async_computation.6 | async-start | bytes 1572864 | tf_op jit(solution)/shard_map/all_to_all | solution.py:28
  150.9 1.6 dynamic-slice_bitcast_fusion
  152.5 2.5 %collective-permute-start.4 = (bf16[224,1024]{1,0:T(8,128)(2,1)S(1)}, bf16[224,1024]{1,0:T(8,128)(2,1)S(1)}, u32[]{:S(2)}, u32[]{:S(2)}) collective-permute-start(bf16[224,1024]{1,0:T(8,128)(2,1)S(1)} %get-tuple-element.25), channel_id=1, source_target_pairs={{0,64},{8,72},{16,80},{24,88},{32,96},{40,104},{48,112},{56,120},{... | collective-permute-start | bytes 1376264 | tf_op jit(solution)/shard_map/ppermute | solution.py:224
  155.0 4.0 %collective-permute-start.5 = (bf16[224,1024]{1,0:T(8,128)(2,1)S(1)}, bf16[224,1024]{1,0:T(8,128)(2,1)S(1)}, u32[]{:S(2)}, u32[]{:S(2)}) collective-permute-start(bf16[224,1024]{1,0:T(8,128)(2,1)S(1)} %get-tuple-element.24), channel_id=1, source_target_pairs={{0,128},{8,136},{16,144},{24,152},{32,160},{40,168},{48,176},{56,1... | collective-permute-start | bytes 1376264 | tf_op jit(solution)/shard_map/ppermute | solution.py:224
  159.1 3.1 %collective-permute-start.6 = (bf16[224,1024]{1,0:T(8,128)(2,1)S(1)}, bf16[224,1024]{1,0:T(8,128)(2,1)S(1)}, u32[]{:S(2)}, u32[]{:S(2)}) collective-permute-start(bf16[224,1024]{1,0:T(8,128)(2,1)S(1)} %get-tuple-element.23), channel_id=1, source_target_pairs={{0,192},{8,200},{16,208},{24,216},{32,224},{40,232},{48,240},{56,2... | collective-permute-start | bytes 1376264 | tf_op jit(solution)/shard_map/ppermute | solution.py:224
  162.1 14.0 %collective-permute-done.4.block1 = bf16[224,1024]{1,0:T(8,128)(2,1)S(1)} collective-permute-done((bf16[224,1024]{1,0:T(8,128)(2,1)S(1)}, bf16[224,1024]{1,0:T(8,128)(2,1)S(1)}, u32[]{:S(2)}, u32[]{:S(2)}) %collective-permute-start.4) | collective-permute-done | bytes 458784 | tf_op jit(solution)/shard_map/ppermute | solution.py:224
  176.2 0.0 collective-permute-done.5.block2
  176.2 2.5 %collective-permute-done.6.block3 = bf16[224,1024]{1,0:T(8,128)(2,1)S(1)} collective-permute-done((bf16[224,1024]{1,0:T(8,128)(2,1)S(1)}, bf16[224,1024]{1,0:T(8,128)(2,1)S(1)}, u32[]{:S(2)}, u32[]{:S(2)}) %collective-permute-start.6) | collective-permute-done | bytes 458784 | tf_op jit(solution)/shard_map/ppermute | solution.py:224
  178.7 0.0 all-to-all-done.6.act
  178.7 1.7 shard_map.112
  180.5 15.1 %all_to_all.48 = bf16[4,224,384]{2,1,0:T(8,128)(2,1)S(1)} all-to-all(bf16[4,224,384]{2,1,0:T(8,128)(2,1)S(1)} %shard_map.112), channel_id=1, replica_groups={{0,64,128,192},{8,72,136,200},{16,80,144,208},{24,88,152,216},{32,96,16..., dimensions={0} | all-to-all | bytes 1376256 | tf_op jit(solution)/shard_map/all_to_all | solution.py:32
  195.6 0.1 reduce_sum.42
  195.7 0.8 copy.32
  196.5 4.3 %all-to-all-start.8 = ((bf16[16,24,224]{2,1,0:T(8,128)(2,1)}), bf16[16,24,224]{2,1,0:T(8,128)(2,1)S(1)}, u32[]{:S(2)}, u32[]{:S(2)}) async-start(bf16[16,24,224]{2,1,0:T(8,128)(2,1)} %bitcast.20), calls=%async_computation.8 | async-start | bytes 393216 | tf_op jit(solution)/shard_map/all_to_all | solution.py:32
  200.8 0.8 fusion.22
  201.6 8.8 %all-to-all-done.8 = bf16[16,24,224]{2,1,0:T(8,128)(2,1)S(1)} async-done(((bf16[16,24,224]{2,1,0:T(8,128)(2,1)}), bf16[16,24,224]{2,1,0:T(8,128)(2,1)S(1)}, u32[]{:S(2)}, u32[]{:S(2)}) %all-to-all-start.8) | async-done | bytes 172064 | tf_op jit(solution)/shard_map/all_to_all | solution.py:32
  210.4 0.2 convolution_bitcast_fusion.1
  210.7 0.8 fusion.2
  (15 shorter events, 0.1 us)
Async XLA Ops:
  0.0 3.1 %copy-start = (bf16[32,32,256]{2,1,0:T(8,128)(2,1)S(1)}, bf16[32,32,256]{2,1,0:T(8,128)(2,1)}, u32[]{:S(2)}) copy-start(bf16[32,32,256]{2,1,0:T(8,128)(2,1)} %param.13) | copy-start | bytes 1572868
  24.1 18.9 %all-to-all-start.1 = ((bf16[8,128,512]{2,1,0:T(8,128)(2,1)}), bf16[8,128,512]{2,1,0:T(8,128)(2,1)S(1)}, u32[]{:S(2)}, u32[]{:S(2)}) async-start(bf16[8,128,512]{2,1,0:T(8,128)(2,1)} %broadcast_in_dim.84), calls=%async_computation.1 | async-start | bytes 2097152 | tf_op jit(solution)/shard_map/all_to_all | solution.py:28
  45.6 30.8 %copy-start.3 = (bf16[64,224]{1,0:T(8,128)(2,1)S(1)}, bf16[64,224]{1,0:T(8,128)(2,1)}, u32[]{:S(2)}) copy-start(bf16[64,224]{1,0:T(8,128)(2,1)} %residual.1) | copy-start | bytes 86020
  45.6 30.8 %collective-permute-start = (bf16[4,896,128]{2,1,0:T(8,128)(2,1)}, bf16[4,896,128]{2,1,0:T(8,128)(2,1)S(1)}, u32[]{:S(2)}, u32[]{:S(2)}) collective-permute-start(bf16[4,896,128]{2,1,0:T(8,128)(2,1)} %bitcast.7), channel_id=1, source_target_pairs={{0,8},{8,0},{16,24},{24,16},{32,40},{40,32},{48,56},{56,48},{64,72... | collective-permute-start | bytes 2752520 | tf_op jit(solution)/shard_map/ppermute | solution.py:231
  50.2 0.9 copy-start.2
  51.6 0.8 copy-start.1
  52.4 23.9 %all-to-all-start.2 = ((bf16[16,64,224]{2,1,0:T(8,128)(2,1)}), bf16[16,64,224]{2,1,0:T(8,128)(2,1)S(1)}, u32[]{:S(2)}, u32[]{:S(2)}) async-start(bf16[16,64,224]{2,1,0:T(8,128)(2,1)} %copy-done.1), calls=%async_computation.2 | async-start | bytes 1048576 | tf_op jit(solution)/shard_map/all_to_all | solution.py:32
  90.9 33.1 %all-to-all-start.4 = ((bf16[4,224,384]{2,1,0:T(8,128)(2,1)}), bf16[4,224,384]{2,1,0:T(8,128)(2,1)S(1)}, u32[]{:S(2)}, u32[]{:S(2)}) async-start(bf16[4,224,384]{2,1,0:T(8,128)(2,1)} %broadcast_in_dim.85), calls=%async_computation.4 | async-start | bytes 1376256 | tf_op jit(solution)/shard_map/all_to_all | solution.py:28
  94.6 10.8 %copy-start.4 = (f32[7168]{0:T(1024)S(1)}, f32[7168]{0:T(1024)}, u32[]{:S(2)}) copy-start(f32[7168]{0:T(1024)} %param.17) | copy-start | bytes 86020
  95.4 15.7 %collective-permute-start.3 = (bf16[2,896,128]{2,1,0:T(8,128)(2,1)}, bf16[2,896,128]{2,1,0:T(8,128)(2,1)}, u32[]{:S(2)}, u32[]{:S(2)}) collective-permute-start(bf16[2,896,128]{2,1,0:T(8,128)(2,1)} %pad_maximum_fusion.2), channel_id=1, source_target_pairs={{0,192},{8,200},{16,208},{24,216},{32,224},{40,232},{48,240},{56,2... | collective-permute-start | bytes 1376264 | tf_op jit(solution)/shard_map/ppermute | solution.py:219
  99.3 17.2 %collective-permute-start.2 = (bf16[2,896,128]{2,1,0:T(8,128)(2,1)}, bf16[2,896,128]{2,1,0:T(8,128)(2,1)}, u32[]{:S(2)}, u32[]{:S(2)}) collective-permute-start(bf16[2,896,128]{2,1,0:T(8,128)(2,1)} %pad_maximum_fusion.1), channel_id=1, source_target_pairs={{0,128},{8,136},{16,144},{24,152},{32,160},{40,168},{48,176},{56,1... | collective-permute-start | bytes 1376264 | tf_op jit(solution)/shard_map/ppermute | solution.py:219
  103.5 20.6 %collective-permute-start.1 = (bf16[2,896,128]{2,1,0:T(8,128)(2,1)}, bf16[2,896,128]{2,1,0:T(8,128)(2,1)}, u32[]{:S(2)}, u32[]{:S(2)}) collective-permute-start(bf16[2,896,128]{2,1,0:T(8,128)(2,1)} %pad_maximum_fusion), channel_id=1, source_target_pairs={{0,64},{8,72},{16,80},{24,88},{32,96},{40,104},{48,112},{56,120},{... | collective-permute-start | bytes 1376264 | tf_op jit(solution)/shard_map/ppermute | solution.py:219
  144.1 34.6 %all-to-all-start.6 = ((bf16[8,384,128]{2,1,0:T(8,128)(2,1)}), bf16[8,384,128]{2,1,0:T(8,128)(2,1)S(1)}, u32[]{:S(2)}, u32[]{:S(2)}) async-start(bf16[8,384,128]{2,1,0:T(8,128)(2,1)} %broadcast_in_dim.86), calls=%async_computation.6 | async-start | bytes 1572864 | tf_op jit(solution)/shard_map/all_to_all | solution.py:28
  152.5 23.6 %collective-permute-start.4 = (bf16[224,1024]{1,0:T(8,128)(2,1)S(1)}, bf16[224,1024]{1,0:T(8,128)(2,1)S(1)}, u32[]{:S(2)}, u32[]{:S(2)}) collective-permute-start(bf16[224,1024]{1,0:T(8,128)(2,1)S(1)} %get-tuple-element.25), channel_id=1, source_target_pairs={{0,64},{8,72},{16,80},{24,88},{32,96},{40,104},{48,112},{56,120},{... | collective-permute-start | bytes 1376264 | tf_op jit(solution)/shard_map/ppermute | solution.py:224
  155.0 21.1 %collective-permute-start.5 = (bf16[224,1024]{1,0:T(8,128)(2,1)S(1)}, bf16[224,1024]{1,0:T(8,128)(2,1)S(1)}, u32[]{:S(2)}, u32[]{:S(2)}) collective-permute-start(bf16[224,1024]{1,0:T(8,128)(2,1)S(1)} %get-tuple-element.24), channel_id=1, source_target_pairs={{0,128},{8,136},{16,144},{24,152},{32,160},{40,168},{48,176},{56,1... | collective-permute-start | bytes 1376264 | tf_op jit(solution)/shard_map/ppermute | solution.py:224
  159.1 19.6 %collective-permute-start.6 = (bf16[224,1024]{1,0:T(8,128)(2,1)S(1)}, bf16[224,1024]{1,0:T(8,128)(2,1)S(1)}, u32[]{:S(2)}, u32[]{:S(2)}) collective-permute-start(bf16[224,1024]{1,0:T(8,128)(2,1)S(1)} %get-tuple-element.23), channel_id=1, source_target_pairs={{0,192},{8,200},{16,208},{24,216},{32,224},{40,232},{48,240},{56,2... | collective-permute-start | bytes 1376264 | tf_op jit(solution)/shard_map/ppermute | solution.py:224
  196.5 13.9 %all-to-all-start.8 = ((bf16[16,24,224]{2,1,0:T(8,128)(2,1)}), bf16[16,24,224]{2,1,0:T(8,128)(2,1)S(1)}, u32[]{:S(2)}, u32[]{:S(2)}) async-start(bf16[16,24,224]{2,1,0:T(8,128)(2,1)} %bitcast.20), calls=%async_computation.8 | async-start | bytes 393216 | tf_op jit(solution)/shard_map/all_to_all | solution.py:32

commit v6 on v5

--- a/solution.py
+++ b/solution.py
@@ -41,11 +41,12 @@
 
 def project_kernel(attn, weight, out):
     run = attn.shape[2]
+    dims = (((1,), (1,)), ((), ()))
     for x in range(NX):
         value = jnp.concatenate(
             [attn[x * PAIR + m].reshape(NZ * run, attn.shape[3]) for m in range(PAIR)], axis=0
         )
-        value = jnp.dot(value, weight[...], preferred_element_type=F32).astype(BF16)
+        value = lax.dot_general(value, weight[...], dims, preferred_element_type=F32).astype(BF16)
         for m in range(PAIR):
             for z in range(NZ):
                 first = (m * NZ + z) * run
@@ -53,7 +54,7 @@
 
 
 def project(attn, weight):
-    rows, columns = PAIR * attn.shape[2], weight.shape[1]
+    rows, columns = PAIR * attn.shape[2], weight.shape[0]
     return pl.pallas_call(
         project_kernel,
         out_shape=jax.ShapeDtypeStruct((NX * NZ, rows, columns), BF16),
@@ -61,7 +62,7 @@
         out_specs=whole(1)[0],
         compiler_params=PARAMS,
         cost_estimate=pl.CostEstimate(
-            flops=2 * NX * NZ * rows * columns * weight.shape[0], bytes_accessed=2 * 2**20, transcendentals=0
+            flops=2 * NX * NZ * rows * columns * weight.shape[1], bytes_accessed=2 * 2**20, transcendentals=0
         ),
     )(attn, weight)
 
@@ -87,13 +88,12 @@
     )(parts, residual, select)
 
 
-def up_kernel(place, rows, gain, own, got, left, far, right, out):
-    x_index, member = place[0], place[1]
+def up_kernel(place, rows, gain, block0, block1, block2, block3, out):
+    x_index = place[0]
     slots, units = rows.shape[2], out.shape[2]
-    depth = NZ * rows.shape[1]
-    value = rows[...].astype(F32).reshape(depth, slots)
-    squares = jnp.sum(value * value, axis=0, keepdims=True)
-    normed = (value * gain[...]).astype(BF16).T
+    value = rows[...].reshape(rows.shape[0] * rows.shape[1], slots)
+    squares = jnp.sum(jnp.square(value.astype(F32)), axis=0, keepdims=True)
+    normed = (value.T.astype(F32) * gain[...]).astype(BF16)
     row = lax.broadcasted_iota(jnp.int32, (16, units), 0)
     count = slots // units
     tail = jnp.zeros((16, units), F32)
@@ -103,26 +103,26 @@
         tail = jnp.where(row == i, high, tail)
         tail = jnp.where(row == count + i, part - high, tail)
     tail = tail.astype(BF16)
-    blocks = [(own[x_index], got[x_index])] + [(b[0], b[1]) for b in (left, far, right)]
-    for step, block in enumerate(blocks):
-        total = jnp.dot(normed, jnp.concatenate(block, axis=1), preferred_element_type=F32).astype(BF16)
-        first = lax.rem(x_index + NX - step, NX) * PAIR
-        for target, part in ((first + member, total[:, :units]), (first + 1 - member, total[:, units:])):
-            out[target, :slots] = part
+    for step, block in ((0, (block0, block1)), (2, (block2, block3))):
+        weight = jnp.concatenate([b[...] for b in block], axis=1)
+        total = jnp.dot(normed, weight, preferred_element_type=F32).astype(BF16)
+        for i in range(2):
+            target = lax.rem(x_index + NX - step - i, NX)
+            out[target, :slots] = total[:, i * units : (i + 1) * units]
             out[target, slots:] = tail
 
 
 def up_product(place, rows, gain, blocks):
-    columns, slots = rows.shape[1:]
-    units = blocks[0].shape[2]
+    count, columns, slots = rows.shape
+    units = blocks[0].shape[1]
     return pl.pallas_call(
         up_kernel,
-        out_shape=jax.ShapeDtypeStruct((NX * PAIR, slots + 16, units), BF16),
-        in_specs=[pl.BlockSpec(memory_space=pltpu.SMEM)] + whole(7),
-        out_specs=whole(1)[0],
-        compiler_params=PARAMS,
-        cost_estimate=pl.CostEstimate(
-            flops=2 * slots * columns * NZ * NX * PAIR * units, bytes_accessed=6 * 2**20, transcendentals=0
+        out_shape=jax.ShapeDtypeStruct((NX, slots + 16, units), BF16),
+        in_specs=[pl.BlockSpec(memory_space=pltpu.SMEM)] + whole(6),
+        out_specs=whole(1)[0],
+        compiler_params=PARAMS,
+        cost_estimate=pl.CostEstimate(
+            flops=2 * slots * columns * count * NX * units, bytes_accessed=6 * 2**20, transcendentals=0
         ),
     )(place, rows, gain, *blocks)
 
@@ -185,7 +185,7 @@
     experts = lax.axis_size(("pool", "tp"))
     block_index = lax.axis_index(("pool", "tp"))
     group_index = lax.axis_index("grp")
-    x_index, member = group_index // (NZ * PAIR), group_index % PAIR
+    x_index = group_index // (NZ * PAIR)
     rows, columns = residual.shape
     top_count = routes.shape[1]
     slot_cap = min(rows, rows * top_count * 2 // experts)
@@ -207,16 +207,10 @@
     combine = jnp.where(here, weight_of[:, None, :], 0.0).reshape(slots, rows)
 
     attn = attend(queries, keys, values, lengths)
-
-    def up_half(which):
-        up_parts = up_weight[0].reshape(NX, NZ, PAIR, columns, units)
-        half = lax.dynamic_index_in_dim(up_parts, which, 2, keepdims=False)
-        return half.reshape(NX, NZ * columns, units)
-
     def up_block(step):
         wanted = (x_index + step) % NX
-        block = [lax.dynamic_index_in_dim(w, wanted, 0, keepdims=False) for w in (own, got)]
-        return lax.ppermute(jnp.stack(block), "grp", moves(step, 0))
+        block = lax.dynamic_slice_in_dim(up_weight[0], wanted * (width // NX), width // NX, 0)
+        return lax.ppermute(block, "grp", moves(step, 0)) if step else block
 
     def down_block(step):
         wanted = (x_index + step) % NX
@@ -225,21 +219,18 @@
 
     attn = spread(attn, NZ, "grp", GATHER)
     attn = spread(attn.reshape(-1, attn.shape[2]), parts, "grp", REDUCE)
-    attn, up_weight = lax.optimization_barrier((attn, up_weight))
-    projected = project(attn.reshape(parts, NZ, -1, attn.shape[2]), out_weight)
+    projected = project(attn.reshape(parts, NZ, -1, attn.shape[2]), out_weight.T)
+    projected, down_weight = lax.optimization_barrier((projected, down_weight))
     projected = exchange(projected, ("pool", "tp"))
-    own, got = up_half(member), lax.ppermute(up_half(1 - member), "grp", moves(0, 1))
-    projected, got = lax.optimization_barrier((projected, got))
+    projected, down1, down3 = lax.optimization_barrier((projected, down_block(1), down_block(3)))
     slot_rows = head_sum(projected, residual, select)
     slot_rows = exchange(slot_rows.reshape(experts, slot_cap, columns), ("pool", "tp"))
-    slot_rows, own, got = lax.optimization_barrier((slot_rows, own, got))
-    slot_rows = spread(slot_rows.reshape(slots, columns).T, NZ, "grp", GATHER)
-    gain = norm_gain.reshape(NX, NZ, PAIR, columns)
-    gain = lax.dynamic_index_in_dim(gain, x_index, 0, keepdims=False)
-    gain = lax.dynamic_index_in_dim(gain, member, 1, keepdims=False).reshape(NZ * columns, 1)
-    place = jnp.stack([x_index, member]).astype(jnp.int32)
-    partial_up = up_product(place, slot_rows, gain, (own, got, up_block(1), up_block(2), up_block(3)))
-    total_up = jnp.sum(exchange(partial_up, "grp", REDUCE).astype(F32), axis=0)
+    slot_rows, up_weight = lax.optimization_barrier((slot_rows, up_weight))
+    slot_rows = spread(slot_rows.reshape(slots, columns).T, 8, "grp", LINE)
+    gain = lax.dynamic_slice_in_dim(norm_gain, x_index * (width // NX), width // NX, 0)[None, :]
+    place = x_index.astype(jnp.int32)[None]
+    partial_up = up_product(place, slot_rows, gain, [up_block(step) for step in range(NX)])
+    total_up = jnp.sum(exchange(partial_up, "grp", CROSS).astype(F32), axis=0)
     count = slots // units
     squares = (total_up[slots : slots + count] + total_up[slots + count : slots + 2 * count]).reshape(slots, 1)
     scale = lax.rsqrt(squares / width + 1e-06)
@@ -247,7 +238,7 @@
 
     act, down_weight = lax.optimization_barrier((act, down_weight))
     act = spread(act, 8, "grp", LINE)
-    partial_out = exchange(down_product(place, act, [down_block(step) for step in range(NX)]), "grp", CROSS)
+    partial_out = exchange(down_product(place, act, (down_block(0), down1, down_block(2), down3)), "grp", CROSS)
     expert_out = jnp.sum(partial_out.astype(F32), axis=0).astype(BF16).T
     returned = exchange(expert_out.reshape(experts, slot_cap, columns), ("pool", "tp"))
     returned = returned.reshape(slots, columns)

time: 213 us -> 200 us (0.939)
  waiting for transfers between devices: 73.4 us -> 56.1 us
  blocking collectives: 64 us -> 80.8 us
  starting transfers between devices: 47.3 us -> 41.5 us
  local copies, waits for them, and re-layouts: 14.6 us -> 11.2 us
  other arithmetic: 3.96 us -> 1.39 us
    all_to_all x1 -> x2, blocking collectives: 19.4 us -> 38.3 us  [spread(): lax.all_to_all(sent, axis, 0, 0, tiled=True, axis_index_groups=groups)]
    all_to_all x2, waiting for transfers between devices: 24.1 us -> 8.84 us  [exchange(): lax.all_to_all(value, axis, 0, 0, tiled=True, axis_index_groups=groups)]
    all_to_all x3 -> x2, starting transfers between devices: 14.6 us -> 7.25 us  [spread(): lax.all_to_all(sent, axis, 0, 0, tiled=True, axis_index_groups=groups)]
    all_to_all x3 -> x2, waiting for transfers between devices: 14.6 us -> 11 us  [spread(): lax.all_to_all(sent, axis, 0, 0, tiled=True, axis_index_groups=groups)]
    unnamed x12 -> x17, local copies, waits for them, and re-layouts: 3.53 us -> 0.04 us
    ppermute x3, waiting for transfers between devices: 16.6 us -> 19.9 us  [down_block(): return lax.ppermute(block, 'grp', moves(step, 0)) if step else block]
    another operation x4 -> x0, other arithmetic: 2.51 us -> none  [the longest x3 2.43 us: up_block(): return lax.ppermute(jnp.stack(block), 'grp', moves(step, 0))]
    ppermute x4 -> x3, waiting for transfers between devices: 18.1 us -> 16.3 us  [up_block(): return lax.ppermute(block, 'grp', moves(step, 0)) if step else block]
  transfers between devices with their start and end apart: 12 -> 10, of which waited for: 8 -> 9; matrix products, arithmetic and copies ran while one was open for 4% -> 4% of each run, Pallas kernels for 0% -> 0%
where the time goes in v6:
time: 200 us; the launch traced here: 199 us
  blocking collectives  80.8 us (40%)
  waiting for transfers between devices  56.1 us (28%)
  starting transfers between devices  41.5 us (21%)
  local copies, waits for them, and re-layouts  11.2 us (6%)
  Pallas kernels  4.63 us (2%)
  matrix products  3.02 us (2%)
    all_to_all x3, blocking collectives, exchange(): lax.all_to_all(value, axis, 0, 0, tiled=True, axis_index_groups=groups)  42.5 us
    all_to_all x2, blocking collectives, spread(): lax.all_to_all(sent, axis, 0, 0, tiled=True, axis_index_groups=groups)  38.3 us
    ppermute x3, waiting for transfers between devices, down_block(): return lax.ppermute(block, 'grp', moves(step, 0)) if step else block  19.9 us
    ppermute x3, waiting for transfers between devices, up_block(): return lax.ppermute(block, 'grp', moves(step, 0)) if step else block  16.3 us
    all_to_all x2, starting transfers between devices, exchange(): lax.all_to_all(value, axis, 0, 0, tiled=True, axis_index_groups=groups)  13.3 us
    all_to_all x2, waiting for transfers between devices, spread(): lax.all_to_all(sent, axis, 0, 0, tiled=True, axis_index_groups=groups)  11 us
    ppermute x3, starting transfers between devices, up_block(): return lax.ppermute(block, 'grp', moves(step, 0)) if step else block  10.9 us
    ppermute x3, starting transfers between devices, down_block(): return lax.ppermute(block, 'grp', moves(step, 0)) if step else block  10.1 us
  transfers between devices with their start and end apart: 10, of which 9 were waited for; matrix products, arithmetic and copies ran while one was open for 4% of the time, Pallas kernels for 0%

profile of v6, /device:TPU:8, one launch (start us, length us, event | category | flops | bytes accessed | tf_op | source)
XLA Modules:
  0.0 198.9 jit_solution(17187359676896856781)
XLA Ops:
  0.0 0.0 copy-start
  0.0 0.8 reshape.94
  0.8 0.7 iota_compare_fusion.4
  1.6 1.3 fusion.5
  2.9 0.2 fusion.29
  3.1 0.0 copy-done
  3.1 0.6 convolution_convert_fusion
  3.6 0.0 copy-start.5
  3.7 19.5 %all_to_all.45 = bf16[4,32,512]{2,1,0:T(8,128)(2,1)S(1)} all-to-all(bf16[4,32,512]{2,1,0:T(8,128)(2,1)S(1)} %broadcast_in_dim.89), channel_id=1, replica_groups={{0,16,32,48},{8,24,40,56},{64,80,96,112},{72,88,104,120},{128,144,160,1..., dimensions={0} | all-to-all | bytes 262144 | tf_op jit(solution)/shard_map/all_to_all | solution.py:28
  23.2 0.1 broadcast_in_dim.91
  23.3 18.8 %all_to_all.46 = bf16[8,128,512]{2,1,0:T(8,128)(2,1)S(1)} all-to-all(bf16[8,128,512]{2,1,0:T(8,128)(2,1)S(1)} %broadcast_in_dim.91), channel_id=1, replica_groups={{0,8,64,72,128,136,192,200},{16,24,80,88,144,152,208,216},{32,40,96,104..., dimensions={0} | all-to-all | bytes 2097152 | tf_op jit(solution)/shard_map/all_to_all | solution.py:28
  42.0 0.0 copy-start.7
  42.0 0.0 copy-done.5
  42.0 1.3 shard_map.109
  43.3 7.7 %all-to-all-start.2 = ((bf16[16,64,224]{2,1,0:T(8,128)(2,1)}), bf16[16,64,224]{2,1,0:T(8,128)(2,1)S(1)}, u32[]{:S(2)}, u32[]{:S(2)}) async-start(bf16[16,64,224]{2,1,0:T(8,128)(2,1)} %shard_map.109), calls=%async_computation.2 | async-start | bytes 1048576 | tf_op jit(solution)/shard_map/all_to_all | solution.py:32
  51.0 0.0 copy-done.7
  51.0 0.9 dynamic-slice_bitcast_fusion.6
  51.9 2.1 %collective-permute-start = (bf16[224,1024]{1,0:T(8,128)(2,1)}, bf16[224,1024]{1,0:T(8,128)(2,1)S(1)}, u32[]{:S(2)}, u32[]{:S(2)}) collective-permute-start(bf16[224,1024]{1,0:T(8,128)(2,1)} %get-tuple-element.30), channel_id=1, source_target_pairs={{0,64},{8,72},{16,80},{24,88},{32,96},{40,104},{48,112},{56,120},{... | collective-permute-start | bytes 1376264 | tf_op jit(solution)/shard_map/ppermute | solution.py:218
  53.9 5.0 %collective-permute-start.1 = (bf16[224,1024]{1,0:T(8,128)(2,1)S(1)}, bf16[224,1024]{1,0:T(8,128)(2,1)S(1)}, u32[]{:S(2)}, u32[]{:S(2)}) collective-permute-start(bf16[224,1024]{1,0:T(8,128)(2,1)S(1)} %get-tuple-element.29), channel_id=1, source_target_pairs={{0,192},{8,200},{16,208},{24,216},{32,224},{40,232},{48,240},{56,2... | collective-permute-start | bytes 1376264 | tf_op jit(solution)/shard_map/ppermute | solution.py:218
  59.0 0.1 eq.57
  59.0 0.8 fusion.21
  59.8 0.1 convolution_convert_fusion.1
  59.9 0.1 fusion.9.select
  60.1 7.7 %collective-permute-done.block1 = bf16[224,1024]{1,0:T(8,128)(2,1)S(1)} collective-permute-done((bf16[224,1024]{1,0:T(8,128)(2,1)}, bf16[224,1024]{1,0:T(8,128)(2,1)S(1)}, u32[]{:S(2)}, u32[]{:S(2)}) %collective-permute-start) | collective-permute-done | bytes 458784 | tf_op jit(solution)/shard_map/ppermute | solution.py:218
  67.8 1.0 collective-permute-done.1.block3
  68.7 0.0 all-to-all-done.2.parts
  68.7 0.0 copy-done.6
  68.7 0.2 shard_map.110
  69.0 16.6 %all_to_all.47 = bf16[16,24,224]{2,1,0:T(8,128)(2,1)S(1)} all-to-all(bf16[16,24,224]{2,1,0:T(8,128)(2,1)S(1)} %bitcast.59), channel_id=1, replica_groups=mesh['pool'=2,'grp'=32,'tp'=8] {'pool','tp'}, dimensions={0} | all-to-all | bytes 344064 | tf_op jit(solution)/shard_map/all_to_all | solution.py:32
  85.6 0.1 copy.16
  85.8 1.2 broadcast_in_dim.92
  87.0 0.0 copy-done.1
  87.0 0.0 copy-done.3
  87.0 3.6 %all-to-all-start.4 = ((bf16[8,224,384]{2,1,0:T(8,128)(2,1)}), bf16[8,224,384]{2,1,0:T(8,128)(2,1)S(1)}, u32[]{:S(2)}, u32[]{:S(2)}) async-start(bf16[8,224,384]{2,1,0:T(8,128)(2,1)} %broadcast_in_dim.92), calls=%async_computation.4 | async-start | bytes 2752512 | tf_op jit(solution)/shard_map/all_to_all | solution.py:28
  90.6 2.5 %dynamic-slice_bitcast_fusion.2 = (bf16[1792,128]{1,0:T(8,128)(2,1)}, bf16[1792,128]{1,0:T(8,128)(2,1)}, bf16[1792,128]{1,0:T(8,128)(2,1)}, bf16[1792,128]{1,0:T(8,128)(2,1)S(1)}) fusion(bf16[1,7168,128]{2,1,0:T(8,128)(2,1)} %param.20, s32[]{:T(128)S(6)} %select_n.92, s32[]{:T(128)S(6)} %select_n.91, s32[]{:T(128)S(6)} %select_n.89, s32[]{:T(128)S(6)} %select_n.88), kind=kLoop, calls=%fused_computation.14 | loop fusion | bytes 3670032 | tf_op jit(solution)/shard_map/dynamic_slice | solution.py:212
  93.2 2.2 %collective-permute-start.2 = (bf16[1792,128]{1,0:T(8,128)(2,1)}, bf16[1792,128]{1,0:T(8,128)(2,1)S(1)}, u32[]{:S(2)}, u32[]{:S(2)}) collective-permute-start(bf16[1792,128]{1,0:T(8,128)(2,1)} %get-tuple-element.27), channel_id=1, source_target_pairs={{0,64},{8,72},{16,80},{24,88},{32,96},{40,104},{48,112},{56,120},{... | collective-permute-start | bytes 1376264 | tf_op jit(solution)/shard_map/ppermute | solution.py:213
  95.4 6.8 %collective-permute-start.3 = (bf16[1792,128]{1,0:T(8,128)(2,1)}, bf16[1792,128]{1,0:T(8,128)(2,1)S(1)}, u32[]{:S(2)}, u32[]{:S(2)}) collective-permute-start(bf16[1792,128]{1,0:T(8,128)(2,1)} %get-tuple-element.26), channel_id=1, source_target_pairs={{0,128},{8,136},{16,144},{24,152},{32,160},{40,168},{48,176},{56,1... | collective-permute-start | bytes 1376264 | tf_op jit(solution)/shard_map/ppermute | solution.py:213
  102.2 1.9 collective-permute-start.4
  104.1 0.8 dynamic_slice.55
  104.9 4.6 %collective-permute-done.2.block1 = bf16[1792,128]{1,0:T(8,128)(2,1)S(1)} collective-permute-done((bf16[1792,128]{1,0:T(8,128)(2,1)}, bf16[1792,128]{1,0:T(8,128)(2,1)S(1)}, u32[]{:S(2)}, u32[]{:S(2)}) %collective-permute-start.2) | collective-permute-done | bytes 458784 | tf_op jit(solution)/shard_map/ppermute | solution.py:213
  109.5 10.2 %collective-permute-done.3.block2 = bf16[1792,128]{1,0:T(8,128)(2,1)S(1)} collective-permute-done((bf16[1792,128]{1,0:T(8,128)(2,1)}, bf16[1792,128]{1,0:T(8,128)(2,1)S(1)}, u32[]{:S(2)}, u32[]{:S(2)}) %collective-permute-start.3) | collective-permute-done | bytes 458784 | tf_op jit(solution)/shard_map/ppermute | solution.py:213
  119.7 1.5 collective-permute-done.4.block3
  121.2 4.6 %all-to-all-done.4.rows = bf16[8,224,384]{2,1,0:T(8,128)(2,1)S(1)} async-done(((bf16[8,224,384]{2,1,0:T(8,128)(2,1)}), bf16[8,224,384]{2,1,0:T(8,128)(2,1)S(1)}, u32[]{:S(2)}, u32[]{:S(2)}) %all-to-all-start.4) | async-done | bytes 1376288 | tf_op jit(solution)/shard_map/all_to_all | solution.py:28
  125.8 1.9 shard_map.111
  127.7 13.1 %all_to_all.48 = bf16[4,400,128]{2,1,0:T(8,128)(2,1)S(1)} all-to-all(bf16[4,400,128]{2,1,0:T(8,128)(2,1)S(1)} %shard_map.111), channel_id=1, replica_groups={{0,64,128,192},{8,72,136,200},{16,80,144,208},{24,88,152,216},{32,96,16..., dimensions={0} | all-to-all | bytes 819200 | tf_op jit(solution)/shard_map/all_to_all | solution.py:32
  140.9 0.1 convert_reduce_fusion
  140.9 0.1 multiply_convert_fusion
  141.1 1.0 broadcast_in_dim.94
  142.1 3.7 %all-to-all-start.6 = ((bf16[8,384,128]{2,1,0:T(8,128)(2,1)}), bf16[8,384,128]{2,1,0:T(8,128)(2,1)S(1)}, u32[]{:S(2)}, u32[]{:S(2)}) async-start(bf16[8,384,128]{2,1,0:T(8,128)(2,1)} %broadcast_in_dim.94), calls=%async_computation.6 | async-start | bytes 1572864 | tf_op jit(solution)/shard_map/all_to_all | solution.py:28
  145.8 1.2 dynamic-slice_bitcast_fusion
  147.0 3.0 %collective-permute-start.5 = (bf16[224,1024]{1,0:T(8,128)(2,1)S(1)}, bf16[224,1024]{1,0:T(8,128)(2,1)S(1)}, u32[]{:S(2)}, u32[]{:S(2)}) collective-permute-start(bf16[224,1024]{1,0:T(8,128)(2,1)S(1)} %get-tuple-element.23), channel_id=1, source_target_pairs={{0,128},{8,136},{16,144},{24,152},{32,160},{40,168},{48,176},{56,1... | collective-permute-start | bytes 1376264 | tf_op jit(solution)/shard_map/ppermute | solution.py:218
  150.1 11.3 %collective-permute-done.5.block2 = bf16[224,1024]{1,0:T(8,128)(2,1)S(1)} collective-permute-done((bf16[224,1024]{1,0:T(8,128)(2,1)S(1)}, bf16[224,1024]{1,0:T(8,128)(2,1)S(1)}, u32[]{:S(2)}, u32[]{:S(2)}) %collective-permute-start.5) | collective-permute-done | bytes 458784 | tf_op jit(solution)/shard_map/ppermute | solution.py:218
  161.3 6.4 %all-to-all-done.6.act = bf16[8,384,128]{2,1,0:T(8,128)(2,1)S(1)} async-done(((bf16[8,384,128]{2,1,0:T(8,128)(2,1)}), bf16[8,384,128]{2,1,0:T(8,128)(2,1)S(1)}, u32[]{:S(2)}, u32[]{:S(2)}) %all-to-all-start.6) | async-done | bytes 786464 | tf_op jit(solution)/shard_map/all_to_all | solution.py:28
  167.7 0.0 copy-done.2
  167.7 0.0 copy-done.4
  167.7 1.2 shard_map.112
  168.9 12.7 %all_to_all.49 = bf16[4,224,384]{2,1,0:T(8,128)(2,1)S(1)} all-to-all(bf16[4,224,384]{2,1,0:T(8,128)(2,1)S(1)} %shard_map.112), channel_id=1, replica_groups={{0,64,128,192},{8,72,136,200},{16,80,144,208},{24,88,152,216},{32,96,16..., dimensions={0} | all-to-all | bytes 1376256 | tf_op jit(solution)/shard_map/all_to_all | solution.py:32
  181.7 0.1 reduce_sum.42
  181.8 0.8 copy.17
  182.6 5.6 %all-to-all-start.8 = ((bf16[16,24,224]{2,1,0:T(8,128)(2,1)}), bf16[16,24,224]{2,1,0:T(8,128)(2,1)S(1)}, u32[]{:S(2)}, u32[]{:S(2)}) async-start(bf16[16,24,224]{2,1,0:T(8,128)(2,1)} %bitcast.21), calls=%async_computation.8 | async-start | bytes 393216 | tf_op jit(solution)/shard_map/all_to_all | solution.py:32
  188.2 0.8 fusion.22
  189.0 8.8 %all-to-all-done.8 = bf16[16,24,224]{2,1,0:T(8,128)(2,1)S(1)} async-done(((bf16[16,24,224]{2,1,0:T(8,128)(2,1)}), bf16[16,24,224]{2,1,0:T(8,128)(2,1)S(1)}, u32[]{:S(2)}, u32[]{:S(2)}) %all-to-all-start.8) | async-done | bytes 172064 | tf_op jit(solution)/shard_map/all_to_all | solution.py:32
  197.8 0.2 convolution_bitcast_fusion.1
  198.0 0.8 fusion.2
  (12 shorter events, 0.1 us)
Async XLA Ops:
  0.0 3.1 %copy-start = (bf16[32,32,256]{2,1,0:T(8,128)(2,1)S(1)}, bf16[32,32,256]{2,1,0:T(8,128)(2,1)}, u32[]{:S(2)}) copy-start(bf16[32,32,256]{2,1,0:T(8,128)(2,1)} %param.13) | copy-start | bytes 1572868
  3.6 38.4 %copy-start.5 = (bf16[512,224]{0,1:T(8,128)(2,1)S(1)}, bf16[512,224]{0,1:T(8,128)(2,1)}, u32[]{:S(2)}) copy-start(bf16[512,224]{0,1:T(8,128)(2,1)} %param.15) | copy-start | bytes 688132
  42.0 9.0 %copy-start.7 = (bf16[1,224,4096]{2,1,0:T(8,128)(2,1)S(1)}, bf16[1,224,4096]{2,1,0:T(8,128)(2,1)}, u32[]{:S(2)}) copy-start(bf16[1,224,4096]{2,1,0:T(8,128)(2,1)} %param.21) | copy-start | bytes 5505028
  43.3 25.4 %copy-start.6 = (bf16[64,224]{1,0:T(8,128)(2,1)S(1)}, bf16[64,224]{1,0:T(8,128)(2,1)}, u32[]{:S(2)}) copy-start(bf16[64,224]{1,0:T(8,128)(2,1)} %residual.1) | copy-start | bytes 86020
  43.3 25.4 %all-to-all-start.2 = ((bf16[16,64,224]{2,1,0:T(8,128)(2,1)}), bf16[16,64,224]{2,1,0:T(8,128)(2,1)S(1)}, u32[]{:S(2)}, u32[]{:S(2)}) async-start(bf16[16,64,224]{2,1,0:T(8,128)(2,1)} %shard_map.109), calls=%async_computation.2 | async-start | bytes 1048576 | tf_op jit(solution)/shard_map/all_to_all | solution.py:32
  51.9 15.9 %collective-permute-start = (bf16[224,1024]{1,0:T(8,128)(2,1)}, bf16[224,1024]{1,0:T(8,128)(2,1)S(1)}, u32[]{:S(2)}, u32[]{:S(2)}) collective-permute-start(bf16[224,1024]{1,0:T(8,128)(2,1)} %get-tuple-element.30), channel_id=1, source_target_pairs={{0,64},{8,72},{16,80},{24,88},{32,96},{40,104},{48,112},{56,120},{... | collective-permute-start | bytes 1376264 | tf_op jit(solution)/shard_map/ppermute | solution.py:218
  53.9 14.8 %collective-permute-start.1 = (bf16[224,1024]{1,0:T(8,128)(2,1)S(1)}, bf16[224,1024]{1,0:T(8,128)(2,1)S(1)}, u32[]{:S(2)}, u32[]{:S(2)}) collective-permute-start(bf16[224,1024]{1,0:T(8,128)(2,1)S(1)} %get-tuple-element.29), channel_id=1, source_target_pairs={{0,192},{8,200},{16,208},{24,216},{32,224},{40,232},{48,240},{56,2... | collective-permute-start | bytes 1376264 | tf_op jit(solution)/shard_map/ppermute | solution.py:218
  67.8 19.2 %copy-start.1 = (bf16[224,1024]{1,0:T(8,128)(2,1)}, bf16[224,1024]{1,0:T(8,128)(2,1)S(1)}, u32[]{:S(2)}) copy-start(bf16[224,1024]{1,0:T(8,128)(2,1)S(1)} %collective-permute-done.block1) | copy-start | bytes 1376260
  68.7 18.3 %copy-start.3 = (bf16[224,1024]{1,0:T(8,128)(2,1)}, bf16[224,1024]{1,0:T(8,128)(2,1)S(1)}, u32[]{:S(2)}) copy-start(bf16[224,1024]{1,0:T(8,128)(2,1)S(1)} %collective-permute-done.1.block3) | copy-start | bytes 1376260
  87.0 38.8 %all-to-all-start.4 = ((bf16[8,224,384]{2,1,0:T(8,128)(2,1)}), bf16[8,224,384]{2,1,0:T(8,128)(2,1)S(1)}, u32[]{:S(2)}, u32[]{:S(2)}) async-start(bf16[8,224,384]{2,1,0:T(8,128)(2,1)} %broadcast_in_dim.92), calls=%async_computation.4 | async-start | bytes 2752512 | tf_op jit(solution)/shard_map/all_to_all | solution.py:28
  93.2 16.3 %collective-permute-start.2 = (bf16[1792,128]{1,0:T(8,128)(2,1)}, bf16[1792,128]{1,0:T(8,128)(2,1)S(1)}, u32[]{:S(2)}, u32[]{:S(2)}) collective-permute-start(bf16[1792,128]{1,0:T(8,128)(2,1)} %get-tuple-element.27), channel_id=1, source_target_pairs={{0,64},{8,72},{16,80},{24,88},{32,96},{40,104},{48,112},{56,120},{... | collective-permute-start | bytes 1376264 | tf_op jit(solution)/shard_map/ppermute | solution.py:213
  95.4 24.3 %collective-permute-start.3 = (bf16[1792,128]{1,0:T(8,128)(2,1)}, bf16[1792,128]{1,0:T(8,128)(2,1)S(1)}, u32[]{:S(2)}, u32[]{:S(2)}) collective-permute-start(bf16[1792,128]{1,0:T(8,128)(2,1)} %get-tuple-element.26), channel_id=1, source_target_pairs={{0,128},{8,136},{16,144},{24,152},{32,160},{40,168},{48,176},{56,1... | collective-permute-start | bytes 1376264 | tf_op jit(solution)/shard_map/ppermute | solution.py:213
  102.2 19.0 %collective-permute-start.4 = (bf16[1792,128]{1,0:T(8,128)(2,1)}, bf16[1792,128]{1,0:T(8,128)(2,1)}, u32[]{:S(2)}, u32[]{:S(2)}) collective-permute-start(bf16[1792,128]{1,0:T(8,128)(2,1)} %get-tuple-element.25), channel_id=1, source_target_pairs={{0,192},{8,200},{16,208},{24,216},{32,224},{40,232},{48,240},{56,2... | collective-permute-start | bytes 1376264 | tf_op jit(solution)/shard_map/ppermute | solution.py:213
  142.1 25.7 %copy-start.2 = (bf16[224,1024]{1,0:T(8,128)(2,1)S(1)}, bf16[224,1024]{1,0:T(8,128)(2,1)}, u32[]{:S(2)}) copy-start(bf16[224,1024]{1,0:T(8,128)(2,1)} %copy-done.1) | copy-start | bytes 1376260
  142.1 25.7 %copy-start.4 = (bf16[224,1024]{1,0:T(8,128)(2,1)S(1)}, bf16[224,1024]{1,0:T(8,128)(2,1)}, u32[]{:S(2)}) copy-start(bf16[224,1024]{1,0:T(8,128)(2,1)} %copy-done.3) | copy-start | bytes 1376260
  142.1 25.7 %all-to-all-start.6 = ((bf16[8,384,128]{2,1,0:T(8,128)(2,1)}), bf16[8,384,128]{2,1,0:T(8,128)(2,1)S(1)}, u32[]{:S(2)}, u32[]{:S(2)}) async-start(bf16[8,384,128]{2,1,0:T(8,128)(2,1)} %broadcast_in_dim.94), calls=%async_computation.6 | async-start | bytes 1572864 | tf_op jit(solution)/shard_map/all_to_all | solution.py:28
  147.0 14.3 %collective-permute-start.5 = (bf16[224,1024]{1,0:T(8,128)(2,1)S(1)}, bf16[224,1024]{1,0:T(8,128)(2,1)S(1)}, u32[]{:S(2)}, u32[]{:S(2)}) collective-permute-start(bf16[224,1024]{1,0:T(8,128)(2,1)S(1)} %get-tuple-element.23), channel_id=1, source_target_pairs={{0,128},{8,136},{16,144},{24,152},{32,160},{40,168},{48,176},{56,1... | collective-permute-start | bytes 1376264 | tf_op jit(solution)/shard_map/ppermute | solution.py:218
  182.6 15.2 %all-to-all-start.8 = ((bf16[16,24,224]{2,1,0:T(8,128)(2,1)}), bf16[16,24,224]{2,1,0:T(8,128)(2,1)S(1)}, u32[]{:S(2)}, u32[]{:S(2)}) async-start(bf16[16,24,224]{2,1,0:T(8,128)(2,1)} %bitcast.21), calls=%async_computation.8 | async-start | bytes 393216 | tf_op jit(solution)/shard_map/all_to_all | solution.py:32

commit v7 on v6

--- a/solution.py
+++ b/solution.py
@@ -21,6 +21,10 @@
         for z in range(NZ)
         for m in range(PAIR)
     ]
+
+
+def turns(by):
+    return [(x * 8 + z, x * 8 + (z + by) % 8) for x in range(NX) for z in range(8)]
 
 
 def spread(value, count, axis, groups=None):
@@ -88,12 +92,15 @@
     )(parts, residual, select)
 
 
-def up_kernel(place, rows, gain, block0, block1, block2, block3, out):
-    x_index = place[0]
-    slots, units = rows.shape[2], out.shape[2]
-    value = rows[...].reshape(rows.shape[0] * rows.shape[1], slots)
-    squares = jnp.sum(jnp.square(value.astype(F32)), axis=0, keepdims=True)
-    normed = (value.T.astype(F32) * gain[...]).astype(BF16)
+def up_kernel(place, same, before, after, gain, block0, block1, block2, block3, out):
+    x_index, member = place[0], place[1]
+    slots, units = same.shape[2], out.shape[2]
+    depth = NZ * same.shape[1]
+    other = jnp.concatenate([r[...].reshape(depth // 2, slots) for r in (before, after)], axis=0)
+    normed, squares = [], 0.0
+    for i, value in enumerate((same[...].reshape(depth, slots), other)):
+        squares += jnp.sum(jnp.square(value.astype(F32)), axis=0, keepdims=True)
+        normed.append((value.T.astype(F32) * gain[i : i + 1, :]).astype(BF16))
     row = lax.broadcasted_iota(jnp.int32, (16, units), 0)
     count = slots // units
     tail = jnp.zeros((16, units), F32)
@@ -104,8 +111,11 @@
         tail = jnp.where(row == count + i, part - high, tail)
     tail = tail.astype(BF16)
     for step, block in ((0, (block0, block1)), (2, (block2, block3))):
-        weight = jnp.concatenate([b[...] for b in block], axis=1)
-        total = jnp.dot(normed, weight, preferred_element_type=F32).astype(BF16)
+        total = 0.0
+        for value, which in zip(normed, (member, 1 - member)):
+            weight = jnp.concatenate([b[:, which].reshape(depth, units) for b in block], axis=1)
+            total += jnp.dot(value, weight, preferred_element_type=F32)
+        total = total.astype(BF16)
         for i in range(2):
             target = lax.rem(x_index + NX - step - i, NX)
             out[target, :slots] = total[:, i * units : (i + 1) * units]
@@ -113,18 +123,18 @@
 
 
 def up_product(place, rows, gain, blocks):
-    count, columns, slots = rows.shape
-    units = blocks[0].shape[1]
+    count, columns, slots = rows[0].shape
+    units = blocks[0].shape[3]
     return pl.pallas_call(
         up_kernel,
         out_shape=jax.ShapeDtypeStruct((NX, slots + 16, units), BF16),
-        in_specs=[pl.BlockSpec(memory_space=pltpu.SMEM)] + whole(6),
-        out_specs=whole(1)[0],
-        compiler_params=PARAMS,
-        cost_estimate=pl.CostEstimate(
-            flops=2 * slots * columns * count * NX * units, bytes_accessed=6 * 2**20, transcendentals=0
-        ),
-    )(place, rows, gain, *blocks)
+        in_specs=[pl.BlockSpec(memory_space=pltpu.SMEM)] + whole(8),
+        out_specs=whole(1)[0],
+        compiler_params=PARAMS,
+        cost_estimate=pl.CostEstimate(
+            flops=4 * slots * columns * count * NX * units, bytes_accessed=6 * 2**20, transcendentals=0
+        ),
+    )(place, *rows, gain, *blocks)
 
 
 def down_kernel(place, act, block0, block1, block2, block3, out):
@@ -185,7 +195,7 @@
     experts = lax.axis_size(("pool", "tp"))
     block_index = lax.axis_index(("pool", "tp"))
     group_index = lax.axis_index("grp")
-    x_index = group_index // (NZ * PAIR)
+    x_index, member = group_index // (NZ * PAIR), group_index % PAIR
     rows, columns = residual.shape
     top_count = routes.shape[1]
     slot_cap = min(rows, rows * top_count * 2 // experts)
@@ -210,7 +220,8 @@
     def up_block(step):
         wanted = (x_index + step) % NX
         block = lax.dynamic_slice_in_dim(up_weight[0], wanted * (width // NX), width // NX, 0)
-        return lax.ppermute(block, "grp", moves(step, 0)) if step else block
+        block = lax.ppermute(block, "grp", moves(step, 0)) if step else block
+        return block.reshape(NZ, PAIR, columns, units)
 
     def down_block(step):
         wanted = (x_index + step) % NX
@@ -226,10 +237,16 @@
     slot_rows = head_sum(projected, residual, select)
     slot_rows = exchange(slot_rows.reshape(experts, slot_cap, columns), ("pool", "tp"))
     slot_rows, up_weight = lax.optimization_barrier((slot_rows, up_weight))
-    slot_rows = spread(slot_rows.reshape(slots, columns).T, 8, "grp", LINE)
-    gain = lax.dynamic_slice_in_dim(norm_gain, x_index * (width // NX), width // NX, 0)[None, :]
-    place = x_index.astype(jnp.int32)[None]
-    partial_up = up_product(place, slot_rows, gain, [up_block(step) for step in range(NX)])
+    same = spread(slot_rows.reshape(slots, columns).T, NZ, "grp", GATHER)
+    same, up1, up3 = lax.optimization_barrier((same, up_block(1), up_block(3)))
+    before = lax.ppermute(same[: NZ // 2], "grp", turns(1))
+    after = lax.ppermute(same[NZ // 2 :], "grp", turns(-1))
+    gain = norm_gain.reshape(NX, NZ, PAIR, columns)
+    gain = lax.dynamic_index_in_dim(gain, x_index, 0, keepdims=False)
+    gain = [lax.dynamic_index_in_dim(gain, m, 1, keepdims=False).reshape(-1) for m in (member, 1 - member)]
+    gain = jnp.stack(gain)
+    place = jnp.stack([x_index, member]).astype(jnp.int32)
+    partial_up = up_product(place, (same, before, after), gain, (up_block(0), up1, up_block(2), up3))
     total_up = jnp.sum(exchange(partial_up, "grp", CROSS).astype(F32), axis=0)
     count = slots // units
     squares = (total_up[slots : slots + count] + total_up[slots + count : slots + 2 * count]).reshape(slots, 1)

time: 200 us -> 208 us (1.040)
  starting transfers between devices: 41.5 us -> 50 us
  blocking collectives: 80.8 us -> 78.4 us
    all_to_all x2, waiting for transfers between devices: 11 us -> 0.01 us  [spread(): lax.all_to_all(sent, axis, 0, 0, tiled=True, axis_index_groups=groups)]
    ppermute x3 -> x5, waiting for transfers between devices: 16.3 us -> 25.7 us  [the longest x3 18.2 us: up_block(): block = lax.ppermute(block, 'grp', moves(step, 0)) if step else block]
    ppermute x3 -> x5, starting transfers between devices: 10.9 us -> 15.4 us  [the longest x3 8.12 us: up_block(): block = lax.ppermute(block, 'grp', moves(step, 0)) if step else block]
    all_to_all x3, blocking collectives: 42.5 us -> 40.1 us  [exchange(): lax.all_to_all(value, axis, 0, 0, tiled=True, axis_index_groups=groups)]
    ppermute x3, starting transfers between devices: 10.1 us -> 12.2 us  [down_block(): return lax.ppermute(block, 'grp', moves(step, 0)) if step else block]
  transfers between devices with their start and end apart: 10 -> 12, of which waited for: 9 -> 8; matrix products, arithmetic and copies ran while one was open for 4% -> 4% of each run, Pallas kernels for 0% -> 0%
where the time goes in v7:
time: 208 us; the launch traced here: 207 us
  blocking collectives  78.4 us (38%)
  waiting for transfers between devices  56 us (27%)
  starting transfers between devices  50 us (24%)
  local copies, waits for them, and re-layouts  12 us (6%)
  Pallas kernels  5.37 us (3%)
  matrix products  3.03 us (1%)
    all_to_all x3, blocking collectives, exchange(): lax.all_to_all(value, axis, 0, 0, tiled=True, axis_index_groups=groups)  40.1 us
    all_to_all x2, blocking collectives, spread(): lax.all_to_all(sent, axis, 0, 0, tiled=True, axis_index_groups=groups)  38.3 us
    ppermute x3, waiting for transfers between devices, down_block(): return lax.ppermute(block, 'grp', moves(step, 0)) if step else block  21.4 us
    ppermute x3, waiting for transfers between devices, up_block(): block = lax.ppermute(block, 'grp', moves(step, 0)) if step else block  18.2 us
    all_to_all x2, starting transfers between devices, exchange(): lax.all_to_all(value, axis, 0, 0, tiled=True, axis_index_groups=groups)  15.3 us
    ppermute x3, starting transfers between devices, down_block(): return lax.ppermute(block, 'grp', moves(step, 0)) if step else block  12.2 us
    all_to_all x2, waiting for transfers between devices, exchange(): lax.all_to_all(value, axis, 0, 0, tiled=True, axis_index_groups=groups)  8.84 us
    ppermute x3, starting transfers between devices, up_block(): block = lax.ppermute(block, 'grp', moves(step, 0)) if step else block  8.12 us
  transfers between devices with their start and end apart: 12, of which 8 were waited for; matrix products, arithmetic and copies ran while one was open for 4% of the time, Pallas kernels for 0%

profile of v7, /device:TPU:8, one launch (start us, length us, event | category | flops | bytes accessed | tf_op | source)
XLA Modules:
  0.0 206.7 jit_solution(2178261239427652006)
XLA Ops:
  0.0 0.0 copy-start
  0.0 0.8 iota_compare_fusion.4
  0.8 0.8 reshape.116
  1.6 1.3 fusion.5
  2.9 0.2 fusion.30
  3.1 0.6 convolution_convert_fusion
  3.6 0.0 copy-start.3
  3.7 19.5 %all_to_all.45 = bf16[4,32,512]{2,1,0:T(8,128)(2,1)S(1)} all-to-all(bf16[4,32,512]{2,1,0:T(8,128)(2,1)S(1)} %broadcast_in_dim.82), channel_id=1, replica_groups={{0,16,32,48},{8,24,40,56},{64,80,96,112},{72,88,104,120},{128,144,160,1..., dimensions={0} | all-to-all | bytes 262144 | tf_op jit(solution)/shard_map/all_to_all | solution.py:32
  23.2 0.1 broadcast_in_dim.84
  23.3 18.8 %all_to_all.46 = bf16[8,128,512]{2,1,0:T(8,128)(2,1)S(1)} all-to-all(bf16[8,128,512]{2,1,0:T(8,128)(2,1)S(1)} %broadcast_in_dim.84), channel_id=1, replica_groups={{0,8,64,72,128,136,192,200},{16,24,80,88,144,152,208,216},{32,40,96,104..., dimensions={0} | all-to-all | bytes 2097152 | tf_op jit(solution)/shard_map/all_to_all | solution.py:32
  42.0 1.3 shard_map.109
  43.3 7.7 %all-to-all-start.2 = ((bf16[16,64,224]{2,1,0:T(8,128)(2,1)}), bf16[16,64,224]{2,1,0:T(8,128)(2,1)S(1)}, u32[]{:S(2)}, u32[]{:S(2)}) async-start(bf16[16,64,224]{2,1,0:T(8,128)(2,1)} %shard_map.109), calls=%async_computation.2 | async-start | bytes 1048576 | tf_op jit(solution)/shard_map/all_to_all | solution.py:36
  51.0 1.0 dynamic-slice_bitcast_fusion.5
  52.0 2.7 %collective-permute-start.1 = (bf16[224,1024]{1,0:T(8,128)(2,1)}, bf16[224,1024]{1,0:T(8,128)(2,1)S(1)}, u32[]{:S(2)}, u32[]{:S(2)}) collective-permute-start(bf16[224,1024]{1,0:T(8,128)(2,1)} %get-tuple-element.37), channel_id=1, source_target_pairs={{0,192},{8,200},{16,208},{24,216},{32,224},{40,232},{48,240},{56,2... | collective-permute-start | bytes 1376264 | tf_op jit(solution)/shard_map/ppermute | solution.py:229
  54.7 3.2 %collective-permute-start = (bf16[224,1024]{1,0:T(8,128)(2,1)}, bf16[224,1024]{1,0:T(8,128)(2,1)S(1)}, u32[]{:S(2)}, u32[]{:S(2)}) collective-permute-start(bf16[224,1024]{1,0:T(8,128)(2,1)} %get-tuple-element.38), channel_id=1, source_target_pairs={{0,64},{8,72},{16,80},{24,88},{32,96},{40,104},{48,112},{56,120},{... | collective-permute-start | bytes 1376264 | tf_op jit(solution)/shard_map/ppermute | solution.py:229
  57.9 0.1 eq.58
  58.0 0.8 fusion.21
  58.8 0.1 convolution_convert_fusion.1
  58.9 0.1 fusion.9.select
  59.0 7.7 %collective-permute-done.1.block3 = bf16[224,1024]{1,0:T(8,128)(2,1)S(1)} collective-permute-done((bf16[224,1024]{1,0:T(8,128)(2,1)}, bf16[224,1024]{1,0:T(8,128)(2,1)S(1)}, u32[]{:S(2)}, u32[]{:S(2)}) %collective-permute-start.1) | collective-permute-done | bytes 458784 | tf_op jit(solution)/shard_map/ppermute | solution.py:229
  66.7 3.6 %collective-permute-done.block1 = bf16[224,1024]{1,0:T(8,128)(2,1)S(1)} collective-permute-done((bf16[224,1024]{1,0:T(8,128)(2,1)}, bf16[224,1024]{1,0:T(8,128)(2,1)S(1)}, u32[]{:S(2)}, u32[]{:S(2)}) %collective-permute-start) | collective-permute-done | bytes 458784 | tf_op jit(solution)/shard_map/ppermute | solution.py:229
  70.3 0.0 all-to-all-done.2.parts
  70.3 0.2 shard_map.110
  70.6 16.6 %all_to_all.47 = bf16[16,24,224]{2,1,0:T(8,128)(2,1)S(1)} all-to-all(bf16[16,24,224]{2,1,0:T(8,128)(2,1)S(1)} %bitcast.63), channel_id=1, replica_groups=mesh['pool'=2,'grp'=32,'tp'=8] {'pool','tp'}, dimensions={0} | all-to-all | bytes 344064 | tf_op jit(solution)/shard_map/all_to_all | solution.py:36
  87.2 0.1 copy.16
  87.4 0.9 broadcast_in_dim.85
  88.3 3.5 %all-to-all-start.4 = ((bf16[4,224,384]{2,1,0:T(8,128)(2,1)}), bf16[4,224,384]{2,1,0:T(8,128)(2,1)S(1)}, u32[]{:S(2)}, u32[]{:S(2)}) async-start(bf16[4,224,384]{2,1,0:T(8,128)(2,1)} %broadcast_in_dim.85), calls=%async_computation.4 | async-start | bytes 1376256 | tf_op jit(solution)/shard_map/all_to_all | solution.py:32
  91.8 2.3 %dynamic-slice_bitcast_fusion.2 = (bf16[1792,128]{1,0:T(8,128)(2,1)}, bf16[1,1792,128]{2,1,0:T(8,128)(2,1)S(1)}, bf16[1792,128]{1,0:T(8,128)(2,1)S(1)}, bf16[1792,128]{1,0:T(8,128)(2,1)S(1)}) fusion(bf16[1,7168,128]{2,1,0:T(8,128)(2,1)} %param.20, s32[]{:T(128)S(6)} %select_n.116, s32[]{:T(128)S(6)} %select_n.114, s32[]{:T(128)S(6)} %select_n.106, ...), kind=kLoop, calls=%fused_computation.14 | loop fusion | bytes 3670032 | tf_op jit(solution)/shard_map/dynamic_slice | solution.py:222
  94.2 1.9 collective-permute-start.3
  96.1 3.9 %collective-permute-start.2 = (bf16[1792,128]{1,0:T(8,128)(2,1)S(1)}, bf16[1792,128]{1,0:T(8,128)(2,1)S(1)}, u32[]{:S(2)}, u32[]{:S(2)}) collective-permute-start(bf16[1792,128]{1,0:T(8,128)(2,1)S(1)} %get-tuple-element.36), channel_id=1, source_target_pairs={{0,64},{8,72},{16,80},{24,88},{32,96},{40,104},{48,112},{56,120},{... | collective-permute-start | bytes 1376264 | tf_op jit(solution)/shard_map/ppermute | solution.py:223
  100.0 2.3 %collective-permute-start.6 = (bf16[1792,128]{1,0:T(8,128)(2,1)}, bf16[1792,128]{1,0:T(8,128)(2,1)S(1)}, u32[]{:S(2)}, u32[]{:S(2)}) collective-permute-start(bf16[1792,128]{1,0:T(8,128)(2,1)} %get-tuple-element.33), channel_id=1, source_target_pairs={{0,128},{8,136},{16,144},{24,152},{32,160},{40,168},{48,176},{56,1... | collective-permute-start | bytes 1376264 | tf_op jit(solution)/shard_map/ppermute | solution.py:223
  102.3 7.2 %collective-permute-done.3 = bf16[1792,128]{1,0:T(8,128)(2,1)S(1)} collective-permute-done((bf16[1792,128]{1,0:T(8,128)(2,1)S(1)}, bf16[1792,128]{1,0:T(8,128)(2,1)S(1)}, u32[]{:S(2)}, u32[]{:S(2)}) %collective-permute-start.3) | collective-permute-done | bytes 458784 | tf_op jit(solution)/shard_map/ppermute | solution.py:223
  109.5 11.0 %collective-permute-done.2 = bf16[1792,128]{1,0:T(8,128)(2,1)S(1)} collective-permute-done((bf16[1792,128]{1,0:T(8,128)(2,1)S(1)}, bf16[1792,128]{1,0:T(8,128)(2,1)S(1)}, u32[]{:S(2)}, u32[]{:S(2)}) %collective-permute-start.2) | collective-permute-done | bytes 458784 | tf_op jit(solution)/shard_map/ppermute | solution.py:223
  120.5 0.0 all-to-all-done.4.same
  120.5 0.9 fusion.29
  121.5 5.3 %collective-permute-start.5 = (bf16[2,224,384]{2,1,0:T(8,128)(2,1)}, bf16[2,224,384]{2,1,0:T(8,128)(2,1)}, u32[]{:S(2)}, u32[]{:S(2)}) collective-permute-start(bf16[2,224,384]{2,1,0:T(8,128)(2,1)} %get-tuple-element.39), channel_id=1, source_target_pairs={{0,56},{8,0},{16,8},{24,16},{32,24},{40,32},{48,40},{56,48},{64,12... | collective-permute-start | bytes 1032200 | tf_op jit(solution)/shard_map/ppermute | solution.py:243
  126.8 1.9 collective-permute-start.4
  128.8 0.8 reshape.122
  129.7 0.1 stack_reshape.6
  129.8 0.1 stack_reshape.7
  129.9 0.1 pad_add_fusion.place
  130.0 0.0 collective-permute-done.6
  130.0 1.9 collective-permute-done.5.after
  131.9 5.6 %collective-permute-done.4.before = bf16[2,224,384]{2,1,0:T(8,128)(2,1)} collective-permute-done((bf16[2,224,384]{2,1,0:T(8,128)(2,1)}, bf16[2,224,384]{2,1,0:T(8,128)(2,1)}, u32[]{:S(2)}, u32[]{:S(2)}) %collective-permute-start.4) | collective-permute-done | bytes 344096 | tf_op jit(solution)/shard_map/ppermute | solution.py:242
  137.5 2.1 %shard_map.111 = bf16[4,400,128]{2,1,0:T(8,128)(2,1)S(1)} custom-call(s32[2]{0:T(128)S(1)} %pad_add_fusion.place, bf16[4,224,384]{2,1,0:T(8,128)(2,1)S(1)} %all-to-all-done.4.same, bf16[2,224,384]{2,1,0:T(8,128)(2,1)} %collective-permute-done.4.before, bf16[2,224,384]{2,1,0:T(8,128)(2,1)} %collective-permute-done.5.after, ...), custom_call_target="tpu_custom_call" | custom-call | flops 704643072 | bytes 6291456 | tf_op jit(solution)/shard_map/pallas_call | solution.py:128
  139.6 10.7 %all_to_all.48 = bf16[4,400,128]{2,1,0:T(8,128)(2,1)S(1)} all-to-all(bf16[4,400,128]{2,1,0:T(8,128)(2,1)S(1)} %shard_map.111), channel_id=1, replica_groups={{0,64,128,192},{8,72,136,200},{16,80,144,208},{24,88,152,216},{32,96,16..., dimensions={0} | all-to-all | bytes 819200 | tf_op jit(solution)/shard_map/all_to_all | solution.py:36
  150.3 0.1 convert_reduce_fusion
  150.4 0.1 multiply_convert_fusion
  150.5 1.0 broadcast_in_dim.86
  151.5 3.7 %all-to-all-start.6 = ((bf16[8,384,128]{2,1,0:T(8,128)(2,1)}), bf16[8,384,128]{2,1,0:T(8,128)(2,1)S(1)}, u32[]{:S(2)}, u32[]{:S(2)}) async-start(bf16[8,384,128]{2,1,0:T(8,128)(2,1)} %broadcast_in_dim.86), calls=%async_computation.6 | async-start | bytes 1572864 | tf_op jit(solution)/shard_map/all_to_all | solution.py:32
  155.2 1.2 dynamic-slice_bitcast_fusion
  156.5 6.3 %collective-permute-start.7 = (bf16[224,1024]{1,0:T(8,128)(2,1)S(1)}, bf16[224,1024]{1,0:T(8,128)(2,1)S(1)}, u32[]{:S(2)}, u32[]{:S(2)}) collective-permute-start(bf16[224,1024]{1,0:T(8,128)(2,1)S(1)} %get-tuple-element.31), channel_id=1, source_target_pairs={{0,128},{8,136},{16,144},{24,152},{32,160},{40,168},{48,176},{56,1... | collective-permute-start | bytes 1376264 | tf_op jit(solution)/shard_map/ppermute | solution.py:229
  162.8 10.1 %collective-permute-done.7.block2 = bf16[224,1024]{1,0:T(8,128)(2,1)S(1)} collective-permute-done((bf16[224,1024]{1,0:T(8,128)(2,1)S(1)}, bf16[224,1024]{1,0:T(8,128)(2,1)S(1)}, u32[]{:S(2)}, u32[]{:S(2)}) %collective-permute-start.7) | collective-permute-done | bytes 458784 | tf_op jit(solution)/shard_map/ppermute | solution.py:229
  172.9 0.0 all-to-all-done.6.act
  172.9 1.7 shard_map.112
  174.7 0.0 copy-start.7
  174.7 12.8 %all_to_all.49 = bf16[4,224,384]{2,1,0:T(8,128)(2,1)S(1)} all-to-all(bf16[4,224,384]{2,1,0:T(8,128)(2,1)S(1)} %shard_map.112), channel_id=1, replica_groups={{0,64,128,192},{8,72,136,200},{16,80,144,208},{24,88,152,216},{32,96,16..., dimensions={0} | all-to-all | bytes 1376256 | tf_op jit(solution)/shard_map/all_to_all | solution.py:36
  187.5 0.1 reduce_sum.42
  187.6 0.8 copy.17
  188.4 7.6 %all-to-all-start.8 = ((bf16[16,24,224]{2,1,0:T(8,128)(2,1)}), bf16[16,24,224]{2,1,0:T(8,128)(2,1)S(1)}, u32[]{:S(2)}, u32[]{:S(2)}) async-start(bf16[16,24,224]{2,1,0:T(8,128)(2,1)} %bitcast.25), calls=%async_computation.8 | async-start | bytes 393216 | tf_op jit(solution)/shard_map/all_to_all | solution.py:36
  196.0 0.8 fusion.22
  196.8 8.8 %all-to-all-done.8 = bf16[16,24,224]{2,1,0:T(8,128)(2,1)S(1)} async-done(((bf16[16,24,224]{2,1,0:T(8,128)(2,1)}), bf16[16,24,224]{2,1,0:T(8,128)(2,1)S(1)}, u32[]{:S(2)}, u32[]{:S(2)}) %all-to-all-start.8) | async-done | bytes 172064 | tf_op jit(solution)/shard_map/all_to_all | solution.py:36
  205.6 0.2 convolution_bitcast_fusion.1
  205.8 0.8 fusion.2
  (21 shorter events, 0.1 us)
Async XLA Ops:
  0.0 3.1 %copy-start = (bf16[32,32,256]{2,1,0:T(8,128)(2,1)S(1)}, bf16[32,32,256]{2,1,0:T(8,128)(2,1)}, u32[]{:S(2)}) copy-start(bf16[32,32,256]{2,1,0:T(8,128)(2,1)} %param.13) | copy-start | bytes 1572868
  3.6 38.4 %copy-start.3 = (bf16[512,224]{0,1:T(8,128)(2,1)S(1)}, bf16[512,224]{0,1:T(8,128)(2,1)}, u32[]{:S(2)}) copy-start(bf16[512,224]{0,1:T(8,128)(2,1)} %param.15) | copy-start | bytes 688132
  42.0 9.0 %copy-start.5 = (bf16[1,224,4096]{2,1,0:T(8,128)(2,1)S(1)}, bf16[1,224,4096]{2,1,0:T(8,128)(2,1)}, u32[]{:S(2)}) copy-start(bf16[1,224,4096]{2,1,0:T(8,128)(2,1)} %param.21) | copy-start | bytes 5505028
  43.3 27.0 %copy-start.4 = (bf16[64,224]{1,0:T(8,128)(2,1)S(1)}, bf16[64,224]{1,0:T(8,128)(2,1)}, u32[]{:S(2)}) copy-start(bf16[64,224]{1,0:T(8,128)(2,1)} %residual.1) | copy-start | bytes 86020
  43.3 27.0 %all-to-all-start.2 = ((bf16[16,64,224]{2,1,0:T(8,128)(2,1)}), bf16[16,64,224]{2,1,0:T(8,128)(2,1)S(1)}, u32[]{:S(2)}, u32[]{:S(2)}) async-start(bf16[16,64,224]{2,1,0:T(8,128)(2,1)} %shard_map.109), calls=%async_computation.2 | async-start | bytes 1048576 | tf_op jit(solution)/shard_map/all_to_all | solution.py:36
  52.0 14.7 %collective-permute-start.1 = (bf16[224,1024]{1,0:T(8,128)(2,1)}, bf16[224,1024]{1,0:T(8,128)(2,1)S(1)}, u32[]{:S(2)}, u32[]{:S(2)}) collective-permute-start(bf16[224,1024]{1,0:T(8,128)(2,1)} %get-tuple-element.37), channel_id=1, source_target_pairs={{0,192},{8,200},{16,208},{24,216},{32,224},{40,232},{48,240},{56,2... | collective-permute-start | bytes 1376264 | tf_op jit(solution)/shard_map/ppermute | solution.py:229
  54.7 15.6 %collective-permute-start = (bf16[224,1024]{1,0:T(8,128)(2,1)}, bf16[224,1024]{1,0:T(8,128)(2,1)S(1)}, u32[]{:S(2)}, u32[]{:S(2)}) collective-permute-start(bf16[224,1024]{1,0:T(8,128)(2,1)} %get-tuple-element.38), channel_id=1, source_target_pairs={{0,64},{8,72},{16,80},{24,88},{32,96},{40,104},{48,112},{56,120},{... | collective-permute-start | bytes 1376264 | tf_op jit(solution)/shard_map/ppermute | solution.py:229
  58.9 29.4 %copy-start.6 = (s32[16,64]{1,0:T(8,128)}, s32[16,64]{1,0:T(8,128)S(1)}, u32[]{:S(2)}) copy-start(s32[16,64]{1,0:T(8,128)S(1)} %convolution_convert_fusion.1) | copy-start | bytes 12292
  70.3 18.0 %copy-start.1 = (bf16[224,1024]{1,0:T(8,128)(2,1)}, bf16[224,1024]{1,0:T(8,128)(2,1)S(1)}, u32[]{:S(2)}) copy-start(bf16[224,1024]{1,0:T(8,128)(2,1)S(1)} %collective-permute-done.block1) | copy-start | bytes 1376260
  88.3 32.2 %all-to-all-start.4 = ((bf16[4,224,384]{2,1,0:T(8,128)(2,1)}), bf16[4,224,384]{2,1,0:T(8,128)(2,1)S(1)}, u32[]{:S(2)}, u32[]{:S(2)}) async-start(bf16[4,224,384]{2,1,0:T(8,128)(2,1)} %broadcast_in_dim.85), calls=%async_computation.4 | async-start | bytes 1376256 | tf_op jit(solution)/shard_map/all_to_all | solution.py:32
  94.2 15.3 %collective-permute-start.3 = (bf16[1792,128]{1,0:T(8,128)(2,1)S(1)}, bf16[1792,128]{1,0:T(8,128)(2,1)S(1)}, u32[]{:S(2)}, u32[]{:S(2)}) collective-permute-start(bf16[1792,128]{1,0:T(8,128)(2,1)S(1)} %get-tuple-element.35), channel_id=1, source_target_pairs={{0,192},{8,200},{16,208},{24,216},{32,224},{40,232},{48,240},{56,2... | collective-permute-start | bytes 1376264 | tf_op jit(solution)/shard_map/ppermute | solution.py:223
  96.1 24.4 %collective-permute-start.2 = (bf16[1792,128]{1,0:T(8,128)(2,1)S(1)}, bf16[1792,128]{1,0:T(8,128)(2,1)S(1)}, u32[]{:S(2)}, u32[]{:S(2)}) collective-permute-start(bf16[1792,128]{1,0:T(8,128)(2,1)S(1)} %get-tuple-element.36), channel_id=1, source_target_pairs={{0,64},{8,72},{16,80},{24,88},{32,96},{40,104},{48,112},{56,120},{... | collective-permute-start | bytes 1376264 | tf_op jit(solution)/shard_map/ppermute | solution.py:223
  100.0 29.9 %collective-permute-start.6 = (bf16[1792,128]{1,0:T(8,128)(2,1)}, bf16[1792,128]{1,0:T(8,128)(2,1)S(1)}, u32[]{:S(2)}, u32[]{:S(2)}) collective-permute-start(bf16[1792,128]{1,0:T(8,128)(2,1)} %get-tuple-element.33), channel_id=1, source_target_pairs={{0,128},{8,136},{16,144},{24,152},{32,160},{40,168},{48,176},{56,1... | collective-permute-start | bytes 1376264 | tf_op jit(solution)/shard_map/ppermute | solution.py:223
  121.5 10.4 %collective-permute-start.5 = (bf16[2,224,384]{2,1,0:T(8,128)(2,1)}, bf16[2,224,384]{2,1,0:T(8,128)(2,1)}, u32[]{:S(2)}, u32[]{:S(2)}) collective-permute-start(bf16[2,224,384]{2,1,0:T(8,128)(2,1)} %get-tuple-element.39), channel_id=1, source_target_pairs={{0,56},{8,0},{16,8},{24,16},{32,24},{40,32},{48,40},{56,48},{64,12... | collective-permute-start | bytes 1032200 | tf_op jit(solution)/shard_map/ppermute | solution.py:243
  126.8 10.7 %collective-permute-start.4 = (bf16[2,224,384]{2,1,0:T(8,128)(2,1)}, bf16[2,224,384]{2,1,0:T(8,128)(2,1)}, u32[]{:S(2)}, u32[]{:S(2)}) collective-permute-start(bf16[2,224,384]{2,1,0:T(8,128)(2,1)} %get-tuple-element.40), channel_id=1, source_target_pairs={{0,8},{8,16},{16,24},{24,32},{32,40},{40,48},{48,56},{56,0},{64,72... | collective-permute-start | bytes 1032200 | tf_op jit(solution)/shard_map/ppermute | solution.py:242
  151.5 21.4 %copy-start.2 = (bf16[224,1024]{1,0:T(8,128)(2,1)S(1)}, bf16[224,1024]{1,0:T(8,128)(2,1)}, u32[]{:S(2)}) copy-start(bf16[224,1024]{1,0:T(8,128)(2,1)} %copy-done.1) | copy-start | bytes 1376260
  151.5 21.4 %all-to-all-start.6 = ((bf16[8,384,128]{2,1,0:T(8,128)(2,1)}), bf16[8,384,128]{2,1,0:T(8,128)(2,1)S(1)}, u32[]{:S(2)}, u32[]{:S(2)}) async-start(bf16[8,384,128]{2,1,0:T(8,128)(2,1)} %broadcast_in_dim.86), calls=%async_computation.6 | async-start | bytes 1572864 | tf_op jit(solution)/shard_map/all_to_all | solution.py:32
  156.5 16.5 %collective-permute-start.7 = (bf16[224,1024]{1,0:T(8,128)(2,1)S(1)}, bf16[224,1024]{1,0:T(8,128)(2,1)S(1)}, u32[]{:S(2)}, u32[]{:S(2)}) collective-permute-start(bf16[224,1024]{1,0:T(8,128)(2,1)S(1)} %get-tuple-element.31), channel_id=1, source_target_pairs={{0,128},{8,136},{16,144},{24,152},{32,160},{40,168},{48,176},{56,1... | collective-permute-start | bytes 1376264 | tf_op jit(solution)/shard_map/ppermute | solution.py:229
  174.7 30.9 %copy-start.7 = (s32[16,64]{1,0:T(8,128)S(1)}, s32[16,64]{1,0:T(8,128)}, u32[]{:S(2)}) copy-start(s32[16,64]{1,0:T(8,128)} %copy-done.6) | copy-start | bytes 12292
  188.4 17.2 %all-to-all-start.8 = ((bf16[16,24,224]{2,1,0:T(8,128)(2,1)}), bf16[16,24,224]{2,1,0:T(8,128)(2,1)S(1)}, u32[]{:S(2)}, u32[]{:S(2)}) async-start(bf16[16,24,224]{2,1,0:T(8,128)(2,1)} %bitcast.25), calls=%async_computation.8 | async-start | bytes 393216 | tf_op jit(solution)/shard_map/all_to_all | solution.py:36

commit v8 on v7

--- a/solution.py
+++ b/solution.py
@@ -231,16 +231,16 @@
     attn = spread(attn, NZ, "grp", GATHER)
     attn = spread(attn.reshape(-1, attn.shape[2]), parts, "grp", REDUCE)
     projected = project(attn.reshape(parts, NZ, -1, attn.shape[2]), out_weight.T)
-    projected, down_weight = lax.optimization_barrier((projected, down_weight))
+    projected, up_weight = lax.optimization_barrier((projected, up_weight))
     projected = exchange(projected, ("pool", "tp"))
-    projected, down1, down3 = lax.optimization_barrier((projected, down_block(1), down_block(3)))
+    projected, up1, up3 = lax.optimization_barrier((projected, up_block(1), up_block(3)))
     slot_rows = head_sum(projected, residual, select)
     slot_rows = exchange(slot_rows.reshape(experts, slot_cap, columns), ("pool", "tp"))
-    slot_rows, up_weight = lax.optimization_barrier((slot_rows, up_weight))
+    slot_rows, up_weight, down_weight = lax.optimization_barrier((slot_rows, up_weight, down_weight))
     same = spread(slot_rows.reshape(slots, columns).T, NZ, "grp", GATHER)
-    same, up1, up3 = lax.optimization_barrier((same, up_block(1), up_block(3)))
     before = lax.ppermute(same[: NZ // 2], "grp", turns(1))
     after = lax.ppermute(same[NZ // 2 :], "grp", turns(-1))
+    before, after, down1, down3 = lax.optimization_barrier((before, after, down_block(1), down_block(3)))
     gain = norm_gain.reshape(NX, NZ, PAIR, columns)
     gain = lax.dynamic_index_in_dim(gain, x_index, 0, keepdims=False)
     gain = [lax.dynamic_index_in_dim(gain, m, 1, keepdims=False).reshape(-1) for m in (member, 1 - member)]

time: 208 us -> 196 us (0.942)
  waiting for transfers between devices: 56 us -> 47.5 us
  blocking collectives: 78.4 us -> 76.2 us
  starting transfers between devices: 50 us -> 47.8 us
    all_to_all x2, waiting for transfers between devices: 0.01 us -> 11.3 us  [spread(): lax.all_to_all(sent, axis, 0, 0, tiled=True, axis_index_groups=groups)]
    ppermute x3, waiting for transfers between devices: 21.4 us -> 10.3 us  [down_block(): return lax.ppermute(block, 'grp', moves(step, 0)) if step else block]
    ppermute x3, waiting for transfers between devices: 18.2 us -> 11.1 us  [up_block(): block = lax.ppermute(block, 'grp', moves(step, 0)) if step else block]
    ppermute x1, starting transfers between devices: 1.92 us -> 5.97 us  [shards(): before = lax.ppermute(same[:NZ // 2], 'grp', turns(1))]
    ppermute x1, starting transfers between devices: 5.34 us -> 1.92 us  [shards(): after = lax.ppermute(same[NZ // 2:], 'grp', turns(-1))]
    ppermute x1, waiting for transfers between devices: 5.61 us -> 2.36 us  [shards(): before = lax.ppermute(same[:NZ // 2], 'grp', turns(1))]
    all_to_all x3, blocking collectives: 40.1 us -> 37.9 us  [exchange(): lax.all_to_all(value, axis, 0, 0, tiled=True, axis_index_groups=groups)]
    ppermute x3, starting transfers between devices: 12.2 us -> 10.1 us  [down_block(): return lax.ppermute(block, 'grp', moves(step, 0)) if step else block]
  transfers between devices with their start and end apart: 12 -> 12, of which waited for: 8 -> 9; matrix products, arithmetic and copies ran while one was open for 4% -> 5% of each run, Pallas kernels for 0% -> 0%
where the time goes in v8:
time: 196 us; the launch traced here: 195 us
  blocking collectives  76.2 us (39%)
  starting transfers between devices  47.8 us (24%)
  waiting for transfers between devices  47.5 us (24%)
  local copies, waits for them, and re-layouts  12.6 us (6%)
  Pallas kernels  5.84 us (3%)
  matrix products  3.02 us (2%)
    all_to_all x2, blocking collectives, spread(): lax.all_to_all(sent, axis, 0, 0, tiled=True, axis_index_groups=groups)  38.3 us
    all_to_all x3, blocking collectives, exchange(): lax.all_to_all(value, axis, 0, 0, tiled=True, axis_index_groups=groups)  37.9 us
    all_to_all x2, starting transfers between devices, exchange(): lax.all_to_all(value, axis, 0, 0, tiled=True, axis_index_groups=groups)  15 us
    all_to_all x2, waiting for transfers between devices, spread(): lax.all_to_all(sent, axis, 0, 0, tiled=True, axis_index_groups=groups)  11.3 us
    ppermute x3, waiting for transfers between devices, up_block(): block = lax.ppermute(block, 'grp', moves(step, 0)) if step else block  11.1 us
    ppermute x3, waiting for transfers between devices, down_block(): return lax.ppermute(block, 'grp', moves(step, 0)) if step else block  10.3 us
    ppermute x3, starting transfers between devices, down_block(): return lax.ppermute(block, 'grp', moves(step, 0)) if step else block  10.1 us
    all_to_all x2, waiting for transfers between devices, exchange(): lax.all_to_all(value, axis, 0, 0, tiled=True, axis_index_groups=groups)  8.84 us
  transfers between devices with their start and end apart: 12, of which 9 were waited for; matrix products, arithmetic and copies ran while one was open for 5% of the time, Pallas kernels for 0%

profile of v8, /device:TPU:8, one launch (start us, length us, event | category | flops | bytes accessed | tf_op | source)
XLA Modules:
  0.0 194.9 jit_solution(577711239612295031)
XLA Ops:
  0.0 0.8 reshape.116
  0.8 0.7 iota_compare_fusion.4
  1.6 1.3 fusion.5
  2.9 0.2 fusion.30
  3.1 0.6 convolution_convert_fusion
  3.6 0.0 copy-start.1
  3.7 19.5 %all_to_all.45 = bf16[4,32,512]{2,1,0:T(8,128)(2,1)S(1)} all-to-all(bf16[4,32,512]{2,1,0:T(8,128)(2,1)S(1)} %broadcast_in_dim.82), channel_id=1, replica_groups={{0,16,32,48},{8,24,40,56},{64,80,96,112},{72,88,104,120},{128,144,160,1..., dimensions={0} | all-to-all | bytes 262144 | tf_op jit(solution)/shard_map/all_to_all | solution.py:32
  23.2 0.1 broadcast_in_dim.84
  23.3 18.8 %all_to_all.46 = bf16[8,128,512]{2,1,0:T(8,128)(2,1)S(1)} all-to-all(bf16[8,128,512]{2,1,0:T(8,128)(2,1)S(1)} %broadcast_in_dim.84), channel_id=1, replica_groups={{0,8,64,72,128,136,192,200},{16,24,80,88,144,152,208,216},{32,40,96,104..., dimensions={0} | all-to-all | bytes 2097152 | tf_op jit(solution)/shard_map/all_to_all | solution.py:32
  42.0 1.3 shard_map.109
  43.3 7.7 %all-to-all-start.2 = ((bf16[16,64,224]{2,1,0:T(8,128)(2,1)}), bf16[16,64,224]{2,1,0:T(8,128)(2,1)S(1)}, u32[]{:S(2)}, u32[]{:S(2)}) async-start(bf16[16,64,224]{2,1,0:T(8,128)(2,1)} %shard_map.109), calls=%async_computation.2 | async-start | bytes 1048576 | tf_op jit(solution)/shard_map/all_to_all | solution.py:36
  51.0 0.8 dynamic-slice_bitcast_fusion.5
  51.9 2.7 %collective-permute-start.1 = (bf16[1792,128]{1,0:T(8,128)(2,1)}, bf16[1792,128]{1,0:T(8,128)(2,1)S(1)}, u32[]{:S(2)}, u32[]{:S(2)}) collective-permute-start(bf16[1792,128]{1,0:T(8,128)(2,1)} %get-tuple-element.41), channel_id=1, source_target_pairs={{0,192},{8,200},{16,208},{24,216},{32,224},{40,232},{48,240},{56,2... | collective-permute-start | bytes 1376264 | tf_op jit(solution)/shard_map/ppermute | solution.py:223
  54.5 3.2 %collective-permute-start = (bf16[1792,128]{1,0:T(8,128)(2,1)S(1)}, bf16[1792,128]{1,0:T(8,128)(2,1)S(1)}, u32[]{:S(2)}, u32[]{:S(2)}) collective-permute-start(bf16[1792,128]{1,0:T(8,128)(2,1)S(1)} %get-tuple-element.42), channel_id=1, source_target_pairs={{0,64},{8,72},{16,80},{24,88},{32,96},{40,104},{48,112},{56,120},{... | collective-permute-start | bytes 1376264 | tf_op jit(solution)/shard_map/ppermute | solution.py:223
  57.7 0.1 eq.58
  57.8 0.8 fusion.21
  58.6 0.1 convolution_convert_fusion.1
  58.7 0.1 fusion.9.select
  58.9 7.7 %collective-permute-done.1 = bf16[1792,128]{1,0:T(8,128)(2,1)S(1)} collective-permute-done((bf16[1792,128]{1,0:T(8,128)(2,1)}, bf16[1792,128]{1,0:T(8,128)(2,1)S(1)}, u32[]{:S(2)}, u32[]{:S(2)}) %collective-permute-start.1) | collective-permute-done | bytes 458784 | tf_op jit(solution)/shard_map/ppermute | solution.py:223
  66.5 3.4 %collective-permute-done = bf16[1792,128]{1,0:T(8,128)(2,1)S(1)} collective-permute-done((bf16[1792,128]{1,0:T(8,128)(2,1)S(1)}, bf16[1792,128]{1,0:T(8,128)(2,1)S(1)}, u32[]{:S(2)}, u32[]{:S(2)}) %collective-permute-start) | collective-permute-done | bytes 458784 | tf_op jit(solution)/shard_map/ppermute | solution.py:223
  69.9 0.3 shard_map.110
  70.2 16.6 %all_to_all.47 = bf16[16,24,224]{2,1,0:T(8,128)(2,1)S(1)} all-to-all(bf16[16,24,224]{2,1,0:T(8,128)(2,1)S(1)} %bitcast.63), channel_id=1, replica_groups=mesh['pool'=2,'grp'=32,'tp'=8] {'pool','tp'}, dimensions={0} | all-to-all | bytes 344064 | tf_op jit(solution)/shard_map/all_to_all | solution.py:36
  86.8 0.1 copy.16
  87.0 0.9 broadcast_in_dim.85
  87.9 3.5 %all-to-all-start.4 = ((bf16[4,224,384]{2,1,0:T(8,128)(2,1)}), bf16[4,224,384]{2,1,0:T(8,128)(2,1)S(1)}, u32[]{:S(2)}, u32[]{:S(2)}) async-start(bf16[4,224,384]{2,1,0:T(8,128)(2,1)} %broadcast_in_dim.85), calls=%async_computation.4 | async-start | bytes 1376256 | tf_op jit(solution)/shard_map/all_to_all | solution.py:32
  91.4 0.0 copy-start.4
  91.5 2.3 %dynamic-slice_bitcast_fusion.3 = (bf16[224,1024]{1,0:T(8,128)(2,1)}, bf16[224,1024]{1,0:T(8,128)(2,1)}) fusion(bf16[1,224,4096]{2,1,0:T(8,128)(2,1)} %param.21, s32[]{:T(128)S(6)} %select_n.106, s32[]{:T(128)S(6)} %select_n.105), kind=kLoop, calls=%fused_computation.15 | loop fusion | bytes 1835016 | tf_op jit(solution)/shard_map/dynamic_slice | solution.py:228
  93.8 1.9 %collective-permute-start.4 = (bf16[224,1024]{1,0:T(8,128)(2,1)}, bf16[224,1024]{1,0:T(8,128)(2,1)S(1)}, u32[]{:S(2)}, u32[]{:S(2)}) collective-permute-start(bf16[224,1024]{1,0:T(8,128)(2,1)} %get-tuple-element.40), channel_id=1, source_target_pairs={{0,64},{8,72},{16,80},{24,88},{32,96},{40,104},{48,112},{56,120},{... | collective-permute-start | bytes 1376264 | tf_op jit(solution)/shard_map/ppermute | solution.py:229
  95.7 5.1 %collective-permute-start.5 = (bf16[224,1024]{1,0:T(8,128)(2,1)}, bf16[224,1024]{1,0:T(8,128)(2,1)}, u32[]{:S(2)}, u32[]{:S(2)}) collective-permute-start(bf16[224,1024]{1,0:T(8,128)(2,1)} %get-tuple-element.39), channel_id=1, source_target_pairs={{0,192},{8,200},{16,208},{24,216},{32,224},{40,232},{48,240},{56,2... | collective-permute-start | bytes 1376264 | tf_op jit(solution)/shard_map/ppermute | solution.py:229
  100.8 0.8 dynamic-slice_bitcast_fusion.2
  101.7 1.9 collective-permute-start.6
  103.6 4.8 %all-to-all-done.4.same = bf16[4,224,384]{2,1,0:T(8,128)(2,1)S(1)} async-done(((bf16[4,224,384]{2,1,0:T(8,128)(2,1)}), bf16[4,224,384]{2,1,0:T(8,128)(2,1)S(1)}, u32[]{:S(2)}, u32[]{:S(2)}) %all-to-all-start.4) | async-done | bytes 688160 | tf_op jit(solution)/shard_map/all_to_all | solution.py:32
  108.4 0.9 fusion.29
  109.3 6.0 %collective-permute-start.2 = (bf16[2,224,384]{2,1,0:T(8,128)(2,1)}, bf16[2,224,384]{2,1,0:T(8,128)(2,1)}, u32[]{:S(2)}, u32[]{:S(2)}) collective-permute-start(bf16[2,224,384]{2,1,0:T(8,128)(2,1)} %get-tuple-element.44), channel_id=1, source_target_pairs={{0,8},{8,16},{16,24},{24,32},{32,40},{40,48},{48,56},{56,0},{64,72... | collective-permute-start | bytes 1032200 | tf_op jit(solution)/shard_map/ppermute | solution.py:241
  115.3 1.9 collective-permute-start.3
  117.2 0.8 reshape.122
  118.1 0.1 stack_reshape.6
  118.2 0.1 stack_reshape.7
  118.3 0.1 pad_add_fusion.place
  118.4 0.0 collective-permute-done.4.block1
  118.4 1.3 collective-permute-done.5.block3
  119.7 2.4 %collective-permute-done.2.before = bf16[2,224,384]{2,1,0:T(8,128)(2,1)} collective-permute-done((bf16[2,224,384]{2,1,0:T(8,128)(2,1)}, bf16[2,224,384]{2,1,0:T(8,128)(2,1)}, u32[]{:S(2)}, u32[]{:S(2)}) %collective-permute-start.2) | collective-permute-done | bytes 344096 | tf_op jit(solution)/shard_map/ppermute | solution.py:241
  122.0 3.6 %collective-permute-done.3.after = bf16[2,224,384]{2,1,0:T(8,128)(2,1)} collective-permute-done((bf16[2,224,384]{2,1,0:T(8,128)(2,1)}, bf16[2,224,384]{2,1,0:T(8,128)(2,1)}, u32[]{:S(2)}, u32[]{:S(2)}) %collective-permute-start.3) | collective-permute-done | bytes 344096 | tf_op jit(solution)/shard_map/ppermute | solution.py:242
  125.6 0.0 collective-permute-done.6
  125.6 2.1 %shard_map.111 = bf16[4,400,128]{2,1,0:T(8,128)(2,1)S(1)} custom-call(s32[2]{0:T(128)S(1)} %pad_add_fusion.place, bf16[4,224,384]{2,1,0:T(8,128)(2,1)S(1)} %all-to-all-done.4.same, bf16[2,224,384]{2,1,0:T(8,128)(2,1)} %collective-permute-done.2.before, bf16[2,224,384]{2,1,0:T(8,128)(2,1)} %collective-permute-done.3.after, ...), custom_call_target="tpu_custom_call" | custom-call | flops 704643072 | bytes 6291456 | tf_op jit(solution)/shard_map/pallas_call | solution.py:128
  127.7 9.8 %all_to_all.48 = bf16[4,400,128]{2,1,0:T(8,128)(2,1)S(1)} all-to-all(bf16[4,400,128]{2,1,0:T(8,128)(2,1)S(1)} %shard_map.111), channel_id=1, replica_groups={{0,64,128,192},{8,72,136,200},{16,80,144,208},{24,88,152,216},{32,96,16..., dimensions={0} | all-to-all | bytes 819200 | tf_op jit(solution)/shard_map/all_to_all | solution.py:36
  137.6 0.1 convert_reduce_fusion
  137.6 0.1 multiply_convert_fusion
  137.8 1.0 broadcast_in_dim.86
  138.8 3.5 %all-to-all-start.6 = ((bf16[8,384,128]{2,1,0:T(8,128)(2,1)}), bf16[8,384,128]{2,1,0:T(8,128)(2,1)S(1)}, u32[]{:S(2)}, u32[]{:S(2)}) async-start(bf16[8,384,128]{2,1,0:T(8,128)(2,1)} %broadcast_in_dim.86), calls=%async_computation.6 | async-start | bytes 1572864 | tf_op jit(solution)/shard_map/all_to_all | solution.py:32
  142.3 1.2 dynamic-slice_bitcast_fusion
  143.6 3.0 %collective-permute-start.7 = (bf16[224,1024]{1,0:T(8,128)(2,1)S(1)}, bf16[224,1024]{1,0:T(8,128)(2,1)S(1)}, u32[]{:S(2)}, u32[]{:S(2)}) collective-permute-start(bf16[224,1024]{1,0:T(8,128)(2,1)S(1)} %get-tuple-element.35), channel_id=1, source_target_pairs={{0,128},{8,136},{16,144},{24,152},{32,160},{40,168},{48,176},{56,1... | collective-permute-start | bytes 1376264 | tf_op jit(solution)/shard_map/ppermute | solution.py:229
  146.6 9.1 %collective-permute-done.7.block2 = bf16[224,1024]{1,0:T(8,128)(2,1)S(1)} collective-permute-done((bf16[224,1024]{1,0:T(8,128)(2,1)S(1)}, bf16[224,1024]{1,0:T(8,128)(2,1)S(1)}, u32[]{:S(2)}, u32[]{:S(2)}) %collective-permute-start.7) | collective-permute-done | bytes 458784 | tf_op jit(solution)/shard_map/ppermute | solution.py:229
  155.7 6.6 %all-to-all-done.6.act = bf16[8,384,128]{2,1,0:T(8,128)(2,1)S(1)} async-done(((bf16[8,384,128]{2,1,0:T(8,128)(2,1)}), bf16[8,384,128]{2,1,0:T(8,128)(2,1)S(1)}, u32[]{:S(2)}, u32[]{:S(2)}) %all-to-all-start.6) | async-done | bytes 786464 | tf_op jit(solution)/shard_map/all_to_all | solution.py:32
  162.2 2.2 %shard_map.112 = bf16[4,224,384]{2,1,0:T(8,128)(2,1)S(1)} custom-call(s32[2]{0:T(128)S(1)} %pad_add_fusion.place, bf16[8,384,128]{2,1,0:T(8,128)(2,1)S(1)} %all-to-all-done.6.act, bf16[224,1024]{1,0:T(8,128)(2,1)S(1)} %get-tuple-element.36.block0, bf16[224,1024]{1,0:T(8,128)(2,1)S(1)} %collective-permute-done.4.block1, ...), custom_call_target="tpu_custom_call" | custom-call | flops 704643072 | bytes 5242880 | tf_op jit(solution)/shard_map/pallas_call | solution.py:156
  164.5 0.0 copy-start.6
  164.5 11.4 %all_to_all.49 = bf16[4,224,384]{2,1,0:T(8,128)(2,1)S(1)} all-to-all(bf16[4,224,384]{2,1,0:T(8,128)(2,1)S(1)} %shard_map.112), channel_id=1, replica_groups={{0,64,128,192},{8,72,136,200},{16,80,144,208},{24,88,152,216},{32,96,16..., dimensions={0} | all-to-all | bytes 1376256 | tf_op jit(solution)/shard_map/all_to_all | solution.py:36
  175.9 0.1 reduce_sum.42
  176.0 0.8 copy.17
  176.9 7.3 %all-to-all-start.8 = ((bf16[16,24,224]{2,1,0:T(8,128)(2,1)}), bf16[16,24,224]{2,1,0:T(8,128)(2,1)S(1)}, u32[]{:S(2)}, u32[]{:S(2)}) async-start(bf16[16,24,224]{2,1,0:T(8,128)(2,1)} %bitcast.25), calls=%async_computation.8 | async-start | bytes 393216 | tf_op jit(solution)/shard_map/all_to_all | solution.py:36
  184.2 0.8 fusion.22
  185.0 8.8 %all-to-all-done.8 = bf16[16,24,224]{2,1,0:T(8,128)(2,1)S(1)} async-done(((bf16[16,24,224]{2,1,0:T(8,128)(2,1)}), bf16[16,24,224]{2,1,0:T(8,128)(2,1)S(1)}, u32[]{:S(2)}, u32[]{:S(2)}) %all-to-all-start.8) | async-done | bytes 172064 | tf_op jit(solution)/shard_map/all_to_all | solution.py:36
  193.8 0.2 convolution_bitcast_fusion.1
  194.0 0.8 fusion.2
  (20 shorter events, 0.1 us)
Async XLA Ops:
  0.0 3.1 %copy-start = (bf16[32,32,256]{2,1,0:T(8,128)(2,1)S(1)}, bf16[32,32,256]{2,1,0:T(8,128)(2,1)}, u32[]{:S(2)}) copy-start(bf16[32,32,256]{2,1,0:T(8,128)(2,1)} %param.13) | copy-start | bytes 1572868
  3.6 38.4 %copy-start.1 = (bf16[512,224]{0,1:T(8,128)(2,1)S(1)}, bf16[512,224]{0,1:T(8,128)(2,1)}, u32[]{:S(2)}) copy-start(bf16[512,224]{0,1:T(8,128)(2,1)} %param.15) | copy-start | bytes 688132
  42.0 9.0 %copy-start.3 = (bf16[1,7168,128]{2,1,0:T(8,128)(2,1)S(1)}, bf16[1,7168,128]{2,1,0:T(8,128)(2,1)}, u32[]{:S(2)}) copy-start(bf16[1,7168,128]{2,1,0:T(8,128)(2,1)} %param.20) | copy-start | bytes 5505028
  43.3 26.6 %copy-start.2 = (bf16[64,224]{1,0:T(8,128)(2,1)S(1)}, bf16[64,224]{1,0:T(8,128)(2,1)}, u32[]{:S(2)}) copy-start(bf16[64,224]{1,0:T(8,128)(2,1)} %residual.1) | copy-start | bytes 86020
  43.3 26.6 %all-to-all-start.2 = ((bf16[16,64,224]{2,1,0:T(8,128)(2,1)}), bf16[16,64,224]{2,1,0:T(8,128)(2,1)S(1)}, u32[]{:S(2)}, u32[]{:S(2)}) async-start(bf16[16,64,224]{2,1,0:T(8,128)(2,1)} %shard_map.109), calls=%async_computation.2 | async-start | bytes 1048576 | tf_op jit(solution)/shard_map/all_to_all | solution.py:36
  51.9 14.7 %collective-permute-start.1 = (bf16[1792,128]{1,0:T(8,128)(2,1)}, bf16[1792,128]{1,0:T(8,128)(2,1)S(1)}, u32[]{:S(2)}, u32[]{:S(2)}) collective-permute-start(bf16[1792,128]{1,0:T(8,128)(2,1)} %get-tuple-element.41), channel_id=1, source_target_pairs={{0,192},{8,200},{16,208},{24,216},{32,224},{40,232},{48,240},{56,2... | collective-permute-start | bytes 1376264 | tf_op jit(solution)/shard_map/ppermute | solution.py:223
  54.5 15.4 %collective-permute-start = (bf16[1792,128]{1,0:T(8,128)(2,1)S(1)}, bf16[1792,128]{1,0:T(8,128)(2,1)S(1)}, u32[]{:S(2)}, u32[]{:S(2)}) collective-permute-start(bf16[1792,128]{1,0:T(8,128)(2,1)S(1)} %get-tuple-element.42), channel_id=1, source_target_pairs={{0,64},{8,72},{16,80},{24,88},{32,96},{40,104},{48,112},{56,120},{... | collective-permute-start | bytes 1376264 | tf_op jit(solution)/shard_map/ppermute | solution.py:223
  58.7 29.2 %copy-start.5 = (s32[16,64]{1,0:T(8,128)}, s32[16,64]{1,0:T(8,128)S(1)}, u32[]{:S(2)}) copy-start(s32[16,64]{1,0:T(8,128)S(1)} %convolution_convert_fusion.1) | copy-start | bytes 12292
  87.9 20.5 %all-to-all-start.4 = ((bf16[4,224,384]{2,1,0:T(8,128)(2,1)}), bf16[4,224,384]{2,1,0:T(8,128)(2,1)S(1)}, u32[]{:S(2)}, u32[]{:S(2)}) async-start(bf16[4,224,384]{2,1,0:T(8,128)(2,1)} %broadcast_in_dim.85), calls=%async_computation.4 | async-start | bytes 1376256 | tf_op jit(solution)/shard_map/all_to_all | solution.py:32
  91.4 9.4 %copy-start.4 = (bf16[1,7168,128]{2,1,0:T(8,128)(2,1)S(1)}, bf16[1,7168,128]{2,1,0:T(8,128)(2,1)}, u32[]{:S(2)}) copy-start(bf16[1,7168,128]{2,1,0:T(8,128)(2,1)} %param.20) | copy-start | bytes 5505028
  93.8 24.6 %collective-permute-start.4 = (bf16[224,1024]{1,0:T(8,128)(2,1)}, bf16[224,1024]{1,0:T(8,128)(2,1)S(1)}, u32[]{:S(2)}, u32[]{:S(2)}) collective-permute-start(bf16[224,1024]{1,0:T(8,128)(2,1)} %get-tuple-element.40), channel_id=1, source_target_pairs={{0,64},{8,72},{16,80},{24,88},{32,96},{40,104},{48,112},{56,120},{... | collective-permute-start | bytes 1376264 | tf_op jit(solution)/shard_map/ppermute | solution.py:229
  95.7 24.0 %collective-permute-start.5 = (bf16[224,1024]{1,0:T(8,128)(2,1)}, bf16[224,1024]{1,0:T(8,128)(2,1)}, u32[]{:S(2)}, u32[]{:S(2)}) collective-permute-start(bf16[224,1024]{1,0:T(8,128)(2,1)} %get-tuple-element.39), channel_id=1, source_target_pairs={{0,192},{8,200},{16,208},{24,216},{32,224},{40,232},{48,240},{56,2... | collective-permute-start | bytes 1376264 | tf_op jit(solution)/shard_map/ppermute | solution.py:229
  101.7 23.9 %collective-permute-start.6 = (bf16[1792,128]{1,0:T(8,128)(2,1)}, bf16[1792,128]{1,0:T(8,128)(2,1)S(1)}, u32[]{:S(2)}, u32[]{:S(2)}) collective-permute-start(bf16[1792,128]{1,0:T(8,128)(2,1)} %get-tuple-element.37), channel_id=1, source_target_pairs={{0,128},{8,136},{16,144},{24,152},{32,160},{40,168},{48,176},{56,1... | collective-permute-start | bytes 1376264 | tf_op jit(solution)/shard_map/ppermute | solution.py:223
  109.3 12.8 %collective-permute-start.2 = (bf16[2,224,384]{2,1,0:T(8,128)(2,1)}, bf16[2,224,384]{2,1,0:T(8,128)(2,1)}, u32[]{:S(2)}, u32[]{:S(2)}) collective-permute-start(bf16[2,224,384]{2,1,0:T(8,128)(2,1)} %get-tuple-element.44), channel_id=1, source_target_pairs={{0,8},{8,16},{16,24},{24,32},{32,40},{40,48},{48,56},{56,0},{64,72... | collective-permute-start | bytes 1032200 | tf_op jit(solution)/shard_map/ppermute | solution.py:241
  115.3 10.3 %collective-permute-start.3 = (bf16[2,224,384]{2,1,0:T(8,128)(2,1)}, bf16[2,224,384]{2,1,0:T(8,128)(2,1)}, u32[]{:S(2)}, u32[]{:S(2)}) collective-permute-start(bf16[2,224,384]{2,1,0:T(8,128)(2,1)} %get-tuple-element.43), channel_id=1, source_target_pairs={{0,56},{8,0},{16,8},{24,16},{32,24},{40,32},{48,40},{56,48},{64,12... | collective-permute-start | bytes 1032200 | tf_op jit(solution)/shard_map/ppermute | solution.py:242
  138.8 23.5 %all-to-all-start.6 = ((bf16[8,384,128]{2,1,0:T(8,128)(2,1)}), bf16[8,384,128]{2,1,0:T(8,128)(2,1)S(1)}, u32[]{:S(2)}, u32[]{:S(2)}) async-start(bf16[8,384,128]{2,1,0:T(8,128)(2,1)} %broadcast_in_dim.86), calls=%async_computation.6 | async-start | bytes 1572864 | tf_op jit(solution)/shard_map/all_to_all | solution.py:32
  143.6 12.1 %collective-permute-start.7 = (bf16[224,1024]{1,0:T(8,128)(2,1)S(1)}, bf16[224,1024]{1,0:T(8,128)(2,1)S(1)}, u32[]{:S(2)}, u32[]{:S(2)}) collective-permute-start(bf16[224,1024]{1,0:T(8,128)(2,1)S(1)} %get-tuple-element.35), channel_id=1, source_target_pairs={{0,128},{8,136},{16,144},{24,152},{32,160},{40,168},{48,176},{56,1... | collective-permute-start | bytes 1376264 | tf_op jit(solution)/shard_map/ppermute | solution.py:229
  164.5 29.3 %copy-start.6 = (s32[16,64]{1,0:T(8,128)S(1)}, s32[16,64]{1,0:T(8,128)}, u32[]{:S(2)}) copy-start(s32[16,64]{1,0:T(8,128)} %copy-done.5) | copy-start | bytes 12292
  176.9 16.9 %all-to-all-start.8 = ((bf16[16,24,224]{2,1,0:T(8,128)(2,1)}), bf16[16,24,224]{2,1,0:T(8,128)(2,1)S(1)}, u32[]{:S(2)}, u32[]{:S(2)}) async-start(bf16[16,24,224]{2,1,0:T(8,128)(2,1)} %bitcast.25), calls=%async_computation.8 | async-start | bytes 393216 | tf_op jit(solution)/shard_map/all_to_all | solution.py:36

commit v9 on v8

--- a/solution.py
+++ b/solution.py
@@ -3,15 +3,13 @@
 from jax import lax
 from jax.experimental import pallas as pl
 from jax.experimental.pallas import tpu as pltpu
+from jax.sharding import Mesh
 from jax.sharding import PartitionSpec as P
 
 BF16 = jnp.bfloat16
 F32 = jnp.float32
 NX, NZ, PAIR = 4, 4, 2
-GATHER = [[x * 8 + z * 2 + m for z in range(NZ)] for x in range(NX) for m in range(PAIR)]
-LINE = [[x * 8 + z for z in range(8)] for x in range(NX)]
-CROSS = [[x * 8 + z for x in range(NX)] for z in range(8)]
-REDUCE = [[x * 8 + z * 2 + m for x in range(NX) for m in range(PAIR)] for z in range(NZ)]
+GRP = ("x", "zpair", "member")
 
 
 def moves(by_x, by_member):
@@ -27,13 +25,12 @@
     return [(x * 8 + z, x * 8 + (z + by) % 8) for x in range(NX) for z in range(8)]
 
 
-def spread(value, count, axis, groups=None):
-    sent = jnp.broadcast_to(value[None], (count,) + value.shape)
-    return lax.all_to_all(sent, axis, 0, 0, tiled=True, axis_index_groups=groups)
-
-
-def exchange(value, axis, groups=None):
-    return lax.all_to_all(value, axis, 0, 0, tiled=True, axis_index_groups=groups)
+def exchange(value, axis):
+    return lax.all_to_all(value, axis, 0, 0, tiled=True)
+
+
+def spread(value, count, axis):
+    return exchange(jnp.broadcast_to(value[None], (count,) + value.shape), axis)
 
 
 def whole(count):
@@ -194,7 +191,7 @@
 ):
     experts = lax.axis_size(("pool", "tp"))
     block_index = lax.axis_index(("pool", "tp"))
-    group_index = lax.axis_index("grp")
+    group_index = lax.axis_index(GRP)
     x_index, member = group_index // (NZ * PAIR), group_index % PAIR
     rows, columns = residual.shape
     top_count = routes.shape[1]
@@ -220,26 +217,27 @@
     def up_block(step):
         wanted = (x_index + step) % NX
         block = lax.dynamic_slice_in_dim(up_weight[0], wanted * (width // NX), width // NX, 0)
-        block = lax.ppermute(block, "grp", moves(step, 0)) if step else block
+        block = lax.ppermute(block, GRP, moves(step, 0)) if step else block
         return block.reshape(NZ, PAIR, columns, units)
 
     def down_block(step):
         wanted = (x_index + step) % NX
         block = lax.dynamic_slice_in_dim(down_weight[0], wanted * (8 * units), 8 * units, 1)
-        return lax.ppermute(block, "grp", moves(step, 0)) if step else block
-
-    attn = spread(attn, NZ, "grp", GATHER)
-    attn = spread(attn.reshape(-1, attn.shape[2]), parts, "grp", REDUCE)
+        return lax.ppermute(block, GRP, moves(step, 0)) if step else block
+
+    attn = spread(attn, NZ, "zpair")
+    attn = spread(attn.reshape(-1, attn.shape[2]), parts, ("x", "member"))
     projected = project(attn.reshape(parts, NZ, -1, attn.shape[2]), out_weight.T)
     projected, up_weight = lax.optimization_barrier((projected, up_weight))
     projected = exchange(projected, ("pool", "tp"))
     projected, up1, up3 = lax.optimization_barrier((projected, up_block(1), up_block(3)))
     slot_rows = head_sum(projected, residual, select)
-    slot_rows = exchange(slot_rows.reshape(experts, slot_cap, columns), ("pool", "tp"))
     slot_rows, up_weight, down_weight = lax.optimization_barrier((slot_rows, up_weight, down_weight))
-    same = spread(slot_rows.reshape(slots, columns).T, NZ, "grp", GATHER)
-    before = lax.ppermute(same[: NZ // 2], "grp", turns(1))
-    after = lax.ppermute(same[NZ // 2 :], "grp", turns(-1))
+    same = jnp.broadcast_to(slot_rows.reshape(experts, 1, slot_cap, columns), (experts, NZ, slot_cap, columns))
+    same = exchange(same.reshape(experts * NZ, slot_cap, columns), ("pool", "tp", "zpair"))
+    same = same.reshape(experts, NZ, slot_cap, columns).transpose(1, 3, 0, 2).reshape(NZ, columns, slots)
+    before = lax.ppermute(same[: NZ // 2], GRP, turns(1))
+    after = lax.ppermute(same[NZ // 2 :], GRP, turns(-1))
     before, after, down1, down3 = lax.optimization_barrier((before, after, down_block(1), down_block(3)))
     gain = norm_gain.reshape(NX, NZ, PAIR, columns)
     gain = lax.dynamic_index_in_dim(gain, x_index, 0, keepdims=False)
@@ -247,15 +245,15 @@
     gain = jnp.stack(gain)
     place = jnp.stack([x_index, member]).astype(jnp.int32)
     partial_up = up_product(place, (same, before, after), gain, (up_block(0), up1, up_block(2), up3))
-    total_up = jnp.sum(exchange(partial_up, "grp", CROSS).astype(F32), axis=0)
+    total_up = jnp.sum(exchange(partial_up, "x").astype(F32), axis=0)
     count = slots // units
     squares = (total_up[slots : slots + count] + total_up[slots + count : slots + 2 * count]).reshape(slots, 1)
     scale = lax.rsqrt(squares / width + 1e-06)
     act = jax.nn.silu(total_up[:slots] * scale).astype(BF16)
 
     act, down_weight = lax.optimization_barrier((act, down_weight))
-    act = spread(act, 8, "grp", LINE)
-    partial_out = exchange(down_product(place, act, (down_block(0), down1, down_block(2), down3)), "grp", CROSS)
+    act = spread(act, 8, ("zpair", "member"))
+    partial_out = exchange(down_product(place, act, (down_block(0), down1, down_block(2), down3)), "x")
     expert_out = jnp.sum(partial_out.astype(F32), axis=0).astype(BF16).T
     returned = exchange(expert_out.reshape(experts, slot_cap, columns), ("pool", "tp"))
     returned = returned.reshape(slots, columns)
@@ -267,19 +265,21 @@
 
 
 def solution(mesh):
+    devices = mesh.devices.reshape(2, NX, NZ, PAIR, 8)
+    finer = Mesh(devices, ("pool",) + GRP + ("tp",), axis_types=(mesh.axis_types[0],) * 5)
     placed = (
-        P("grp", ("pool", "tp")),
-        P("grp", None, None),
-        P("grp", None, None),
-        P("grp"),
-        P(("pool", "tp"), "grp"),
-        P(("pool", "tp"), "grp"),
+        P(GRP, ("pool", "tp")),
+        P(GRP, None, None),
+        P(GRP, None, None),
+        P(GRP),
+        P(("pool", "tp"), GRP),
+        P(("pool", "tp"), GRP),
         P(),
         P(),
         P(),
-        P(("pool", "tp"), None, "grp"),
-        P(("pool", "tp"), "grp", None),
+        P(("pool", "tp"), None, GRP),
+        P(("pool", "tp"), GRP, None),
     )
     return jax.shard_map(
-        shards, mesh=mesh, in_specs=placed, out_specs=P(("pool", "tp"), "grp"), check_vma=False
+        shards, mesh=finer, in_specs=placed, out_specs=P(("pool", "tp"), GRP), check_vma=False
     )

time: 196 us -> 198 us (1.010)
  blocking collectives: 76.2 us -> 62.3 us
  local copies, waits for them, and re-layouts: 12.6 us -> 19.5 us
  starting transfers between devices: 47.8 us -> 54.6 us
    all_to_all x5 -> x4, blocking collectives: 76.2 us -> 62.3 us  [exchange(): return lax.all_to_all(value, axis, 0, 0, tiled=True)]
    all_to_all x4, waiting for transfers between devices: 20.2 us -> 26.2 us  [exchange(): return lax.all_to_all(value, axis, 0, 0, tiled=True)]
    all_to_all x4, starting transfers between devices: 22.1 us -> 26.7 us  [exchange(): return lax.all_to_all(value, axis, 0, 0, tiled=True)]
    ppermute x8, waiting for transfers between devices: 27.4 us -> 23.2 us  [the longest x3 10.5 us: down_block(): return lax.ppermute(block, GRP, moves(step, 0)) if step else block]
    slice x1 -> x5, local copies, waits for them, and re-layouts: 0.92 us -> 4.81 us  [the longest x3 3.86 us: shards(): after = lax.ppermute(same[NZ // 2:], GRP, turns(-1))]
    ppermute x8, starting transfers between devices: 25.7 us -> 28 us  [the longest x3 10.5 us: down_block(): return lax.ppermute(block, GRP, moves(step, 0)) if step else block]
  transfers between devices with their start and end apart: 12 -> 12, of which waited for: 9 -> 8; matrix products, arithmetic and copies ran while one was open for 5% -> 8% of each run, Pallas kernels for 0% -> 0%
where the time goes in v9:
time: 198 us; the launch traced here: 197 us
  blocking collectives  62.3 us (31%)
  starting transfers between devices  54.6 us (28%)
  waiting for transfers between devices  49.4 us (25%)
  local copies, waits for them, and re-layouts  19.5 us (10%)
  Pallas kernels  5.82 us (3%)
  matrix products  3.02 us (2%)
    all_to_all x4, blocking collectives, exchange(): return lax.all_to_all(value, axis, 0, 0, tiled=True)  62.3 us
    all_to_all x4, starting transfers between devices, exchange(): return lax.all_to_all(value, axis, 0, 0, tiled=True)  26.7 us
    all_to_all x4, waiting for transfers between devices, exchange(): return lax.all_to_all(value, axis, 0, 0, tiled=True)  26.2 us
    ppermute x3, starting transfers between devices, down_block(): return lax.ppermute(block, GRP, moves(step, 0)) if step else block  10.5 us
    ppermute x3, waiting for transfers between devices, down_block(): return lax.ppermute(block, GRP, moves(step, 0)) if step else block  10.5 us
    ppermute x3, starting transfers between devices, up_block(): block = lax.ppermute(block, GRP, moves(step, 0)) if step else block  10.4 us
    ppermute x3, waiting for transfers between devices, up_block(): block = lax.ppermute(block, GRP, moves(step, 0)) if step else block  8.65 us
    ppermute x1, starting transfers between devices, shards(): after = lax.ppermute(same[NZ // 2:], GRP, turns(-1))  4.28 us
  transfers between devices with their start and end apart: 12, of which 8 were waited for; matrix products, arithmetic and copies ran while one was open for 8% of the time, Pallas kernels for 0%

profile of v9, /device:TPU:8, one launch (start us, length us, event | category | flops | bytes accessed | tf_op | source)
XLA Modules:
  0.0 196.6 jit_solution(15177327414027056521)
XLA Ops:
  0.0 0.8 reshape.122
  0.8 0.7 iota_compare_fusion.4
  1.6 1.3 fusion.5
  2.9 0.2 fusion.30
  3.1 0.6 convolution_convert_fusion
  3.6 0.0 copy-start.1
  3.7 19.5 %all_to_all.40 = bf16[4,32,512]{2,1,0:T(8,128)(2,1)S(1)} all-to-all(bf16[4,32,512]{2,1,0:T(8,128)(2,1)S(1)} %broadcast_in_dim.83), channel_id=1, replica_groups=mesh['pool'=2,'x'=4,'zpair'=4,'member'=2,'tp'=8] {'zpair'}, dimensions={0} | all-to-all | bytes 262144 | tf_op jit(solution)/shard_map/all_to_all | solution.py:29
  23.2 0.1 broadcast_in_dim.85
  23.3 18.8 %all_to_all.41 = bf16[8,128,512]{2,1,0:T(8,128)(2,1)S(1)} all-to-all(bf16[8,128,512]{2,1,0:T(8,128)(2,1)S(1)} %broadcast_in_dim.85), channel_id=1, replica_groups=mesh['pool'=2,'x'=4,'zpair'=4,'member'=2,'tp'=8] {'x','member'}, dimensions={0} | all-to-all | bytes 2097152 | tf_op jit(solution)/shard_map/all_to_all | solution.py:29
  42.0 1.2 shard_map.109
  43.3 7.7 %all-to-all-start.2 = ((bf16[16,64,224]{2,1,0:T(8,128)(2,1)}), bf16[16,64,224]{2,1,0:T(8,128)(2,1)S(1)}, u32[]{:S(2)}, u32[]{:S(2)}) async-start(bf16[16,64,224]{2,1,0:T(8,128)(2,1)} %shard_map.109), calls=%async_computation.2 | async-start | bytes 1048576 | tf_op jit(solution)/shard_map/all_to_all | solution.py:29
  51.0 1.2 dynamic-slice_bitcast_fusion.5
  52.2 2.1 %collective-permute-start = (bf16[1792,128]{1,0:T(8,128)(2,1)S(1)}, bf16[1792,128]{1,0:T(8,128)(2,1)S(1)}, u32[]{:S(2)}, u32[]{:S(2)}) collective-permute-start(bf16[1792,128]{1,0:T(8,128)(2,1)S(1)} %get-tuple-element.42), channel_id=1, source_target_pairs={{0,64},{8,72},{16,80},{24,88},{32,96},{40,104},{48,112},{56,120},{... | collective-permute-start | bytes 1376264 | tf_op jit(solution)/shard_map/ppermute | solution.py:220
  54.3 5.0 %collective-permute-start.1 = (bf16[1792,128]{1,0:T(8,128)(2,1)S(1)}, bf16[1792,128]{1,0:T(8,128)(2,1)S(1)}, u32[]{:S(2)}, u32[]{:S(2)}) collective-permute-start(bf16[1792,128]{1,0:T(8,128)(2,1)S(1)} %get-tuple-element.41), channel_id=1, source_target_pairs={{0,192},{8,200},{16,208},{24,216},{32,224},{40,232},{48,240},{56,2... | collective-permute-start | bytes 1376264 | tf_op jit(solution)/shard_map/ppermute | solution.py:220
  59.3 0.1 eq.58
  59.4 0.8 fusion.21
  60.2 0.1 convolution_convert_fusion.1
  60.3 0.1 fusion.9.select
  60.4 7.5 %collective-permute-done = bf16[1792,128]{1,0:T(8,128)(2,1)S(1)} collective-permute-done((bf16[1792,128]{1,0:T(8,128)(2,1)S(1)}, bf16[1792,128]{1,0:T(8,128)(2,1)S(1)}, u32[]{:S(2)}, u32[]{:S(2)}) %collective-permute-start) | collective-permute-done | bytes 458784 | tf_op jit(solution)/shard_map/ppermute | solution.py:220
  67.9 1.2 collective-permute-done.1
  69.1 0.0 all-to-all-done.2.parts
  69.1 0.2 shard_map.110
  69.3 0.0 copy-start.3
  69.3 1.0 broadcast_in_dim.87
  70.3 8.7 %all-to-all-start.3 = ((bf16[64,24,224]{2,1,0:T(8,128)(2,1)}), bf16[64,24,224]{2,1,0:T(8,128)(2,1)}, u32[]{:S(2)}, u32[]{:S(2)}) async-start(bf16[64,24,224]{2,1,0:T(8,128)(2,1)} %bitcast.14), calls=%async_computation.3 | async-start | bytes 1572864 | tf_op jit(solution)/shard_map/all_to_all | solution.py:29
  79.1 1.0 dynamic-slice_bitcast_fusion.3
  80.1 2.2 %collective-permute-start.4 = (bf16[224,1024]{1,0:T(8,128)(2,1)}, bf16[224,1024]{1,0:T(8,128)(2,1)S(1)}, u32[]{:S(2)}, u32[]{:S(2)}) collective-permute-start(bf16[224,1024]{1,0:T(8,128)(2,1)} %get-tuple-element.40), channel_id=1, source_target_pairs={{0,64},{8,72},{16,80},{24,88},{32,96},{40,104},{48,112},{56,120},{... | collective-permute-start | bytes 1376264 | tf_op jit(solution)/shard_map/ppermute | solution.py:226
  82.3 5.3 %collective-permute-start.5 = (bf16[224,1024]{1,0:T(8,128)(2,1)}, bf16[224,1024]{1,0:T(8,128)(2,1)}, u32[]{:S(2)}, u32[]{:S(2)}) collective-permute-start(bf16[224,1024]{1,0:T(8,128)(2,1)} %get-tuple-element.39), channel_id=1, source_target_pairs={{0,192},{8,200},{16,208},{24,216},{32,224},{40,232},{48,240},{56,2... | collective-permute-start | bytes 1376264 | tf_op jit(solution)/shard_map/ppermute | solution.py:226
  87.6 2.0 %dynamic-slice_bitcast_fusion.2 = (bf16[1792,128]{1,0:T(8,128)(2,1)}, bf16[1,1792,128]{2,1,0:T(8,128)(2,1)S(1)}) fusion(bf16[1,7168,128]{2,1,0:T(8,128)(2,1)} %param.20, s32[]{:T(128)S(6)} %select_n.116, s32[]{:T(128)S(6)} %select_n.114), kind=kLoop, calls=%fused_computation.14 | loop fusion | bytes 1835016 | tf_op jit(solution)/shard_map/dynamic_slice | solution.py:219
  89.7 3.4 %collective-permute-start.6 = (bf16[1792,128]{1,0:T(8,128)(2,1)}, bf16[1792,128]{1,0:T(8,128)(2,1)S(1)}, u32[]{:S(2)}, u32[]{:S(2)}) collective-permute-start(bf16[1792,128]{1,0:T(8,128)(2,1)} %get-tuple-element.37), channel_id=1, source_target_pairs={{0,128},{8,136},{16,144},{24,152},{32,160},{40,168},{48,176},{56,1... | collective-permute-start | bytes 1376264 | tf_op jit(solution)/shard_map/ppermute | solution.py:220
  93.0 10.8 %all-to-all-done.3 = bf16[64,24,224]{2,1,0:T(8,128)(2,1)} async-done(((bf16[64,24,224]{2,1,0:T(8,128)(2,1)}), bf16[64,24,224]{2,1,0:T(8,128)(2,1)}, u32[]{:S(2)}, u32[]{:S(2)}) %all-to-all-start.3) | async-done | bytes 688160 | tf_op jit(solution)/shard_map/all_to_all | solution.py:29
  103.8 1.9 fusion.29
  105.8 0.9 copy.27
  106.7 2.8 %collective-permute-start.2 = (bf16[2,224,384]{2,1,0:T(8,128)(2,1)}, bf16[2,224,384]{2,1,0:T(8,128)(2,1)}, u32[]{:S(2)}, u32[]{:S(2)}) collective-permute-start(bf16[2,224,384]{2,1,0:T(8,128)(2,1)} %copy.27), channel_id=1, source_target_pairs={{0,8},{8,16},{16,24},{24,32},{32,40},{40,48},{48,56},{56,0},{64,72... | collective-permute-start | bytes 1032200 | tf_op jit(solution)/shard_map/ppermute | solution.py:239
  109.5 1.0 copy.28
  110.5 0.9 copy.29
  111.4 4.3 %collective-permute-start.3 = (bf16[2,224,384]{2,1,0:T(8,128)(2,1)}, bf16[2,224,384]{2,1,0:T(8,128)(2,1)}, u32[]{:S(2)}, u32[]{:S(2)}) collective-permute-start(bf16[2,224,384]{2,1,0:T(8,128)(2,1)} %copy.29), channel_id=1, source_target_pairs={{0,56},{8,0},{16,8},{24,16},{32,24},{40,32},{48,40},{56,48},{64,12... | collective-permute-start | bytes 1032200 | tf_op jit(solution)/shard_map/ppermute | solution.py:240
  115.7 0.1 reshape.129
  115.9 0.1 stack_reshape.7
  116.0 0.1 stack_reshape.6
  116.1 0.1 pad_add_fusion.place
  116.2 2.1 %copy.25 = bf16[4,224,16,24]{1,3,2,0:T(8,128)(2,1)} copy(bf16[4,224,16,24]{1,3,0,2:T(8,128)(2,1)} %bitcast.16) | data formatting | bytes 1376256 | tf_op jit(solution)/shard_map/transpose | solution.py:238
  118.3 1.5 copy.30.same
  119.8 0.9 collective-permute-done.2.before
  120.6 3.2 %collective-permute-done.3.after = bf16[2,224,384]{2,1,0:T(8,128)(2,1)} collective-permute-done((bf16[2,224,384]{2,1,0:T(8,128)(2,1)}, bf16[2,224,384]{2,1,0:T(8,128)(2,1)}, u32[]{:S(2)}, u32[]{:S(2)}) %collective-permute-start.3) | collective-permute-done | bytes 344096 | tf_op jit(solution)/shard_map/ppermute | solution.py:240
  123.9 2.1 %shard_map.111 = bf16[4,400,128]{2,1,0:T(8,128)(2,1)S(1)} custom-call(s32[2]{0:T(128)S(1)} %pad_add_fusion.place, bf16[4,224,384]{2,1,0:T(8,128)(2,1)S(1)} %copy.30.same, bf16[2,224,384]{2,1,0:T(8,128)(2,1)} %collective-permute-done.2.before, bf16[2,224,384]{2,1,0:T(8,128)(2,1)} %collective-permute-done.3.after, f32[2,896]{1,0:T(2,128)S(1)} %pad_maximum_fusion.gain, ...), custom_call_target="tpu_custom_call" | custom-call | flops 704643072 | bytes 6291456 | tf_op jit(solution)/shard_map/pallas_call | solution.py:125
  126.0 12.6 %all_to_all.42 = bf16[4,400,128]{2,1,0:T(8,128)(2,1)S(1)} all-to-all(bf16[4,400,128]{2,1,0:T(8,128)(2,1)S(1)} %shard_map.111), channel_id=1, replica_groups=mesh['pool'=2,'x'=4,'zpair'=4,'member'=2,'tp'=8] {'x'}, dimensions={0} | all-to-all | bytes 819200 | tf_op jit(solution)/shard_map/all_to_all | solution.py:29
  138.6 0.1 convert_reduce_fusion
  138.7 0.1 multiply_convert_fusion
  138.8 1.0 broadcast_in_dim.88
  139.8 4.8 %all-to-all-start.5 = ((bf16[8,384,128]{2,1,0:T(8,128)(2,1)}), bf16[8,384,128]{2,1,0:T(8,128)(2,1)S(1)}, u32[]{:S(2)}, u32[]{:S(2)}) async-start(bf16[8,384,128]{2,1,0:T(8,128)(2,1)} %broadcast_in_dim.88), calls=%async_computation.5 | async-start | bytes 1572864 | tf_op jit(solution)/shard_map/all_to_all | solution.py:29
  144.7 1.2 dynamic-slice_bitcast_fusion
  145.9 3.0 %collective-permute-start.7 = (bf16[224,1024]{1,0:T(8,128)(2,1)S(1)}, bf16[224,1024]{1,0:T(8,128)(2,1)S(1)}, u32[]{:S(2)}, u32[]{:S(2)}) collective-permute-start(bf16[224,1024]{1,0:T(8,128)(2,1)S(1)} %get-tuple-element.35), channel_id=1, source_target_pairs={{0,128},{8,136},{16,144},{24,152},{32,160},{40,168},{48,176},{56,1... | collective-permute-start | bytes 1376264 | tf_op jit(solution)/shard_map/ppermute | solution.py:226
  148.9 10.5 %collective-permute-done.7.block2 = bf16[224,1024]{1,0:T(8,128)(2,1)S(1)} collective-permute-done((bf16[224,1024]{1,0:T(8,128)(2,1)S(1)}, bf16[224,1024]{1,0:T(8,128)(2,1)S(1)}, u32[]{:S(2)}, u32[]{:S(2)}) %collective-permute-start.7) | collective-permute-done | bytes 458784 | tf_op jit(solution)/shard_map/ppermute | solution.py:226
  159.4 6.6 %all-to-all-done.5.act = bf16[8,384,128]{2,1,0:T(8,128)(2,1)S(1)} async-done(((bf16[8,384,128]{2,1,0:T(8,128)(2,1)}), bf16[8,384,128]{2,1,0:T(8,128)(2,1)S(1)}, u32[]{:S(2)}, u32[]{:S(2)}) %all-to-all-start.5) | async-done | bytes 786464 | tf_op jit(solution)/shard_map/all_to_all | solution.py:29
  165.9 2.2 %shard_map.112 = bf16[4,224,384]{2,1,0:T(8,128)(2,1)S(1)} custom-call(s32[2]{0:T(128)S(1)} %pad_add_fusion.place, bf16[8,384,128]{2,1,0:T(8,128)(2,1)S(1)} %all-to-all-done.5.act, bf16[224,1024]{1,0:T(8,128)(2,1)S(1)} %get-tuple-element.36.block0, bf16[224,1024]{1,0:T(8,128)(2,1)S(1)} %collective-permute-done.4.block1, ...), custom_call_target="tpu_custom_call" | custom-call | flops 704643072 | bytes 5242880 | tf_op jit(solution)/shard_map/pallas_call | solution.py:153
  168.2 11.4 %all_to_all.43 = bf16[4,224,384]{2,1,0:T(8,128)(2,1)S(1)} all-to-all(bf16[4,224,384]{2,1,0:T(8,128)(2,1)S(1)} %shard_map.112), channel_id=1, replica_groups=mesh['pool'=2,'x'=4,'zpair'=4,'member'=2,'tp'=8] {'x'}, dimensions={0} | all-to-all | bytes 1376256 | tf_op jit(solution)/shard_map/all_to_all | solution.py:29
  179.6 0.1 reduce_sum.42
  179.7 0.8 copy.31
  180.5 5.4 %all-to-all-start.7 = ((bf16[16,24,224]{2,1,0:T(8,128)(2,1)}), bf16[16,24,224]{2,1,0:T(8,128)(2,1)S(1)}, u32[]{:S(2)}, u32[]{:S(2)}) async-start(bf16[16,24,224]{2,1,0:T(8,128)(2,1)} %bitcast.30), calls=%async_computation.7 | async-start | bytes 393216 | tf_op jit(solution)/shard_map/all_to_all | solution.py:29
  185.9 0.8 fusion.22
  186.6 8.9 %all-to-all-done.7 = bf16[16,24,224]{2,1,0:T(8,128)(2,1)S(1)} async-done(((bf16[16,24,224]{2,1,0:T(8,128)(2,1)}), bf16[16,24,224]{2,1,0:T(8,128)(2,1)S(1)}, u32[]{:S(2)}, u32[]{:S(2)}) %all-to-all-start.7) | async-done | bytes 172064 | tf_op jit(solution)/shard_map/all_to_all | solution.py:29
  195.5 0.2 convolution_bitcast_fusion.1
  195.7 0.8 fusion.2
  (20 shorter events, 0.2 us)
Async XLA Ops:
  0.0 3.1 %copy-start = (bf16[32,32,256]{2,1,0:T(8,128)(2,1)S(1)}, bf16[32,32,256]{2,1,0:T(8,128)(2,1)}, u32[]{:S(2)}) copy-start(bf16[32,32,256]{2,1,0:T(8,128)(2,1)} %param.13) | copy-start | bytes 1572868
  3.6 38.4 %copy-start.1 = (bf16[512,224]{0,1:T(8,128)(2,1)S(1)}, bf16[512,224]{0,1:T(8,128)(2,1)}, u32[]{:S(2)}) copy-start(bf16[512,224]{0,1:T(8,128)(2,1)} %param.15) | copy-start | bytes 688132
  43.3 25.8 %copy-start.2 = (bf16[64,224]{1,0:T(8,128)(2,1)S(1)}, bf16[64,224]{1,0:T(8,128)(2,1)}, u32[]{:S(2)}) copy-start(bf16[64,224]{1,0:T(8,128)(2,1)} %residual.1) | copy-start | bytes 86020
  43.3 25.8 %all-to-all-start.2 = ((bf16[16,64,224]{2,1,0:T(8,128)(2,1)}), bf16[16,64,224]{2,1,0:T(8,128)(2,1)S(1)}, u32[]{:S(2)}, u32[]{:S(2)}) async-start(bf16[16,64,224]{2,1,0:T(8,128)(2,1)} %shard_map.109), calls=%async_computation.2 | async-start | bytes 1048576 | tf_op jit(solution)/shard_map/all_to_all | solution.py:29
  52.2 15.7 %collective-permute-start = (bf16[1792,128]{1,0:T(8,128)(2,1)S(1)}, bf16[1792,128]{1,0:T(8,128)(2,1)S(1)}, u32[]{:S(2)}, u32[]{:S(2)}) collective-permute-start(bf16[1792,128]{1,0:T(8,128)(2,1)S(1)} %get-tuple-element.42), channel_id=1, source_target_pairs={{0,64},{8,72},{16,80},{24,88},{32,96},{40,104},{48,112},{56,120},{... | collective-permute-start | bytes 1376264 | tf_op jit(solution)/shard_map/ppermute | solution.py:220
  54.3 14.8 %collective-permute-start.1 = (bf16[1792,128]{1,0:T(8,128)(2,1)S(1)}, bf16[1792,128]{1,0:T(8,128)(2,1)S(1)}, u32[]{:S(2)}, u32[]{:S(2)}) collective-permute-start(bf16[1792,128]{1,0:T(8,128)(2,1)S(1)} %get-tuple-element.41), channel_id=1, source_target_pairs={{0,192},{8,200},{16,208},{24,216},{32,224},{40,232},{48,240},{56,2... | collective-permute-start | bytes 1376264 | tf_op jit(solution)/shard_map/ppermute | solution.py:220
  69.3 9.8 %copy-start.3 = (bf16[1,224,4096]{2,1,0:T(8,128)(2,1)S(1)}, bf16[1,224,4096]{2,1,0:T(8,128)(2,1)}, u32[]{:S(2)}) copy-start(bf16[1,224,4096]{2,1,0:T(8,128)(2,1)} %param.21) | copy-start | bytes 5505028
  70.3 33.5 %all-to-all-start.3 = ((bf16[64,24,224]{2,1,0:T(8,128)(2,1)}), bf16[64,24,224]{2,1,0:T(8,128)(2,1)}, u32[]{:S(2)}, u32[]{:S(2)}) async-start(bf16[64,24,224]{2,1,0:T(8,128)(2,1)} %bitcast.14), calls=%async_computation.3 | async-start | bytes 1572864 | tf_op jit(solution)/shard_map/all_to_all | solution.py:29
  80.1 39.6 %collective-permute-start.4 = (bf16[224,1024]{1,0:T(8,128)(2,1)}, bf16[224,1024]{1,0:T(8,128)(2,1)S(1)}, u32[]{:S(2)}, u32[]{:S(2)}) collective-permute-start(bf16[224,1024]{1,0:T(8,128)(2,1)} %get-tuple-element.40), channel_id=1, source_target_pairs={{0,64},{8,72},{16,80},{24,88},{32,96},{40,104},{48,112},{56,120},{... | collective-permute-start | bytes 1376264 | tf_op jit(solution)/shard_map/ppermute | solution.py:226
  82.3 37.4 %collective-permute-start.5 = (bf16[224,1024]{1,0:T(8,128)(2,1)}, bf16[224,1024]{1,0:T(8,128)(2,1)}, u32[]{:S(2)}, u32[]{:S(2)}) collective-permute-start(bf16[224,1024]{1,0:T(8,128)(2,1)} %get-tuple-element.39), channel_id=1, source_target_pairs={{0,192},{8,200},{16,208},{24,216},{32,224},{40,232},{48,240},{56,2... | collective-permute-start | bytes 1376264 | tf_op jit(solution)/shard_map/ppermute | solution.py:226
  89.7 34.2 %collective-permute-start.6 = (bf16[1792,128]{1,0:T(8,128)(2,1)}, bf16[1792,128]{1,0:T(8,128)(2,1)S(1)}, u32[]{:S(2)}, u32[]{:S(2)}) collective-permute-start(bf16[1792,128]{1,0:T(8,128)(2,1)} %get-tuple-element.37), channel_id=1, source_target_pairs={{0,128},{8,136},{16,144},{24,152},{32,160},{40,168},{48,176},{56,1... | collective-permute-start | bytes 1376264 | tf_op jit(solution)/shard_map/ppermute | solution.py:220
  105.8 10.0 %copy-start.4 = (f32[7168]{0:T(1024)S(1)}, f32[7168]{0:T(1024)}, u32[]{:S(2)}) copy-start(f32[7168]{0:T(1024)} %param.17) | copy-start | bytes 86020
  106.7 13.9 %collective-permute-start.2 = (bf16[2,224,384]{2,1,0:T(8,128)(2,1)}, bf16[2,224,384]{2,1,0:T(8,128)(2,1)}, u32[]{:S(2)}, u32[]{:S(2)}) collective-permute-start(bf16[2,224,384]{2,1,0:T(8,128)(2,1)} %copy.27), channel_id=1, source_target_pairs={{0,8},{8,16},{16,24},{24,32},{32,40},{40,48},{48,56},{56,0},{64,72... | collective-permute-start | bytes 1032200 | tf_op jit(solution)/shard_map/ppermute | solution.py:239
  111.4 12.4 %collective-permute-start.3 = (bf16[2,224,384]{2,1,0:T(8,128)(2,1)}, bf16[2,224,384]{2,1,0:T(8,128)(2,1)}, u32[]{:S(2)}, u32[]{:S(2)}) collective-permute-start(bf16[2,224,384]{2,1,0:T(8,128)(2,1)} %copy.29), channel_id=1, source_target_pairs={{0,56},{8,0},{16,8},{24,16},{32,24},{40,32},{48,40},{56,48},{64,12... | collective-permute-start | bytes 1032200 | tf_op jit(solution)/shard_map/ppermute | solution.py:240
  139.8 26.1 %all-to-all-start.5 = ((bf16[8,384,128]{2,1,0:T(8,128)(2,1)}), bf16[8,384,128]{2,1,0:T(8,128)(2,1)S(1)}, u32[]{:S(2)}, u32[]{:S(2)}) async-start(bf16[8,384,128]{2,1,0:T(8,128)(2,1)} %broadcast_in_dim.88), calls=%async_computation.5 | async-start | bytes 1572864 | tf_op jit(solution)/shard_map/all_to_all | solution.py:29
  145.9 13.5 %collective-permute-start.7 = (bf16[224,1024]{1,0:T(8,128)(2,1)S(1)}, bf16[224,1024]{1,0:T(8,128)(2,1)S(1)}, u32[]{:S(2)}, u32[]{:S(2)}) collective-permute-start(bf16[224,1024]{1,0:T(8,128)(2,1)S(1)} %get-tuple-element.35), channel_id=1, source_target_pairs={{0,128},{8,136},{16,144},{24,152},{32,160},{40,168},{48,176},{56,1... | collective-permute-start | bytes 1376264 | tf_op jit(solution)/shard_map/ppermute | solution.py:226
  180.5 15.0 %all-to-all-start.7 = ((bf16[16,24,224]{2,1,0:T(8,128)(2,1)}), bf16[16,24,224]{2,1,0:T(8,128)(2,1)S(1)}, u32[]{:S(2)}, u32[]{:S(2)}) async-start(bf16[16,24,224]{2,1,0:T(8,128)(2,1)} %bitcast.30), calls=%async_computation.7 | async-start | bytes 393216 | tf_op jit(solution)/shard_map/all_to_all | solution.py:29

commit v10 on v9

--- a/solution.py
+++ b/solution.py
@@ -91,26 +91,33 @@
 
 def up_kernel(place, same, before, after, gain, block0, block1, block2, block3, out):
     x_index, member = place[0], place[1]
-    slots, units = same.shape[2], out.shape[2]
-    depth = NZ * same.shape[1]
-    other = jnp.concatenate([r[...].reshape(depth // 2, slots) for r in (before, after)], axis=0)
+    slots, units = same.shape[1], out.shape[2]
+    ones = jnp.ones((16, same.shape[2]), BF16)
+    dims = (((1,), (1,)), ((), ()))
+    rows = [same[z] for z in range(NZ)] + [r[z] for r in (before, after) for z in range(NZ // 2)]
     normed, squares = [], 0.0
-    for i, value in enumerate((same[...].reshape(depth, slots), other)):
-        squares += jnp.sum(jnp.square(value.astype(F32)), axis=0, keepdims=True)
-        normed.append((value.T.astype(F32) * gain[i : i + 1, :]).astype(BF16))
+    for i, value in enumerate(rows):
+        value = value.astype(F32)
+        normed.append((value * gain[i : i + 1, :]).astype(BF16))
+        square = value * value
+        high = square.astype(BF16)
+        low = (square - high.astype(F32)).astype(BF16)
+        squares += lax.dot_general(ones, high, dims, preferred_element_type=F32)
+        squares += lax.dot_general(ones, low, dims, preferred_element_type=F32)
     row = lax.broadcasted_iota(jnp.int32, (16, units), 0)
     count = slots // units
     tail = jnp.zeros((16, units), F32)
     for i in range(count):
-        part = jnp.broadcast_to(squares[:, i * units : (i + 1) * units], (16, units))
+        part = squares[:, i * units : (i + 1) * units]
         high = part.astype(BF16).astype(F32)
         tail = jnp.where(row == i, high, tail)
         tail = jnp.where(row == count + i, part - high, tail)
     tail = tail.astype(BF16)
     for step, block in ((0, (block0, block1)), (2, (block2, block3))):
         total = 0.0
-        for value, which in zip(normed, (member, 1 - member)):
-            weight = jnp.concatenate([b[:, which].reshape(depth, units) for b in block], axis=1)
+        for i, value in enumerate(normed):
+            which = member if i < NZ else 1 - member
+            weight = jnp.concatenate([b[i % NZ, which] for b in block], axis=1)
             total += jnp.dot(value, weight, preferred_element_type=F32)
         total = total.astype(BF16)
         for i in range(2):
@@ -120,7 +127,7 @@
 
 
 def up_product(place, rows, gain, blocks):
-    count, columns, slots = rows[0].shape
+    count, slots, columns = rows[0].shape
     units = blocks[0].shape[3]
     return pl.pallas_call(
         up_kernel,
@@ -233,16 +240,16 @@
     projected, up1, up3 = lax.optimization_barrier((projected, up_block(1), up_block(3)))
     slot_rows = head_sum(projected, residual, select)
     slot_rows, up_weight, down_weight = lax.optimization_barrier((slot_rows, up_weight, down_weight))
-    same = jnp.broadcast_to(slot_rows.reshape(experts, 1, slot_cap, columns), (experts, NZ, slot_cap, columns))
-    same = exchange(same.reshape(experts * NZ, slot_cap, columns), ("pool", "tp", "zpair"))
-    same = same.reshape(experts, NZ, slot_cap, columns).transpose(1, 3, 0, 2).reshape(NZ, columns, slots)
+    same = jnp.broadcast_to(slot_rows.reshape(1, experts, slot_cap, columns), (NZ, experts, slot_cap, columns))
+    same = exchange(same.reshape(NZ * experts, slot_cap, columns), ("zpair", "pool", "tp"))
+    same = same.reshape(NZ, slots, columns)
     before = lax.ppermute(same[: NZ // 2], GRP, turns(1))
     after = lax.ppermute(same[NZ // 2 :], GRP, turns(-1))
     before, after, down1, down3 = lax.optimization_barrier((before, after, down_block(1), down_block(3)))
     gain = norm_gain.reshape(NX, NZ, PAIR, columns)
     gain = lax.dynamic_index_in_dim(gain, x_index, 0, keepdims=False)
-    gain = [lax.dynamic_index_in_dim(gain, m, 1, keepdims=False).reshape(-1) for m in (member, 1 - member)]
-    gain = jnp.stack(gain)
+    gain = [lax.dynamic_index_in_dim(gain, m, 1, keepdims=False) for m in (member, 1 - member)]
+    gain = jnp.concatenate(gain)
     place = jnp.stack([x_index, member]).astype(jnp.int32)
     partial_up = up_product(place, (same, before, after), gain, (up_block(0), up1, up_block(2), up3))
     total_up = jnp.sum(exchange(partial_up, "x").astype(F32), axis=0)

time: 198 us -> 197 us (level)
  local copies, waits for them, and re-layouts: 19.5 us -> 11.1 us
  waiting for transfers between devices: 49.4 us -> 56.5 us
  blocking collectives: 62.3 us -> 59.6 us
  starting transfers between devices: 54.6 us -> 57.3 us
    ppermute x1, waiting for transfers between devices: 0.85 us -> 6.5 us  [shards(): before = lax.ppermute(same[:NZ // 2], GRP, turns(1))]
    all_to_all x4, starting transfers between devices: 26.7 us -> 32.2 us  [exchange(): return lax.all_to_all(value, axis, 0, 0, tiled=True)]
    slice x3 -> x1, local copies, waits for them, and re-layouts: 3.86 us -> 0.05 us  [shards(): after = lax.ppermute(same[NZ // 2:], GRP, turns(-1))]
    all_to_all x4, blocking collectives: 62.3 us -> 59.6 us  [exchange(): return lax.all_to_all(value, axis, 0, 0, tiled=True)]
    ppermute x3, waiting for transfers between devices: 8.65 us -> 11.1 us  [up_block(): block = lax.ppermute(block, GRP, moves(step, 0)) if step else block]
    ppermute x3, starting transfers between devices: 10.4 us -> 8.04 us  [up_block(): block = lax.ppermute(block, GRP, moves(step, 0)) if step else block]
    transpose x1 -> x0, local copies, waits for them, and re-layouts: 2.09 us -> none  [shards(): same.reshape(experts, NZ, slot_cap, columns).transpose(1, 3, 0, 2)]
  transfers between devices with their start and end apart: 12 -> 12, of which waited for: 8 -> 8; matrix products, arithmetic and copies ran while one was open for 8% -> 4% of each run, Pallas kernels for 0% -> 0%
where the time goes in v10:
time: 197 us; the launch traced here: 196 us
  blocking collectives  59.6 us (30%)
  starting transfers between devices  57.3 us (29%)
  waiting for transfers between devices  56.5 us (29%)
  local copies, waits for them, and re-layouts  11.1 us (6%)
  Pallas kernels  6.55 us (3%)
  matrix products  3.03 us (2%)
    all_to_all x4, blocking collectives, exchange(): return lax.all_to_all(value, axis, 0, 0, tiled=True)  59.6 us
    all_to_all x4, starting transfers between devices, exchange(): return lax.all_to_all(value, axis, 0, 0, tiled=True)  32.2 us
    all_to_all x4, waiting for transfers between devices, exchange(): return lax.all_to_all(value, axis, 0, 0, tiled=True)  27 us
    ppermute x3, waiting for transfers between devices, up_block(): block = lax.ppermute(block, GRP, moves(step, 0)) if step else block  11.1 us
    ppermute x3, starting transfers between devices, down_block(): return lax.ppermute(block, GRP, moves(step, 0)) if step else block  10.1 us
    ppermute x3, waiting for transfers between devices, down_block(): return lax.ppermute(block, GRP, moves(step, 0)) if step else block  9.6 us
    ppermute x3, starting transfers between devices, up_block(): block = lax.ppermute(block, GRP, moves(step, 0)) if step else block  8.04 us
    ppermute x1, waiting for transfers between devices, shards(): before = lax.ppermute(same[:NZ // 2], GRP, turns(1))  6.5 us
  transfers between devices with their start and end apart: 12, of which 8 were waited for; matrix products, arithmetic and copies ran while one was open for 4% of the time, Pallas kernels for 0%

profile of v10, /device:TPU:8, one launch (start us, length us, event | category | flops | bytes accessed | tf_op | source)
XLA Modules:
  0.0 195.9 jit_solution(10167362363535316187)
XLA Ops:
  0.0 0.0 copy-start
  0.0 0.8 reshape.117
  0.8 0.7 iota_compare_fusion.4
  1.6 1.3 fusion.5
  2.9 0.2 fusion.30
  3.1 0.6 convolution_convert_fusion
  3.6 0.0 copy-start.1
  3.7 19.5 %all_to_all.40 = bf16[4,32,512]{2,1,0:T(8,128)(2,1)S(1)} all-to-all(bf16[4,32,512]{2,1,0:T(8,128)(2,1)S(1)} %broadcast_in_dim.83), channel_id=1, replica_groups=mesh['pool'=2,'x'=4,'zpair'=4,'member'=2,'tp'=8] {'zpair'}, dimensions={0} | all-to-all | bytes 262144 | tf_op jit(solution)/shard_map/all_to_all | solution.py:29
  23.2 0.1 broadcast_in_dim.85
  23.3 18.8 %all_to_all.41 = bf16[8,128,512]{2,1,0:T(8,128)(2,1)S(1)} all-to-all(bf16[8,128,512]{2,1,0:T(8,128)(2,1)S(1)} %broadcast_in_dim.85), channel_id=1, replica_groups=mesh['pool'=2,'x'=4,'zpair'=4,'member'=2,'tp'=8] {'x','member'}, dimensions={0} | all-to-all | bytes 2097152 | tf_op jit(solution)/shard_map/all_to_all | solution.py:29
  42.0 0.0 copy-done.1
  42.0 1.3 shard_map.109
  43.3 7.7 %all-to-all-start.2 = ((bf16[16,64,224]{2,1,0:T(8,128)(2,1)}), bf16[16,64,224]{2,1,0:T(8,128)(2,1)S(1)}, u32[]{:S(2)}, u32[]{:S(2)}) async-start(bf16[16,64,224]{2,1,0:T(8,128)(2,1)} %shard_map.109), calls=%async_computation.2 | async-start | bytes 1048576 | tf_op jit(solution)/shard_map/all_to_all | solution.py:29
  51.0 1.2 dynamic-slice_bitcast_fusion.5
  52.2 2.7 %collective-permute-start.1 = (bf16[1792,128]{1,0:T(8,128)(2,1)S(1)}, bf16[1792,128]{1,0:T(8,128)(2,1)S(1)}, u32[]{:S(2)}, u32[]{:S(2)}) collective-permute-start(bf16[1792,128]{1,0:T(8,128)(2,1)S(1)} %get-tuple-element.39), channel_id=1, source_target_pairs={{0,192},{8,200},{16,208},{24,216},{32,224},{40,232},{48,240},{56,2... | collective-permute-start | bytes 1376264 | tf_op jit(solution)/shard_map/ppermute | solution.py:227
  54.9 3.2 %collective-permute-start = (bf16[1792,128]{1,0:T(8,128)(2,1)S(1)}, bf16[1792,128]{1,0:T(8,128)(2,1)S(1)}, u32[]{:S(2)}, u32[]{:S(2)}) collective-permute-start(bf16[1792,128]{1,0:T(8,128)(2,1)S(1)} %get-tuple-element.40), channel_id=1, source_target_pairs={{0,64},{8,72},{16,80},{24,88},{32,96},{40,104},{48,112},{56,120},{... | collective-permute-start | bytes 1376264 | tf_op jit(solution)/shard_map/ppermute | solution.py:227
  58.1 0.0 copy-start.4
  58.1 0.1 eq.58
  58.2 0.8 fusion.21
  59.0 0.1 convolution_convert_fusion.1
  59.1 0.1 fusion.9.select
  59.2 7.5 %collective-permute-done.1 = bf16[1792,128]{1,0:T(8,128)(2,1)S(1)} collective-permute-done((bf16[1792,128]{1,0:T(8,128)(2,1)S(1)}, bf16[1792,128]{1,0:T(8,128)(2,1)S(1)}, u32[]{:S(2)}, u32[]{:S(2)}) %collective-permute-start.1) | collective-permute-done | bytes 458784 | tf_op jit(solution)/shard_map/ppermute | solution.py:227
  66.7 3.6 %collective-permute-done = bf16[1792,128]{1,0:T(8,128)(2,1)S(1)} collective-permute-done((bf16[1792,128]{1,0:T(8,128)(2,1)S(1)}, bf16[1792,128]{1,0:T(8,128)(2,1)S(1)}, u32[]{:S(2)}, u32[]{:S(2)}) %collective-permute-start) | collective-permute-done | bytes 458784 | tf_op jit(solution)/shard_map/ppermute | solution.py:227
  70.3 0.0 all-to-all-done.2.parts
  70.3 0.0 copy-done.2
  70.3 0.2 shard_map.110
  70.6 0.9 broadcast_in_dim.87
  71.5 8.6 %all-to-all-start.3 = ((bf16[64,24,224]{2,1,0:T(8,128)(2,1)}), bf16[64,24,224]{2,1,0:T(8,128)(2,1)S(1)}, u32[]{:S(2)}, u32[]{:S(2)}) async-start(bf16[64,24,224]{2,1,0:T(8,128)(2,1)} %bitcast.14), calls=%async_computation.3 | async-start | bytes 1572864 | tf_op jit(solution)/shard_map/all_to_all | solution.py:29
  80.2 0.1 reshape.123
  80.4 0.0 copy-start.3
  80.4 2.1 %dynamic-slice_bitcast_fusion.2 = (bf16[1792,128]{1,0:T(8,128)(2,1)}, bf16[1,1792,128]{2,1,0:T(8,128)(2,1)S(1)}) fusion(bf16[1,7168,128]{2,1,0:T(8,128)(2,1)} %param.20, s32[]{:T(128)S(6)} %select_n.116, s32[]{:T(128)S(6)} %select_n.114), kind=kLoop, calls=%fused_computation.14 | loop fusion | bytes 1835016 | tf_op jit(solution)/shard_map/dynamic_slice | solution.py:226
  82.5 2.2 %collective-permute-start.6 = (bf16[1792,128]{1,0:T(8,128)(2,1)}, bf16[1792,128]{1,0:T(8,128)(2,1)}, u32[]{:S(2)}, u32[]{:S(2)}) collective-permute-start(bf16[1792,128]{1,0:T(8,128)(2,1)} %get-tuple-element.35), channel_id=1, source_target_pairs={{0,128},{8,136},{16,144},{24,152},{32,160},{40,168},{48,176},{56,1... | collective-permute-start | bytes 1376264 | tf_op jit(solution)/shard_map/ppermute | solution.py:227
  84.8 1.0 dynamic-slice_bitcast_fusion.3
  85.8 2.1 %collective-permute-start.4 = (bf16[224,1024]{1,0:T(8,128)(2,1)}, bf16[224,1024]{1,0:T(8,128)(2,1)S(1)}, u32[]{:S(2)}, u32[]{:S(2)}) collective-permute-start(bf16[224,1024]{1,0:T(8,128)(2,1)} %get-tuple-element.38), channel_id=1, source_target_pairs={{0,64},{8,72},{16,80},{24,88},{32,96},{40,104},{48,112},{56,120},{... | collective-permute-start | bytes 1376264 | tf_op jit(solution)/shard_map/ppermute | solution.py:233
  87.9 5.0 %collective-permute-start.5 = (bf16[224,1024]{1,0:T(8,128)(2,1)}, bf16[224,1024]{1,0:T(8,128)(2,1)}, u32[]{:S(2)}, u32[]{:S(2)}) collective-permute-start(bf16[224,1024]{1,0:T(8,128)(2,1)} %get-tuple-element.37), channel_id=1, source_target_pairs={{0,192},{8,200},{16,208},{24,216},{32,224},{40,232},{48,240},{56,2... | collective-permute-start | bytes 1376264 | tf_op jit(solution)/shard_map/ppermute | solution.py:233
  92.9 11.6 %all-to-all-done.3 = bf16[64,24,224]{2,1,0:T(8,128)(2,1)S(1)} async-done(((bf16[64,24,224]{2,1,0:T(8,128)(2,1)}), bf16[64,24,224]{2,1,0:T(8,128)(2,1)S(1)}, u32[]{:S(2)}, u32[]{:S(2)}) %all-to-all-start.3) | async-done | bytes 688160 | tf_op jit(solution)/shard_map/all_to_all | solution.py:29
  104.5 0.1 fusion.29
  104.5 3.3 %collective-permute-start.2 = (bf16[2,384,224]{2,1,0:T(8,128)(2,1)S(1)}, bf16[2,384,224]{2,1,0:T(8,128)(2,1)S(1)}, u32[]{:S(2)}, u32[]{:S(2)}) collective-permute-start(bf16[2,384,224]{2,1,0:T(8,128)(2,1)S(1)} %bitcast.76), channel_id=1, source_target_pairs={{0,8},{8,16},{16,24},{24,32},{32,40},{40,48},{48,56},{56,0},{64,72... | collective-permute-start | bytes 1032200 | tf_op jit(solution)/shard_map/ppermute | solution.py:246
  107.8 3.8 %collective-permute-start.3 = (bf16[2,384,224]{2,1,0:T(8,128)(2,1)S(1)}, bf16[2,384,224]{2,1,0:T(8,128)(2,1)S(1)}, u32[]{:S(2)}, u32[]{:S(2)}) collective-permute-start(bf16[2,384,224]{2,1,0:T(8,128)(2,1)S(1)} %bitcast.75), channel_id=1, source_target_pairs={{0,56},{8,0},{16,8},{24,16},{32,24},{40,32},{48,40},{56,48},{64,12... | collective-permute-start | bytes 1032200 | tf_op jit(solution)/shard_map/ppermute | solution.py:247
  111.6 0.1 pad_add_fusion.place
  111.7 0.0 collective-permute-done.4.block1
  111.7 0.0 collective-permute-done.5.block3
  111.7 6.5 %collective-permute-done.2.before = bf16[2,384,224]{2,1,0:T(8,128)(2,1)S(1)} collective-permute-done((bf16[2,384,224]{2,1,0:T(8,128)(2,1)S(1)}, bf16[2,384,224]{2,1,0:T(8,128)(2,1)S(1)}, u32[]{:S(2)}, u32[]{:S(2)}) %collective-permute-start.2) | collective-permute-done | bytes 344096 | tf_op jit(solution)/shard_map/ppermute | solution.py:246
  118.2 2.3 %collective-permute-done.3.after = bf16[2,384,224]{2,1,0:T(8,128)(2,1)S(1)} collective-permute-done((bf16[2,384,224]{2,1,0:T(8,128)(2,1)S(1)}, bf16[2,384,224]{2,1,0:T(8,128)(2,1)S(1)}, u32[]{:S(2)}, u32[]{:S(2)}) %collective-permute-start.3) | collective-permute-done | bytes 344096 | tf_op jit(solution)/shard_map/ppermute | solution.py:247
  120.5 0.0 collective-permute-done.6
  120.5 2.8 %shard_map.111 = bf16[4,400,128]{2,1,0:T(8,128)(2,1)S(1)} custom-call(s32[2]{0:T(128)S(1)} %pad_add_fusion.place, bf16[4,384,224]{2,1,0:T(8,128)(2,1)S(1)} %bitcast.66, bf16[2,384,224]{2,1,0:T(8,128)(2,1)S(1)} %collective-permute-done.2.before, bf16[2,384,224]{2,1,0:T(8,128)(2,1)S(1)} %collective-permute-done.3.after, f32[8,224]{1,0:T(8,128)S(1)} %pad_maximum_fusion.gain, ...), custom_call_target="tpu_custom_call" | custom-call | flops 704643072 | bytes 6291456 | tf_op jit(solution)/shard_map/pallas_call | solution.py:132
  123.3 9.8 %all_to_all.42 = bf16[4,400,128]{2,1,0:T(8,128)(2,1)S(1)} all-to-all(bf16[4,400,128]{2,1,0:T(8,128)(2,1)S(1)} %shard_map.111), channel_id=1, replica_groups=mesh['pool'=2,'x'=4,'zpair'=4,'member'=2,'tp'=8] {'x'}, dimensions={0} | all-to-all | bytes 819200 | tf_op jit(solution)/shard_map/all_to_all | solution.py:29
  133.2 0.1 convert_reduce_fusion
  133.2 0.1 multiply_convert_fusion
  133.4 1.0 broadcast_in_dim.88
  134.4 4.6 %all-to-all-start.5 = ((bf16[8,384,128]{2,1,0:T(8,128)(2,1)}), bf16[8,384,128]{2,1,0:T(8,128)(2,1)S(1)}, u32[]{:S(2)}, u32[]{:S(2)}) async-start(bf16[8,384,128]{2,1,0:T(8,128)(2,1)} %broadcast_in_dim.88), calls=%async_computation.5 | async-start | bytes 1572864 | tf_op jit(solution)/shard_map/all_to_all | solution.py:29
  138.9 1.2 dynamic-slice_bitcast_fusion
  140.2 3.0 %collective-permute-start.7 = (bf16[224,1024]{1,0:T(8,128)(2,1)S(1)}, bf16[224,1024]{1,0:T(8,128)(2,1)S(1)}, u32[]{:S(2)}, u32[]{:S(2)}) collective-permute-start(bf16[224,1024]{1,0:T(8,128)(2,1)S(1)} %get-tuple-element.33), channel_id=1, source_target_pairs={{0,128},{8,136},{16,144},{24,152},{32,160},{40,168},{48,176},{56,1... | collective-permute-start | bytes 1376264 | tf_op jit(solution)/shard_map/ppermute | solution.py:233
  143.2 9.6 %collective-permute-done.7.block2 = bf16[224,1024]{1,0:T(8,128)(2,1)S(1)} collective-permute-done((bf16[224,1024]{1,0:T(8,128)(2,1)S(1)}, bf16[224,1024]{1,0:T(8,128)(2,1)S(1)}, u32[]{:S(2)}, u32[]{:S(2)}) %collective-permute-start.7) | collective-permute-done | bytes 458784 | tf_op jit(solution)/shard_map/ppermute | solution.py:233
  152.8 6.6 %all-to-all-done.5.act = bf16[8,384,128]{2,1,0:T(8,128)(2,1)S(1)} async-done(((bf16[8,384,128]{2,1,0:T(8,128)(2,1)}), bf16[8,384,128]{2,1,0:T(8,128)(2,1)S(1)}, u32[]{:S(2)}, u32[]{:S(2)}) %all-to-all-start.5) | async-done | bytes 786464 | tf_op jit(solution)/shard_map/all_to_all | solution.py:29
  159.4 2.2 %shard_map.112 = bf16[4,224,384]{2,1,0:T(8,128)(2,1)S(1)} custom-call(s32[2]{0:T(128)S(1)} %pad_add_fusion.place, bf16[8,384,128]{2,1,0:T(8,128)(2,1)S(1)} %all-to-all-done.5.act, bf16[224,1024]{1,0:T(8,128)(2,1)S(1)} %get-tuple-element.34.block0, bf16[224,1024]{1,0:T(8,128)(2,1)S(1)} %collective-permute-done.4.block1, ...), custom_call_target="tpu_custom_call" | custom-call | flops 704643072 | bytes 5242880 | tf_op jit(solution)/shard_map/pallas_call | solution.py:160
  161.6 11.5 %all_to_all.43 = bf16[4,224,384]{2,1,0:T(8,128)(2,1)S(1)} all-to-all(bf16[4,224,384]{2,1,0:T(8,128)(2,1)S(1)} %shard_map.112), channel_id=1, replica_groups=mesh['pool'=2,'x'=4,'zpair'=4,'member'=2,'tp'=8] {'x'}, dimensions={0} | all-to-all | bytes 1376256 | tf_op jit(solution)/shard_map/all_to_all | solution.py:29
  173.0 0.1 reduce_sum.42
  173.2 0.8 copy.13
  174.0 11.3 %all-to-all-start.7 = ((bf16[16,24,224]{2,1,0:T(8,128)(2,1)}), bf16[16,24,224]{2,1,0:T(8,128)(2,1)S(1)}, u32[]{:S(2)}, u32[]{:S(2)}) async-start(bf16[16,24,224]{2,1,0:T(8,128)(2,1)} %bitcast.27), calls=%async_computation.7 | async-start | bytes 393216 | tf_op jit(solution)/shard_map/all_to_all | solution.py:29
  185.2 0.8 fusion.22
  186.0 8.8 %all-to-all-done.7 = bf16[16,24,224]{2,1,0:T(8,128)(2,1)S(1)} async-done(((bf16[16,24,224]{2,1,0:T(8,128)(2,1)}), bf16[16,24,224]{2,1,0:T(8,128)(2,1)S(1)}, u32[]{:S(2)}, u32[]{:S(2)}) %all-to-all-start.7) | async-done | bytes 172064 | tf_op jit(solution)/shard_map/all_to_all | solution.py:29
  194.8 0.2 convolution_bitcast_fusion.1
  195.1 0.8 fusion.2
  (13 shorter events, 0.1 us)
Async XLA Ops:
  0.0 3.1 %copy-start = (bf16[32,32,256]{2,1,0:T(8,128)(2,1)S(1)}, bf16[32,32,256]{2,1,0:T(8,128)(2,1)}, u32[]{:S(2)}) copy-start(bf16[32,32,256]{2,1,0:T(8,128)(2,1)} %param.13) | copy-start | bytes 1572868
  3.6 38.4 %copy-start.1 = (bf16[512,224]{0,1:T(8,128)(2,1)S(1)}, bf16[512,224]{0,1:T(8,128)(2,1)}, u32[]{:S(2)}) copy-start(bf16[512,224]{0,1:T(8,128)(2,1)} %param.15) | copy-start | bytes 688132
  43.3 27.0 %copy-start.2 = (bf16[64,224]{1,0:T(8,128)(2,1)S(1)}, bf16[64,224]{1,0:T(8,128)(2,1)}, u32[]{:S(2)}) copy-start(bf16[64,224]{1,0:T(8,128)(2,1)} %residual.1) | copy-start | bytes 86020
  43.3 27.0 %all-to-all-start.2 = ((bf16[16,64,224]{2,1,0:T(8,128)(2,1)}), bf16[16,64,224]{2,1,0:T(8,128)(2,1)S(1)}, u32[]{:S(2)}, u32[]{:S(2)}) async-start(bf16[16,64,224]{2,1,0:T(8,128)(2,1)} %shard_map.109), calls=%async_computation.2 | async-start | bytes 1048576 | tf_op jit(solution)/shard_map/all_to_all | solution.py:29
  52.2 14.5 %collective-permute-start.1 = (bf16[1792,128]{1,0:T(8,128)(2,1)S(1)}, bf16[1792,128]{1,0:T(8,128)(2,1)S(1)}, u32[]{:S(2)}, u32[]{:S(2)}) collective-permute-start(bf16[1792,128]{1,0:T(8,128)(2,1)S(1)} %get-tuple-element.39), channel_id=1, source_target_pairs={{0,192},{8,200},{16,208},{24,216},{32,224},{40,232},{48,240},{56,2... | collective-permute-start | bytes 1376264 | tf_op jit(solution)/shard_map/ppermute | solution.py:227
  54.9 15.4 %collective-permute-start = (bf16[1792,128]{1,0:T(8,128)(2,1)S(1)}, bf16[1792,128]{1,0:T(8,128)(2,1)S(1)}, u32[]{:S(2)}, u32[]{:S(2)}) collective-permute-start(bf16[1792,128]{1,0:T(8,128)(2,1)S(1)} %get-tuple-element.40), channel_id=1, source_target_pairs={{0,64},{8,72},{16,80},{24,88},{32,96},{40,104},{48,112},{56,120},{... | collective-permute-start | bytes 1376264 | tf_op jit(solution)/shard_map/ppermute | solution.py:227
  58.1 22.2 %copy-start.4 = (f32[7168]{0:T(1024)S(1)}, f32[7168]{0:T(1024)}, u32[]{:S(2)}) copy-start(f32[7168]{0:T(1024)} %param.17) | copy-start | bytes 86020
  71.5 33.0 %all-to-all-start.3 = ((bf16[64,24,224]{2,1,0:T(8,128)(2,1)}), bf16[64,24,224]{2,1,0:T(8,128)(2,1)S(1)}, u32[]{:S(2)}, u32[]{:S(2)}) async-start(bf16[64,24,224]{2,1,0:T(8,128)(2,1)} %bitcast.14), calls=%async_computation.3 | async-start | bytes 1572864 | tf_op jit(solution)/shard_map/all_to_all | solution.py:29
  80.4 4.4 %copy-start.3 = (bf16[1,224,4096]{2,1,0:T(8,128)(2,1)S(1)}, bf16[1,224,4096]{2,1,0:T(8,128)(2,1)}, u32[]{:S(2)}) copy-start(bf16[1,224,4096]{2,1,0:T(8,128)(2,1)} %param.21) | copy-start | bytes 5505028
  82.5 38.0 %collective-permute-start.6 = (bf16[1792,128]{1,0:T(8,128)(2,1)}, bf16[1792,128]{1,0:T(8,128)(2,1)}, u32[]{:S(2)}, u32[]{:S(2)}) collective-permute-start(bf16[1792,128]{1,0:T(8,128)(2,1)} %get-tuple-element.35), channel_id=1, source_target_pairs={{0,128},{8,136},{16,144},{24,152},{32,160},{40,168},{48,176},{56,1... | collective-permute-start | bytes 1376264 | tf_op jit(solution)/shard_map/ppermute | solution.py:227
  85.8 25.9 %collective-permute-start.4 = (bf16[224,1024]{1,0:T(8,128)(2,1)}, bf16[224,1024]{1,0:T(8,128)(2,1)S(1)}, u32[]{:S(2)}, u32[]{:S(2)}) collective-permute-start(bf16[224,1024]{1,0:T(8,128)(2,1)} %get-tuple-element.38), channel_id=1, source_target_pairs={{0,64},{8,72},{16,80},{24,88},{32,96},{40,104},{48,112},{56,120},{... | collective-permute-start | bytes 1376264 | tf_op jit(solution)/shard_map/ppermute | solution.py:233
  87.9 23.8 %collective-permute-start.5 = (bf16[224,1024]{1,0:T(8,128)(2,1)}, bf16[224,1024]{1,0:T(8,128)(2,1)}, u32[]{:S(2)}, u32[]{:S(2)}) collective-permute-start(bf16[224,1024]{1,0:T(8,128)(2,1)} %get-tuple-element.37), channel_id=1, source_target_pairs={{0,192},{8,200},{16,208},{24,216},{32,224},{40,232},{48,240},{56,2... | collective-permute-start | bytes 1376264 | tf_op jit(solution)/shard_map/ppermute | solution.py:233
  104.5 13.7 %collective-permute-start.2 = (bf16[2,384,224]{2,1,0:T(8,128)(2,1)S(1)}, bf16[2,384,224]{2,1,0:T(8,128)(2,1)S(1)}, u32[]{:S(2)}, u32[]{:S(2)}) collective-permute-start(bf16[2,384,224]{2,1,0:T(8,128)(2,1)S(1)} %bitcast.76), channel_id=1, source_target_pairs={{0,8},{8,16},{16,24},{24,32},{32,40},{40,48},{48,56},{56,0},{64,72... | collective-permute-start | bytes 1032200 | tf_op jit(solution)/shard_map/ppermute | solution.py:246
  107.8 12.7 %collective-permute-start.3 = (bf16[2,384,224]{2,1,0:T(8,128)(2,1)S(1)}, bf16[2,384,224]{2,1,0:T(8,128)(2,1)S(1)}, u32[]{:S(2)}, u32[]{:S(2)}) collective-permute-start(bf16[2,384,224]{2,1,0:T(8,128)(2,1)S(1)} %bitcast.75), channel_id=1, source_target_pairs={{0,56},{8,0},{16,8},{24,16},{32,24},{40,32},{48,40},{56,48},{64,12... | collective-permute-start | bytes 1032200 | tf_op jit(solution)/shard_map/ppermute | solution.py:247
  134.4 25.0 %all-to-all-start.5 = ((bf16[8,384,128]{2,1,0:T(8,128)(2,1)}), bf16[8,384,128]{2,1,0:T(8,128)(2,1)S(1)}, u32[]{:S(2)}, u32[]{:S(2)}) async-start(bf16[8,384,128]{2,1,0:T(8,128)(2,1)} %broadcast_in_dim.88), calls=%async_computation.5 | async-start | bytes 1572864 | tf_op jit(solution)/shard_map/all_to_all | solution.py:29
  140.2 12.6 %collective-permute-start.7 = (bf16[224,1024]{1,0:T(8,128)(2,1)S(1)}, bf16[224,1024]{1,0:T(8,128)(2,1)S(1)}, u32[]{:S(2)}, u32[]{:S(2)}) collective-permute-start(bf16[224,1024]{1,0:T(8,128)(2,1)S(1)} %get-tuple-element.33), channel_id=1, source_target_pairs={{0,128},{8,136},{16,144},{24,152},{32,160},{40,168},{48,176},{56,1... | collective-permute-start | bytes 1376264 | tf_op jit(solution)/shard_map/ppermute | solution.py:233
  174.0 20.9 %all-to-all-start.7 = ((bf16[16,24,224]{2,1,0:T(8,128)(2,1)}), bf16[16,24,224]{2,1,0:T(8,128)(2,1)S(1)}, u32[]{:S(2)}, u32[]{:S(2)}) async-start(bf16[16,24,224]{2,1,0:T(8,128)(2,1)} %bitcast.27), calls=%async_computation.7 | async-start | bytes 393216 | tf_op jit(solution)/shard_map/all_to_all | solution.py:29

commit v11 on v10

--- a/solution.py
+++ b/solution.py
@@ -72,14 +72,16 @@
     total = residual[...].astype(F32)
     for i in range(parts.shape[0]):
         total += parts[i].astype(F32)
-    out[...] = jnp.dot(select[...], total.astype(BF16), preferred_element_type=F32).astype(BF16)
+    value = jnp.dot(select[...], total.astype(BF16), preferred_element_type=F32).astype(BF16)
+    for z in range(NZ):
+        out[z] = value
 
 
 def head_sum(parts, residual, select):
     slots, columns = select.shape[0], residual.shape[1]
     return pl.pallas_call(
         head_sum_kernel,
-        out_shape=jax.ShapeDtypeStruct((slots, columns), BF16),
+        out_shape=jax.ShapeDtypeStruct((NZ, slots, columns), BF16),
         in_specs=whole(3),
         out_specs=whole(1)[0],
         compiler_params=PARAMS,
@@ -221,46 +223,53 @@
     combine = jnp.where(here, weight_of[:, None, :], 0.0).reshape(slots, rows)
 
     attn = attend(queries, keys, values, lengths)
-    def up_block(step):
+    def up_cut(step):
         wanted = (x_index + step) % NX
-        block = lax.dynamic_slice_in_dim(up_weight[0], wanted * (width // NX), width // NX, 0)
-        block = lax.ppermute(block, GRP, moves(step, 0)) if step else block
-        return block.reshape(NZ, PAIR, columns, units)
-
-    def down_block(step):
+        return lax.dynamic_slice_in_dim(up_weight[0], wanted * (width // NX), width // NX, 0)
+
+    def down_cut(step):
         wanted = (x_index + step) % NX
-        block = lax.dynamic_slice_in_dim(down_weight[0], wanted * (8 * units), 8 * units, 1)
-        return lax.ppermute(block, GRP, moves(step, 0)) if step else block
+        return lax.dynamic_slice_in_dim(down_weight[0], wanted * (8 * units), 8 * units, 1)
+
+    def along(block, step):
+        return lax.ppermute(block, GRP, moves(step, 0))
 
     attn = spread(attn, NZ, "zpair")
+    attn, up1, up3 = lax.optimization_barrier((attn, up_cut(1), up_cut(3)))
     attn = spread(attn.reshape(-1, attn.shape[2]), parts, ("x", "member"))
     projected = project(attn.reshape(parts, NZ, -1, attn.shape[2]), out_weight.T)
-    projected, up_weight = lax.optimization_barrier((projected, up_weight))
+    projected, up1, up3, up_weight, down_weight = lax.optimization_barrier(
+        (projected, up1, up3, up_weight, down_weight)
+    )
     projected = exchange(projected, ("pool", "tp"))
-    projected, up1, up3 = lax.optimization_barrier((projected, up_block(1), up_block(3)))
+    up = [up_cut(0), along(up1, 1), up_cut(2), along(up3, 3)]
+    down = [down_cut(step) for step in range(NX)]
+    projected, up, down = lax.optimization_barrier((projected, up, down))
     slot_rows = head_sum(projected, residual, select)
-    slot_rows, up_weight, down_weight = lax.optimization_barrier((slot_rows, up_weight, down_weight))
-    same = jnp.broadcast_to(slot_rows.reshape(1, experts, slot_cap, columns), (NZ, experts, slot_cap, columns))
-    same = exchange(same.reshape(NZ * experts, slot_cap, columns), ("zpair", "pool", "tp"))
+    slot_rows, up, down = lax.optimization_barrier((slot_rows, up, down))
+    same = exchange(slot_rows.reshape(NZ * experts, slot_cap, columns), ("zpair", "pool", "tp"))
     same = same.reshape(NZ, slots, columns)
     before = lax.ppermute(same[: NZ // 2], GRP, turns(1))
     after = lax.ppermute(same[NZ // 2 :], GRP, turns(-1))
-    before, after, down1, down3 = lax.optimization_barrier((before, after, down_block(1), down_block(3)))
+    down[1], down[3], up[2] = along(down[1], 1), along(down[3], 3), along(up[2], 2)
+    before, after, down[1], down[3] = lax.optimization_barrier((before, after, down[1], down[3]))
+    up = [w.reshape(NZ, PAIR, columns, units) for w in up]
     gain = norm_gain.reshape(NX, NZ, PAIR, columns)
     gain = lax.dynamic_index_in_dim(gain, x_index, 0, keepdims=False)
     gain = [lax.dynamic_index_in_dim(gain, m, 1, keepdims=False) for m in (member, 1 - member)]
     gain = jnp.concatenate(gain)
     place = jnp.stack([x_index, member]).astype(jnp.int32)
-    partial_up = up_product(place, (same, before, after), gain, (up_block(0), up1, up_block(2), up3))
+    partial_up = up_product(place, (same, before, after), gain, up)
     total_up = jnp.sum(exchange(partial_up, "x").astype(F32), axis=0)
     count = slots // units
     squares = (total_up[slots : slots + count] + total_up[slots + count : slots + 2 * count]).reshape(slots, 1)
     scale = lax.rsqrt(squares / width + 1e-06)
     act = jax.nn.silu(total_up[:slots] * scale).astype(BF16)
 
-    act, down_weight = lax.optimization_barrier((act, down_weight))
+    act, down[2] = lax.optimization_barrier((act, down[2]))
+    down[2] = along(down[2], 2)
     act = spread(act, 8, ("zpair", "member"))
-    partial_out = exchange(down_product(place, act, (down_block(0), down1, down_block(2), down3)), "x")
+    partial_out = exchange(down_product(place, act, down), "x")
     expert_out = jnp.sum(partial_out.astype(F32), axis=0).astype(BF16).T
     returned = exchange(expert_out.reshape(experts, slot_cap, columns), ("pool", "tp"))
     returned = returned.reshape(slots, columns)

time: 197 us -> 197 us (level)
  blocking collectives: 59.6 us -> 23.5 us
  waiting for transfers between devices: 56.5 us -> 76.9 us
  starting transfers between devices: 57.3 us -> 72.7 us
    all_to_all x4 -> x2, blocking collectives: 59.6 us -> 23.5 us  [exchange(): return lax.all_to_all(value, axis, 0, 0, tiled=True)]
    all_to_all x4 -> x6, waiting for transfers between devices: 27 us -> 52.9 us  [exchange(): return lax.all_to_all(value, axis, 0, 0, tiled=True)]
    all_to_all x4 -> x6, starting transfers between devices: 32.2 us -> 44.8 us  [exchange(): return lax.all_to_all(value, axis, 0, 0, tiled=True)]
    ppermute x6, waiting for transfers between devices: 20.7 us -> 15.2 us  [along(): return lax.ppermute(block, GRP, moves(step, 0))]
    ppermute x6, starting transfers between devices: 18.1 us -> 20.9 us  [along(): return lax.ppermute(block, GRP, moves(step, 0))]
    dynamic_slice x4 -> x3, local copies, waits for them, and re-layouts: 5.61 us -> 4.55 us  [the longest x1 2.72 us: down_cut(): lax.dynamic_slice_in_dim(down_weight[0], wanted * (8 * units), 8 * units, 1)]
  transfers between devices with their start and end apart: 12 -> 14, of which waited for: 8 -> 10; matrix products, arithmetic and copies ran while one was open for 4% -> 3% of each run, Pallas kernels for 0% -> 0%
where the time goes in v11:
time: 197 us; the launch traced here: 196 us
  waiting for transfers between devices  76.9 us (39%)
  starting transfers between devices  72.7 us (37%)
  blocking collectives  23.5 us (12%)
  local copies, waits for them, and re-layouts  10.7 us (5%)
  Pallas kernels  7.6 us (4%)
  matrix products  3.03 us (2%)
    all_to_all x6, waiting for transfers between devices, exchange(): return lax.all_to_all(value, axis, 0, 0, tiled=True)  52.9 us
    all_to_all x6, starting transfers between devices, exchange(): return lax.all_to_all(value, axis, 0, 0, tiled=True)  44.8 us
    all_to_all x2, blocking collectives, exchange(): return lax.all_to_all(value, axis, 0, 0, tiled=True)  23.5 us
    ppermute x6, starting transfers between devices, along(): return lax.ppermute(block, GRP, moves(step, 0))  20.9 us
    ppermute x6, waiting for transfers between devices, along(): return lax.ppermute(block, GRP, moves(step, 0))  15.2 us
    ppermute x1, waiting for transfers between devices, shards(): before = lax.ppermute(same[:NZ // 2], GRP, turns(1))  6.44 us
    ppermute x1, starting transfers between devices, shards(): after = lax.ppermute(same[NZ // 2:], GRP, turns(-1))  4.09 us
  transfers between devices with their start and end apart: 14, of which 10 were waited for; matrix products, arithmetic and copies ran while one was open for 3% of the time, Pallas kernels for 0%

profile of v11, /device:TPU:8, one launch (start us, length us, event | category | flops | bytes accessed | tf_op | source)
XLA Modules:
  0.0 196.3 jit_solution(1277606247621666759)
XLA Ops:
  0.0 0.0 copy-start
  0.0 0.9 iota_compare_fusion.4
  0.9 0.8 reshape.114
  1.7 1.3 fusion.5
  2.9 0.2 fusion.30
  3.2 0.6 convolution_convert_fusion
  3.7 0.7 broadcast_in_dim.76
  4.4 10.3 %all-to-all-start = ((bf16[4,32,512]{2,1,0:T(8,128)(2,1)}), bf16[4,32,512]{2,1,0:T(8,128)(2,1)S(1)}, u32[]{:S(2)}, u32[]{:S(2)}) async-start(bf16[4,32,512]{2,1,0:T(8,128)(2,1)} %broadcast_in_dim.76), calls=%async_computation | async-start | bytes 262144 | tf_op jit(solution)/shard_map/all_to_all | solution.py:29
  14.7 0.0 copy-done.3
  14.7 1.0 dynamic-slice_bitcast_fusion.6
  15.7 8.3 %all-to-all-done = bf16[4,32,512]{2,1,0:T(8,128)(2,1)S(1)} async-done(((bf16[4,32,512]{2,1,0:T(8,128)(2,1)}), bf16[4,32,512]{2,1,0:T(8,128)(2,1)S(1)}, u32[]{:S(2)}, u32[]{:S(2)}) %all-to-all-start) | async-done | bytes 131104 | tf_op jit(solution)/shard_map/all_to_all | solution.py:29
  24.0 1.1 broadcast_in_dim.78
  25.0 4.3 %all-to-all-start.1 = ((bf16[8,128,512]{2,1,0:T(8,128)(2,1)}), bf16[8,128,512]{2,1,0:T(8,128)(2,1)S(1)}, u32[]{:S(2)}, u32[]{:S(2)}) async-start(bf16[8,128,512]{2,1,0:T(8,128)(2,1)} %broadcast_in_dim.78), calls=%async_computation.1 | async-start | bytes 2097152 | tf_op jit(solution)/shard_map/all_to_all | solution.py:29
  29.3 14.6 %all-to-all-done.1 = bf16[8,128,512]{2,1,0:T(8,128)(2,1)S(1)} async-done(((bf16[8,128,512]{2,1,0:T(8,128)(2,1)}), bf16[8,128,512]{2,1,0:T(8,128)(2,1)S(1)}, u32[]{:S(2)}, u32[]{:S(2)}) %all-to-all-start.1) | async-done | bytes 1048608 | tf_op jit(solution)/shard_map/all_to_all | solution.py:29
  44.0 0.0 copy-done.1
  44.0 1.3 shard_map.109
  45.2 7.6 %all-to-all-start.2 = ((bf16[16,64,224]{2,1,0:T(8,128)(2,1)}), bf16[16,64,224]{2,1,0:T(8,128)(2,1)S(1)}, u32[]{:S(2)}, u32[]{:S(2)}) async-start(bf16[16,64,224]{2,1,0:T(8,128)(2,1)} %shard_map.109), calls=%async_computation.2 | async-start | bytes 1048576 | tf_op jit(solution)/shard_map/all_to_all | solution.py:29
  52.8 0.8 fusion.21
  53.6 1.9 collective-permute-start
  55.5 5.1 %collective-permute-start.1 = (bf16[1792,128]{1,0:T(8,128)(2,1)}, bf16[1792,128]{1,0:T(8,128)(2,1)S(1)}, u32[]{:S(2)}, u32[]{:S(2)}) collective-permute-start(bf16[1792,128]{1,0:T(8,128)(2,1)} %get-tuple-element.43), channel_id=1, source_target_pairs={{0,192},{8,200},{16,208},{24,216},{32,224},{40,232},{48,240},{56,2... | collective-permute-start | bytes 1376264 | tf_op jit(solution)/shard_map/ppermute | solution.py:235
  60.6 0.1 convolution_convert_fusion.1
  60.8 0.1 eq.58
  60.9 0.1 fusion.9.select
  61.0 0.0 copy-start.4
  61.0 2.7 %dynamic-slice_bitcast_fusion = (bf16[224,1024]{1,0:T(8,128)(2,1)}, bf16[224,1024]{1,0:T(8,128)(2,1)}, bf16[224,1024]{1,0:T(8,128)(2,1)}, bf16[224,1024]{1,0:T(8,128)(2,1)S(1)}) fusion(bf16[1,224,4096]{2,1,0:T(8,128)(2,1)} %param.21, s32[]{:T(128)S(6)} %select_n.112, s32[]{:T(128)S(6)} %select_n.111, s32[]{:T(128)S(6)} %select_n.110, s32[]{:T(128)S(6)} %select_n.109), kind=kLoop, calls=%fused_computation.12 | loop fusion | bytes 3670032 | tf_op jit(solution)/shard_map/dynamic_slice | solution.py:232
  63.8 0.0 copy-done.4
  63.8 0.8 dynamic-slice_bitcast_fusion.4
  64.6 4.9 %collective-permute-done = bf16[1792,128]{1,0:T(8,128)(2,1)S(1)} collective-permute-done((bf16[1792,128]{1,0:T(8,128)(2,1)}, bf16[1792,128]{1,0:T(8,128)(2,1)S(1)}, u32[]{:S(2)}, u32[]{:S(2)}) %collective-permute-start) | collective-permute-done | bytes 458784 | tf_op jit(solution)/shard_map/ppermute | solution.py:235
  69.5 1.3 collective-permute-done.1
  70.7 0.0 all-to-all-done.2.parts
  70.7 1.1 shard_map.110
  71.9 8.6 %all-to-all-start.3 = ((bf16[64,24,224]{2,1,0:T(8,128)(2,1)}), bf16[64,24,224]{2,1,0:T(8,128)(2,1)S(1)}, u32[]{:S(2)}, u32[]{:S(2)}) async-start(bf16[64,24,224]{2,1,0:T(8,128)(2,1)} %bitcast.17), calls=%async_computation.3 | async-start | bytes 1572864 | tf_op jit(solution)/shard_map/all_to_all | solution.py:29
  80.6 0.1 reshape.118
  80.7 1.9 collective-permute-start.4
  82.7 5.5 %collective-permute-start.5 = (bf16[224,1024]{1,0:T(8,128)(2,1)}, bf16[224,1024]{1,0:T(8,128)(2,1)}, u32[]{:S(2)}, u32[]{:S(2)}) collective-permute-start(bf16[224,1024]{1,0:T(8,128)(2,1)} %get-tuple-element.56), channel_id=1, source_target_pairs={{0,192},{8,200},{16,208},{24,216},{32,224},{40,232},{48,240},{56,2... | collective-permute-start | bytes 1376264 | tf_op jit(solution)/shard_map/ppermute | solution.py:235
  88.2 3.4 %collective-permute-start.6 = (bf16[1792,128]{1,0:T(8,128)(2,1)}, bf16[1792,128]{1,0:T(8,128)(2,1)}, u32[]{:S(2)}, u32[]{:S(2)}) collective-permute-start(bf16[1792,128]{1,0:T(8,128)(2,1)} %get-tuple-element.61), channel_id=1, source_target_pairs={{0,128},{8,136},{16,144},{24,152},{32,160},{40,168},{48,176},{56,1... | collective-permute-start | bytes 1376264 | tf_op jit(solution)/shard_map/ppermute | solution.py:235
  91.5 13.4 %all-to-all-done.3 = bf16[64,24,224]{2,1,0:T(8,128)(2,1)S(1)} async-done(((bf16[64,24,224]{2,1,0:T(8,128)(2,1)}), bf16[64,24,224]{2,1,0:T(8,128)(2,1)S(1)}, u32[]{:S(2)}, u32[]{:S(2)}) %all-to-all-start.3) | async-done | bytes 688160 | tf_op jit(solution)/shard_map/all_to_all | solution.py:29
  104.9 0.1 fusion.29
  105.0 3.0 %collective-permute-start.2 = (bf16[2,384,224]{2,1,0:T(8,128)(2,1)S(1)}, bf16[2,384,224]{2,1,0:T(8,128)(2,1)S(1)}, u32[]{:S(2)}, u32[]{:S(2)}) collective-permute-start(bf16[2,384,224]{2,1,0:T(8,128)(2,1)S(1)} %bitcast.76), channel_id=1, source_target_pairs={{0,8},{8,16},{16,24},{24,32},{32,40},{40,48},{48,56},{56,0},{64,72... | collective-permute-start | bytes 1032200 | tf_op jit(solution)/shard_map/ppermute | solution.py:252
  107.9 4.1 %collective-permute-start.3 = (bf16[2,384,224]{2,1,0:T(8,128)(2,1)S(1)}, bf16[2,384,224]{2,1,0:T(8,128)(2,1)S(1)}, u32[]{:S(2)}, u32[]{:S(2)}) collective-permute-start(bf16[2,384,224]{2,1,0:T(8,128)(2,1)S(1)} %bitcast.75), channel_id=1, source_target_pairs={{0,56},{8,0},{16,8},{24,16},{32,24},{40,32},{48,40},{56,48},{64,12... | collective-permute-start | bytes 1032200 | tf_op jit(solution)/shard_map/ppermute | solution.py:253
  112.0 0.1 pad_add_fusion.place
  112.1 0.0 collective-permute-done.4.block1
  112.1 0.0 collective-permute-done.5.block3
  112.2 6.4 %collective-permute-done.2.before = bf16[2,384,224]{2,1,0:T(8,128)(2,1)S(1)} collective-permute-done((bf16[2,384,224]{2,1,0:T(8,128)(2,1)S(1)}, bf16[2,384,224]{2,1,0:T(8,128)(2,1)S(1)}, u32[]{:S(2)}, u32[]{:S(2)}) %collective-permute-start.2) | collective-permute-done | bytes 344096 | tf_op jit(solution)/shard_map/ppermute | solution.py:252
  118.6 2.3 %collective-permute-done.3.after = bf16[2,384,224]{2,1,0:T(8,128)(2,1)S(1)} collective-permute-done((bf16[2,384,224]{2,1,0:T(8,128)(2,1)S(1)}, bf16[2,384,224]{2,1,0:T(8,128)(2,1)S(1)}, u32[]{:S(2)}, u32[]{:S(2)}) %collective-permute-start.3) | collective-permute-done | bytes 344096 | tf_op jit(solution)/shard_map/ppermute | solution.py:253
  120.9 0.0 collective-permute-done.6
  120.9 2.8 %shard_map.111 = bf16[4,400,128]{2,1,0:T(8,128)(2,1)S(1)} custom-call(s32[2]{0:T(128)S(1)} %pad_add_fusion.place, bf16[4,384,224]{2,1,0:T(8,128)(2,1)S(1)} %bitcast.67, bf16[2,384,224]{2,1,0:T(8,128)(2,1)S(1)} %collective-permute-done.2.before, bf16[2,384,224]{2,1,0:T(8,128)(2,1)S(1)} %collective-permute-done.3.after, f32[8,224]{1,0:T(8,128)S(1)} %pad_maximum_fusion.gain, ...), custom_call_target="tpu_custom_call" | custom-call | flops 704643072 | bytes 6291456 | tf_op jit(solution)/shard_map/pallas_call | solution.py:134
  123.7 12.1 %all_to_all.40 = bf16[4,400,128]{2,1,0:T(8,128)(2,1)S(1)} all-to-all(bf16[4,400,128]{2,1,0:T(8,128)(2,1)S(1)} %shard_map.111), channel_id=1, replica_groups=mesh['pool'=2,'x'=4,'zpair'=4,'member'=2,'tp'=8] {'x'}, dimensions={0} | all-to-all | bytes 819200 | tf_op jit(solution)/shard_map/all_to_all | solution.py:29
  135.9 0.1 convert_reduce_fusion
  135.9 0.1 multiply_convert_fusion
  136.1 1.0 broadcast_in_dim.79
  137.1 4.3 %all-to-all-start.5 = ((bf16[8,384,128]{2,1,0:T(8,128)(2,1)}), bf16[8,384,128]{2,1,0:T(8,128)(2,1)S(1)}, u32[]{:S(2)}, u32[]{:S(2)}) async-start(bf16[8,384,128]{2,1,0:T(8,128)(2,1)} %broadcast_in_dim.79), calls=%async_computation.5 | async-start | bytes 1572864 | tf_op jit(solution)/shard_map/all_to_all | solution.py:29
  141.4 3.0 %collective-permute-start.7 = (bf16[224,1024]{1,0:T(8,128)(2,1)S(1)}, bf16[224,1024]{1,0:T(8,128)(2,1)S(1)}, u32[]{:S(2)}, u32[]{:S(2)}) collective-permute-start(bf16[224,1024]{1,0:T(8,128)(2,1)S(1)} %copy-done.5), channel_id=1, source_target_pairs={{0,128},{8,136},{16,144},{24,152},{32,160},{40,168},{48,176},{56,1... | collective-permute-start | bytes 1376264 | tf_op jit(solution)/shard_map/ppermute | solution.py:235
  144.4 9.1 %collective-permute-done.7.block2 = bf16[224,1024]{1,0:T(8,128)(2,1)S(1)} collective-permute-done((bf16[224,1024]{1,0:T(8,128)(2,1)S(1)}, bf16[224,1024]{1,0:T(8,128)(2,1)S(1)}, u32[]{:S(2)}, u32[]{:S(2)}) %collective-permute-start.7) | collective-permute-done | bytes 458784 | tf_op jit(solution)/shard_map/ppermute | solution.py:235
  153.5 7.8 %all-to-all-done.5.act = bf16[8,384,128]{2,1,0:T(8,128)(2,1)S(1)} async-done(((bf16[8,384,128]{2,1,0:T(8,128)(2,1)}), bf16[8,384,128]{2,1,0:T(8,128)(2,1)S(1)}, u32[]{:S(2)}, u32[]{:S(2)}) %all-to-all-start.5) | async-done | bytes 786464 | tf_op jit(solution)/shard_map/all_to_all | solution.py:29
  161.3 2.4 %shard_map.112 = bf16[4,224,384]{2,1,0:T(8,128)(2,1)S(1)} custom-call(s32[2]{0:T(128)S(1)} %pad_add_fusion.place, bf16[8,384,128]{2,1,0:T(8,128)(2,1)S(1)} %all-to-all-done.5.act, bf16[224,1024]{1,0:T(8,128)(2,1)S(1)} %get-tuple-element.65.block0, bf16[224,1024]{1,0:T(8,128)(2,1)} %collective-permute-done.4.block1, ...), custom_call_target="tpu_custom_call" | custom-call | flops 704643072 | bytes 5242880 | tf_op jit(solution)/shard_map/pallas_call | solution.py:162
  163.7 11.3 %all_to_all.41 = bf16[4,224,384]{2,1,0:T(8,128)(2,1)S(1)} all-to-all(bf16[4,224,384]{2,1,0:T(8,128)(2,1)S(1)} %shard_map.112), channel_id=1, replica_groups=mesh['pool'=2,'x'=4,'zpair'=4,'member'=2,'tp'=8] {'x'}, dimensions={0} | all-to-all | bytes 1376256 | tf_op jit(solution)/shard_map/all_to_all | solution.py:29
  175.0 0.1 reduce_sum.42
  175.1 0.8 copy.13
  175.9 9.6 %all-to-all-start.7 = ((bf16[16,24,224]{2,1,0:T(8,128)(2,1)}), bf16[16,24,224]{2,1,0:T(8,128)(2,1)S(1)}, u32[]{:S(2)}, u32[]{:S(2)}) async-start(bf16[16,24,224]{2,1,0:T(8,128)(2,1)} %bitcast.27), calls=%async_computation.7 | async-start | bytes 393216 | tf_op jit(solution)/shard_map/all_to_all | solution.py:29
  185.6 0.8 fusion.22
  186.3 8.8 %all-to-all-done.7 = bf16[16,24,224]{2,1,0:T(8,128)(2,1)S(1)} async-done(((bf16[16,24,224]{2,1,0:T(8,128)(2,1)}), bf16[16,24,224]{2,1,0:T(8,128)(2,1)S(1)}, u32[]{:S(2)}, u32[]{:S(2)}) %all-to-all-start.7) | async-done | bytes 172064 | tf_op jit(solution)/shard_map/all_to_all | solution.py:29
  195.2 0.2 convolution_bitcast_fusion.1
  195.4 0.8 fusion.2
  (17 shorter events, 0.1 us)
Async XLA Ops:
  0.0 3.2 %copy-start = (bf16[32,32,256]{2,1,0:T(8,128)(2,1)S(1)}, bf16[32,32,256]{2,1,0:T(8,128)(2,1)}, u32[]{:S(2)}) copy-start(bf16[32,32,256]{2,1,0:T(8,128)(2,1)} %param.13) | copy-start | bytes 1572868
  0.0 14.7 %copy-start.3 = (bf16[1,7168,128]{2,1,0:T(8,128)(2,1)S(1)}, bf16[1,7168,128]{2,1,0:T(8,128)(2,1)}, u32[]{:S(2)}) copy-start(bf16[1,7168,128]{2,1,0:T(8,128)(2,1)} %param.20) | copy-start | bytes 5505028
  4.4 19.6 %all-to-all-start = ((bf16[4,32,512]{2,1,0:T(8,128)(2,1)}), bf16[4,32,512]{2,1,0:T(8,128)(2,1)S(1)}, u32[]{:S(2)}, u32[]{:S(2)}) async-start(bf16[4,32,512]{2,1,0:T(8,128)(2,1)} %broadcast_in_dim.76), calls=%async_computation | async-start | bytes 262144 | tf_op jit(solution)/shard_map/all_to_all | solution.py:29
  15.7 28.3 %copy-start.1 = (bf16[512,224]{0,1:T(8,128)(2,1)S(1)}, bf16[512,224]{0,1:T(8,128)(2,1)}, u32[]{:S(2)}) copy-start(bf16[512,224]{0,1:T(8,128)(2,1)} %param.15) | copy-start | bytes 688132
  25.0 18.9 %all-to-all-start.1 = ((bf16[8,128,512]{2,1,0:T(8,128)(2,1)}), bf16[8,128,512]{2,1,0:T(8,128)(2,1)S(1)}, u32[]{:S(2)}, u32[]{:S(2)}) async-start(bf16[8,128,512]{2,1,0:T(8,128)(2,1)} %broadcast_in_dim.78), calls=%async_computation.1 | async-start | bytes 2097152 | tf_op jit(solution)/shard_map/all_to_all | solution.py:29
  45.2 25.5 %all-to-all-start.2 = ((bf16[16,64,224]{2,1,0:T(8,128)(2,1)}), bf16[16,64,224]{2,1,0:T(8,128)(2,1)S(1)}, u32[]{:S(2)}, u32[]{:S(2)}) async-start(bf16[16,64,224]{2,1,0:T(8,128)(2,1)} %shard_map.109), calls=%async_computation.2 | async-start | bytes 1048576 | tf_op jit(solution)/shard_map/all_to_all | solution.py:29
  53.6 15.9 %collective-permute-start = (bf16[1792,128]{1,0:T(8,128)(2,1)}, bf16[1792,128]{1,0:T(8,128)(2,1)S(1)}, u32[]{:S(2)}, u32[]{:S(2)}) collective-permute-start(bf16[1792,128]{1,0:T(8,128)(2,1)} %get-tuple-element.42), channel_id=1, source_target_pairs={{0,64},{8,72},{16,80},{24,88},{32,96},{40,104},{48,112},{56,120},{... | collective-permute-start | bytes 1376264 | tf_op jit(solution)/shard_map/ppermute | solution.py:235
  55.5 15.2 %collective-permute-start.1 = (bf16[1792,128]{1,0:T(8,128)(2,1)}, bf16[1792,128]{1,0:T(8,128)(2,1)S(1)}, u32[]{:S(2)}, u32[]{:S(2)}) collective-permute-start(bf16[1792,128]{1,0:T(8,128)(2,1)} %get-tuple-element.43), channel_id=1, source_target_pairs={{0,192},{8,200},{16,208},{24,216},{32,224},{40,232},{48,240},{56,2... | collective-permute-start | bytes 1376264 | tf_op jit(solution)/shard_map/ppermute | solution.py:235
  61.0 2.7 %copy-start.4 = (bf16[1,7168,128]{2,1,0:T(8,128)(2,1)S(1)}, bf16[1,7168,128]{2,1,0:T(8,128)(2,1)}, u32[]{:S(2)}) copy-start(bf16[1,7168,128]{2,1,0:T(8,128)(2,1)} %param.20) | copy-start | bytes 5505028
  63.8 7.0 %copy-start.2 = (bf16[64,224]{1,0:T(8,128)(2,1)S(1)}, bf16[64,224]{1,0:T(8,128)(2,1)}, u32[]{:S(2)}) copy-start(bf16[64,224]{1,0:T(8,128)(2,1)} %residual.1) | copy-start | bytes 86020
  64.6 16.0 %copy-start.6 = (f32[7168]{0:T(1024)S(1)}, f32[7168]{0:T(1024)}, u32[]{:S(2)}) copy-start(f32[7168]{0:T(1024)} %param.17) | copy-start | bytes 86020
  71.9 33.0 %all-to-all-start.3 = ((bf16[64,24,224]{2,1,0:T(8,128)(2,1)}), bf16[64,24,224]{2,1,0:T(8,128)(2,1)S(1)}, u32[]{:S(2)}, u32[]{:S(2)}) async-start(bf16[64,24,224]{2,1,0:T(8,128)(2,1)} %bitcast.17), calls=%async_computation.3 | async-start | bytes 1572864 | tf_op jit(solution)/shard_map/all_to_all | solution.py:29
  80.7 31.4 %collective-permute-start.4 = (bf16[224,1024]{1,0:T(8,128)(2,1)}, bf16[224,1024]{1,0:T(8,128)(2,1)}, u32[]{:S(2)}, u32[]{:S(2)}) collective-permute-start(bf16[224,1024]{1,0:T(8,128)(2,1)} %get-tuple-element.55), channel_id=1, source_target_pairs={{0,64},{8,72},{16,80},{24,88},{32,96},{40,104},{48,112},{56,120},{... | collective-permute-start | bytes 1376264 | tf_op jit(solution)/shard_map/ppermute | solution.py:235
  82.7 29.5 %collective-permute-start.5 = (bf16[224,1024]{1,0:T(8,128)(2,1)}, bf16[224,1024]{1,0:T(8,128)(2,1)}, u32[]{:S(2)}, u32[]{:S(2)}) collective-permute-start(bf16[224,1024]{1,0:T(8,128)(2,1)} %get-tuple-element.56), channel_id=1, source_target_pairs={{0,192},{8,200},{16,208},{24,216},{32,224},{40,232},{48,240},{56,2... | collective-permute-start | bytes 1376264 | tf_op jit(solution)/shard_map/ppermute | solution.py:235
  88.2 32.7 %collective-permute-start.6 = (bf16[1792,128]{1,0:T(8,128)(2,1)}, bf16[1792,128]{1,0:T(8,128)(2,1)}, u32[]{:S(2)}, u32[]{:S(2)}) collective-permute-start(bf16[1792,128]{1,0:T(8,128)(2,1)} %get-tuple-element.61), channel_id=1, source_target_pairs={{0,128},{8,136},{16,144},{24,152},{32,160},{40,168},{48,176},{56,1... | collective-permute-start | bytes 1376264 | tf_op jit(solution)/shard_map/ppermute | solution.py:235
  105.0 13.6 %collective-permute-start.2 = (bf16[2,384,224]{2,1,0:T(8,128)(2,1)S(1)}, bf16[2,384,224]{2,1,0:T(8,128)(2,1)S(1)}, u32[]{:S(2)}, u32[]{:S(2)}) collective-permute-start(bf16[2,384,224]{2,1,0:T(8,128)(2,1)S(1)} %bitcast.76), channel_id=1, source_target_pairs={{0,8},{8,16},{16,24},{24,32},{32,40},{40,48},{48,56},{56,0},{64,72... | collective-permute-start | bytes 1032200 | tf_op jit(solution)/shard_map/ppermute | solution.py:252
  107.9 13.0 %collective-permute-start.3 = (bf16[2,384,224]{2,1,0:T(8,128)(2,1)S(1)}, bf16[2,384,224]{2,1,0:T(8,128)(2,1)S(1)}, u32[]{:S(2)}, u32[]{:S(2)}) collective-permute-start(bf16[2,384,224]{2,1,0:T(8,128)(2,1)S(1)} %bitcast.75), channel_id=1, source_target_pairs={{0,56},{8,0},{16,8},{24,16},{32,24},{40,32},{48,40},{56,48},{64,12... | collective-permute-start | bytes 1032200 | tf_op jit(solution)/shard_map/ppermute | solution.py:253
  135.9 5.5 %copy-start.5 = (bf16[224,1024]{1,0:T(8,128)(2,1)S(1)}, bf16[224,1024]{1,0:T(8,128)(2,1)}, u32[]{:S(2)}) copy-start(bf16[224,1024]{1,0:T(8,128)(2,1)} %get-tuple-element.67) | copy-start | bytes 1376260
  137.1 24.2 %all-to-all-start.5 = ((bf16[8,384,128]{2,1,0:T(8,128)(2,1)}), bf16[8,384,128]{2,1,0:T(8,128)(2,1)S(1)}, u32[]{:S(2)}, u32[]{:S(2)}) async-start(bf16[8,384,128]{2,1,0:T(8,128)(2,1)} %broadcast_in_dim.79), calls=%async_computation.5 | async-start | bytes 1572864 | tf_op jit(solution)/shard_map/all_to_all | solution.py:29
  141.4 12.1 %collective-permute-start.7 = (bf16[224,1024]{1,0:T(8,128)(2,1)S(1)}, bf16[224,1024]{1,0:T(8,128)(2,1)S(1)}, u32[]{:S(2)}, u32[]{:S(2)}) collective-permute-start(bf16[224,1024]{1,0:T(8,128)(2,1)S(1)} %copy-done.5), channel_id=1, source_target_pairs={{0,128},{8,136},{16,144},{24,152},{32,160},{40,168},{48,176},{56,1... | collective-permute-start | bytes 1376264 | tf_op jit(solution)/shard_map/ppermute | solution.py:235
  175.9 19.3 %all-to-all-start.7 = ((bf16[16,24,224]{2,1,0:T(8,128)(2,1)}), bf16[16,24,224]{2,1,0:T(8,128)(2,1)S(1)}, u32[]{:S(2)}, u32[]{:S(2)}) async-start(bf16[16,24,224]{2,1,0:T(8,128)(2,1)} %bitcast.27), calls=%async_computation.7 | async-start | bytes 393216 | tf_op jit(solution)/shard_map/all_to_all | solution.py:29

commit v12 on v11

--- a/solution.py
+++ b/solution.py
@@ -242,7 +242,7 @@
         (projected, up1, up3, up_weight, down_weight)
     )
     projected = exchange(projected, ("pool", "tp"))
-    up = [up_cut(0), along(up1, 1), up_cut(2), along(up3, 3)]
+    up = [up_cut(0), up1, up_cut(2), along(up3, 3)]
     down = [down_cut(step) for step in range(NX)]
     projected, up, down = lax.optimization_barrier((projected, up, down))
     slot_rows = head_sum(projected, residual, select)
@@ -251,7 +251,7 @@
     same = same.reshape(NZ, slots, columns)
     before = lax.ppermute(same[: NZ // 2], GRP, turns(1))
     after = lax.ppermute(same[NZ // 2 :], GRP, turns(-1))
-    down[1], down[3], up[2] = along(down[1], 1), along(down[3], 3), along(up[2], 2)
+    up[1], up[2], down[1], down[3] = along(up[1], 1), along(up[2], 2), along(down[1], 1), along(down[3], 3)
     before, after, down[1], down[3] = lax.optimization_barrier((before, after, down[1], down[3]))
     up = [w.reshape(NZ, PAIR, columns, units) for w in up]
     gain = norm_gain.reshape(NX, NZ, PAIR, columns)

time: 197 us -> 193 us (0.980)
  starting transfers between devices: 72.7 us -> 70.3 us
where the time goes in v12:
time: 193 us; the launch traced here: 192 us
  waiting for transfers between devices  76.7 us (40%)
  starting transfers between devices  70.3 us (36%)
  blocking collectives  22.2 us (12%)
  local copies, waits for them, and re-layouts  10.5 us (5%)
  Pallas kernels  7.56 us (4%)
  matrix products  3.03 us (2%)
    all_to_all x6, waiting for transfers between devices, exchange(): return lax.all_to_all(value, axis, 0, 0, tiled=True)  51.5 us
    all_to_all x6, starting transfers between devices, exchange(): return lax.all_to_all(value, axis, 0, 0, tiled=True)  43.6 us
    all_to_all x2, blocking collectives, exchange(): return lax.all_to_all(value, axis, 0, 0, tiled=True)  22.2 us
    ppermute x6, starting transfers between devices, along(): return lax.ppermute(block, GRP, moves(step, 0))  19.6 us
    ppermute x6, waiting for transfers between devices, along(): return lax.ppermute(block, GRP, moves(step, 0))  16.5 us
    ppermute x1, waiting for transfers between devices, shards(): before = lax.ppermute(same[:NZ // 2], GRP, turns(1))  6.44 us
    ppermute x1, starting transfers between devices, shards(): after = lax.ppermute(same[NZ // 2:], GRP, turns(-1))  4.09 us
  transfers between devices with their start and end apart: 14, of which 10 were waited for; matrix products, arithmetic and copies ran while one was open for 3% of the time, Pallas kernels for 0%

profile of v12, /device:TPU:8, one launch (start us, length us, event | category | flops | bytes accessed | tf_op | source)
XLA Modules:
  0.0 192.3 jit_solution(3242382619237157557)
XLA Ops:
  0.0 0.0 copy-start
  0.0 0.9 iota_compare_fusion.4
  0.9 0.8 reshape.114
  1.7 1.3 fusion.5
  2.9 0.2 fusion.30
  3.2 0.6 convolution_convert_fusion
  3.7 0.7 broadcast_in_dim.76
  4.4 10.3 %all-to-all-start = ((bf16[4,32,512]{2,1,0:T(8,128)(2,1)}), bf16[4,32,512]{2,1,0:T(8,128)(2,1)S(1)}, u32[]{:S(2)}, u32[]{:S(2)}) async-start(bf16[4,32,512]{2,1,0:T(8,128)(2,1)} %broadcast_in_dim.76), calls=%async_computation | async-start | bytes 262144 | tf_op jit(solution)/shard_map/all_to_all | solution.py:29
  14.7 0.0 copy-done.3
  14.7 0.8 dynamic-slice_bitcast_fusion.6
  15.5 8.4 %all-to-all-done = bf16[4,32,512]{2,1,0:T(8,128)(2,1)S(1)} async-done(((bf16[4,32,512]{2,1,0:T(8,128)(2,1)}), bf16[4,32,512]{2,1,0:T(8,128)(2,1)S(1)}, u32[]{:S(2)}, u32[]{:S(2)}) %all-to-all-start) | async-done | bytes 131104 | tf_op jit(solution)/shard_map/all_to_all | solution.py:29
  24.0 1.1 broadcast_in_dim.78
  25.0 4.3 %all-to-all-start.1 = ((bf16[8,128,512]{2,1,0:T(8,128)(2,1)}), bf16[8,128,512]{2,1,0:T(8,128)(2,1)S(1)}, u32[]{:S(2)}, u32[]{:S(2)}) async-start(bf16[8,128,512]{2,1,0:T(8,128)(2,1)} %broadcast_in_dim.78), calls=%async_computation.1 | async-start | bytes 2097152 | tf_op jit(solution)/shard_map/all_to_all | solution.py:29
  29.4 14.6 %all-to-all-done.1 = bf16[8,128,512]{2,1,0:T(8,128)(2,1)S(1)} async-done(((bf16[8,128,512]{2,1,0:T(8,128)(2,1)}), bf16[8,128,512]{2,1,0:T(8,128)(2,1)S(1)}, u32[]{:S(2)}, u32[]{:S(2)}) %all-to-all-start.1) | async-done | bytes 1048608 | tf_op jit(solution)/shard_map/all_to_all | solution.py:29
  44.0 0.0 copy-done.1
  44.0 1.3 shard_map.109
  45.2 7.6 %all-to-all-start.2 = ((bf16[16,64,224]{2,1,0:T(8,128)(2,1)}), bf16[16,64,224]{2,1,0:T(8,128)(2,1)S(1)}, u32[]{:S(2)}, u32[]{:S(2)}) async-start(bf16[16,64,224]{2,1,0:T(8,128)(2,1)} %shard_map.109), calls=%async_computation.2 | async-start | bytes 1048576 | tf_op jit(solution)/shard_map/all_to_all | solution.py:29
  52.8 0.8 fusion.21
  53.6 3.1 %collective-permute-start = (bf16[1792,128]{1,0:T(8,128)(2,1)S(1)}, bf16[1792,128]{1,0:T(8,128)(2,1)S(1)}, u32[]{:S(2)}, u32[]{:S(2)}) collective-permute-start(bf16[1792,128]{1,0:T(8,128)(2,1)S(1)} %get-tuple-element.43), channel_id=1, source_target_pairs={{0,192},{8,200},{16,208},{24,216},{32,224},{40,232},{48,240},{56,2... | collective-permute-start | bytes 1376264 | tf_op jit(solution)/shard_map/ppermute | solution.py:235
  56.7 0.1 convolution_convert_fusion.1
  56.8 0.1 eq.58
  57.0 0.1 fusion.9.select
  57.1 0.0 copy-start.4
  57.1 2.7 %dynamic-slice_bitcast_fusion = (bf16[224,1024]{1,0:T(8,128)(2,1)}, bf16[224,1024]{1,0:T(8,128)(2,1)}, bf16[224,1024]{1,0:T(8,128)(2,1)}, bf16[224,1024]{1,0:T(8,128)(2,1)S(1)}) fusion(bf16[1,224,4096]{2,1,0:T(8,128)(2,1)} %param.21, s32[]{:T(128)S(6)} %select_n.112, s32[]{:T(128)S(6)} %select_n.111, s32[]{:T(128)S(6)} %select_n.110, s32[]{:T(128)S(6)} %select_n.109), kind=kLoop, calls=%fused_computation.12 | loop fusion | bytes 3670032 | tf_op jit(solution)/shard_map/dynamic_slice | solution.py:232
  59.8 0.0 copy-done.4
  59.8 0.8 dynamic-slice_bitcast_fusion.4
  60.7 7.4 %collective-permute-done = bf16[1792,128]{1,0:T(8,128)(2,1)S(1)} collective-permute-done((bf16[1792,128]{1,0:T(8,128)(2,1)S(1)}, bf16[1792,128]{1,0:T(8,128)(2,1)S(1)}, u32[]{:S(2)}, u32[]{:S(2)}) %collective-permute-start) | collective-permute-done | bytes 458784 | tf_op jit(solution)/shard_map/ppermute | solution.py:235
  68.0 1.2 all-to-all-done.2.parts
  69.2 1.1 shard_map.110
  70.3 7.5 %all-to-all-start.3 = ((bf16[64,24,224]{2,1,0:T(8,128)(2,1)}), bf16[64,24,224]{2,1,0:T(8,128)(2,1)S(1)}, u32[]{:S(2)}, u32[]{:S(2)}) async-start(bf16[64,24,224]{2,1,0:T(8,128)(2,1)} %bitcast.17), calls=%async_computation.3 | async-start | bytes 1572864 | tf_op jit(solution)/shard_map/all_to_all | solution.py:29
  77.8 1.9 collective-permute-start.3
  79.8 0.1 reshape.118
  79.9 5.1 %collective-permute-start.4 = (bf16[224,1024]{1,0:T(8,128)(2,1)}, bf16[224,1024]{1,0:T(8,128)(2,1)}, u32[]{:S(2)}, u32[]{:S(2)}) collective-permute-start(bf16[224,1024]{1,0:T(8,128)(2,1)} %get-tuple-element.56), channel_id=1, source_target_pairs={{0,192},{8,200},{16,208},{24,216},{32,224},{40,232},{48,240},{56,2... | collective-permute-start | bytes 1376264 | tf_op jit(solution)/shard_map/ppermute | solution.py:235
  85.1 1.9 collective-permute-start.5
  87.0 4.5 %collective-permute-start.6 = (bf16[1792,128]{1,0:T(8,128)(2,1)}, bf16[1792,128]{1,0:T(8,128)(2,1)}, u32[]{:S(2)}, u32[]{:S(2)}) collective-permute-start(bf16[1792,128]{1,0:T(8,128)(2,1)} %get-tuple-element.61), channel_id=1, source_target_pairs={{0,128},{8,136},{16,144},{24,152},{32,160},{40,168},{48,176},{56,1... | collective-permute-start | bytes 1376264 | tf_op jit(solution)/shard_map/ppermute | solution.py:235
  91.5 10.7 %all-to-all-done.3 = bf16[64,24,224]{2,1,0:T(8,128)(2,1)S(1)} async-done(((bf16[64,24,224]{2,1,0:T(8,128)(2,1)}), bf16[64,24,224]{2,1,0:T(8,128)(2,1)S(1)}, u32[]{:S(2)}, u32[]{:S(2)}) %all-to-all-start.3) | async-done | bytes 688160 | tf_op jit(solution)/shard_map/all_to_all | solution.py:29
  102.2 0.1 fusion.29
  102.2 3.0 %collective-permute-start.1 = (bf16[2,384,224]{2,1,0:T(8,128)(2,1)S(1)}, bf16[2,384,224]{2,1,0:T(8,128)(2,1)S(1)}, u32[]{:S(2)}, u32[]{:S(2)}) collective-permute-start(bf16[2,384,224]{2,1,0:T(8,128)(2,1)S(1)} %bitcast.75), channel_id=1, source_target_pairs={{0,8},{8,16},{16,24},{24,32},{32,40},{40,48},{48,56},{56,0},{64,72... | collective-permute-start | bytes 1032200 | tf_op jit(solution)/shard_map/ppermute | solution.py:252
  105.2 0.0 collective-permute-done.3.block1
  105.2 4.1 %collective-permute-start.2 = (bf16[2,384,224]{2,1,0:T(8,128)(2,1)S(1)}, bf16[2,384,224]{2,1,0:T(8,128)(2,1)S(1)}, u32[]{:S(2)}, u32[]{:S(2)}) collective-permute-start(bf16[2,384,224]{2,1,0:T(8,128)(2,1)S(1)} %bitcast.74), channel_id=1, source_target_pairs={{0,56},{8,0},{16,8},{24,16},{32,24},{40,32},{48,40},{56,48},{64,12... | collective-permute-start | bytes 1032200 | tf_op jit(solution)/shard_map/ppermute | solution.py:253
  109.3 0.1 pad_add_fusion.place
  109.4 0.0 collective-permute-done.4.block3
  109.4 6.4 %collective-permute-done.1.before = bf16[2,384,224]{2,1,0:T(8,128)(2,1)S(1)} collective-permute-done((bf16[2,384,224]{2,1,0:T(8,128)(2,1)S(1)}, bf16[2,384,224]{2,1,0:T(8,128)(2,1)S(1)}, u32[]{:S(2)}, u32[]{:S(2)}) %collective-permute-start.1) | collective-permute-done | bytes 344096 | tf_op jit(solution)/shard_map/ppermute | solution.py:252
  115.9 2.3 %collective-permute-done.2.after = bf16[2,384,224]{2,1,0:T(8,128)(2,1)S(1)} collective-permute-done((bf16[2,384,224]{2,1,0:T(8,128)(2,1)S(1)}, bf16[2,384,224]{2,1,0:T(8,128)(2,1)S(1)}, u32[]{:S(2)}, u32[]{:S(2)}) %collective-permute-start.2) | collective-permute-done | bytes 344096 | tf_op jit(solution)/shard_map/ppermute | solution.py:253
  118.2 0.0 collective-permute-done.5
  118.2 0.0 collective-permute-done.6
  118.2 3.0 %shard_map.111 = bf16[4,400,128]{2,1,0:T(8,128)(2,1)S(1)} custom-call(s32[2]{0:T(128)S(1)} %pad_add_fusion.place, bf16[4,384,224]{2,1,0:T(8,128)(2,1)S(1)} %bitcast.67, bf16[2,384,224]{2,1,0:T(8,128)(2,1)S(1)} %collective-permute-done.1.before, bf16[2,384,224]{2,1,0:T(8,128)(2,1)S(1)} %collective-permute-done.2.after, f32[8,224]{1,0:T(8,128)S(1)} %pad_maximum_fusion.gain, ...), custom_call_target="tpu_custom_call" | custom-call | flops 704643072 | bytes 6291456 | tf_op jit(solution)/shard_map/pallas_call | solution.py:134
  121.1 10.9 %all_to_all.40 = bf16[4,400,128]{2,1,0:T(8,128)(2,1)S(1)} all-to-all(bf16[4,400,128]{2,1,0:T(8,128)(2,1)S(1)} %shard_map.111), channel_id=1, replica_groups=mesh['pool'=2,'x'=4,'zpair'=4,'member'=2,'tp'=8] {'x'}, dimensions={0} | all-to-all | bytes 819200 | tf_op jit(solution)/shard_map/all_to_all | solution.py:29
  132.0 0.1 convert_reduce_fusion
  132.1 0.1 multiply_convert_fusion
  132.3 1.0 broadcast_in_dim.79
  133.3 4.3 %all-to-all-start.5 = ((bf16[8,384,128]{2,1,0:T(8,128)(2,1)}), bf16[8,384,128]{2,1,0:T(8,128)(2,1)S(1)}, u32[]{:S(2)}, u32[]{:S(2)}) async-start(bf16[8,384,128]{2,1,0:T(8,128)(2,1)} %broadcast_in_dim.79), calls=%async_computation.5 | async-start | bytes 1572864 | tf_op jit(solution)/shard_map/all_to_all | solution.py:29
  137.6 3.0 %collective-permute-start.7 = (bf16[224,1024]{1,0:T(8,128)(2,1)S(1)}, bf16[224,1024]{1,0:T(8,128)(2,1)S(1)}, u32[]{:S(2)}, u32[]{:S(2)}) collective-permute-start(bf16[224,1024]{1,0:T(8,128)(2,1)S(1)} %copy-done.5), channel_id=1, source_target_pairs={{0,128},{8,136},{16,144},{24,152},{32,160},{40,168},{48,176},{56,1... | collective-permute-start | bytes 1376264 | tf_op jit(solution)/shard_map/ppermute | solution.py:235
  140.6 9.1 %collective-permute-done.7.block2 = bf16[224,1024]{1,0:T(8,128)(2,1)S(1)} collective-permute-done((bf16[224,1024]{1,0:T(8,128)(2,1)S(1)}, bf16[224,1024]{1,0:T(8,128)(2,1)S(1)}, u32[]{:S(2)}, u32[]{:S(2)}) %collective-permute-start.7) | collective-permute-done | bytes 458784 | tf_op jit(solution)/shard_map/ppermute | solution.py:235
  149.7 7.8 %all-to-all-done.5.act = bf16[8,384,128]{2,1,0:T(8,128)(2,1)S(1)} async-done(((bf16[8,384,128]{2,1,0:T(8,128)(2,1)}), bf16[8,384,128]{2,1,0:T(8,128)(2,1)S(1)}, u32[]{:S(2)}, u32[]{:S(2)}) %all-to-all-start.5) | async-done | bytes 786464 | tf_op jit(solution)/shard_map/all_to_all | solution.py:29
  157.5 2.2 %shard_map.112 = bf16[4,224,384]{2,1,0:T(8,128)(2,1)S(1)} custom-call(s32[2]{0:T(128)S(1)} %pad_add_fusion.place, bf16[8,384,128]{2,1,0:T(8,128)(2,1)S(1)} %all-to-all-done.5.act, bf16[224,1024]{1,0:T(8,128)(2,1)S(1)} %get-tuple-element.65.block0, bf16[224,1024]{1,0:T(8,128)(2,1)S(1)} %collective-permute-done.3.block1, ...), custom_call_target="tpu_custom_call" | custom-call | flops 704643072 | bytes 5242880 | tf_op jit(solution)/shard_map/pallas_call | solution.py:162
  159.7 11.3 %all_to_all.41 = bf16[4,224,384]{2,1,0:T(8,128)(2,1)S(1)} all-to-all(bf16[4,224,384]{2,1,0:T(8,128)(2,1)S(1)} %shard_map.112), channel_id=1, replica_groups=mesh['pool'=2,'x'=4,'zpair'=4,'member'=2,'tp'=8] {'x'}, dimensions={0} | all-to-all | bytes 1376256 | tf_op jit(solution)/shard_map/all_to_all | solution.py:29
  171.1 0.1 reduce_sum.42
  171.2 0.8 copy.13
  172.0 9.6 %all-to-all-start.7 = ((bf16[16,24,224]{2,1,0:T(8,128)(2,1)}), bf16[16,24,224]{2,1,0:T(8,128)(2,1)S(1)}, u32[]{:S(2)}, u32[]{:S(2)}) async-start(bf16[16,24,224]{2,1,0:T(8,128)(2,1)} %bitcast.27), calls=%async_computation.7 | async-start | bytes 393216 | tf_op jit(solution)/shard_map/all_to_all | solution.py:29
  181.6 0.8 fusion.22
  182.4 8.8 %all-to-all-done.7 = bf16[16,24,224]{2,1,0:T(8,128)(2,1)S(1)} async-done(((bf16[16,24,224]{2,1,0:T(8,128)(2,1)}), bf16[16,24,224]{2,1,0:T(8,128)(2,1)S(1)}, u32[]{:S(2)}, u32[]{:S(2)}) %all-to-all-start.7) | async-done | bytes 172064 | tf_op jit(solution)/shard_map/all_to_all | solution.py:29
  191.2 0.2 convolution_bitcast_fusion.1
  191.5 0.8 fusion.2
  (17 shorter events, 0.1 us)
Async XLA Ops:
  0.0 3.2 %copy-start = (bf16[32,32,256]{2,1,0:T(8,128)(2,1)S(1)}, bf16[32,32,256]{2,1,0:T(8,128)(2,1)}, u32[]{:S(2)}) copy-start(bf16[32,32,256]{2,1,0:T(8,128)(2,1)} %param.13) | copy-start | bytes 1572868
  0.0 14.7 %copy-start.3 = (bf16[1,7168,128]{2,1,0:T(8,128)(2,1)S(1)}, bf16[1,7168,128]{2,1,0:T(8,128)(2,1)}, u32[]{:S(2)}) copy-start(bf16[1,7168,128]{2,1,0:T(8,128)(2,1)} %param.20) | copy-start | bytes 5505028
  4.4 19.6 %all-to-all-start = ((bf16[4,32,512]{2,1,0:T(8,128)(2,1)}), bf16[4,32,512]{2,1,0:T(8,128)(2,1)S(1)}, u32[]{:S(2)}, u32[]{:S(2)}) async-start(bf16[4,32,512]{2,1,0:T(8,128)(2,1)} %broadcast_in_dim.76), calls=%async_computation | async-start | bytes 262144 | tf_op jit(solution)/shard_map/all_to_all | solution.py:29
  15.5 28.4 %copy-start.1 = (bf16[512,224]{0,1:T(8,128)(2,1)S(1)}, bf16[512,224]{0,1:T(8,128)(2,1)}, u32[]{:S(2)}) copy-start(bf16[512,224]{0,1:T(8,128)(2,1)} %param.15) | copy-start | bytes 688132
  25.0 18.9 %all-to-all-start.1 = ((bf16[8,128,512]{2,1,0:T(8,128)(2,1)}), bf16[8,128,512]{2,1,0:T(8,128)(2,1)S(1)}, u32[]{:S(2)}, u32[]{:S(2)}) async-start(bf16[8,128,512]{2,1,0:T(8,128)(2,1)} %broadcast_in_dim.78), calls=%async_computation.1 | async-start | bytes 2097152 | tf_op jit(solution)/shard_map/all_to_all | solution.py:29
  45.2 24.0 %all-to-all-start.2 = ((bf16[16,64,224]{2,1,0:T(8,128)(2,1)}), bf16[16,64,224]{2,1,0:T(8,128)(2,1)S(1)}, u32[]{:S(2)}, u32[]{:S(2)}) async-start(bf16[16,64,224]{2,1,0:T(8,128)(2,1)} %shard_map.109), calls=%async_computation.2 | async-start | bytes 1048576 | tf_op jit(solution)/shard_map/all_to_all | solution.py:29
  53.6 14.5 %collective-permute-start = (bf16[1792,128]{1,0:T(8,128)(2,1)S(1)}, bf16[1792,128]{1,0:T(8,128)(2,1)S(1)}, u32[]{:S(2)}, u32[]{:S(2)}) collective-permute-start(bf16[1792,128]{1,0:T(8,128)(2,1)S(1)} %get-tuple-element.43), channel_id=1, source_target_pairs={{0,192},{8,200},{16,208},{24,216},{32,224},{40,232},{48,240},{56,2... | collective-permute-start | bytes 1376264 | tf_op jit(solution)/shard_map/ppermute | solution.py:235
  57.1 2.7 %copy-start.4 = (bf16[1,7168,128]{2,1,0:T(8,128)(2,1)S(1)}, bf16[1,7168,128]{2,1,0:T(8,128)(2,1)}, u32[]{:S(2)}) copy-start(bf16[1,7168,128]{2,1,0:T(8,128)(2,1)} %param.20) | copy-start | bytes 5505028
  59.8 9.4 %copy-start.2 = (bf16[64,224]{1,0:T(8,128)(2,1)S(1)}, bf16[64,224]{1,0:T(8,128)(2,1)}, u32[]{:S(2)}) copy-start(bf16[64,224]{1,0:T(8,128)(2,1)} %residual.1) | copy-start | bytes 86020
  60.7 19.1 %copy-start.6 = (f32[7168]{0:T(1024)S(1)}, f32[7168]{0:T(1024)}, u32[]{:S(2)}) copy-start(f32[7168]{0:T(1024)} %param.17) | copy-start | bytes 86020
  70.3 31.9 %all-to-all-start.3 = ((bf16[64,24,224]{2,1,0:T(8,128)(2,1)}), bf16[64,24,224]{2,1,0:T(8,128)(2,1)S(1)}, u32[]{:S(2)}, u32[]{:S(2)}) async-start(bf16[64,24,224]{2,1,0:T(8,128)(2,1)} %bitcast.17), calls=%async_computation.3 | async-start | bytes 1572864 | tf_op jit(solution)/shard_map/all_to_all | solution.py:29
  77.8 27.4 %collective-permute-start.3 = (bf16[224,1024]{1,0:T(8,128)(2,1)}, bf16[224,1024]{1,0:T(8,128)(2,1)S(1)}, u32[]{:S(2)}, u32[]{:S(2)}) collective-permute-start(bf16[224,1024]{1,0:T(8,128)(2,1)} %get-tuple-element.55), channel_id=1, source_target_pairs={{0,64},{8,72},{16,80},{24,88},{32,96},{40,104},{48,112},{56,120},{... | collective-permute-start | bytes 1376264 | tf_op jit(solution)/shard_map/ppermute | solution.py:235
  79.9 29.5 %collective-permute-start.4 = (bf16[224,1024]{1,0:T(8,128)(2,1)}, bf16[224,1024]{1,0:T(8,128)(2,1)}, u32[]{:S(2)}, u32[]{:S(2)}) collective-permute-start(bf16[224,1024]{1,0:T(8,128)(2,1)} %get-tuple-element.56), channel_id=1, source_target_pairs={{0,192},{8,200},{16,208},{24,216},{32,224},{40,232},{48,240},{56,2... | collective-permute-start | bytes 1376264 | tf_op jit(solution)/shard_map/ppermute | solution.py:235
  85.1 33.1 %collective-permute-start.5 = (bf16[1792,128]{1,0:T(8,128)(2,1)}, bf16[1792,128]{1,0:T(8,128)(2,1)}, u32[]{:S(2)}, u32[]{:S(2)}) collective-permute-start(bf16[1792,128]{1,0:T(8,128)(2,1)} %get-tuple-element.60), channel_id=1, source_target_pairs={{0,64},{8,72},{16,80},{24,88},{32,96},{40,104},{48,112},{56,120},{... | collective-permute-start | bytes 1376264 | tf_op jit(solution)/shard_map/ppermute | solution.py:235
  87.0 31.2 %collective-permute-start.6 = (bf16[1792,128]{1,0:T(8,128)(2,1)}, bf16[1792,128]{1,0:T(8,128)(2,1)}, u32[]{:S(2)}, u32[]{:S(2)}) collective-permute-start(bf16[1792,128]{1,0:T(8,128)(2,1)} %get-tuple-element.61), channel_id=1, source_target_pairs={{0,128},{8,136},{16,144},{24,152},{32,160},{40,168},{48,176},{56,1... | collective-permute-start | bytes 1376264 | tf_op jit(solution)/shard_map/ppermute | solution.py:235
  102.2 13.6 %collective-permute-start.1 = (bf16[2,384,224]{2,1,0:T(8,128)(2,1)S(1)}, bf16[2,384,224]{2,1,0:T(8,128)(2,1)S(1)}, u32[]{:S(2)}, u32[]{:S(2)}) collective-permute-start(bf16[2,384,224]{2,1,0:T(8,128)(2,1)S(1)} %bitcast.75), channel_id=1, source_target_pairs={{0,8},{8,16},{16,24},{24,32},{32,40},{40,48},{48,56},{56,0},{64,72... | collective-permute-start | bytes 1032200 | tf_op jit(solution)/shard_map/ppermute | solution.py:252
  105.2 13.0 %collective-permute-start.2 = (bf16[2,384,224]{2,1,0:T(8,128)(2,1)S(1)}, bf16[2,384,224]{2,1,0:T(8,128)(2,1)S(1)}, u32[]{:S(2)}, u32[]{:S(2)}) collective-permute-start(bf16[2,384,224]{2,1,0:T(8,128)(2,1)S(1)} %bitcast.74), channel_id=1, source_target_pairs={{0,56},{8,0},{16,8},{24,16},{32,24},{40,32},{48,40},{56,48},{64,12... | collective-permute-start | bytes 1032200 | tf_op jit(solution)/shard_map/ppermute | solution.py:253
  132.1 5.5 %copy-start.5 = (bf16[224,1024]{1,0:T(8,128)(2,1)S(1)}, bf16[224,1024]{1,0:T(8,128)(2,1)}, u32[]{:S(2)}) copy-start(bf16[224,1024]{1,0:T(8,128)(2,1)} %get-tuple-element.67) | copy-start | bytes 1376260
  133.3 24.2 %all-to-all-start.5 = ((bf16[8,384,128]{2,1,0:T(8,128)(2,1)}), bf16[8,384,128]{2,1,0:T(8,128)(2,1)S(1)}, u32[]{:S(2)}, u32[]{:S(2)}) async-start(bf16[8,384,128]{2,1,0:T(8,128)(2,1)} %broadcast_in_dim.79), calls=%async_computation.5 | async-start | bytes 1572864 | tf_op jit(solution)/shard_map/all_to_all | solution.py:29
  137.6 12.1 %collective-permute-start.7 = (bf16[224,1024]{1,0:T(8,128)(2,1)S(1)}, bf16[224,1024]{1,0:T(8,128)(2,1)S(1)}, u32[]{:S(2)}, u32[]{:S(2)}) collective-permute-start(bf16[224,1024]{1,0:T(8,128)(2,1)S(1)} %copy-done.5), channel_id=1, source_target_pairs={{0,128},{8,136},{16,144},{24,152},{32,160},{40,168},{48,176},{56,1... | collective-permute-start | bytes 1376264 | tf_op jit(solution)/shard_map/ppermute | solution.py:235
  172.0 19.2 %all-to-all-start.7 = ((bf16[16,24,224]{2,1,0:T(8,128)(2,1)}), bf16[16,24,224]{2,1,0:T(8,128)(2,1)S(1)}, u32[]{:S(2)}, u32[]{:S(2)}) async-start(bf16[16,24,224]{2,1,0:T(8,128)(2,1)} %bitcast.27), calls=%async_computation.7 | async-start | bytes 393216 | tf_op jit(solution)/shard_map/all_to_all | solution.py:29

commit v13 on v12

--- a/solution.py
+++ b/solution.py
@@ -242,7 +242,7 @@
         (projected, up1, up3, up_weight, down_weight)
     )
     projected = exchange(projected, ("pool", "tp"))
-    up = [up_cut(0), up1, up_cut(2), along(up3, 3)]
+    up = [up_cut(0), up1, up_cut(2), up3]
     down = [down_cut(step) for step in range(NX)]
     projected, up, down = lax.optimization_barrier((projected, up, down))
     slot_rows = head_sum(projected, residual, select)
@@ -251,7 +251,8 @@
     same = same.reshape(NZ, slots, columns)
     before = lax.ppermute(same[: NZ // 2], GRP, turns(1))
     after = lax.ppermute(same[NZ // 2 :], GRP, turns(-1))
-    up[1], up[2], down[1], down[3] = along(up[1], 1), along(up[2], 2), along(down[1], 1), along(down[3], 3)
+    up[1:] = [along(up[step], step) for step in range(1, NX)]
+    down[1], down[3] = along(down[1], 1), along(down[3], 3)
     before, after, down[1], down[3] = lax.optimization_barrier((before, after, down[1], down[3]))
     up = [w.reshape(NZ, PAIR, columns, units) for w in up]
     gain = norm_gain.reshape(NX, NZ, PAIR, columns)

time: 193 us -> 190 us (0.984)
  starting transfers between devices: 70.3 us -> 68.3 us
    all_to_all x6, waiting for transfers between devices: 51.5 us -> 58.7 us  [exchange(): return lax.all_to_all(value, axis, 0, 0, tiled=True)]
    ppermute x6, waiting for transfers between devices: 16.5 us -> 9.77 us  [along(): return lax.ppermute(block, GRP, moves(step, 0))]
    all_to_all x6, starting transfers between devices: 43.6 us -> 41.4 us  [exchange(): return lax.all_to_all(value, axis, 0, 0, tiled=True)]
  transfers between devices with their start and end apart: 14 -> 14, of which waited for: 10 -> 10; matrix products, arithmetic and copies ran while one was open for 3% -> 4% of each run, Pallas kernels for 0% -> 0%
where the time goes in v13:
time: 190 us; the launch traced here: 189 us
  waiting for transfers between devices  75.7 us (40%)
  starting transfers between devices  68.3 us (36%)
  blocking collectives  21.8 us (11%)
  local copies, waits for them, and re-layouts  10.7 us (6%)
  Pallas kernels  7.23 us (4%)
  matrix products  3.03 us (2%)
    all_to_all x6, waiting for transfers between devices, exchange(): return lax.all_to_all(value, axis, 0, 0, tiled=True)  58.7 us
    all_to_all x6, starting transfers between devices, exchange(): return lax.all_to_all(value, axis, 0, 0, tiled=True)  41.4 us
    all_to_all x2, blocking collectives, exchange(): return lax.all_to_all(value, axis, 0, 0, tiled=True)  21.8 us
    ppermute x6, starting transfers between devices, along(): return lax.ppermute(block, GRP, moves(step, 0))  19.1 us
    ppermute x6, waiting for transfers between devices, along(): return lax.ppermute(block, GRP, moves(step, 0))  9.77 us
    ppermute x1, waiting for transfers between devices, shards(): before = lax.ppermute(same[:NZ // 2], GRP, turns(1))  4.94 us
    ppermute x1, starting transfers between devices, shards(): after = lax.ppermute(same[NZ // 2:], GRP, turns(-1))  4.89 us
  transfers between devices with their start and end apart: 14, of which 10 were waited for; matrix products, arithmetic and copies ran while one was open for 4% of the time, Pallas kernels for 0%

profile of v13, /device:TPU:8, one launch (start us, length us, event | category | flops | bytes accessed | tf_op | source)
XLA Modules:
  0.0 188.6 jit_solution(5153247574703926752)
XLA Ops:
  0.0 0.0 copy-start
  0.0 0.9 iota_compare_fusion.4
  0.9 0.8 reshape.114
  1.7 1.3 fusion.5
  2.9 0.2 fusion.30
  3.2 0.0 copy-done
  3.2 0.6 convolution_convert_fusion
  3.7 0.7 broadcast_in_dim.76
  4.4 10.3 %all-to-all-start = ((bf16[4,32,512]{2,1,0:T(8,128)(2,1)}), bf16[4,32,512]{2,1,0:T(8,128)(2,1)S(1)}, u32[]{:S(2)}, u32[]{:S(2)}) async-start(bf16[4,32,512]{2,1,0:T(8,128)(2,1)} %broadcast_in_dim.76), calls=%async_computation | async-start | bytes 262144 | tf_op jit(solution)/shard_map/all_to_all | solution.py:29
  14.7 1.0 dynamic-slice_bitcast_fusion.6
  15.7 8.3 %all-to-all-done = bf16[4,32,512]{2,1,0:T(8,128)(2,1)S(1)} async-done(((bf16[4,32,512]{2,1,0:T(8,128)(2,1)}), bf16[4,32,512]{2,1,0:T(8,128)(2,1)S(1)}, u32[]{:S(2)}, u32[]{:S(2)}) %all-to-all-start) | async-done | bytes 131104 | tf_op jit(solution)/shard_map/all_to_all | solution.py:29
  24.0 1.1 broadcast_in_dim.78
  25.1 4.3 %all-to-all-start.1 = ((bf16[8,128,512]{2,1,0:T(8,128)(2,1)}), bf16[8,128,512]{2,1,0:T(8,128)(2,1)S(1)}, u32[]{:S(2)}, u32[]{:S(2)}) async-start(bf16[8,128,512]{2,1,0:T(8,128)(2,1)} %broadcast_in_dim.78), calls=%async_computation.1 | async-start | bytes 2097152 | tf_op jit(solution)/shard_map/all_to_all | solution.py:29
  29.4 14.6 %all-to-all-done.1 = bf16[8,128,512]{2,1,0:T(8,128)(2,1)S(1)} async-done(((bf16[8,128,512]{2,1,0:T(8,128)(2,1)}), bf16[8,128,512]{2,1,0:T(8,128)(2,1)S(1)}, u32[]{:S(2)}, u32[]{:S(2)}) %all-to-all-start.1) | async-done | bytes 1048608 | tf_op jit(solution)/shard_map/all_to_all | solution.py:29
  44.0 0.0 copy-done.1
  44.0 1.2 shard_map.109
  45.3 7.6 %all-to-all-start.2 = ((bf16[16,64,224]{2,1,0:T(8,128)(2,1)}), bf16[16,64,224]{2,1,0:T(8,128)(2,1)S(1)}, u32[]{:S(2)}, u32[]{:S(2)}) async-start(bf16[16,64,224]{2,1,0:T(8,128)(2,1)} %shard_map.109), calls=%async_computation.2 | async-start | bytes 1048576 | tf_op jit(solution)/shard_map/all_to_all | solution.py:29
  52.8 0.1 eq.58
  52.9 0.8 fusion.21
  53.7 0.1 convolution_convert_fusion.1
  53.9 0.1 fusion.9.select
  54.0 0.0 copy-start.4
  54.0 2.7 %dynamic-slice_bitcast_fusion = (bf16[224,1024]{1,0:T(8,128)(2,1)}, bf16[224,1024]{1,0:T(8,128)(2,1)}, bf16[224,1024]{1,0:T(8,128)(2,1)}, bf16[224,1024]{1,0:T(8,128)(2,1)S(1)}) fusion(bf16[1,224,4096]{2,1,0:T(8,128)(2,1)} %param.21, s32[]{:T(128)S(6)} %select_n.112, s32[]{:T(128)S(6)} %select_n.111, s32[]{:T(128)S(6)} %select_n.110, s32[]{:T(128)S(6)} %select_n.109), kind=kLoop, calls=%fused_computation.12 | loop fusion | bytes 3670032 | tf_op jit(solution)/shard_map/dynamic_slice | solution.py:232
  56.7 0.8 dynamic-slice_bitcast_fusion.4
  57.5 11.7 %all-to-all-done.2.parts = bf16[16,64,224]{2,1,0:T(8,128)(2,1)S(1)} async-done(((bf16[16,64,224]{2,1,0:T(8,128)(2,1)}), bf16[16,64,224]{2,1,0:T(8,128)(2,1)S(1)}, u32[]{:S(2)}, u32[]{:S(2)}) %all-to-all-start.2) | async-done | bytes 458784 | tf_op jit(solution)/shard_map/all_to_all | solution.py:29
  69.2 0.0 copy-done.2
  69.2 1.2 shard_map.110
  70.4 5.3 %all-to-all-start.3 = ((bf16[64,24,224]{2,1,0:T(8,128)(2,1)}), bf16[64,24,224]{2,1,0:T(8,128)(2,1)S(1)}, u32[]{:S(2)}, u32[]{:S(2)}) async-start(bf16[64,24,224]{2,1,0:T(8,128)(2,1)} %bitcast.17), calls=%async_computation.3 | async-start | bytes 1572864 | tf_op jit(solution)/shard_map/all_to_all | solution.py:29
  75.6 1.9 %collective-permute-start.2 = (bf16[224,1024]{1,0:T(8,128)(2,1)}, bf16[224,1024]{1,0:T(8,128)(2,1)S(1)}, u32[]{:S(2)}, u32[]{:S(2)}) collective-permute-start(bf16[224,1024]{1,0:T(8,128)(2,1)} %get-tuple-element.55), channel_id=1, source_target_pairs={{0,64},{8,72},{16,80},{24,88},{32,96},{40,104},{48,112},{56,120},{... | collective-permute-start | bytes 1376264 | tf_op jit(solution)/shard_map/ppermute | solution.py:235
  77.6 5.1 %collective-permute-start.3 = (bf16[224,1024]{1,0:T(8,128)(2,1)}, bf16[224,1024]{1,0:T(8,128)(2,1)S(1)}, u32[]{:S(2)}, u32[]{:S(2)}) collective-permute-start(bf16[224,1024]{1,0:T(8,128)(2,1)} %get-tuple-element.56), channel_id=1, source_target_pairs={{0,192},{8,200},{16,208},{24,216},{32,224},{40,232},{48,240},{56,2... | collective-permute-start | bytes 1376264 | tf_op jit(solution)/shard_map/ppermute | solution.py:235
  82.7 0.1 reshape.118
  82.9 1.9 %collective-permute-start.4 = (bf16[1792,128]{1,0:T(8,128)(2,1)}, bf16[1792,128]{1,0:T(8,128)(2,1)}, u32[]{:S(2)}, u32[]{:S(2)}) collective-permute-start(bf16[1792,128]{1,0:T(8,128)(2,1)} %get-tuple-element.60), channel_id=1, source_target_pairs={{0,64},{8,72},{16,80},{24,88},{32,96},{40,104},{48,112},{56,120},{... | collective-permute-start | bytes 1376264 | tf_op jit(solution)/shard_map/ppermute | solution.py:235
  84.8 3.4 %collective-permute-start.5 = (bf16[1792,128]{1,0:T(8,128)(2,1)}, bf16[1792,128]{1,0:T(8,128)(2,1)}, u32[]{:S(2)}, u32[]{:S(2)}) collective-permute-start(bf16[1792,128]{1,0:T(8,128)(2,1)} %get-tuple-element.61), channel_id=1, source_target_pairs={{0,128},{8,136},{16,144},{24,152},{32,160},{40,168},{48,176},{56,1... | collective-permute-start | bytes 1376264 | tf_op jit(solution)/shard_map/ppermute | solution.py:235
  88.2 3.7 %collective-permute-start.6 = (bf16[1792,128]{1,0:T(8,128)(2,1)}, bf16[1792,128]{1,0:T(8,128)(2,1)}, u32[]{:S(2)}, u32[]{:S(2)}) collective-permute-start(bf16[1792,128]{1,0:T(8,128)(2,1)} %get-tuple-element.62), channel_id=1, source_target_pairs={{0,192},{8,200},{16,208},{24,216},{32,224},{40,232},{48,240},{56,2... | collective-permute-start | bytes 1376264 | tf_op jit(solution)/shard_map/ppermute | solution.py:235
  91.9 8.1 %all-to-all-done.3 = bf16[64,24,224]{2,1,0:T(8,128)(2,1)S(1)} async-done(((bf16[64,24,224]{2,1,0:T(8,128)(2,1)}), bf16[64,24,224]{2,1,0:T(8,128)(2,1)S(1)}, u32[]{:S(2)}, u32[]{:S(2)}) %all-to-all-start.3) | async-done | bytes 688160 | tf_op jit(solution)/shard_map/all_to_all | solution.py:29
  100.0 0.1 fusion.29
  100.0 0.0 collective-permute-done.2.block1
  100.1 3.0 %collective-permute-start = (bf16[2,384,224]{2,1,0:T(8,128)(2,1)S(1)}, bf16[2,384,224]{2,1,0:T(8,128)(2,1)S(1)}, u32[]{:S(2)}, u32[]{:S(2)}) collective-permute-start(bf16[2,384,224]{2,1,0:T(8,128)(2,1)S(1)} %bitcast.74), channel_id=1, source_target_pairs={{0,8},{8,16},{16,24},{24,32},{32,40},{40,48},{48,56},{56,0},{64,72... | collective-permute-start | bytes 1032200 | tf_op jit(solution)/shard_map/ppermute | solution.py:252
  103.0 0.7 collective-permute-done.3.block3
  103.7 4.9 %collective-permute-start.1 = (bf16[2,384,224]{2,1,0:T(8,128)(2,1)S(1)}, bf16[2,384,224]{2,1,0:T(8,128)(2,1)S(1)}, u32[]{:S(2)}, u32[]{:S(2)}) collective-permute-start(bf16[2,384,224]{2,1,0:T(8,128)(2,1)S(1)} %bitcast.73), channel_id=1, source_target_pairs={{0,56},{8,0},{16,8},{24,16},{32,24},{40,32},{48,40},{56,48},{64,12... | collective-permute-start | bytes 1032200 | tf_op jit(solution)/shard_map/ppermute | solution.py:253
  108.6 0.1 pad_add_fusion.place
  108.7 4.9 %collective-permute-done.before = bf16[2,384,224]{2,1,0:T(8,128)(2,1)S(1)} collective-permute-done((bf16[2,384,224]{2,1,0:T(8,128)(2,1)S(1)}, bf16[2,384,224]{2,1,0:T(8,128)(2,1)S(1)}, u32[]{:S(2)}, u32[]{:S(2)}) %collective-permute-start) | collective-permute-done | bytes 344096 | tf_op jit(solution)/shard_map/ppermute | solution.py:252
  113.7 2.3 %collective-permute-done.1.after = bf16[2,384,224]{2,1,0:T(8,128)(2,1)S(1)} collective-permute-done((bf16[2,384,224]{2,1,0:T(8,128)(2,1)S(1)}, bf16[2,384,224]{2,1,0:T(8,128)(2,1)S(1)}, u32[]{:S(2)}, u32[]{:S(2)}) %collective-permute-start.1) | collective-permute-done | bytes 344096 | tf_op jit(solution)/shard_map/ppermute | solution.py:253
  116.0 0.0 collective-permute-done.4
  116.0 0.0 collective-permute-done.5
  116.0 0.0 collective-permute-done.6
  116.0 3.1 %shard_map.111 = bf16[4,400,128]{2,1,0:T(8,128)(2,1)S(1)} custom-call(s32[2]{0:T(128)S(1)} %pad_add_fusion.place, bf16[4,384,224]{2,1,0:T(8,128)(2,1)S(1)} %bitcast.67, bf16[2,384,224]{2,1,0:T(8,128)(2,1)S(1)} %collective-permute-done.before, bf16[2,384,224]{2,1,0:T(8,128)(2,1)S(1)} %collective-permute-done.1.after, f32[8,224]{1,0:T(8,128)S(1)} %pad_maximum_fusion.gain, ...), custom_call_target="tpu_custom_call" | custom-call | flops 704643072 | bytes 6291456 | tf_op jit(solution)/shard_map/pallas_call | solution.py:134
  119.1 10.5 %all_to_all.40 = bf16[4,400,128]{2,1,0:T(8,128)(2,1)S(1)} all-to-all(bf16[4,400,128]{2,1,0:T(8,128)(2,1)S(1)} %shard_map.111), channel_id=1, replica_groups=mesh['pool'=2,'x'=4,'zpair'=4,'member'=2,'tp'=8] {'x'}, dimensions={0} | all-to-all | bytes 819200 | tf_op jit(solution)/shard_map/all_to_all | solution.py:29
  129.6 0.1 convert_reduce_fusion
  129.6 0.1 multiply_convert_fusion
  129.8 1.0 broadcast_in_dim.79
  130.8 6.7 %all-to-all-start.5 = ((bf16[8,384,128]{2,1,0:T(8,128)(2,1)}), bf16[8,384,128]{2,1,0:T(8,128)(2,1)S(1)}, u32[]{:S(2)}, u32[]{:S(2)}) async-start(bf16[8,384,128]{2,1,0:T(8,128)(2,1)} %broadcast_in_dim.79), calls=%async_computation.5 | async-start | bytes 1572864 | tf_op jit(solution)/shard_map/all_to_all | solution.py:29
  137.5 3.0 %collective-permute-start.7 = (bf16[224,1024]{1,0:T(8,128)(2,1)}, bf16[224,1024]{1,0:T(8,128)(2,1)S(1)}, u32[]{:S(2)}, u32[]{:S(2)}) collective-permute-start(bf16[224,1024]{1,0:T(8,128)(2,1)} %get-tuple-element.67), channel_id=1, source_target_pairs={{0,128},{8,136},{16,144},{24,152},{32,160},{40,168},{48,176},{56,1... | collective-permute-start | bytes 1376264 | tf_op jit(solution)/shard_map/ppermute | solution.py:235
  140.5 9.0 %collective-permute-done.7.block2 = bf16[224,1024]{1,0:T(8,128)(2,1)S(1)} collective-permute-done((bf16[224,1024]{1,0:T(8,128)(2,1)}, bf16[224,1024]{1,0:T(8,128)(2,1)S(1)}, u32[]{:S(2)}, u32[]{:S(2)}) %collective-permute-start.7) | collective-permute-done | bytes 458784 | tf_op jit(solution)/shard_map/ppermute | solution.py:235
  149.5 7.2 %all-to-all-done.5.act = bf16[8,384,128]{2,1,0:T(8,128)(2,1)S(1)} async-done(((bf16[8,384,128]{2,1,0:T(8,128)(2,1)}), bf16[8,384,128]{2,1,0:T(8,128)(2,1)S(1)}, u32[]{:S(2)}, u32[]{:S(2)}) %all-to-all-start.5) | async-done | bytes 786464 | tf_op jit(solution)/shard_map/all_to_all | solution.py:29
  156.7 1.7 shard_map.112
  158.4 11.3 %all_to_all.41 = bf16[4,224,384]{2,1,0:T(8,128)(2,1)S(1)} all-to-all(bf16[4,224,384]{2,1,0:T(8,128)(2,1)S(1)} %shard_map.112), channel_id=1, replica_groups=mesh['pool'=2,'x'=4,'zpair'=4,'member'=2,'tp'=8] {'x'}, dimensions={0} | all-to-all | bytes 1376256 | tf_op jit(solution)/shard_map/all_to_all | solution.py:29
  169.8 0.1 reduce_sum.42
  169.9 0.8 copy.13
  170.7 7.2 %all-to-all-start.7 = ((bf16[16,24,224]{2,1,0:T(8,128)(2,1)}), bf16[16,24,224]{2,1,0:T(8,128)(2,1)S(1)}, u32[]{:S(2)}, u32[]{:S(2)}) async-start(bf16[16,24,224]{2,1,0:T(8,128)(2,1)} %bitcast.27), calls=%async_computation.7 | async-start | bytes 393216 | tf_op jit(solution)/shard_map/all_to_all | solution.py:29
  178.0 0.8 fusion.22
  178.7 8.8 %all-to-all-done.7 = bf16[16,24,224]{2,1,0:T(8,128)(2,1)S(1)} async-done(((bf16[16,24,224]{2,1,0:T(8,128)(2,1)}), bf16[16,24,224]{2,1,0:T(8,128)(2,1)S(1)}, u32[]{:S(2)}, u32[]{:S(2)}) %all-to-all-start.7) | async-done | bytes 172064 | tf_op jit(solution)/shard_map/all_to_all | solution.py:29
  187.6 0.2 convolution_bitcast_fusion.1
  187.8 0.8 fusion.2
  (15 shorter events, 0.1 us)
Async XLA Ops:
  0.0 3.2 %copy-start = (bf16[32,32,256]{2,1,0:T(8,128)(2,1)S(1)}, bf16[32,32,256]{2,1,0:T(8,128)(2,1)}, u32[]{:S(2)}) copy-start(bf16[32,32,256]{2,1,0:T(8,128)(2,1)} %param.13) | copy-start | bytes 1572868
  0.0 14.7 %copy-start.3 = (bf16[1,7168,128]{2,1,0:T(8,128)(2,1)S(1)}, bf16[1,7168,128]{2,1,0:T(8,128)(2,1)}, u32[]{:S(2)}) copy-start(bf16[1,7168,128]{2,1,0:T(8,128)(2,1)} %param.20) | copy-start | bytes 5505028
  4.4 19.6 %all-to-all-start = ((bf16[4,32,512]{2,1,0:T(8,128)(2,1)}), bf16[4,32,512]{2,1,0:T(8,128)(2,1)S(1)}, u32[]{:S(2)}, u32[]{:S(2)}) async-start(bf16[4,32,512]{2,1,0:T(8,128)(2,1)} %broadcast_in_dim.76), calls=%async_computation | async-start | bytes 262144 | tf_op jit(solution)/shard_map/all_to_all | solution.py:29
  15.7 28.3 %copy-start.1 = (bf16[512,224]{0,1:T(8,128)(2,1)S(1)}, bf16[512,224]{0,1:T(8,128)(2,1)}, u32[]{:S(2)}) copy-start(bf16[512,224]{0,1:T(8,128)(2,1)} %param.15) | copy-start | bytes 688132
  25.1 18.9 %all-to-all-start.1 = ((bf16[8,128,512]{2,1,0:T(8,128)(2,1)}), bf16[8,128,512]{2,1,0:T(8,128)(2,1)S(1)}, u32[]{:S(2)}, u32[]{:S(2)}) async-start(bf16[8,128,512]{2,1,0:T(8,128)(2,1)} %broadcast_in_dim.78), calls=%async_computation.1 | async-start | bytes 2097152 | tf_op jit(solution)/shard_map/all_to_all | solution.py:29
  45.3 24.0 %all-to-all-start.2 = ((bf16[16,64,224]{2,1,0:T(8,128)(2,1)}), bf16[16,64,224]{2,1,0:T(8,128)(2,1)S(1)}, u32[]{:S(2)}, u32[]{:S(2)}) async-start(bf16[16,64,224]{2,1,0:T(8,128)(2,1)} %shard_map.109), calls=%async_computation.2 | async-start | bytes 1048576 | tf_op jit(solution)/shard_map/all_to_all | solution.py:29
  54.0 2.7 %copy-start.4 = (bf16[1,7168,128]{2,1,0:T(8,128)(2,1)S(1)}, bf16[1,7168,128]{2,1,0:T(8,128)(2,1)}, u32[]{:S(2)}) copy-start(bf16[1,7168,128]{2,1,0:T(8,128)(2,1)} %param.20) | copy-start | bytes 5505028
  56.7 12.5 %copy-start.2 = (bf16[64,224]{1,0:T(8,128)(2,1)S(1)}, bf16[64,224]{1,0:T(8,128)(2,1)}, u32[]{:S(2)}) copy-start(bf16[64,224]{1,0:T(8,128)(2,1)} %residual.1) | copy-start | bytes 86020
  57.5 25.2 %copy-start.5 = (f32[7168]{0:T(1024)S(1)}, f32[7168]{0:T(1024)}, u32[]{:S(2)}) copy-start(f32[7168]{0:T(1024)} %param.17) | copy-start | bytes 86020
  70.4 29.6 %all-to-all-start.3 = ((bf16[64,24,224]{2,1,0:T(8,128)(2,1)}), bf16[64,24,224]{2,1,0:T(8,128)(2,1)S(1)}, u32[]{:S(2)}, u32[]{:S(2)}) async-start(bf16[64,24,224]{2,1,0:T(8,128)(2,1)} %bitcast.17), calls=%async_computation.3 | async-start | bytes 1572864 | tf_op jit(solution)/shard_map/all_to_all | solution.py:29
  75.6 24.4 %collective-permute-start.2 = (bf16[224,1024]{1,0:T(8,128)(2,1)}, bf16[224,1024]{1,0:T(8,128)(2,1)S(1)}, u32[]{:S(2)}, u32[]{:S(2)}) collective-permute-start(bf16[224,1024]{1,0:T(8,128)(2,1)} %get-tuple-element.55), channel_id=1, source_target_pairs={{0,64},{8,72},{16,80},{24,88},{32,96},{40,104},{48,112},{56,120},{... | collective-permute-start | bytes 1376264 | tf_op jit(solution)/shard_map/ppermute | solution.py:235
  77.6 26.2 %collective-permute-start.3 = (bf16[224,1024]{1,0:T(8,128)(2,1)}, bf16[224,1024]{1,0:T(8,128)(2,1)S(1)}, u32[]{:S(2)}, u32[]{:S(2)}) collective-permute-start(bf16[224,1024]{1,0:T(8,128)(2,1)} %get-tuple-element.56), channel_id=1, source_target_pairs={{0,192},{8,200},{16,208},{24,216},{32,224},{40,232},{48,240},{56,2... | collective-permute-start | bytes 1376264 | tf_op jit(solution)/shard_map/ppermute | solution.py:235
  82.9 33.1 %collective-permute-start.4 = (bf16[1792,128]{1,0:T(8,128)(2,1)}, bf16[1792,128]{1,0:T(8,128)(2,1)}, u32[]{:S(2)}, u32[]{:S(2)}) collective-permute-start(bf16[1792,128]{1,0:T(8,128)(2,1)} %get-tuple-element.60), channel_id=1, source_target_pairs={{0,64},{8,72},{16,80},{24,88},{32,96},{40,104},{48,112},{56,120},{... | collective-permute-start | bytes 1376264 | tf_op jit(solution)/shard_map/ppermute | solution.py:235
  84.8 31.2 %collective-permute-start.5 = (bf16[1792,128]{1,0:T(8,128)(2,1)}, bf16[1792,128]{1,0:T(8,128)(2,1)}, u32[]{:S(2)}, u32[]{:S(2)}) collective-permute-start(bf16[1792,128]{1,0:T(8,128)(2,1)} %get-tuple-element.61), channel_id=1, source_target_pairs={{0,128},{8,136},{16,144},{24,152},{32,160},{40,168},{48,176},{56,1... | collective-permute-start | bytes 1376264 | tf_op jit(solution)/shard_map/ppermute | solution.py:235
  88.2 27.8 %collective-permute-start.6 = (bf16[1792,128]{1,0:T(8,128)(2,1)}, bf16[1792,128]{1,0:T(8,128)(2,1)}, u32[]{:S(2)}, u32[]{:S(2)}) collective-permute-start(bf16[1792,128]{1,0:T(8,128)(2,1)} %get-tuple-element.62), channel_id=1, source_target_pairs={{0,192},{8,200},{16,208},{24,216},{32,224},{40,232},{48,240},{56,2... | collective-permute-start | bytes 1376264 | tf_op jit(solution)/shard_map/ppermute | solution.py:235
  100.1 13.6 %collective-permute-start = (bf16[2,384,224]{2,1,0:T(8,128)(2,1)S(1)}, bf16[2,384,224]{2,1,0:T(8,128)(2,1)S(1)}, u32[]{:S(2)}, u32[]{:S(2)}) collective-permute-start(bf16[2,384,224]{2,1,0:T(8,128)(2,1)S(1)} %bitcast.74), channel_id=1, source_target_pairs={{0,8},{8,16},{16,24},{24,32},{32,40},{40,48},{48,56},{56,0},{64,72... | collective-permute-start | bytes 1032200 | tf_op jit(solution)/shard_map/ppermute | solution.py:252
  103.7 12.2 %collective-permute-start.1 = (bf16[2,384,224]{2,1,0:T(8,128)(2,1)S(1)}, bf16[2,384,224]{2,1,0:T(8,128)(2,1)S(1)}, u32[]{:S(2)}, u32[]{:S(2)}) collective-permute-start(bf16[2,384,224]{2,1,0:T(8,128)(2,1)S(1)} %bitcast.73), channel_id=1, source_target_pairs={{0,56},{8,0},{16,8},{24,16},{32,24},{40,32},{48,40},{56,48},{64,12... | collective-permute-start | bytes 1032200 | tf_op jit(solution)/shard_map/ppermute | solution.py:253
  130.8 25.9 %all-to-all-start.5 = ((bf16[8,384,128]{2,1,0:T(8,128)(2,1)}), bf16[8,384,128]{2,1,0:T(8,128)(2,1)S(1)}, u32[]{:S(2)}, u32[]{:S(2)}) async-start(bf16[8,384,128]{2,1,0:T(8,128)(2,1)} %broadcast_in_dim.79), calls=%async_computation.5 | async-start | bytes 1572864 | tf_op jit(solution)/shard_map/all_to_all | solution.py:29
  137.5 12.1 %collective-permute-start.7 = (bf16[224,1024]{1,0:T(8,128)(2,1)}, bf16[224,1024]{1,0:T(8,128)(2,1)S(1)}, u32[]{:S(2)}, u32[]{:S(2)}) collective-permute-start(bf16[224,1024]{1,0:T(8,128)(2,1)} %get-tuple-element.67), channel_id=1, source_target_pairs={{0,128},{8,136},{16,144},{24,152},{32,160},{40,168},{48,176},{56,1... | collective-permute-start | bytes 1376264 | tf_op jit(solution)/shard_map/ppermute | solution.py:235
  170.7 16.8 %all-to-all-start.7 = ((bf16[16,24,224]{2,1,0:T(8,128)(2,1)}), bf16[16,24,224]{2,1,0:T(8,128)(2,1)S(1)}, u32[]{:S(2)}, u32[]{:S(2)}) async-start(bf16[16,24,224]{2,1,0:T(8,128)(2,1)} %bitcast.27), calls=%async_computation.7 | async-start | bytes 393216 | tf_op jit(solution)/shard_map/all_to_all | solution.py:29

commit v14 on v13

--- a/solution.py
+++ b/solution.py
@@ -1,3 +1,5 @@
+import functools
+
 import jax
 import jax.numpy as jnp
 from jax import lax
@@ -143,6 +145,35 @@
     )(place, *rows, gain, *blocks)
 
 
+def act_kernel(parts, out, *, width):
+    units = parts.shape[2]
+    slots = parts.shape[1] - 16
+    count = slots // units
+    total = 0.0
+    for i in range(parts.shape[0]):
+        total += parts[i].astype(F32)
+    tail = total[slots:]
+    for i in range(count):
+        squares = tail[i : i + 1] + tail[count + i : count + i + 1]
+        scale = lax.rsqrt(jnp.broadcast_to(squares, (units, units)).T / width + 1e-06)
+        value = total[i * units : (i + 1) * units] * scale
+        value = (value / (1.0 + jnp.exp(-value))).astype(BF16)
+        for z in range(out.shape[0]):
+            out[z, i * units : (i + 1) * units] = value
+
+
+def activate(parts, width):
+    slots, units = parts.shape[1] - 16, parts.shape[2]
+    return pl.pallas_call(
+        functools.partial(act_kernel, width=width),
+        out_shape=jax.ShapeDtypeStruct((8, slots, units), BF16),
+        in_specs=whole(1),
+        out_specs=whole(1)[0],
+        compiler_params=PARAMS,
+        cost_estimate=pl.CostEstimate(flops=8 * slots * units, bytes_accessed=2**20, transcendentals=slots * units),
+    )(parts)
+
+
 def down_kernel(place, act, block0, block1, block2, block3, out):
     x_index = place[0]
     count, units = act.shape[0], act.shape[2]
@@ -261,15 +292,10 @@
     gain = jnp.concatenate(gain)
     place = jnp.stack([x_index, member]).astype(jnp.int32)
     partial_up = up_product(place, (same, before, after), gain, up)
-    total_up = jnp.sum(exchange(partial_up, "x").astype(F32), axis=0)
-    count = slots // units
-    squares = (total_up[slots : slots + count] + total_up[slots + count : slots + 2 * count]).reshape(slots, 1)
-    scale = lax.rsqrt(squares / width + 1e-06)
-    act = jax.nn.silu(total_up[:slots] * scale).astype(BF16)
-
+    act = activate(exchange(partial_up, "x"), width)
     act, down[2] = lax.optimization_barrier((act, down[2]))
     down[2] = along(down[2], 2)
-    act = spread(act, 8, ("zpair", "member"))
+    act = exchange(act, ("zpair", "member"))
     partial_out = exchange(down_product(place, act, down), "x")
     expert_out = jnp.sum(partial_out.astype(F32), axis=0).astype(BF16).T
     returned = exchange(expert_out.reshape(experts, slot_cap, columns), ("pool", "tp"))

time: 190 us -> 190 us (level)
  no operation moved by 1% of the time
where the time goes in v14:
time: 190 us; the launch traced here: 189 us
  waiting for transfers between devices  75.7 us (40%)
  starting transfers between devices  68.3 us (36%)
  blocking collectives  21.8 us (11%)
  local copies, waits for them, and re-layouts  9.75 us (5%)
  Pallas kernels  8.32 us (4%)
  matrix products  3.03 us (2%)
    all_to_all x6, waiting for transfers between devices, exchange(): return lax.all_to_all(value, axis, 0, 0, tiled=True)  58.6 us
    all_to_all x6, starting transfers between devices, exchange(): return lax.all_to_all(value, axis, 0, 0, tiled=True)  41.4 us
    all_to_all x2, blocking collectives, exchange(): return lax.all_to_all(value, axis, 0, 0, tiled=True)  21.8 us
    ppermute x6, starting transfers between devices, along(): return lax.ppermute(block, GRP, moves(step, 0))  19.1 us
    ppermute x6, waiting for transfers between devices, along(): return lax.ppermute(block, GRP, moves(step, 0))  9.77 us
    ppermute x1, waiting for transfers between devices, shards(): before = lax.ppermute(same[:NZ // 2], GRP, turns(1))  4.93 us
    ppermute x1, starting transfers between devices, shards(): after = lax.ppermute(same[NZ // 2:], GRP, turns(-1))  4.9 us
  transfers between devices with their start and end apart: 14, of which 10 were waited for; matrix products, arithmetic and copies ran while one was open for 4% of the time, Pallas kernels for 0%

profile of v14, /device:TPU:8, one launch (start us, length us, event | category | flops | bytes accessed | tf_op | source)
XLA Modules:
  0.0 188.6 jit_solution(16025698595144771966)
XLA Ops:
  0.0 0.0 copy-start
  0.0 0.9 iota_compare_fusion.4
  0.9 0.8 reshape.96
  1.7 1.3 fusion.5
  2.9 0.2 fusion.26
  3.2 0.0 copy-done
  3.2 0.6 convolution_convert_fusion
  3.7 0.7 broadcast_in_dim.70
  4.4 10.3 %all-to-all-start = ((bf16[4,32,512]{2,1,0:T(8,128)(2,1)}), bf16[4,32,512]{2,1,0:T(8,128)(2,1)S(1)}, u32[]{:S(2)}, u32[]{:S(2)}) async-start(bf16[4,32,512]{2,1,0:T(8,128)(2,1)} %broadcast_in_dim.70), calls=%async_computation | async-start | bytes 262144 | tf_op jit(solution)/shard_map/all_to_all | solution.py:31
  14.7 0.0 copy-done.3
  14.7 1.0 dynamic-slice_bitcast_fusion.6
  15.7 8.3 %all-to-all-done = bf16[4,32,512]{2,1,0:T(8,128)(2,1)S(1)} async-done(((bf16[4,32,512]{2,1,0:T(8,128)(2,1)}), bf16[4,32,512]{2,1,0:T(8,128)(2,1)S(1)}, u32[]{:S(2)}, u32[]{:S(2)}) %all-to-all-start) | async-done | bytes 131104 | tf_op jit(solution)/shard_map/all_to_all | solution.py:31
  24.0 1.1 broadcast_in_dim.72
  25.1 4.3 %all-to-all-start.1 = ((bf16[8,128,512]{2,1,0:T(8,128)(2,1)}), bf16[8,128,512]{2,1,0:T(8,128)(2,1)S(1)}, u32[]{:S(2)}, u32[]{:S(2)}) async-start(bf16[8,128,512]{2,1,0:T(8,128)(2,1)} %broadcast_in_dim.72), calls=%async_computation.1 | async-start | bytes 2097152 | tf_op jit(solution)/shard_map/all_to_all | solution.py:31
  29.4 14.6 %all-to-all-done.1 = bf16[8,128,512]{2,1,0:T(8,128)(2,1)S(1)} async-done(((bf16[8,128,512]{2,1,0:T(8,128)(2,1)}), bf16[8,128,512]{2,1,0:T(8,128)(2,1)S(1)}, u32[]{:S(2)}, u32[]{:S(2)}) %all-to-all-start.1) | async-done | bytes 1048608 | tf_op jit(solution)/shard_map/all_to_all | solution.py:31
  44.0 0.0 copy-done.1
  44.0 1.3 shard_map.109
  45.3 7.6 %all-to-all-start.2 = ((bf16[16,64,224]{2,1,0:T(8,128)(2,1)}), bf16[16,64,224]{2,1,0:T(8,128)(2,1)S(1)}, u32[]{:S(2)}, u32[]{:S(2)}) async-start(bf16[16,64,224]{2,1,0:T(8,128)(2,1)} %shard_map.109), calls=%async_computation.2 | async-start | bytes 1048576 | tf_op jit(solution)/shard_map/all_to_all | solution.py:31
  52.9 0.1 eq.58
  53.0 0.8 fusion.21
  53.8 0.1 convolution_convert_fusion.1
  53.9 0.1 fusion.9.select
  54.0 0.0 copy-start.4
  54.0 2.7 %dynamic-slice_bitcast_fusion = (bf16[224,1024]{1,0:T(8,128)(2,1)}, bf16[224,1024]{1,0:T(8,128)(2,1)}, bf16[224,1024]{1,0:T(8,128)(2,1)}, bf16[224,1024]{1,0:T(8,128)(2,1)S(1)}) fusion(bf16[1,224,4096]{2,1,0:T(8,128)(2,1)} %param.21, s32[]{:T(128)S(6)} %select_n.112, s32[]{:T(128)S(6)} %select_n.111, s32[]{:T(128)S(6)} %select_n.110, s32[]{:T(128)S(6)} %select_n.109), kind=kLoop, calls=%fused_computation.11 | loop fusion | bytes 3670032 | tf_op jit(solution)/shard_map/dynamic_slice | solution.py:263
  56.8 0.0 copy-done.4
  56.8 0.8 dynamic-slice_bitcast_fusion.4
  57.6 11.6 %all-to-all-done.2.parts = bf16[16,64,224]{2,1,0:T(8,128)(2,1)S(1)} async-done(((bf16[16,64,224]{2,1,0:T(8,128)(2,1)}), bf16[16,64,224]{2,1,0:T(8,128)(2,1)S(1)}, u32[]{:S(2)}, u32[]{:S(2)}) %all-to-all-start.2) | async-done | bytes 458784 | tf_op jit(solution)/shard_map/all_to_all | solution.py:31
  69.2 1.1 shard_map.110
  70.4 5.3 %all-to-all-start.3 = ((bf16[64,24,224]{2,1,0:T(8,128)(2,1)}), bf16[64,24,224]{2,1,0:T(8,128)(2,1)S(1)}, u32[]{:S(2)}, u32[]{:S(2)}) async-start(bf16[64,24,224]{2,1,0:T(8,128)(2,1)} %bitcast.17), calls=%async_computation.3 | async-start | bytes 1572864 | tf_op jit(solution)/shard_map/all_to_all | solution.py:31
  75.7 1.9 %collective-permute-start.2 = (bf16[224,1024]{1,0:T(8,128)(2,1)}, bf16[224,1024]{1,0:T(8,128)(2,1)S(1)}, u32[]{:S(2)}, u32[]{:S(2)}) collective-permute-start(bf16[224,1024]{1,0:T(8,128)(2,1)} %get-tuple-element.55), channel_id=1, source_target_pairs={{0,64},{8,72},{16,80},{24,88},{32,96},{40,104},{48,112},{56,120},{... | collective-permute-start | bytes 1376264 | tf_op jit(solution)/shard_map/ppermute | solution.py:266
  77.6 5.1 %collective-permute-start.3 = (bf16[224,1024]{1,0:T(8,128)(2,1)}, bf16[224,1024]{1,0:T(8,128)(2,1)S(1)}, u32[]{:S(2)}, u32[]{:S(2)}) collective-permute-start(bf16[224,1024]{1,0:T(8,128)(2,1)} %get-tuple-element.56), channel_id=1, source_target_pairs={{0,192},{8,200},{16,208},{24,216},{32,224},{40,232},{48,240},{56,2... | collective-permute-start | bytes 1376264 | tf_op jit(solution)/shard_map/ppermute | solution.py:266
  82.8 0.0 copy-done.5
  82.8 0.1 reshape.100
  82.9 1.9 %collective-permute-start.4 = (bf16[1792,128]{1,0:T(8,128)(2,1)}, bf16[1792,128]{1,0:T(8,128)(2,1)}, u32[]{:S(2)}, u32[]{:S(2)}) collective-permute-start(bf16[1792,128]{1,0:T(8,128)(2,1)} %get-tuple-element.60), channel_id=1, source_target_pairs={{0,64},{8,72},{16,80},{24,88},{32,96},{40,104},{48,112},{56,120},{... | collective-permute-start | bytes 1376264 | tf_op jit(solution)/shard_map/ppermute | solution.py:266
  84.8 3.4 %collective-permute-start.5 = (bf16[1792,128]{1,0:T(8,128)(2,1)}, bf16[1792,128]{1,0:T(8,128)(2,1)}, u32[]{:S(2)}, u32[]{:S(2)}) collective-permute-start(bf16[1792,128]{1,0:T(8,128)(2,1)} %get-tuple-element.61), channel_id=1, source_target_pairs={{0,128},{8,136},{16,144},{24,152},{32,160},{40,168},{48,176},{56,1... | collective-permute-start | bytes 1376264 | tf_op jit(solution)/shard_map/ppermute | solution.py:266
  88.2 3.7 %collective-permute-start.6 = (bf16[1792,128]{1,0:T(8,128)(2,1)}, bf16[1792,128]{1,0:T(8,128)(2,1)}, u32[]{:S(2)}, u32[]{:S(2)}) collective-permute-start(bf16[1792,128]{1,0:T(8,128)(2,1)} %get-tuple-element.62), channel_id=1, source_target_pairs={{0,192},{8,200},{16,208},{24,216},{32,224},{40,232},{48,240},{56,2... | collective-permute-start | bytes 1376264 | tf_op jit(solution)/shard_map/ppermute | solution.py:266
  91.9 8.1 %all-to-all-done.3 = bf16[64,24,224]{2,1,0:T(8,128)(2,1)S(1)} async-done(((bf16[64,24,224]{2,1,0:T(8,128)(2,1)}), bf16[64,24,224]{2,1,0:T(8,128)(2,1)S(1)}, u32[]{:S(2)}, u32[]{:S(2)}) %all-to-all-start.3) | async-done | bytes 688160 | tf_op jit(solution)/shard_map/all_to_all | solution.py:31
  100.0 0.1 fusion.25
  100.1 0.0 collective-permute-done.2.block1
  100.1 3.0 %collective-permute-start = (bf16[2,384,224]{2,1,0:T(8,128)(2,1)S(1)}, bf16[2,384,224]{2,1,0:T(8,128)(2,1)S(1)}, u32[]{:S(2)}, u32[]{:S(2)}) collective-permute-start(bf16[2,384,224]{2,1,0:T(8,128)(2,1)S(1)} %bitcast.72), channel_id=1, source_target_pairs={{0,8},{8,16},{16,24},{24,32},{32,40},{40,48},{48,56},{56,0},{64,72... | collective-permute-start | bytes 1032200 | tf_op jit(solution)/shard_map/ppermute | solution.py:283
  103.0 0.7 collective-permute-done.3.block3
  103.8 4.9 %collective-permute-start.1 = (bf16[2,384,224]{2,1,0:T(8,128)(2,1)S(1)}, bf16[2,384,224]{2,1,0:T(8,128)(2,1)S(1)}, u32[]{:S(2)}, u32[]{:S(2)}) collective-permute-start(bf16[2,384,224]{2,1,0:T(8,128)(2,1)S(1)} %bitcast.71), channel_id=1, source_target_pairs={{0,56},{8,0},{16,8},{24,16},{32,24},{40,32},{48,40},{56,48},{64,12... | collective-permute-start | bytes 1032200 | tf_op jit(solution)/shard_map/ppermute | solution.py:284
  108.7 0.1 pad_add_fusion.place
  108.8 4.9 %collective-permute-done.before = bf16[2,384,224]{2,1,0:T(8,128)(2,1)S(1)} collective-permute-done((bf16[2,384,224]{2,1,0:T(8,128)(2,1)S(1)}, bf16[2,384,224]{2,1,0:T(8,128)(2,1)S(1)}, u32[]{:S(2)}, u32[]{:S(2)}) %collective-permute-start) | collective-permute-done | bytes 344096 | tf_op jit(solution)/shard_map/ppermute | solution.py:283
  113.7 2.3 %collective-permute-done.1.after = bf16[2,384,224]{2,1,0:T(8,128)(2,1)S(1)} collective-permute-done((bf16[2,384,224]{2,1,0:T(8,128)(2,1)S(1)}, bf16[2,384,224]{2,1,0:T(8,128)(2,1)S(1)}, u32[]{:S(2)}, u32[]{:S(2)}) %collective-permute-start.1) | collective-permute-done | bytes 344096 | tf_op jit(solution)/shard_map/ppermute | solution.py:284
  116.0 0.0 collective-permute-done.4
  116.0 0.0 collective-permute-done.5
  116.0 0.0 collective-permute-done.6
  116.0 3.1 %shard_map.111 = bf16[4,400,128]{2,1,0:T(8,128)(2,1)S(1)} custom-call(s32[2]{0:T(128)S(1)} %pad_add_fusion.place, bf16[4,384,224]{2,1,0:T(8,128)(2,1)S(1)} %bitcast.65, bf16[2,384,224]{2,1,0:T(8,128)(2,1)S(1)} %collective-permute-done.before, bf16[2,384,224]{2,1,0:T(8,128)(2,1)S(1)} %collective-permute-done.1.after, f32[8,224]{1,0:T(8,128)S(1)} %pad_maximum_fusion.gain, ...), custom_call_target="tpu_custom_call" | custom-call | flops 704643072 | bytes 6291456 | tf_op jit(solution)/shard_map/pallas_call | solution.py:136
  119.1 10.5 %all_to_all.40.parts = bf16[4,400,128]{2,1,0:T(8,128)(2,1)S(1)} all-to-all(bf16[4,400,128]{2,1,0:T(8,128)(2,1)S(1)} %shard_map.111), channel_id=1, replica_groups=mesh['pool'=2,'x'=4,'zpair'=4,'member'=2,'tp'=8] {'x'}, dimensions={0} | all-to-all | bytes 819200 | tf_op jit(solution)/shard_map/all_to_all | solution.py:31
  129.6 1.1 shard_map.112
  130.7 6.7 %all-to-all-start.5 = ((bf16[8,384,128]{2,1,0:T(8,128)(2,1)}), bf16[8,384,128]{2,1,0:T(8,128)(2,1)S(1)}, u32[]{:S(2)}, u32[]{:S(2)}) async-start(bf16[8,384,128]{2,1,0:T(8,128)(2,1)} %shard_map.112), calls=%async_computation.5 | async-start | bytes 1572864 | tf_op jit(solution)/shard_map/all_to_all | solution.py:31
  137.4 3.0 %collective-permute-start.7 = (bf16[224,1024]{1,0:T(8,128)(2,1)}, bf16[224,1024]{1,0:T(8,128)(2,1)S(1)}, u32[]{:S(2)}, u32[]{:S(2)}) collective-permute-start(bf16[224,1024]{1,0:T(8,128)(2,1)} %get-tuple-element.67), channel_id=1, source_target_pairs={{0,128},{8,136},{16,144},{24,152},{32,160},{40,168},{48,176},{56,1... | collective-permute-start | bytes 1376264 | tf_op jit(solution)/shard_map/ppermute | solution.py:266
  140.4 9.0 %collective-permute-done.7.block2 = bf16[224,1024]{1,0:T(8,128)(2,1)S(1)} collective-permute-done((bf16[224,1024]{1,0:T(8,128)(2,1)}, bf16[224,1024]{1,0:T(8,128)(2,1)S(1)}, u32[]{:S(2)}, u32[]{:S(2)}) %collective-permute-start.7) | collective-permute-done | bytes 458784 | tf_op jit(solution)/shard_map/ppermute | solution.py:266
  149.5 7.2 %all-to-all-done.5.act = bf16[8,384,128]{2,1,0:T(8,128)(2,1)S(1)} async-done(((bf16[8,384,128]{2,1,0:T(8,128)(2,1)}), bf16[8,384,128]{2,1,0:T(8,128)(2,1)S(1)}, u32[]{:S(2)}, u32[]{:S(2)}) %all-to-all-start.5) | async-done | bytes 786464 | tf_op jit(solution)/shard_map/all_to_all | solution.py:31
  156.6 1.7 shard_map.113
  158.3 11.3 %all_to_all.41 = bf16[4,224,384]{2,1,0:T(8,128)(2,1)S(1)} all-to-all(bf16[4,224,384]{2,1,0:T(8,128)(2,1)S(1)} %shard_map.113), channel_id=1, replica_groups=mesh['pool'=2,'x'=4,'zpair'=4,'member'=2,'tp'=8] {'x'}, dimensions={0} | all-to-all | bytes 1376256 | tf_op jit(solution)/shard_map/all_to_all | solution.py:31
  169.7 0.1 reduce_sum.32
  169.8 0.8 copy.13
  170.6 7.2 %all-to-all-start.7 = ((bf16[16,24,224]{2,1,0:T(8,128)(2,1)}), bf16[16,24,224]{2,1,0:T(8,128)(2,1)S(1)}, u32[]{:S(2)}, u32[]{:S(2)}) async-start(bf16[16,24,224]{2,1,0:T(8,128)(2,1)} %bitcast.26), calls=%async_computation.7 | async-start | bytes 393216 | tf_op jit(solution)/shard_map/all_to_all | solution.py:31
  177.9 0.8 fusion.22
  178.6 8.8 %all-to-all-done.7 = bf16[16,24,224]{2,1,0:T(8,128)(2,1)S(1)} async-done(((bf16[16,24,224]{2,1,0:T(8,128)(2,1)}), bf16[16,24,224]{2,1,0:T(8,128)(2,1)S(1)}, u32[]{:S(2)}, u32[]{:S(2)}) %all-to-all-start.7) | async-done | bytes 172064 | tf_op jit(solution)/shard_map/all_to_all | solution.py:31
  187.5 0.2 convolution_bitcast_fusion.1
  187.7 0.8 fusion.2
  (12 shorter events, 0.1 us)
Async XLA Ops:
  0.0 3.2 %copy-start = (bf16[32,32,256]{2,1,0:T(8,128)(2,1)S(1)}, bf16[32,32,256]{2,1,0:T(8,128)(2,1)}, u32[]{:S(2)}) copy-start(bf16[32,32,256]{2,1,0:T(8,128)(2,1)} %param.13) | copy-start | bytes 1572868
  0.0 14.7 %copy-start.3 = (bf16[1,7168,128]{2,1,0:T(8,128)(2,1)S(1)}, bf16[1,7168,128]{2,1,0:T(8,128)(2,1)}, u32[]{:S(2)}) copy-start(bf16[1,7168,128]{2,1,0:T(8,128)(2,1)} %param.20) | copy-start | bytes 5505028
  4.4 19.6 %all-to-all-start = ((bf16[4,32,512]{2,1,0:T(8,128)(2,1)}), bf16[4,32,512]{2,1,0:T(8,128)(2,1)S(1)}, u32[]{:S(2)}, u32[]{:S(2)}) async-start(bf16[4,32,512]{2,1,0:T(8,128)(2,1)} %broadcast_in_dim.70), calls=%async_computation | async-start | bytes 262144 | tf_op jit(solution)/shard_map/all_to_all | solution.py:31
  15.7 28.3 %copy-start.1 = (bf16[512,224]{0,1:T(8,128)(2,1)S(1)}, bf16[512,224]{0,1:T(8,128)(2,1)}, u32[]{:S(2)}) copy-start(bf16[512,224]{0,1:T(8,128)(2,1)} %param.15) | copy-start | bytes 688132
  25.1 18.9 %all-to-all-start.1 = ((bf16[8,128,512]{2,1,0:T(8,128)(2,1)}), bf16[8,128,512]{2,1,0:T(8,128)(2,1)S(1)}, u32[]{:S(2)}, u32[]{:S(2)}) async-start(bf16[8,128,512]{2,1,0:T(8,128)(2,1)} %broadcast_in_dim.72), calls=%async_computation.1 | async-start | bytes 2097152 | tf_op jit(solution)/shard_map/all_to_all | solution.py:31
  45.3 23.9 %all-to-all-start.2 = ((bf16[16,64,224]{2,1,0:T(8,128)(2,1)}), bf16[16,64,224]{2,1,0:T(8,128)(2,1)S(1)}, u32[]{:S(2)}, u32[]{:S(2)}) async-start(bf16[16,64,224]{2,1,0:T(8,128)(2,1)} %shard_map.109), calls=%async_computation.2 | async-start | bytes 1048576 | tf_op jit(solution)/shard_map/all_to_all | solution.py:31
  54.0 2.7 %copy-start.4 = (bf16[1,7168,128]{2,1,0:T(8,128)(2,1)S(1)}, bf16[1,7168,128]{2,1,0:T(8,128)(2,1)}, u32[]{:S(2)}) copy-start(bf16[1,7168,128]{2,1,0:T(8,128)(2,1)} %param.20) | copy-start | bytes 5505028
  56.8 12.5 %copy-start.2 = (bf16[64,224]{1,0:T(8,128)(2,1)S(1)}, bf16[64,224]{1,0:T(8,128)(2,1)}, u32[]{:S(2)}) copy-start(bf16[64,224]{1,0:T(8,128)(2,1)} %residual.1) | copy-start | bytes 86020
  57.6 25.2 %copy-start.5 = (f32[7168]{0:T(1024)S(1)}, f32[7168]{0:T(1024)}, u32[]{:S(2)}) copy-start(f32[7168]{0:T(1024)} %param.17) | copy-start | bytes 86020
  70.4 29.6 %all-to-all-start.3 = ((bf16[64,24,224]{2,1,0:T(8,128)(2,1)}), bf16[64,24,224]{2,1,0:T(8,128)(2,1)S(1)}, u32[]{:S(2)}, u32[]{:S(2)}) async-start(bf16[64,24,224]{2,1,0:T(8,128)(2,1)} %bitcast.17), calls=%async_computation.3 | async-start | bytes 1572864 | tf_op jit(solution)/shard_map/all_to_all | solution.py:31
  75.7 24.4 %collective-permute-start.2 = (bf16[224,1024]{1,0:T(8,128)(2,1)}, bf16[224,1024]{1,0:T(8,128)(2,1)S(1)}, u32[]{:S(2)}, u32[]{:S(2)}) collective-permute-start(bf16[224,1024]{1,0:T(8,128)(2,1)} %get-tuple-element.55), channel_id=1, source_target_pairs={{0,64},{8,72},{16,80},{24,88},{32,96},{40,104},{48,112},{56,120},{... | collective-permute-start | bytes 1376264 | tf_op jit(solution)/shard_map/ppermute | solution.py:266
  77.6 26.2 %collective-permute-start.3 = (bf16[224,1024]{1,0:T(8,128)(2,1)}, bf16[224,1024]{1,0:T(8,128)(2,1)S(1)}, u32[]{:S(2)}, u32[]{:S(2)}) collective-permute-start(bf16[224,1024]{1,0:T(8,128)(2,1)} %get-tuple-element.56), channel_id=1, source_target_pairs={{0,192},{8,200},{16,208},{24,216},{32,224},{40,232},{48,240},{56,2... | collective-permute-start | bytes 1376264 | tf_op jit(solution)/shard_map/ppermute | solution.py:266
  82.9 33.1 %collective-permute-start.4 = (bf16[1792,128]{1,0:T(8,128)(2,1)}, bf16[1792,128]{1,0:T(8,128)(2,1)}, u32[]{:S(2)}, u32[]{:S(2)}) collective-permute-start(bf16[1792,128]{1,0:T(8,128)(2,1)} %get-tuple-element.60), channel_id=1, source_target_pairs={{0,64},{8,72},{16,80},{24,88},{32,96},{40,104},{48,112},{56,120},{... | collective-permute-start | bytes 1376264 | tf_op jit(solution)/shard_map/ppermute | solution.py:266
  84.8 31.2 %collective-permute-start.5 = (bf16[1792,128]{1,0:T(8,128)(2,1)}, bf16[1792,128]{1,0:T(8,128)(2,1)}, u32[]{:S(2)}, u32[]{:S(2)}) collective-permute-start(bf16[1792,128]{1,0:T(8,128)(2,1)} %get-tuple-element.61), channel_id=1, source_target_pairs={{0,128},{8,136},{16,144},{24,152},{32,160},{40,168},{48,176},{56,1... | collective-permute-start | bytes 1376264 | tf_op jit(solution)/shard_map/ppermute | solution.py:266
  88.2 27.8 %collective-permute-start.6 = (bf16[1792,128]{1,0:T(8,128)(2,1)}, bf16[1792,128]{1,0:T(8,128)(2,1)}, u32[]{:S(2)}, u32[]{:S(2)}) collective-permute-start(bf16[1792,128]{1,0:T(8,128)(2,1)} %get-tuple-element.62), channel_id=1, source_target_pairs={{0,192},{8,200},{16,208},{24,216},{32,224},{40,232},{48,240},{56,2... | collective-permute-start | bytes 1376264 | tf_op jit(solution)/shard_map/ppermute | solution.py:266
  100.1 13.6 %collective-permute-start = (bf16[2,384,224]{2,1,0:T(8,128)(2,1)S(1)}, bf16[2,384,224]{2,1,0:T(8,128)(2,1)S(1)}, u32[]{:S(2)}, u32[]{:S(2)}) collective-permute-start(bf16[2,384,224]{2,1,0:T(8,128)(2,1)S(1)} %bitcast.72), channel_id=1, source_target_pairs={{0,8},{8,16},{16,24},{24,32},{32,40},{40,48},{48,56},{56,0},{64,72... | collective-permute-start | bytes 1032200 | tf_op jit(solution)/shard_map/ppermute | solution.py:283
  103.8 12.2 %collective-permute-start.1 = (bf16[2,384,224]{2,1,0:T(8,128)(2,1)S(1)}, bf16[2,384,224]{2,1,0:T(8,128)(2,1)S(1)}, u32[]{:S(2)}, u32[]{:S(2)}) collective-permute-start(bf16[2,384,224]{2,1,0:T(8,128)(2,1)S(1)} %bitcast.71), channel_id=1, source_target_pairs={{0,56},{8,0},{16,8},{24,16},{32,24},{40,32},{48,40},{56,48},{64,12... | collective-permute-start | bytes 1032200 | tf_op jit(solution)/shard_map/ppermute | solution.py:284
  130.7 25.9 %all-to-all-start.5 = ((bf16[8,384,128]{2,1,0:T(8,128)(2,1)}), bf16[8,384,128]{2,1,0:T(8,128)(2,1)S(1)}, u32[]{:S(2)}, u32[]{:S(2)}) async-start(bf16[8,384,128]{2,1,0:T(8,128)(2,1)} %shard_map.112), calls=%async_computation.5 | async-start | bytes 1572864 | tf_op jit(solution)/shard_map/all_to_all | solution.py:31
  137.4 12.1 %collective-permute-start.7 = (bf16[224,1024]{1,0:T(8,128)(2,1)}, bf16[224,1024]{1,0:T(8,128)(2,1)S(1)}, u32[]{:S(2)}, u32[]{:S(2)}) collective-permute-start(bf16[224,1024]{1,0:T(8,128)(2,1)} %get-tuple-element.67), channel_id=1, source_target_pairs={{0,128},{8,136},{16,144},{24,152},{32,160},{40,168},{48,176},{56,1... | collective-permute-start | bytes 1376264 | tf_op jit(solution)/shard_map/ppermute | solution.py:266
  170.6 16.9 %all-to-all-start.7 = ((bf16[16,24,224]{2,1,0:T(8,128)(2,1)}), bf16[16,24,224]{2,1,0:T(8,128)(2,1)S(1)}, u32[]{:S(2)}, u32[]{:S(2)}) async-start(bf16[16,24,224]{2,1,0:T(8,128)(2,1)} %bitcast.26), calls=%async_computation.7 | async-start | bytes 393216 | tf_op jit(solution)/shard_map/all_to_all | solution.py:31
